TPU v7x, 32 devices: a whole 2x2x4 slice. The times are simulated.
32 devices in a mesh: row: 8 (over z, x), col: 4 (over y, core).
Axes of the slice: x: 2, y: 2, z: 4, core: 2. Of those that a mesh axis runs over, the one named last changes fastest.
Arguments:
- cam_jac: float32 [128, 18, 512], P(('row', 'col')), may hold values from -1 to 1
- land_jac: float32 [128, 6, 512], P(('row', 'col')), may hold values from -5 to 5
- resid: float32 [128, 2, 512], P(('row', 'col')), may hold values from -20 to 20
- obs_cam: int32 [128, 512], P(('row', 'col')), may hold values from 0 to 127
- obs_land: int32 [128, 512], P(('row', 'col')), may hold values from 0 to 127
- pairs: int32 [128, 2], P(('row', 'col')), may hold values from 0 to 31, as said below
- cam_damp: float32 [18432], P(('row', 'col')), may hold values from 1 to 10
Outputs:
- cam_step: float32 [18432], P(('row', 'col'))
- land_step: float32 [128, 3, 128], P(('row', 'col'))
Inputs may be any that keep to these rules, and one draw needn't show every extreme that they name: `pairs`: clusters are laid out device by device, 4 a device, devices in order of row, then col. A cluster held at grid row r and grid column c is seen by a first group in [r * 4, (r + 1) * 4) and a different second group in [c * 8, (c + 1) * 8).
All inputs are finite; a program needn't handle non-finite values.
Results may differ from a plain program's by a relative error of at most 0.0003.
Values sent between devices are 32-bit elements; how exact they have to be, the bound alone decides.
No kernel may reach another device: no remote copies, remote signals or barrier semaphores. Data moves between devices by JAX's collectives and lax.ppermute only.
A program may use at most 384 MiB of HBM per device.

v0:
```python
import jax
import jax.numpy as jnp
from jax import lax
from jax.sharding import PartitionSpec as P

G = 32
CAM = 64
LM = 128
ITERS = 2


DAMPING = 1.0
HIGHEST = lax.Precision.HIGHEST


def cholesky_three(normal):
    root_first = jnp.sqrt(normal[0])
    inv_first = 1.0 / root_first
    low_one = normal[1] * inv_first
    low_two = normal[2] * inv_first
    inv_second = 1.0 / jnp.sqrt(normal[4] - low_one * low_one)
    low_three = (normal[5] - low_two * low_one) * inv_second
    inv_third = 1.0 / jnp.sqrt(normal[8] - low_two * low_two - low_three * low_three)
    return jnp.stack([inv_first, low_one, low_two, inv_second, low_three, inv_third])


def lower_solve(factor, first, second, third):
    out_one = first * factor[0]
    out_two = (second - factor[1] * out_one) * factor[3]
    out_three = (third - factor[2] * out_one - factor[4] * out_two) * factor[5]
    return jnp.stack([out_one, out_two, out_three])


def upper_solve(factor, first, second, third):
    out_three = third * factor[5]
    out_two = (second - factor[4] * out_three) * factor[3]
    out_one = (first - factor[1] * out_two - factor[2] * out_three) * factor[0]
    return jnp.stack([out_one, out_two, out_three])


def cluster_schur(cam_jac, land_jac, resid, obs_cam, obs_land):
    count = obs_cam.shape[0]
    width = CAM * 9
    cam_rows = cam_jac.reshape(2, 9, count)
    land_rows = land_jac.reshape(2, 3, count)
    coupled = (
        cam_rows[0][:, None, :] * land_rows[0][None] + cam_rows[1][:, None, :] * land_rows[1][None]
    )
    land_outer = (
        land_rows[0][:, None, :] * land_rows[0][None]
        + land_rows[1][:, None, :] * land_rows[1][None]
    ).reshape(9, count)
    cam_outer = (
        cam_rows[0][:, None, :] * cam_rows[0][None] + cam_rows[1][:, None, :] * cam_rows[1][None]
    ).reshape(81, count)
    cam_grad = cam_rows[0] * resid[0] + cam_rows[1] * resid[1]
    land_grad = land_rows[0] * resid[0] + land_rows[1] * resid[1]
    land_onehot = (obs_land[None, :] == jnp.arange(LM, dtype=jnp.int32)[:, None]).astype(
        jnp.float32
    )
    cam_onehot = (obs_cam[None, :] == jnp.arange(2 * CAM, dtype=jnp.int32)[:, None]).astype(
        jnp.float32
    )
    land_normal = jnp.dot(land_outer, land_onehot.T, precision=HIGHEST) + DAMPING * jnp.eye(
        3, dtype=jnp.float32
    ).reshape(9, 1)
    land_total = jnp.dot(land_grad, land_onehot.T, precision=HIGHEST)
    cam_normal = jnp.dot(cam_outer, cam_onehot.T, precision=HIGHEST)
    cam_total = jnp.dot(cam_grad, cam_onehot.T, precision=HIGHEST)
    factor = cholesky_three(land_normal)
    obs_factor = jnp.dot(factor, land_onehot, precision=HIGHEST)
    solved = jnp.stack(
        [
            lower_solve(obs_factor, coupled[param, 0], coupled[param, 1], coupled[param, 2])
            for param in range(9)
        ]
    )
    spread = solved.reshape(27, 1, count) * land_onehot[None]
    placed = jnp.einsum("co,xlo->cxl", cam_onehot, spread, precision=HIGHEST)
    coupling = placed.reshape(2 * width, 3 * LM)
    tvector = lower_solve(factor, land_total[0], land_total[1], land_total[2]).reshape(3 * LM)
    blocks = cam_normal.T.reshape(2, CAM, 9, 9)
    eye_cam = jnp.eye(CAM, dtype=jnp.float32)
    upper_first = (eye_cam[:, None, :, None] * blocks[0][:, :, None, :]).reshape(width, width)
    upper_second = (eye_cam[:, None, :, None] * blocks[1][:, :, None, :]).reshape(width, width)
    coupling_first = coupling[:width]
    coupling_second = coupling[width:]
    diag_first = upper_first - jnp.dot(coupling_first, coupling_first.T, precision=HIGHEST)
    cross = -jnp.dot(coupling_first, coupling_second.T, precision=HIGHEST)
    diag_second = upper_second - jnp.dot(coupling_second, coupling_second.T, precision=HIGHEST)
    right = -cam_total.T.reshape(2 * width) + jnp.dot(coupling, tvector, precision=HIGHEST)
    return (diag_first, cross, diag_second, right[:width], right[width:], coupling, tvector, factor)


def add_block(target, block, row_start, col_start):
    current = lax.dynamic_slice(target, (row_start, col_start), block.shape)
    return lax.dynamic_update_slice(target, current + block, (row_start, col_start))


def add_segment(target, piece, start):
    current = lax.dynamic_slice_in_dim(target, start, piece.shape[0], 0)
    return lax.dynamic_update_slice_in_dim(target, current + piece, start, 0)


def whole_vector(shard_vector):
    segment = lax.all_gather(shard_vector, "col", axis=0, tiled=True)
    whole = lax.all_gather(segment, "row", axis=0, tiled=True)
    return whole


def residual_weight(residual, precon_res):
    return lax.psum(jnp.sum(residual * precon_res), ("row", "col"))


def per_device(cam_jac, land_jac, resid, obs_cam, obs_land, pairs, cam_damp):
    n_row = lax.axis_size("row")
    n_col = lax.axis_size("col")
    row_pos = lax.axis_index("row")
    col_pos = lax.axis_index("col")
    width = CAM * 9
    total = G * width
    rows_seg = total // n_row
    cols_seg = total // n_col
    shard = total // (n_row * n_col)
    grid = jnp.zeros((rows_seg, cols_seg), jnp.float32)
    row_stack = jnp.zeros((rows_seg, width), jnp.float32)
    row_right = jnp.zeros((rows_seg,), jnp.float32)
    col_stack = jnp.zeros((cols_seg, width), jnp.float32)
    col_right = jnp.zeros((cols_seg,), jnp.float32)
    kept = []
    for local in range(cam_jac.shape[0]):
        diag_first, cross, diag_second, right_first, right_second, coupling, tvector, factor = (
            cluster_schur(
                cam_jac[local], land_jac[local], resid[local], obs_cam[local], obs_land[local]
            )
        )
        first = pairs[local, 0]
        second = pairs[local, 1]
        row_start = first * width - row_pos * rows_seg
        col_start = second * width - col_pos * cols_seg
        grid = add_block(grid, cross, row_start, col_start)
        row_stack = add_block(row_stack, diag_first, row_start, 0)
        row_right = add_segment(row_right, right_first, row_start)
        col_stack = add_block(col_stack, diag_second, col_start, 0)
        col_right = add_segment(col_right, right_second, col_start)
        kept.append((coupling, tvector, factor, first, second))
    col_sum, col_right = lax.psum((col_stack, col_right), "row")
    offset = row_pos * rows_seg - col_pos * cols_seg
    on_diag = ((offset >= 0) & (offset + rows_seg <= cols_seg)).astype(jnp.float32)
    start = jnp.clip(offset, 0, cols_seg - rows_seg)
    row_stack = row_stack + on_diag * lax.dynamic_slice_in_dim(col_sum, start, rows_seg, 0)
    row_right = row_right + on_diag * lax.dynamic_slice_in_dim(col_right, start, rows_seg, 0)
    my_rows, my_right = (
        lax.psum_scatter(row_stack, "col", scatter_dimension=0, tiled=True),
        lax.psum_scatter(row_right, "col", scatter_dimension=0, tiled=True),
    )
    first_index = row_pos * rows_seg + col_pos * shard
    group_start = first_index // width * width
    inner = first_index - group_start
    diag_values = jnp.diagonal(lax.dynamic_slice_in_dim(my_rows, inner, shard, 1))
    precond = 1.0 / (diag_values + cam_damp)
    solution = jnp.zeros((shard,), jnp.float32)
    residual = my_right
    precon_res = precond * residual
    direction = precon_res
    norm_now = residual_weight(residual, precon_res)
    for step in range(ITERS):
        whole = whole_vector(direction)
        col_part = lax.dynamic_slice_in_dim(whole, col_pos * cols_seg, cols_seg)
        row_part = lax.dynamic_slice_in_dim(whole, row_pos * rows_seg, rows_seg)
        group_part = lax.dynamic_slice_in_dim(whole, group_start, width)
        forward = jnp.dot(grid, col_part, precision=HIGHEST)
        backward = jnp.dot(row_part, grid, precision=HIGHEST)
        partial_sum = jnp.zeros((total,), jnp.float32)
        partial_sum = add_segment(partial_sum, forward, row_pos * rows_seg)
        partial_sum = add_segment(partial_sum, backward, col_pos * cols_seg)
        image = lax.psum_scatter(partial_sum, ("row", "col"), scatter_dimension=0, tiled=True)
        image = image + jnp.dot(my_rows, group_part, precision=HIGHEST) + cam_damp * direction
        alpha = norm_now / lax.psum(jnp.sum(direction * image), ("row", "col"))
        solution = solution + alpha * direction
        residual = residual - alpha * image
        if step + 1 < ITERS:
            precon_res = precond * residual
            norm_next = residual_weight(residual, precon_res)
            direction = precon_res + norm_next / norm_now * direction
            norm_now = norm_next
    whole_solution = whole_vector(solution)
    steps_out = []
    for coupling, tvector, factor, first, second in kept:
        first_part = lax.dynamic_slice_in_dim(whole_solution, first * width, width)
        second_part = lax.dynamic_slice_in_dim(whole_solution, second * width, width)
        camera_part = jnp.concatenate([first_part, second_part])
        summed = (tvector + jnp.dot(camera_part, coupling, precision=HIGHEST)).reshape(3, LM)
        steps_out.append(-upper_solve(factor, summed[0], summed[1], summed[2]))
    return (solution, jnp.stack(steps_out))


def solution(mesh):
    in_specs = (
        P(("row", "col"), None, None),
        P(("row", "col"), None, None),
        P(("row", "col"), None, None),
        P(("row", "col"), None),
        P(("row", "col"), None),
        P(("row", "col"), None),
        P(("row", "col")),
    )
    out_specs = (P(("row", "col")), P(("row", "col"), None, None))
    return jax.shard_map(
        per_device, mesh=mesh, in_specs=in_specs, out_specs=out_specs, check_vma=False
    )
```

profile of v0, /device:TPU:0, one launch (start us, length us, event | category | flops | bytes accessed | tf_op | source)
XLA Modules:
  0.0 1401.5 jit_solution(12219204302558757887)
XLA Ops:
  62.6 51.3 %broadcast_multiply_fusion = (f32[64,9,64,9]{3,2,1,0:T(8,128)}, f32[64,9,64,9]{3,2,1,0:T(8,128)}, f32[64,9,64,9]{3,2,1,0:T(8,128)}, f32[64,9,64,9]{3,2,1,0:T(8,1...) fusion(f32[64,9,9]{2,1,0:T(8,128)S(1)} %copy.112, ...), kind=kLoop, calls=%fused_computation.1 | loop fusion | flops 2654208 | bytes 10799104 | tf_op jit(solution)/shard_map/mul | solution.py:85
  114.0 14.0 mul.2804
  132.5 14.7 %mul.2808 = f32[576,576]{1,0:T(8,128)} reshape(f32[64,9,64,9]{3,2,1,0:T(8,128)} %get-tuple-element.260) | data formatting | bytes 2654208 | tf_op jit(solution)/shard_map/mul | solution.py:85
  185.9 14.7 %mul.2812 = f32[576,576]{1,0:T(8,128)} reshape(f32[64,9,64,9]{3,2,1,0:T(8,128)} %get-tuple-element.261) | data formatting | bytes 2654208 | tf_op jit(solution)/shard_map/mul | solution.py:85
  220.8 14.7 %mul.2816 = f32[576,576]{1,0:T(8,128)} reshape(f32[64,9,64,9]{3,2,1,0:T(8,128)} %get-tuple-element.255) | data formatting | bytes 2654208 | tf_op jit(solution)/shard_map/mul | solution.py:85
  258.2 15.0 %mul.2769 = f32[576,576]{1,0:T(8,128)S(1)} reshape(f32[64,9,64,9]{3,2,1,0:T(8,128)} %get-tuple-element.262) | data formatting | bytes 2654208 | tf_op jit(solution)/shard_map/mul | solution.py:84
  276.7 14.3 %mul.2779 = f32[576,576]{1,0:T(8,128)S(1)} reshape(f32[64,9,64,9]{3,2,1,0:T(8,128)} %get-tuple-element.256) | data formatting | bytes 2654208 | tf_op jit(solution)/shard_map/mul | solution.py:84
  327.7 14.9 %mul.2789 = f32[576,576]{1,0:T(8,128)} reshape(f32[64,9,64,9]{3,2,1,0:T(8,128)} %get-tuple-element.257) | data formatting | bytes 2654208 | tf_op jit(solution)/shard_map/mul | solution.py:84
  361.7 14.7 %mul.2799 = f32[576,576]{1,0:T(8,128)} reshape(f32[64,9,64,9]{3,2,1,0:T(8,128)} %get-tuple-element.258) | data formatting | bytes 2654208 | tf_op jit(solution)/shard_map/mul | solution.py:84
  395.5 191.4 %all-reduce.11.cloned.1.call-done = f32[4608,576]{0,1:T(8,128)} async-done(((f32[4608,576]{0,1:T(8,128)}), f32[4608,576]{0,1:T(8,128)}) %all-reduce.11.cloned.1.call-update) | async-done | bytes 10616848 | tf_op jit(solution)/shard_map/psum | solution.py:147
  631.4 14.0 %broadcast_in_dim.16 = f32[2304,4608]{1,0:T(8,128)} broadcast(f32[]{:T(128)} %constant.21.clone.1), dimensions={} | broadcast | bytes 42467332 | tf_op jit(solution)/shard_map/broadcast_in_dim | solution.py:125
  708.3 34.6 %psum.42 = f32[4608]{0:T(1024)S(1)} all-reduce(f32[4608]{0:T(1024)S(1)} %get-tuple-element.271), channel_id=1, replica_groups=mesh['row'=8,'col'=4] {'row'}, use_global_device_ids=true, to_apply=%region_0.0 | all-reduce | flops 4608 | bytes 36864 | tf_op jit(solution)/shard_map/psum | solution.py:147
  770.2 30.6 %all-gather = f32[8,1,2304]{2,1,0:T(1,128)S(1)} all-gather(f32[1,1,2304]{2,1,0:T(1,128)S(1)} %reshape.829), channel_id=1, replica_groups=mesh['row'=8,'col'=4] {'row'}, dimensions={0}, use_global_device_ids=true | all-gather | bytes 82944 | tf_op jit(solution)/shard_map/all_gather | solution.py:107
  801.0 39.7 %convolution_reduce_fusion.3 = f32[2304]{0:T(1024)S(1)} fusion(f32[2304,4608]{1,0:T(8,128)} %dynamic_update_slice.91, f32[4608,1]{0,1:T(1,128)S(1)} %reshape.853), kind=kOutput, calls=%fused_computation.41 | convolution fusion | flops 127401984 | bytes 42494976 | tf_op jit(solution)/shard_map/dot_general | solution.py:172
  840.7 25.3 %convolution_reduce_fusion.1 = f32[4608]{0:T(1024)S(1)} fusion(f32[2304,1]{0,1:T(1,128)S(1)} %reshape.855, f32[2304,4608]{1,0:T(8,128)} %dynamic_update_slice.91), kind=kOutput, calls=%fused_computation.39 | convolution fusion | flops 127401984 | bytes 42494976 | tf_op jit(solution)/shard_map/dot_general | solution.py:173
  869.0 114.4 %all-reduce.13.cloned.1.call-done = f32[18432]{0:T(1024)} async-done(((f32[18432]{0:T(1024)}), f32[18432]{0:T(1024)}) %all-reduce.13.cloned.1.call-update) | async-done | bytes 73744
  984.8 42.3 %all-reduce.6 = (f32[]{:T(128)}, f32[]{:T(128)}) all-reduce(f32[]{:T(128)} %get-tuple-element.9, f32[]{:T(128)} %get-tuple-element.8), channel_id=1, replica_groups=mesh['row'=8,'col'=4] {'row','col'}, use_global_device_ids=true, to_apply=%region_5.6 | all-reduce | flops 2 | bytes 16 | tf_op jit(solution)/shard_map/psum | solution.py:112
  1029.0 40.4 %psum.46 = f32[]{:T(128)} all-reduce(f32[]{:T(128)} %multiply_reduce_fusion), channel_id=1, replica_groups=mesh['row'=8,'col'=4] {'row','col'}, use_global_device_ids=true, to_apply=%region_10.11 | all-reduce | flops 1 | bytes 8 | tf_op jit(solution)/shard_map/psum | solution.py:112
  1081.2 30.6 %all-gather.1 = f32[8,1,2304]{2,1,0:T(1,128)S(1)} all-gather(f32[1,1,2304]{2,1,0:T(1,128)S(1)} %reshape.831), channel_id=1, replica_groups=mesh['row'=8,'col'=4] {'row'}, dimensions={0}, use_global_device_ids=true | all-gather | bytes 82944 | tf_op jit(solution)/shard_map/all_gather | solution.py:107
  1112.0 39.3 %convolution_reduce_fusion.2 = f32[2304]{0:T(1024)S(1)} fusion(f32[2304,4608]{1,0:T(8,128)} %dynamic_update_slice.91, f32[4608,1]{0,1:T(1,128)S(1)} %reshape.859), kind=kOutput, calls=%fused_computation.40 | convolution fusion | flops 127401984 | bytes 42494976 | tf_op jit(solution)/shard_map/dot_general | solution.py:172
  1151.3 25.2 %convolution_reduce_fusion = f32[4608]{0:T(1024)S(1)} fusion(f32[2304,1]{0,1:T(1,128)S(1)} %reshape.861, f32[2304,4608]{1,0:T(8,128)} %dynamic_update_slice.91), kind=kOutput, calls=%fused_computation.38 | convolution fusion | flops 127401984 | bytes 42494976 | tf_op jit(solution)/shard_map/dot_general | solution.py:173
  1179.5 116.8 %all-reduce.15.cloned.1.call-done = f32[18432]{0:T(1024)} async-done(((f32[18432]{0:T(1024)}), f32[18432]{0:T(1024)}) %all-reduce.15.cloned.1.call-update) | async-done | bytes 73744
  1297.7 42.2 %psum.47 = f32[]{:T(128)} all-reduce(f32[]{:T(128)} %fusion.105), channel_id=1, replica_groups=mesh['row'=8,'col'=4] {'row','col'}, use_global_device_ids=true, to_apply=%region_13.14 | all-reduce | flops 1 | bytes 8 | tf_op jit(solution)/shard_map/psum | solution.py:179
  1352.9 30.6 %all-gather.2 = f32[8,1,2304]{2,1,0:T(1,128)S(1)} all-gather(f32[1,1,2304]{2,1,0:T(1,128)S(1)} %reshape.833), channel_id=1, replica_groups=mesh['row'=8,'col'=4] {'row'}, dimensions={0}, use_global_device_ids=true | all-gather | bytes 82944 | tf_op jit(solution)/shard_map/all_gather | solution.py:107
  (594 shorter events, 388.7 us)
Async XLA Ops:
  7.2 579.7 %all-reduce.11.cloned.1.call-start = ((), (), s32[]{:S(2)}) async-start(), calls=%async_computation.1 | async-start | bytes 21233664 | tf_op jit(solution)/shard_map/psum | solution.py:147
  8.1 15.8 %copy-start.114 = (f32[1,1,512]{2,1,0:T(1,128)}, f32[1,1,512]{2,1,0:T(1,128)S(1)}, u32[]{:S(2)}) copy-start(f32[1,1,512]{2,1,0:T(1,128)S(1)} %get-tuple-element.263) | copy-start | bytes 6148
  8.1 15.8 %copy-start.116 = (f32[1,1,512]{2,1,0:T(1,128)}, f32[1,1,512]{2,1,0:T(1,128)S(1)}, u32[]{:S(2)}) copy-start(f32[1,1,512]{2,1,0:T(1,128)S(1)} %get-tuple-element.270) | copy-start | bytes 6148
  9.5 12.7 copy-start.40
  9.5 12.7 copy-start.42
  9.5 12.7 copy-start.44
  9.5 12.7 copy-start.46
  9.6 12.7 copy-start.48
  9.6 15.4 %copy-start.36 = (f32[1,9,512]{2,0,1:T(1,128)}, f32[1,9,512]{2,0,1:T(1,128)S(1)}, u32[]{:S(2)}) copy-start(f32[1,9,512]{2,0,1:T(1,128)S(1)} %get-tuple-element.175) | copy-start | bytes 55300
  9.6 15.4 %copy-start.38 = (f32[1,9,512]{2,0,1:T(1,128)}, f32[1,9,512]{2,0,1:T(1,128)S(1)}, u32[]{:S(2)}) copy-start(f32[1,9,512]{2,0,1:T(1,128)S(1)} %get-tuple-element.176) | copy-start | bytes 55300
  26.4 16.9 %copy-start.57 = (s32[1,512]{1,0:T(1,128)}, s32[1,512]{1,0:T(1,128)S(1)}, u32[]{:S(2)}) copy-start(s32[1,512]{1,0:T(1,128)S(1)} %get-tuple-element.285) | copy-start | bytes 6148
  26.4 22.8 %copy-start.55 = (s32[1,512]{1,0:T(1,128)}, s32[1,512]{1,0:T(1,128)S(1)}, u32[]{:S(2)}) copy-start(s32[1,512]{1,0:T(1,128)S(1)} %get-tuple-element.287) | copy-start | bytes 6148
  153.3 18.7 %copy-start.4 = (f32[576,384]{1,0:T(8,128)}, f32[576,384]{1,0:T(8,128)S(1)}, u32[]{:S(2)}) copy-start(f32[576,384]{1,0:T(8,128)S(1)} %slice.1317) | copy-start | bytes 2654212
  255.5 497.6 %reduce-scatter.4.cloned.1.call-start = ((), (), s32[]{:S(2)}) async-start(), calls=%async_computation.2 | async-start | bytes 7372800
  276.7 20.2 %copy-start.10 = (f32[576,384]{1,0:T(8,128)}, f32[576,384]{1,0:T(8,128)S(1)}, u32[]{:S(2)}) copy-start(f32[576,384]{1,0:T(8,128)S(1)} %slice.1302) | copy-start | bytes 2654212
  296.9 16.7 %copy-start.11 = (f32[576,384]{1,0:T(8,128)}, f32[576,384]{1,0:T(8,128)S(1)}, u32[]{:S(2)}) copy-start(f32[576,384]{1,0:T(8,128)S(1)} %slice.1305) | copy-start | bytes 2654212
  601.2 382.2 %all-reduce.13.cloned.1.call-start = ((), (), s32[]{:S(2)}) async-start(), calls=%async_computation.3 | async-start | bytes 147456
  840.7 26.8 %copy-start.14 = (f32[576,576]{1,0:T(8,128)S(1)}, f32[576,576]{1,0:T(8,128)}, u32[]{:S(2)}) copy-start(f32[576,576]{1,0:T(8,128)} %reduce-scatter.4.cloned.1.call-done) | copy-start | bytes 3981316
  867.5 428.8 %all-reduce.15.cloned.1.call-start = ((), (), s32[]{:S(2)}) async-start(), calls=%async_computation.4 | async-start | bytes 147456
  1178.0 208.3 %copy-start.93 = (f32[1,128]{1,0:T(1,128)S(1)}, f32[1,128]{1,0:T(1,128)}, u32[]{:S(2)}) copy-start(f32[1,128]{1,0:T(1,128)} %copy-done.92) | copy-start | bytes 1540
  1178.0 208.3 %copy-start.95 = (f32[1,128]{1,0:T(1,128)S(1)}, f32[1,128]{1,0:T(1,128)}, u32[]{:S(2)}) copy-start(f32[1,128]{1,0:T(1,128)} %copy-done.94) | copy-start | bytes 1540
  1178.0 208.3 %copy-start.97 = (f32[1,128]{1,0:T(1,128)S(1)}, f32[1,128]{1,0:T(1,128)}, u32[]{:S(2)}) copy-start(f32[1,128]{1,0:T(1,128)} %copy-done.96) | copy-start | bytes 1540
  1178.0 208.3 %copy-start.99 = (f32[1,128]{1,0:T(1,128)S(1)}, f32[1,128]{1,0:T(1,128)}, u32[]{:S(2)}) copy-start(f32[1,128]{1,0:T(1,128)} %copy-done.98) | copy-start | bytes 1540
  1178.0 208.3 %copy-start.101 = (f32[1,128]{1,0:T(1,128)S(1)}, f32[1,128]{1,0:T(1,128)}, u32[]{:S(2)}) copy-start(f32[1,128]{1,0:T(1,128)} %copy-done.100) | copy-start | bytes 1540
  (115 other events, 415.6 us)
Sparse Core Ops, SparseCore 0:
  255.6 331.1 all-reduce.10
  601.3 54.6 reduce-scatter.3
  867.6 115.7 all-reduce.12
  1178.1 118.1 all-reduce.14
where the time goes:
time: 1420 us; the launch traced here: 1400 us
  waiting for transfers between devices  423 us (30%)
  local copies, waits for them, and re-layouts  349 us (25%)
  blocking collectives  293 us (21%)
  matrix products  234 us (16%)
  other arithmetic  75.3 us (5%)
  between operations  27.3 us (2%)
    unnamed x7, waiting for transfers between devices  231 us
    psum x1, waiting for transfers between devices, per_device(): col_sum, col_right = lax.psum((col_stack, col_right), 'row')  191 us
    dynamic_update_slice x12, local copies, waits for them, and re-layouts, add_block(): lax.dynamic_update_slice(target, current + block, (row_start, col_start))  108 us
    all_gather x3, blocking collectives, whole_vector(): whole = lax.all_gather(segment, 'row', axis=0, tiled=True)  91.7 us
    psum x2, blocking collectives, residual_weight(): return lax.psum(jnp.sum(residual * precon_res), ('row', 'col'))  82.7 us
    dot_general x2, matrix products, per_device(): forward = jnp.dot(grid, col_part, precision=HIGHEST)  78.9 us
    mul x16, local copies, waits for them, and re-layouts, cluster_schur(): eye_cam[:, None, :, None] * blocks[0][:, :, None, :]  68.9 us
    mul x16, local copies, waits for them, and re-layouts, cluster_schur(): eye_cam[:, None, :, None] * blocks[1][:, :, None, :]  67.5 us
  transfers between devices with their start and end apart: 4, of which 3 were waited for; matrix products, arithmetic and copies ran while one was open for 17% of the time, Pallas kernels for 0%

commit v1 on v0

v1 whole, which is shorter than its diff:
```python
import functools

import jax
import jax.numpy as jnp
from jax import lax
from jax.experimental import pallas as pl
from jax.experimental.pallas import tpu as pltpu
from jax.sharding import PartitionSpec as P

CAM = 64
LM = 128
LANES = 128
AXES = ("row", "col")
DAMPING = 1.0

NN = (((1,), (0,)), ((), ()))
NT = (((1,), (1,)), ((), ()))


def split3(x):
    hi = x.astype(jnp.bfloat16)
    rest = x - hi.astype(jnp.float32)
    mid = rest.astype(jnp.bfloat16)
    low = (rest - mid.astype(jnp.float32)).astype(jnp.bfloat16)
    return jnp.concatenate([hi, mid, low], axis=0)


def dot3(x, exact, dims):
    n = x.shape[0]
    y = lax.dot_general(split3(x), exact, dims, preferred_element_type=jnp.float32)
    return (y[2 * n :] + y[n : 2 * n]) + y[:n]


def onehot(index_row, size):
    ids = lax.broadcasted_iota(jnp.int32, (size, index_row.shape[1]), 0)
    return jnp.where(ids == index_row, 1.0, 0.0).astype(jnp.bfloat16)


def pad_rows(x, rows):
    return jnp.concatenate([x, jnp.zeros((rows - x.shape[0], x.shape[1]), x.dtype)], axis=0)


def stack_rows(rows, total):
    rows = list(rows)
    rows.append(jnp.zeros((total - len(rows), rows[0].shape[1]), jnp.float32))
    return jnp.concatenate(rows, axis=0)


def cholesky_three(v00, v01, v02, v11, v12, v22):
    inv_first = 1.0 / jnp.sqrt(v00)
    low_one = v01 * inv_first
    low_two = v02 * inv_first
    inv_second = 1.0 / jnp.sqrt(v11 - low_one * low_one)
    low_three = (v12 - low_two * low_one) * inv_second
    inv_third = 1.0 / jnp.sqrt(v22 - low_two * low_two - low_three * low_three)
    return (inv_first, low_one, low_two, inv_second, low_three, inv_third)


def lower_solve(factor, first, second, third):
    out_one = first * factor[0]
    out_two = (second - factor[1] * out_one) * factor[3]
    out_three = (third - factor[2] * out_one - factor[4] * out_two) * factor[5]
    return (out_one, out_two, out_three)


def upper_solve(factor, first, second, third):
    out_three = third * factor[5]
    out_two = (second - factor[4] * out_three) * factor[3]
    out_one = (first - factor[1] * out_two - factor[2] * out_three) * factor[0]
    return (out_one, out_two, out_three)


def row_list(x, count):
    return [x[i : i + 1] for i in range(count)]


def lane_ids(rows):
    return lax.broadcasted_iota(jnp.int32, (rows, LANES), 1)


def to_first(x, half):
    return pltpu.roll(x, half * CAM, 1)


def to_second(x, half):
    return pltpu.roll(x, (1 - half) * CAM, 1)


def load_tile(ref, tiles, t):
    ninth = ref[tiles + t // 8, pl.ds(t % 8, 1), :]
    return jnp.concatenate([ref[t], ninth, jnp.zeros((7, LANES), jnp.float32)], axis=0)


def add_tile(ref, tiles, t, value):
    ref[t] += value[:8]
    ref[tiles + t // 8, pl.ds(t % 8, 1), :] += value[8:9]


def shard_select(shard, lane_offset):
    entry = lax.broadcasted_iota(jnp.int32, (shard, LANES), 0)
    start = 9 * (lax.broadcasted_iota(jnp.int32, (shard, LANES), 1) - lane_offset)
    inside = (entry >= start) & (entry < start + 9)
    return jnp.where(inside, 1.0, 0.0).astype(jnp.bfloat16)


def param_mask(shard):
    entry = lax.broadcasted_iota(jnp.int32, (16, shard), 1).astype(jnp.float32)
    camera = jnp.floor((entry + 0.5) * (1.0 / 9.0))
    param = entry - 9.0 * camera
    return param == lax.broadcasted_iota(jnp.int32, (16, shard), 0).astype(jnp.float32)


def place(pairs_ref, k, n_row, n_col, groups):
    first = pairs_ref[k, 0] - lax.axis_index("row") * (groups // n_row)
    second = pairs_ref[k, 1] - lax.axis_index("col") * (groups // n_col)
    return first // 2, first % 2, second // 2, second % 2


def scatter_pair(value, ref, tiles, row_tiles, spot):
    t_first, h_first, t_second, h_second = spot
    lower = lane_ids(value.shape[0]) < CAM
    add_tile(ref, tiles, t_first, to_first(jnp.where(lower, value, 0.0), h_first))
    add_tile(ref, tiles, row_tiles + t_second, to_second(jnp.where(lower, 0.0, value), h_second))


def own_place(n_row, n_col, cams):
    shard_cams = cams // (n_row * n_col)
    start = lax.axis_index("col") * shard_cams
    return start // LANES, start % LANES


def build_kernel(n_row, n_col, cams, pairs_ref, cam_ref, land_ref, resid_ref, ocam_ref, oland_ref, damp_ref, part_ref, m_ref, fac_ref, damp_tile_ref):
    groups = cams // CAM
    row_tiles = cams // n_row // LANES
    tiles = row_tiles + cams // n_col // LANES
    count = cam_ref.shape[0]
    obs = cam_ref.shape[2]
    shard = damp_ref.shape[1]
    part_ref[...] = jnp.zeros(part_ref.shape, jnp.float32)
    rhs_ref, diag_ref = part_ref.at[0], part_ref.at[1]

    own_tile, own_lane = own_place(n_row, n_col, cams)
    spread = jnp.where(param_mask(shard), damp_ref[...], 0.0)
    damp_tile = dot3(spread, shard_select(shard, own_lane), NN)
    damp_tile_ref[...] = damp_tile
    add_tile(diag_ref, tiles, own_tile, damp_tile)

    key = ocam_ref[...] * LM + oland_ref[...]
    key = jnp.concatenate([key.astype(jnp.float32), jnp.full((8 - count, obs), -1.0, jnp.float32)], axis=0)
    key_t = jnp.transpose(key)

    for k in range(count):
        cam_hot = onehot(ocam_ref[k : k + 1, :], 2 * CAM)
        land_hot = onehot(oland_ref[k : k + 1, :], LM)
        lj = [land_ref[k, i : i + 1, :] for i in range(6)]
        e0, e1 = resid_ref[k, 0:1, :], resid_ref[k, 1:2, :]

        def outer(i, j):
            return lj[i] * lj[j] + lj[3 + i] * lj[3 + j]

        entries = [outer(0, 0), outer(0, 1), outer(0, 2), outer(1, 1), outer(1, 2), outer(2, 2)]
        entries += [lj[b] * e0 + lj[3 + b] * e1 for b in range(3)]
        sums = row_list(dot3(stack_rows(entries, 16), land_hot, NT), 9)
        factor = cholesky_three(
            sums[0] + DAMPING, sums[1], sums[2], sums[3] + DAMPING, sums[4], sums[5] + DAMPING
        )
        tvec = lower_solve(factor, sums[6], sums[7], sums[8])
        land_values = stack_rows(list(factor) + list(tvec), 16)
        fac_ref[k] = land_values
        at_obs = row_list(dot3(land_values, land_hot, NN), 9)
        m0 = lower_solve(at_obs, lj[0], lj[1], lj[2])
        m1 = lower_solve(at_obs, lj[3], lj[4], lj[5])
        m_ref[k] = stack_rows(m0 + m1, 8)
        w0 = m0[0] * at_obs[6] + m0[1] * at_obs[7] + m0[2] * at_obs[8] - e0
        w1 = m1[0] * at_obs[6] + m1[1] * at_obs[7] + m1[2] * at_obs[8] - e1
        j0 = pad_rows(cam_ref[k, 0:9, :], 16)
        j1 = pad_rows(cam_ref[k, 9:18, :], 16)
        rhs = j0 * w0 + j1 * w1
        coupled = jnp.concatenate([j0 * m0[b] + j1 * m1[b] for b in range(3)], axis=0)
        same = jnp.where(key_t[:, k : k + 1] == key[k : k + 1, :], 1.0, 0.0).astype(jnp.bfloat16)
        prod = coupled * dot3(coupled, same, NN)
        diag = j0 * j0 + j1 * j1 - (prod[0:16] + prod[16:32] + prod[32:48])
        both = dot3(jnp.concatenate([rhs, diag], axis=0), cam_hot, NT)
        spot = place(pairs_ref, k, n_row, n_col, groups)
        scatter_pair(both[:16], rhs_ref, tiles, row_tiles, spot)
        scatter_pair(both[16:], diag_ref, tiles, row_tiles, spot)


def half_product(k, p_ref, pairs_ref, cam_ref, ocam_ref, oland_ref, m_ref):
    cams_tiles = p_ref.shape[0] * 8 // 9
    first, second = pairs_ref[k, 0], pairs_ref[k, 1]
    p_first = to_first(load_tile(p_ref, cams_tiles, first // 2), first % 2)
    p_second = to_second(load_tile(p_ref, cams_tiles, second // 2), second % 2)
    p_here = jnp.where(lane_ids(16) < CAM, p_first, p_second)
    cam_hot = onehot(ocam_ref[k : k + 1, :], 2 * CAM)
    land_hot = onehot(oland_ref[k : k + 1, :], LM)
    at_obs = dot3(p_here, cam_hot, NN)[:9]
    u0 = jnp.sum(cam_ref[k, 0:9, :] * at_obs, axis=0, keepdims=True)
    u1 = jnp.sum(cam_ref[k, 9:18, :] * at_obs, axis=0, keepdims=True)
    m = [m_ref[k, i : i + 1, :] for i in range(6)]
    y = [m[b] * u0 + m[3 + b] * u1 for b in range(3)]
    y_land = dot3(stack_rows(y, 16), land_hot, NT)
    return cam_hot, land_hot, u0, u1, m, y_land


def first_kernel(n_row, n_col, cams, pairs_ref, sums_ref, cam_ref, ocam_ref, oland_ref, m_ref, fac_ref, damp_tile_ref, part_ref, back_ref, p_ref):
    groups = cams // CAM
    row_tiles = cams // n_row // LANES
    tiles = row_tiles + cams // n_col // LANES
    count = cam_ref.shape[0]
    p_ref[...] = sums_ref[0] * (1.0 / sums_ref[1])
    part_ref[...] = jnp.zeros(part_ref.shape, jnp.float32)
    own_tile, _ = own_place(n_row, n_col, cams)
    whole_tile = lax.axis_index("row") * row_tiles + own_tile
    own = load_tile(p_ref, cams // LANES, whole_tile)
    add_tile(part_ref, tiles, own_tile, own * damp_tile_ref[...])
    for k in range(count):
        cam_hot, land_hot, u0, u1, m, y_land = half_product(k, p_ref, pairs_ref, cam_ref, ocam_ref, oland_ref, m_ref)
        factor = row_list(fac_ref[k], 9)
        solved = upper_solve(factor, y_land[0:1], y_land[1:2], y_land[2:3])
        from_t = upper_solve(factor, factor[6], factor[7], factor[8])
        back_ref[k] = stack_rows(solved + from_t, 8)
        y_obs = row_list(dot3(y_land, land_hot, NN), 3)
        v0 = u0 - (m[0] * y_obs[0] + m[1] * y_obs[1] + m[2] * y_obs[2])
        v1 = u1 - (m[3] * y_obs[0] + m[4] * y_obs[1] + m[5] * y_obs[2])
        image = pad_rows(cam_ref[k, 0:9, :] * v0 + cam_ref[k, 9:18, :] * v1, 16)
        image = dot3(image, cam_hot, NT)
        scatter_pair(image, part_ref, tiles, row_tiles, place(pairs_ref, k, n_row, n_col, groups))


def total_sum(x):
    x = jnp.sum(x, axis=0)
    return jnp.sum(jnp.sum(x, axis=0, keepdims=True), axis=1, keepdims=True)


def second_kernel(n_row, n_col, cams, pairs_ref, sums_ref, image_ref, cam_ref, ocam_ref, oland_ref, m_ref, fac_ref, damp_tile_ref, back_ref, energy_ref, cam_out_ref, land_base_ref, land_slope_ref, p_ref, d_ref):
    row_tiles = cams // n_row // LANES
    count = cam_ref.shape[0]
    shard = cam_out_ref.shape[1]
    right, image = sums_ref[0], image_ref[...]
    precond = 1.0 / sums_ref[1]
    start = right * precond
    norm_now = total_sum(right * start)
    alpha = norm_now / total_sum(start * image)
    residual = right - alpha * image
    precon_res = precond * residual
    norm_next = total_sum(residual * precon_res)
    p_ref[...] = start
    d_ref[...] = precon_res + norm_next / norm_now * start

    own_tile, own_lane = own_place(n_row, n_col, cams)
    whole_tile = lax.axis_index("row") * row_tiles + own_tile
    own_first = load_tile(p_ref, cams // LANES, whole_tile)
    own_second = load_tile(d_ref, cams // LANES, whole_tile)
    energy = own_second * own_second * damp_tile_ref[...]
    energy = jnp.sum(jnp.sum(energy, axis=0, keepdims=True), axis=1, keepdims=True)

    select = shard_select(shard, own_lane)
    mask = param_mask(shard)
    flat = dot3(jnp.concatenate([own_first, own_second], axis=0), select, NT)
    flat_first = jnp.sum(jnp.where(mask, flat[:16], 0.0), axis=0, keepdims=True)
    flat_second = jnp.sum(jnp.where(mask, flat[16:], 0.0), axis=0, keepdims=True)
    cam_out_ref[0:1, :] = alpha * flat_first
    cam_out_ref[1:2, :] = norm_next * flat_second

    for k in range(count):
        _, land_hot, u0, u1, m, y_land = half_product(k, d_ref, pairs_ref, cam_ref, ocam_ref, oland_ref, m_ref)
        factor = row_list(fac_ref[k], 9)
        solved = upper_solve(factor, y_land[0:1], y_land[1:2], y_land[2:3])
        for b in range(3):
            land_base_ref[k, b : b + 1, :] = -(back_ref[k, 3 + b : 4 + b, :] + alpha * back_ref[k, b : b + 1, :])
            land_slope_ref[k, b : b + 1, :] = -norm_next * solved[b]
        y_obs = row_list(dot3(y_land, land_hot, NN), 3)
        v0 = u0 - (m[0] * y_obs[0] + m[1] * y_obs[1] + m[2] * y_obs[2])
        v1 = u1 - (m[3] * y_obs[0] + m[4] * y_obs[1] + m[5] * y_obs[2])
        energy = energy + jnp.sum(u0 * v0 + u1 * v1, axis=1, keepdims=True)
    energy_ref[...] = jnp.broadcast_to(energy, energy_ref.shape)


def hyper(x, n_row, n_col):
    n = n_row * n_col
    bit = 1
    while bit < n:
        x = x + lax.ppermute(x, AXES, [(i, i ^ bit) for i in range(n)])
        bit *= 2
    return x


def per_device(n_row, n_col, cam_jac, land_jac, resid, obs_cam, obs_land, pairs, cam_damp):
    f32 = jnp.float32
    count, _, obs = cam_jac.shape
    shard = cam_damp.shape[0]
    n_dev = n_row * n_col
    cams = shard * n_dev // 9
    row_tiles = cams // n_row // LANES
    tiles = row_tiles + cams // n_col // LANES
    part_tiles = tiles + (tiles + 7) // 8
    whole_tiles = cams // LANES
    whole_packed = whole_tiles + (whole_tiles + 7) // 8
    vmem = pl.BlockSpec(memory_space=pltpu.VMEM)
    smem = pl.BlockSpec(memory_space=pltpu.SMEM)

    def shape(*dims):
        return jax.ShapeDtypeStruct(dims, f32)

    part, m, fac, damp_tile = pl.pallas_call(
        functools.partial(build_kernel, n_row, n_col, cams),
        out_shape=(shape(2, part_tiles, 8, LANES), shape(count, 8, obs), shape(count, 16, LM), shape(16, LANES)),
        in_specs=[smem] + [vmem] * 6,
        out_specs=(vmem,) * 4,
    )(pairs, cam_jac, land_jac, resid, obs_cam, obs_land, cam_damp.reshape(1, shard))

    def expand(x):
        whole = jnp.zeros((whole_packed, 8, LANES), f32)

        def put(whole, lo, hi, start):
            old = lax.dynamic_slice_in_dim(whole, start, hi - lo, 0)
            return lax.dynamic_update_slice_in_dim(whole, old + x[lo:hi], start, 0)

        whole = put(whole, 0, row_tiles, lax.axis_index("row") * row_tiles)
        whole = put(whole, row_tiles, tiles, lax.axis_index("col") * (tiles - row_tiles))
        ninth = jnp.zeros((whole_tiles, LANES), f32)
        flat = x[tiles:].reshape(-1, LANES)
        for lo, hi, start in (
            (0, row_tiles, lax.axis_index("row") * row_tiles),
            (row_tiles, tiles, lax.axis_index("col") * (tiles - row_tiles)),
        ):
            old = lax.dynamic_slice_in_dim(ninth, start, hi - lo, 0)
            ninth = lax.dynamic_update_slice_in_dim(ninth, old + flat[lo:hi], start, 0)
        ninth = ninth.reshape(-1, 8, LANES)
        return lax.dynamic_update_slice_in_dim(whole, ninth, whole_tiles, 0)

    sums = hyper(jnp.stack([expand(part[0]), expand(part[1])]), n_row, n_col)

    image, back = pl.pallas_call(
        functools.partial(first_kernel, n_row, n_col, cams),
        out_shape=(shape(part_tiles, 8, LANES), shape(count, 8, LM)),
        in_specs=[smem] + [vmem] * 7,
        out_specs=(vmem,) * 2,
        scratch_shapes=[pltpu.VMEM((whole_packed, 8, LANES), f32)],
    )(pairs, sums, cam_jac, obs_cam, obs_land, m, fac, damp_tile)

    image = hyper(expand(image), n_row, n_col)

    energy, cam_out, land_base, land_slope = pl.pallas_call(
        functools.partial(second_kernel, n_row, n_col, cams),
        out_shape=(shape(8, LANES), shape(2, shard), shape(count, 3, LM), shape(count, 3, LM)),
        in_specs=[smem] + [vmem] * 9,
        out_specs=(vmem,) * 4,
        scratch_shapes=[pltpu.VMEM((whole_packed, 8, LANES), f32)] * 2,
    )(pairs, sums, image, cam_jac, obs_cam, obs_land, m, fac, damp_tile, back)

    spread = jnp.broadcast_to(energy[0:1][None], (n_dev, 1, LANES))
    gathered = lax.all_to_all(spread, AXES, 0, 0, tiled=True)
    inverse = 1.0 / jnp.sum(gathered, axis=0)[0, 0]
    return cam_out[0] + inverse * cam_out[1], land_base + inverse * land_slope


def solution(mesh):
    n_row, n_col = mesh.shape["row"], mesh.shape["col"]
    both = P(AXES)
    in_specs = (P(AXES, None, None),) * 3 + (P(AXES, None),) * 3 + (both,)
    out_specs = (both, P(AXES, None, None))
    return jax.shard_map(
        functools.partial(per_device, n_row, n_col),
        mesh=mesh,
        in_specs=in_specs,
        out_specs=out_specs,
        check_vma=False,
    )
```

time: 1420 us -> 83.5 us (0.06); the launches traced: 1400 us -> 83 us
  waiting for transfers between devices: 423 us -> 31.2 us
  local copies, waits for them, and re-layouts: 349 us -> 7.94 us
  blocking collectives: 293 us -> 12.6 us
  matrix products: 234 us -> 0 us
  other arithmetic: 75.3 us -> 2.82 us
  between operations: 27.3 us -> 0.87 us
  starting transfers between devices: 0.57 us -> 16.5 us
    dot_general x50 -> x0, matrix products: 234 us -> none  [the longest x2 78.9 us: per_device(): forward = jnp.dot(grid, col_part, precision=HIGHEST)]
    unnamed x7 -> x0, waiting for transfers between devices: 231 us -> none
    psum x1 -> x0, waiting for transfers between devices: 191 us -> none  [per_device(): col_sum, col_right = lax.psum((col_stack, col_right), 'row')]
    psum x4 -> x0, blocking collectives: 159 us -> none  [the longest x2 82.7 us: residual_weight(): return lax.psum(jnp.sum(residual * precon_res), ('row', 'col'))]
    mul x38 -> x0, local copies, waits for them, and re-layouts: 139 us -> none  [the longest x16 68.9 us: cluster_schur(): eye_cam[:, None, :, None] * blocks[0][:, :, None, :]]
    dynamic_update_slice x15 -> x8, local copies, waits for them, and re-layouts: 109 us -> 0.74 us  [the longest x3 0.72 us: expand(): ninth = lax.dynamic_update_slice_in_dim(ninth, old + flat[lo:hi], start, 0)]
    all_gather x3 -> x0, blocking collectives: 91.7 us -> none  [whole_vector(): whole = lax.all_gather(segment, 'row', axis=0, tiled=True)]
    mul x25 -> x0, other arithmetic: 54.5 us -> none  [the longest x1 51.3 us: cluster_schur(): eye_cam[:, None, :, None] * blocks[1][:, :, None, :]]
  transfers between devices with their start and end apart: 4 -> 10, of which waited for: 3 -> 10; matrix products, arithmetic and copies ran while one was open for 17% -> 0% of each run, Pallas kernels for 0% -> 0%
where the time goes in v1:
time: 83.5 us; the launch traced here: 83 us
  waiting for transfers between devices  31.2 us (37%)
  starting transfers between devices  16.5 us (20%)
  blocking collectives  12.6 us (15%)
  Pallas kernels  11.1 us (13%)
  local copies, waits for them, and re-layouts  7.94 us (10%)
  other arithmetic  2.82 us (3%)
  between operations  0.87 us (1%)
    ppermute x10, waiting for transfers between devices, hyper(): x = x + lax.ppermute(x, AXES, [(i, i ^ bit) for i in range(n)])  31.2 us
    ppermute x10, starting transfers between devices, hyper(): x = x + lax.ppermute(x, AXES, [(i, i ^ bit) for i in range(n)])  16.5 us
    all_to_all x1, blocking collectives, per_device(): gathered = lax.all_to_all(spread, AXES, 0, 0, tiled=True)  12.6 us
    unnamed x22, local copies, waits for them, and re-layouts  5.9 us
    pallas_call x1, Pallas kernels, per_device(): pl.pallas_call(functools.partial(build_kernel, n_row, n_col, cams), out_s...  4.22 us
    pallas_call x1, Pallas kernels, per_device(): pl.pallas_call(functools.partial(second_kernel, n_row, n_col, cams), out_...  3.69 us
    pallas_call x1, Pallas kernels, per_device(): pl.pallas_call(functools.partial(first_kernel, n_row, n_col, cams), out_s...  3.16 us
  transfers between devices with their start and end apart: 10, of which 10 were waited for; matrix products, arithmetic and copies ran while one was open for 0% of the time, Pallas kernels for 0%

profile of v1, /device:TPU:0, one launch (start us, length us, event | category | flops | bytes accessed | tf_op | source)
XLA Modules:
  0.0 83.0 jit_solution(17294987653949094647)
XLA Ops:
  0.7 1.7 %copy.26.cam_ref = f32[4,18,512]{2,1,0:T(8,128)} copy(f32[4,18,512]{2,0,1:T(4,128)} %param.7) | data formatting | bytes 294912 | tf_op args[0]
  4.3 4.2 %shard_map.86 = (f32[2,7,8,128]{3,2,1,0:T(8,128)}, f32[4,8,512]{2,1,0:T(8,128)}, f32[4,16,128]{2,1,0:T(8,128)}, f32[16,128]{1,0:T(8,128)}) custom-call(s32[4,2]{1,0:T(4,128)} %copy.30.pairs_ref, f32[4,18,512]{2,1,0:T(8,128)} %copy.26.cam_ref, f32[4,6,512]{2,1,0:T(8,128)} %copy.27.land_ref, f32[4,2,512]{2,1,0:T(2,128)} %resid_ref.1, s32[4,512]{1,0:T(4,128)} %ocam_ref.5, ...), custom_call_target="tpu_custom_call" | custom-call | tf_op jit(solution)/shard_map/pallas_call | solution.py:306
  8.5 0.8 copy-done
  10.0 1.0 %collective-permute-done = f32[2,18,8,128]{3,2,1,0:T(8,128)S(1)} collective-permute-done((f32[2,18,8,128]{3,2,1,0:T(8,128)S(1)}, f32[2,18,8,128]{3,2,1,0:T(8,128)S(1)}, u32[]{:S(2)}, u32[]{:S(2)}) %collective-permute-start) | collective-permute-done | bytes 147488 | tf_op jit(solution)/shard_map/ppermute | solution.py:284
  11.0 2.9 %collective-permute-start.1 = (f32[2,18,8,128]{3,2,1,0:T(8,128)S(1)}, f32[2,18,8,128]{3,2,1,0:T(8,128)S(1)}, u32[]{:S(2)}, u32[]{:S(2)}) collective-permute-start(f32[2,18,8,128]{3,2,1,0:T(8,128)S(1)} %fusion.3), channel_id=1, source_target_pairs={{0,2},{1,3},{2,0},{3,1},{4,6},{5,7},{6,4},{7,5},{8,10},{9,11},{10,... | collective-permute-start | bytes 442376 | tf_op jit(solution)/shard_map/ppermute | solution.py:284
  14.0 4.2 %collective-permute-done.1 = f32[2,18,8,128]{3,2,1,0:T(8,128)S(1)} collective-permute-done((f32[2,18,8,128]{3,2,1,0:T(8,128)S(1)}, f32[2,18,8,128]{3,2,1,0:T(8,128)S(1)}, u32[]{:S(2)}, u32[]{:S(2)}) %collective-permute-start.1) | collective-permute-done | bytes 147488 | tf_op jit(solution)/shard_map/ppermute | solution.py:284
  18.2 1.8 %collective-permute-start.2 = (f32[2,18,8,128]{3,2,1,0:T(8,128)S(1)}, f32[2,18,8,128]{3,2,1,0:T(8,128)S(1)}, u32[]{:S(2)}, u32[]{:S(2)}) collective-permute-start(f32[2,18,8,128]{3,2,1,0:T(8,128)S(1)} %fusion.4), channel_id=1, source_target_pairs={{0,4},{1,5},{2,6},{3,7},{4,0},{5,1},{6,2},{7,3},{8,12},{9,13},{10,... | collective-permute-start | bytes 442376 | tf_op jit(solution)/shard_map/ppermute | solution.py:284
  20.0 3.7 %collective-permute-done.2 = f32[2,18,8,128]{3,2,1,0:T(8,128)S(1)} collective-permute-done((f32[2,18,8,128]{3,2,1,0:T(8,128)S(1)}, f32[2,18,8,128]{3,2,1,0:T(8,128)S(1)}, u32[]{:S(2)}, u32[]{:S(2)}) %collective-permute-start.2) | collective-permute-done | bytes 147488 | tf_op jit(solution)/shard_map/ppermute | solution.py:284
  23.7 1.6 %collective-permute-start.3 = (f32[2,18,8,128]{3,2,1,0:T(8,128)S(1)}, f32[2,18,8,128]{3,2,1,0:T(8,128)S(1)}, u32[]{:S(2)}, u32[]{:S(2)}) collective-permute-start(f32[2,18,8,128]{3,2,1,0:T(8,128)S(1)} %add.93), channel_id=1, source_target_pairs={{0,8},{1,9},{2,10},{3,11},{4,12},{5,13},{6,14},{7,15},{8,0},{9,1},... | collective-permute-start | bytes 442376 | tf_op jit(solution)/shard_map/ppermute | solution.py:284
  25.3 3.6 %collective-permute-done.3 = f32[2,18,8,128]{3,2,1,0:T(8,128)S(1)} collective-permute-done((f32[2,18,8,128]{3,2,1,0:T(8,128)S(1)}, f32[2,18,8,128]{3,2,1,0:T(8,128)S(1)}, u32[]{:S(2)}, u32[]{:S(2)}) %collective-permute-start.3) | collective-permute-done | bytes 147488 | tf_op jit(solution)/shard_map/ppermute | solution.py:284
  28.9 3.0 %collective-permute-start.4 = (f32[2,18,8,128]{3,2,1,0:T(8,128)S(1)}, f32[2,18,8,128]{3,2,1,0:T(8,128)S(1)}, u32[]{:S(2)}, u32[]{:S(2)}) collective-permute-start(f32[2,18,8,128]{3,2,1,0:T(8,128)S(1)} %add.94), channel_id=1, source_target_pairs={{0,16},{1,17},{2,18},{3,19},{4,20},{5,21},{6,22},{7,23},{8,24},{9,... | collective-permute-start | bytes 442376 | tf_op jit(solution)/shard_map/ppermute | solution.py:284
  31.9 4.7 %collective-permute-done.4 = f32[2,18,8,128]{3,2,1,0:T(8,128)S(1)} collective-permute-done((f32[2,18,8,128]{3,2,1,0:T(8,128)S(1)}, f32[2,18,8,128]{3,2,1,0:T(8,128)S(1)}, u32[]{:S(2)}, u32[]{:S(2)}) %collective-permute-start.4) | collective-permute-done | bytes 147488 | tf_op jit(solution)/shard_map/ppermute | solution.py:284
  37.3 3.2 %shard_map.87 = (f32[7,8,128]{2,1,0:T(8,128)}, f32[4,8,128]{2,1,0:T(8,128)}) custom-call(s32[4,2]{1,0:T(4,128)} %copy.30.pairs_ref, f32[2,18,8,128]{3,2,1,0:T(8,128)} %add.95.sums_ref, f32[4,18,512]{2,1,0:T(8,128)} %copy.26.cam_ref, s32[4,512]{1,0:T(4,128)} %ocam_ref.5, s32[4,512]{1,0:T(4,128)} %oland_ref.5, f32[4,8,512]{2,1,0:T(8,128)} %get-tuple-element.13.m_ref, ...), custom_call_target="tpu_custom_call" | custom-call | tf_op jit(solution)/shard_map/pallas_call | solution.py:335
  42.7 1.3 %collective-permute-done.5 = f32[18,8,128]{2,1,0:T(8,128)S(1)} collective-permute-done((f32[18,8,128]{2,1,0:T(8,128)S(1)}, f32[18,8,128]{2,1,0:T(8,128)S(1)}, u32[]{:S(2)}, u32[]{:S(2)}) %collective-permute-start.5) | collective-permute-done | bytes 73760 | tf_op jit(solution)/shard_map/ppermute | solution.py:284
  43.9 1.6 %collective-permute-start.6 = (f32[18,8,128]{2,1,0:T(8,128)S(1)}, f32[18,8,128]{2,1,0:T(8,128)S(1)}, u32[]{:S(2)}, u32[]{:S(2)}) collective-permute-start(f32[18,8,128]{2,1,0:T(8,128)S(1)} %add.98), channel_id=1, source_target_pairs={{0,2},{1,3},{2,0},{3,1},{4,6},{5,7},{6,4},{7,5},{8,10},{9,11},{10,... | collective-permute-start | bytes 221192 | tf_op jit(solution)/shard_map/ppermute | solution.py:284
  45.5 2.8 %collective-permute-done.6 = f32[18,8,128]{2,1,0:T(8,128)S(1)} collective-permute-done((f32[18,8,128]{2,1,0:T(8,128)S(1)}, f32[18,8,128]{2,1,0:T(8,128)S(1)}, u32[]{:S(2)}, u32[]{:S(2)}) %collective-permute-start.6) | collective-permute-done | bytes 73760 | tf_op jit(solution)/shard_map/ppermute | solution.py:284
  48.4 1.6 %collective-permute-start.7 = (f32[18,8,128]{2,1,0:T(8,128)S(1)}, f32[18,8,128]{2,1,0:T(8,128)S(1)}, u32[]{:S(2)}, u32[]{:S(2)}) collective-permute-start(f32[18,8,128]{2,1,0:T(8,128)S(1)} %add.99), channel_id=1, source_target_pairs={{0,4},{1,5},{2,6},{3,7},{4,0},{5,1},{6,2},{7,3},{8,12},{9,13},{10,... | collective-permute-start | bytes 221192 | tf_op jit(solution)/shard_map/ppermute | solution.py:284
  49.9 2.8 %collective-permute-done.7 = f32[18,8,128]{2,1,0:T(8,128)S(1)} collective-permute-done((f32[18,8,128]{2,1,0:T(8,128)S(1)}, f32[18,8,128]{2,1,0:T(8,128)S(1)}, u32[]{:S(2)}, u32[]{:S(2)}) %collective-permute-start.7) | collective-permute-done | bytes 73760 | tf_op jit(solution)/shard_map/ppermute | solution.py:284
  52.8 0.8 collective-permute-start.8
  53.6 3.6 %collective-permute-done.8 = f32[18,8,128]{2,1,0:T(8,128)S(1)} collective-permute-done((f32[18,8,128]{2,1,0:T(8,128)S(1)}, f32[18,8,128]{2,1,0:T(8,128)S(1)}, u32[]{:S(2)}, u32[]{:S(2)}) %collective-permute-start.8) | collective-permute-done | bytes 73760 | tf_op jit(solution)/shard_map/ppermute | solution.py:284
  57.2 2.6 %collective-permute-start.9 = (f32[18,8,128]{2,1,0:T(8,128)S(1)}, f32[18,8,128]{2,1,0:T(8,128)S(1)}, u32[]{:S(2)}, u32[]{:S(2)}) collective-permute-start(f32[18,8,128]{2,1,0:T(8,128)S(1)} %add.101), channel_id=1, source_target_pairs={{0,16},{1,17},{2,18},{3,19},{4,20},{5,21},{6,22},{7,23},{8,24},{9,... | collective-permute-start | bytes 221192 | tf_op jit(solution)/shard_map/ppermute | solution.py:284
  59.8 3.5 %collective-permute-done.9 = f32[18,8,128]{2,1,0:T(8,128)S(1)} collective-permute-done((f32[18,8,128]{2,1,0:T(8,128)S(1)}, f32[18,8,128]{2,1,0:T(8,128)S(1)}, u32[]{:S(2)}, u32[]{:S(2)}) %collective-permute-start.9) | collective-permute-done | bytes 73760 | tf_op jit(solution)/shard_map/ppermute | solution.py:284
  64.0 3.7 %shard_map.88 = (f32[8,128]{1,0:T(8,128)}, f32[2,576]{1,0:T(2,128)}, f32[4,3,128]{2,1,0:T(4,128)}, f32[4,3,128]{2,1,0:T(4,128)}) custom-call(s32[4,2]{1,0:T(4,128)} %copy.30.pairs_ref, f32[2,18,8,128]{3,2,1,0:T(8,128)} %add.95.sums_ref, f32[18,8,128]{2,1,0:T(8,128)} %add.102.image_ref, f32[4,18,512]{2,1,0:T(8,128)} %copy.26.cam_ref, s32[4,512]{1,0:T(4,128)} %ocam_ref.5, ...), custom_call_target="tpu_custom_call" | custom-call | tf_op jit(solution)/shard_map/pallas_call | solution.py:345
  68.3 12.6 %all_to_all.5 = f32[32,1,128]{2,1,0:T(1,128)S(1)} all-to-all(f32[32,1,128]{2,1,0:T(1,128)S(1)} %broadcast_in_dim.9), channel_id=1, replica_groups=mesh['row'=8,'col'=4] {'row','col'}, dimensions={0} | all-to-all | bytes 32768 | tf_op jit(solution)/shard_map/all_to_all | solution.py:354
  (57 shorter events, 8.9 us)
Async XLA Ops:
  0.6 1.7 %copy-start.7 = (s32[4,2]{0,1:T(2,128)S(1)}, s32[4,2]{0,1:T(2,128)}, u32[]{:S(2)}) copy-start(s32[4,2]{0,1:T(2,128)} %param.12) | copy-start | bytes 100
  0.6 2.3 %copy-start.1 = (f32[4,6,512]{2,0,1:T(4,128)S(1)}, f32[4,6,512]{2,0,1:T(4,128)}, u32[]{:S(2)}) copy-start(f32[4,6,512]{2,0,1:T(4,128)} %param.8) | copy-start | bytes 147460
  3.0 0.7 copy-start.6
  8.5 0.8 copy-start
  9.5 1.5 %collective-permute-start = (f32[2,18,8,128]{3,2,1,0:T(8,128)S(1)}, f32[2,18,8,128]{3,2,1,0:T(8,128)S(1)}, u32[]{:S(2)}, u32[]{:S(2)}) collective-permute-start(f32[2,18,8,128]{3,2,1,0:T(8,128)S(1)} %pad_maximum_fusion), channel_id=1, source_target_pairs={{0,1},{1,0},{2,3},{3,2},{4,5},{5,4},{6,7},{7,6},{8,9},{9,8},{10,11... | collective-permute-start | bytes 442376 | tf_op jit(solution)/shard_map/ppermute | solution.py:284
  11.0 7.1 %collective-permute-start.1 = (f32[2,18,8,128]{3,2,1,0:T(8,128)S(1)}, f32[2,18,8,128]{3,2,1,0:T(8,128)S(1)}, u32[]{:S(2)}, u32[]{:S(2)}) collective-permute-start(f32[2,18,8,128]{3,2,1,0:T(8,128)S(1)} %fusion.3), channel_id=1, source_target_pairs={{0,2},{1,3},{2,0},{3,1},{4,6},{5,7},{6,4},{7,5},{8,10},{9,11},{10,... | collective-permute-start | bytes 442376 | tf_op jit(solution)/shard_map/ppermute | solution.py:284
  18.2 5.5 %collective-permute-start.2 = (f32[2,18,8,128]{3,2,1,0:T(8,128)S(1)}, f32[2,18,8,128]{3,2,1,0:T(8,128)S(1)}, u32[]{:S(2)}, u32[]{:S(2)}) collective-permute-start(f32[2,18,8,128]{3,2,1,0:T(8,128)S(1)} %fusion.4), channel_id=1, source_target_pairs={{0,4},{1,5},{2,6},{3,7},{4,0},{5,1},{6,2},{7,3},{8,12},{9,13},{10,... | collective-permute-start | bytes 442376 | tf_op jit(solution)/shard_map/ppermute | solution.py:284
  23.7 5.2 %collective-permute-start.3 = (f32[2,18,8,128]{3,2,1,0:T(8,128)S(1)}, f32[2,18,8,128]{3,2,1,0:T(8,128)S(1)}, u32[]{:S(2)}, u32[]{:S(2)}) collective-permute-start(f32[2,18,8,128]{3,2,1,0:T(8,128)S(1)} %add.93), channel_id=1, source_target_pairs={{0,8},{1,9},{2,10},{3,11},{4,12},{5,13},{6,14},{7,15},{8,0},{9,1},... | collective-permute-start | bytes 442376 | tf_op jit(solution)/shard_map/ppermute | solution.py:284
  28.9 7.7 %collective-permute-start.4 = (f32[2,18,8,128]{3,2,1,0:T(8,128)S(1)}, f32[2,18,8,128]{3,2,1,0:T(8,128)S(1)}, u32[]{:S(2)}, u32[]{:S(2)}) collective-permute-start(f32[2,18,8,128]{3,2,1,0:T(8,128)S(1)} %add.94), channel_id=1, source_target_pairs={{0,16},{1,17},{2,18},{3,19},{4,20},{5,21},{6,22},{7,23},{8,24},{9,... | collective-permute-start | bytes 442376 | tf_op jit(solution)/shard_map/ppermute | solution.py:284
  41.8 0.7 copy-start.2
  42.6 1.3 %collective-permute-start.5 = (f32[18,8,128]{2,1,0:T(8,128)S(1)}, f32[18,8,128]{2,1,0:T(8,128)S(1)}, u32[]{:S(2)}, u32[]{:S(2)}) collective-permute-start(f32[18,8,128]{2,1,0:T(8,128)S(1)} %bitcast_dynamic-update-slice_fusion.2), channel_id=1, source_target_pairs={{0,1},{1,0},{2,3},{3,2},{4,5},{5,4},{6,7},{7,6},{8,9},{9,8},{10,11... | collective-permute-start | bytes 221192 | tf_op jit(solution)/shard_map/ppermute | solution.py:284
  43.9 4.4 %collective-permute-start.6 = (f32[18,8,128]{2,1,0:T(8,128)S(1)}, f32[18,8,128]{2,1,0:T(8,128)S(1)}, u32[]{:S(2)}, u32[]{:S(2)}) collective-permute-start(f32[18,8,128]{2,1,0:T(8,128)S(1)} %add.98), channel_id=1, source_target_pairs={{0,2},{1,3},{2,0},{3,1},{4,6},{5,7},{6,4},{7,5},{8,10},{9,11},{10,... | collective-permute-start | bytes 221192 | tf_op jit(solution)/shard_map/ppermute | solution.py:284
  48.4 4.4 %collective-permute-start.7 = (f32[18,8,128]{2,1,0:T(8,128)S(1)}, f32[18,8,128]{2,1,0:T(8,128)S(1)}, u32[]{:S(2)}, u32[]{:S(2)}) collective-permute-start(f32[18,8,128]{2,1,0:T(8,128)S(1)} %add.99), channel_id=1, source_target_pairs={{0,4},{1,5},{2,6},{3,7},{4,0},{5,1},{6,2},{7,3},{8,12},{9,13},{10,... | collective-permute-start | bytes 221192 | tf_op jit(solution)/shard_map/ppermute | solution.py:284
  52.8 4.4 %collective-permute-start.8 = (f32[18,8,128]{2,1,0:T(8,128)S(1)}, f32[18,8,128]{2,1,0:T(8,128)S(1)}, u32[]{:S(2)}, u32[]{:S(2)}) collective-permute-start(f32[18,8,128]{2,1,0:T(8,128)S(1)} %add.100), channel_id=1, source_target_pairs={{0,8},{1,9},{2,10},{3,11},{4,12},{5,13},{6,14},{7,15},{8,0},{9,1},... | collective-permute-start | bytes 221192 | tf_op jit(solution)/shard_map/ppermute | solution.py:284
  57.2 6.1 %collective-permute-start.9 = (f32[18,8,128]{2,1,0:T(8,128)S(1)}, f32[18,8,128]{2,1,0:T(8,128)S(1)}, u32[]{:S(2)}, u32[]{:S(2)}) collective-permute-start(f32[18,8,128]{2,1,0:T(8,128)S(1)} %add.101), channel_id=1, source_target_pairs={{0,16},{1,17},{2,18},{3,19},{4,20},{5,21},{6,22},{7,23},{8,24},{9,... | collective-permute-start | bytes 221192 | tf_op jit(solution)/shard_map/ppermute | solution.py:284
  81.0 0.7 copy-start.4
  81.0 0.7 copy-start.3
  81.7 0.7 copy-start.5

commit v2 on v1

--- a/solution.py
+++ b/solution.py
@@ -111,8 +111,8 @@
 
 
 def place(pairs_ref, k, n_row, n_col, groups):
-    first = pairs_ref[k, 0] - lax.axis_index("row") * (groups // n_row)
-    second = pairs_ref[k, 1] - lax.axis_index("col") * (groups // n_col)
+    first = pairs_ref[0, k] - lax.axis_index("row") * (groups // n_row)
+    second = pairs_ref[1, k] - lax.axis_index("col") * (groups // n_col)
     return first // 2, first % 2, second // 2, second % 2
 
 
@@ -129,12 +129,11 @@
     return start // LANES, start % LANES
 
 
-def build_kernel(n_row, n_col, cams, pairs_ref, cam_ref, land_ref, resid_ref, ocam_ref, oland_ref, damp_ref, part_ref, m_ref, fac_ref, damp_tile_ref):
+def build_kernel(n_row, n_col, cams, pairs_ref, cam_ref, land_ref, resid_ref, ocam_ref, oland_ref, damp_ref, part_ref, jac_ref, m_ref, fac_ref, damp_tile_ref):
     groups = cams // CAM
     row_tiles = cams // n_row // LANES
     tiles = row_tiles + cams // n_col // LANES
-    count = cam_ref.shape[0]
-    obs = cam_ref.shape[2]
+    count, obs = ocam_ref.shape
     shard = damp_ref.shape[1]
     part_ref[...] = jnp.zeros(part_ref.shape, jnp.float32)
     rhs_ref, diag_ref = part_ref.at[0], part_ref.at[1]
@@ -152,8 +151,8 @@
     for k in range(count):
         cam_hot = onehot(ocam_ref[k : k + 1, :], 2 * CAM)
         land_hot = onehot(oland_ref[k : k + 1, :], LM)
-        lj = [land_ref[k, i : i + 1, :] for i in range(6)]
-        e0, e1 = resid_ref[k, 0:1, :], resid_ref[k, 1:2, :]
+        lj = [land_ref[i, k : k + 1, :] for i in range(6)]
+        e0, e1 = resid_ref[0, k : k + 1, :], resid_ref[1, k : k + 1, :]
 
         def outer(i, j):
             return lj[i] * lj[j] + lj[3 + i] * lj[3 + j]
@@ -173,8 +172,10 @@
         m_ref[k] = stack_rows(m0 + m1, 8)
         w0 = m0[0] * at_obs[6] + m0[1] * at_obs[7] + m0[2] * at_obs[8] - e0
         w1 = m1[0] * at_obs[6] + m1[1] * at_obs[7] + m1[2] * at_obs[8] - e1
-        j0 = pad_rows(cam_ref[k, 0:9, :], 16)
-        j1 = pad_rows(cam_ref[k, 9:18, :], 16)
+        j0 = pad_rows(cam_ref[0:9, k, :], 16)
+        j1 = pad_rows(cam_ref[9:18, k, :], 16)
+        jac_ref[k, 0] = j0
+        jac_ref[k, 1] = j1
         rhs = j0 * w0 + j1 * w1
         coupled = jnp.concatenate([j0 * m0[b] + j1 * m1[b] for b in range(3)], axis=0)
         same = jnp.where(key_t[:, k : k + 1] == key[k : k + 1, :], 1.0, 0.0).astype(jnp.bfloat16)
@@ -186,28 +187,29 @@
         scatter_pair(both[16:], diag_ref, tiles, row_tiles, spot)
 
 
-def half_product(k, p_ref, pairs_ref, cam_ref, ocam_ref, oland_ref, m_ref):
+def half_product(k, p_ref, pairs_ref, jac_ref, ocam_ref, oland_ref, m_ref):
     cams_tiles = p_ref.shape[0] * 8 // 9
-    first, second = pairs_ref[k, 0], pairs_ref[k, 1]
+    first, second = pairs_ref[0, k], pairs_ref[1, k]
     p_first = to_first(load_tile(p_ref, cams_tiles, first // 2), first % 2)
     p_second = to_second(load_tile(p_ref, cams_tiles, second // 2), second % 2)
     p_here = jnp.where(lane_ids(16) < CAM, p_first, p_second)
     cam_hot = onehot(ocam_ref[k : k + 1, :], 2 * CAM)
     land_hot = onehot(oland_ref[k : k + 1, :], LM)
-    at_obs = dot3(p_here, cam_hot, NN)[:9]
-    u0 = jnp.sum(cam_ref[k, 0:9, :] * at_obs, axis=0, keepdims=True)
-    u1 = jnp.sum(cam_ref[k, 9:18, :] * at_obs, axis=0, keepdims=True)
+    at_obs = dot3(p_here, cam_hot, NN)
+    u0 = jnp.sum(jac_ref[k, 0] * at_obs, axis=0, keepdims=True)
+    u1 = jnp.sum(jac_ref[k, 1] * at_obs, axis=0, keepdims=True)
     m = [m_ref[k, i : i + 1, :] for i in range(6)]
     y = [m[b] * u0 + m[3 + b] * u1 for b in range(3)]
     y_land = dot3(stack_rows(y, 16), land_hot, NT)
     return cam_hot, land_hot, u0, u1, m, y_land
 
 
-def first_kernel(n_row, n_col, cams, pairs_ref, sums_ref, cam_ref, ocam_ref, oland_ref, m_ref, fac_ref, damp_tile_ref, part_ref, back_ref, p_ref):
+def first_kernel(n_row, n_col, cams, pairs_ref, sums_ref, jac_ref, ocam_ref, oland_ref, m_ref, fac_ref, damp_tile_ref, parts_ref, back_ref, p_ref):
+    part_ref = parts_ref.at[0]
     groups = cams // CAM
     row_tiles = cams // n_row // LANES
     tiles = row_tiles + cams // n_col // LANES
-    count = cam_ref.shape[0]
+    count = jac_ref.shape[0]
     p_ref[...] = sums_ref[0] * (1.0 / sums_ref[1])
     part_ref[...] = jnp.zeros(part_ref.shape, jnp.float32)
     own_tile, _ = own_place(n_row, n_col, cams)
@@ -215,7 +217,7 @@
     own = load_tile(p_ref, cams // LANES, whole_tile)
     add_tile(part_ref, tiles, own_tile, own * damp_tile_ref[...])
     for k in range(count):
-        cam_hot, land_hot, u0, u1, m, y_land = half_product(k, p_ref, pairs_ref, cam_ref, ocam_ref, oland_ref, m_ref)
+        cam_hot, land_hot, u0, u1, m, y_land = half_product(k, p_ref, pairs_ref, jac_ref, ocam_ref, oland_ref, m_ref)
         factor = row_list(fac_ref[k], 9)
         solved = upper_solve(factor, y_land[0:1], y_land[1:2], y_land[2:3])
         from_t = upper_solve(factor, factor[6], factor[7], factor[8])
@@ -223,7 +225,7 @@
         y_obs = row_list(dot3(y_land, land_hot, NN), 3)
         v0 = u0 - (m[0] * y_obs[0] + m[1] * y_obs[1] + m[2] * y_obs[2])
         v1 = u1 - (m[3] * y_obs[0] + m[4] * y_obs[1] + m[5] * y_obs[2])
-        image = pad_rows(cam_ref[k, 0:9, :] * v0 + cam_ref[k, 9:18, :] * v1, 16)
+        image = jac_ref[k, 0] * v0 + jac_ref[k, 1] * v1
         image = dot3(image, cam_hot, NT)
         scatter_pair(image, part_ref, tiles, row_tiles, place(pairs_ref, k, n_row, n_col, groups))
 
@@ -233,11 +235,11 @@
     return jnp.sum(jnp.sum(x, axis=0, keepdims=True), axis=1, keepdims=True)
 
 
-def second_kernel(n_row, n_col, cams, pairs_ref, sums_ref, image_ref, cam_ref, ocam_ref, oland_ref, m_ref, fac_ref, damp_tile_ref, back_ref, energy_ref, cam_out_ref, land_base_ref, land_slope_ref, p_ref, d_ref):
+def second_kernel(n_row, n_col, cams, pairs_ref, sums_ref, image_ref, jac_ref, ocam_ref, oland_ref, m_ref, fac_ref, damp_tile_ref, back_ref, energy_ref, cam_out_ref, land_base_ref, land_slope_ref, p_ref, d_ref):
     row_tiles = cams // n_row // LANES
-    count = cam_ref.shape[0]
+    count = jac_ref.shape[0]
     shard = cam_out_ref.shape[1]
-    right, image = sums_ref[0], image_ref[...]
+    right, image = sums_ref[0], image_ref[0]
     precond = 1.0 / sums_ref[1]
     start = right * precond
     norm_now = total_sum(right * start)
@@ -264,12 +266,12 @@
     cam_out_ref[1:2, :] = norm_next * flat_second
 
     for k in range(count):
-        _, land_hot, u0, u1, m, y_land = half_product(k, d_ref, pairs_ref, cam_ref, ocam_ref, oland_ref, m_ref)
+        _, land_hot, u0, u1, m, y_land = half_product(k, d_ref, pairs_ref, jac_ref, ocam_ref, oland_ref, m_ref)
         factor = row_list(fac_ref[k], 9)
         solved = upper_solve(factor, y_land[0:1], y_land[1:2], y_land[2:3])
         for b in range(3):
-            land_base_ref[k, b : b + 1, :] = -(back_ref[k, 3 + b : 4 + b, :] + alpha * back_ref[k, b : b + 1, :])
-            land_slope_ref[k, b : b + 1, :] = -norm_next * solved[b]
+            land_base_ref[b, k : k + 1, :] = -(back_ref[k, 3 + b : 4 + b, :] + alpha * back_ref[k, b : b + 1, :])
+            land_slope_ref[b, k : k + 1, :] = -norm_next * solved[b]
         y_obs = row_list(dot3(y_land, land_hot, NN), 3)
         v0 = u0 - (m[0] * y_obs[0] + m[1] * y_obs[1] + m[2] * y_obs[2])
         v1 = u1 - (m[3] * y_obs[0] + m[4] * y_obs[1] + m[5] * y_obs[2])
@@ -277,13 +279,39 @@
     energy_ref[...] = jnp.broadcast_to(energy, energy_ref.shape)
 
 
-def hyper(x, n_row, n_col):
-    n = n_row * n_col
-    bit = 1
-    while bit < n:
-        x = x + lax.ppermute(x, AXES, [(i, i ^ bit) for i in range(n)])
-        bit *= 2
-    return x
+def merge_kernel(n_row, n_col, cams, radix, *refs):
+    *part_refs, whole_ref = refs
+    row_tiles = cams // n_row // LANES
+    col_tiles = cams // n_col // LANES
+    tiles = row_tiles + col_tiles
+    whole_tiles = cams // LANES
+    row, col = lax.axis_index("row"), lax.axis_index("col")
+    whole_ref[...] = jnp.zeros(whole_ref.shape, jnp.float32)
+    for v in range(whole_ref.shape[0]):
+
+        def add(t, local, x):
+            whole_ref[v, t] += x[local]
+            ninth = x[tiles + local // 8, local % 8 : local % 8 + 1]
+            whole_ref[v, whole_tiles + t // 8, pl.ds(t % 8, 1), :] += ninth
+
+        parts = [ref[v] for ref in part_refs]
+        for digit, part in enumerate(parts):
+            start = (row ^ (digit * (n_row // radix))) * row_tiles
+            for i in range(row_tiles):
+                add(start + i, i, part)
+        total = parts[0]
+        for part in parts[1:]:
+            total = total + part
+        for i in range(col_tiles):
+            add(col * col_tiles + i, row_tiles + i, total)
+
+
+def exchange(x, masks, n_dev):
+    return [lax.ppermute(x, AXES, [(i, i ^ mask) for i in range(n_dev)]) for mask in masks]
+
+
+def in_vmem(x):
+    return pltpu.with_memory_space_constraint(x, pltpu.VMEM)
 
 
 def per_device(n_row, n_col, cam_jac, land_jac, resid, obs_cam, obs_land, pairs, cam_damp):
@@ -301,59 +329,70 @@
     smem = pl.BlockSpec(memory_space=pltpu.SMEM)
 
     def shape(*dims):
-        return jax.ShapeDtypeStruct(dims, f32)
-
-    part, m, fac, damp_tile = pl.pallas_call(
+        return pltpu.VMEM(dims, f32)
+
+    radix = min(n_row, 4)
+    low = n_row // radix
+    lead = [digit * low * n_col for digit in range(1, radix)]
+    ones = [digit * n_col for digit in range(1, low)]
+    twos = [digit * 2 for digit in range(1, n_col // 2)]
+    if len(ones) == 1 and len(twos) == 1:
+        rounds = [[ones[0], twos[0], ones[0] + twos[0]], [1]]
+    else:
+        rounds = [ones, twos, [1]]
+
+    def all_reduce(part):
+        pieces = [part] + exchange(part, lead, n_dev)
+        x = pl.pallas_call(
+            functools.partial(merge_kernel, n_row, n_col, cams, radix),
+            out_shape=shape(part.shape[0], whole_packed, 8, LANES),
+            in_specs=[vmem] * radix,
+            out_specs=vmem,
+        )(*map(in_vmem, pieces))
+        for masks in rounds:
+            for y in exchange(x, masks, n_dev):
+                x = x + y
+        return x
+
+    part, jac, m, fac, damp_tile = pl.pallas_call(
         functools.partial(build_kernel, n_row, n_col, cams),
-        out_shape=(shape(2, part_tiles, 8, LANES), shape(count, 8, obs), shape(count, 16, LM), shape(16, LANES)),
+        out_shape=(shape(2, part_tiles, 8, LANES), shape(count, 2, 16, obs), shape(count, 8, obs), shape(count, 16, LM), shape(16, LANES)),
         in_specs=[smem] + [vmem] * 6,
-        out_specs=(vmem,) * 4,
-    )(pairs, cam_jac, land_jac, resid, obs_cam, obs_land, cam_damp.reshape(1, shard))
-
-    def expand(x):
-        whole = jnp.zeros((whole_packed, 8, LANES), f32)
-
-        def put(whole, lo, hi, start):
-            old = lax.dynamic_slice_in_dim(whole, start, hi - lo, 0)
-            return lax.dynamic_update_slice_in_dim(whole, old + x[lo:hi], start, 0)
-
-        whole = put(whole, 0, row_tiles, lax.axis_index("row") * row_tiles)
-        whole = put(whole, row_tiles, tiles, lax.axis_index("col") * (tiles - row_tiles))
-        ninth = jnp.zeros((whole_tiles, LANES), f32)
-        flat = x[tiles:].reshape(-1, LANES)
-        for lo, hi, start in (
-            (0, row_tiles, lax.axis_index("row") * row_tiles),
-            (row_tiles, tiles, lax.axis_index("col") * (tiles - row_tiles)),
-        ):
-            old = lax.dynamic_slice_in_dim(ninth, start, hi - lo, 0)
-            ninth = lax.dynamic_update_slice_in_dim(ninth, old + flat[lo:hi], start, 0)
-        ninth = ninth.reshape(-1, 8, LANES)
-        return lax.dynamic_update_slice_in_dim(whole, ninth, whole_tiles, 0)
-
-    sums = hyper(jnp.stack([expand(part[0]), expand(part[1])]), n_row, n_col)
+        out_specs=(vmem,) * 5,
+    )(
+        pairs.T,
+        jnp.transpose(cam_jac, (1, 0, 2)),
+        jnp.transpose(land_jac, (1, 0, 2)),
+        jnp.transpose(resid, (1, 0, 2)),
+        obs_cam,
+        obs_land,
+        cam_damp.reshape(1, shard),
+    )
+    sums = all_reduce(part)
 
     image, back = pl.pallas_call(
         functools.partial(first_kernel, n_row, n_col, cams),
-        out_shape=(shape(part_tiles, 8, LANES), shape(count, 8, LM)),
+        out_shape=(shape(1, part_tiles, 8, LANES), shape(count, 8, LM)),
         in_specs=[smem] + [vmem] * 7,
         out_specs=(vmem,) * 2,
         scratch_shapes=[pltpu.VMEM((whole_packed, 8, LANES), f32)],
-    )(pairs, sums, cam_jac, obs_cam, obs_land, m, fac, damp_tile)
-
-    image = hyper(expand(image), n_row, n_col)
+    )(pairs.T, *map(in_vmem, (sums, jac, obs_cam, obs_land, m, fac, damp_tile)))
+
+    image = all_reduce(image)
 
     energy, cam_out, land_base, land_slope = pl.pallas_call(
         functools.partial(second_kernel, n_row, n_col, cams),
-        out_shape=(shape(8, LANES), shape(2, shard), shape(count, 3, LM), shape(count, 3, LM)),
+        out_shape=(shape(8, LANES), shape(2, shard), shape(3, count, LM), shape(3, count, LM)),
         in_specs=[smem] + [vmem] * 9,
         out_specs=(vmem,) * 4,
         scratch_shapes=[pltpu.VMEM((whole_packed, 8, LANES), f32)] * 2,
-    )(pairs, sums, image, cam_jac, obs_cam, obs_land, m, fac, damp_tile, back)
+    )(pairs.T, *map(in_vmem, (sums, image, jac, obs_cam, obs_land, m, fac, damp_tile, back)))
 
     spread = jnp.broadcast_to(energy[0:1][None], (n_dev, 1, LANES))
     gathered = lax.all_to_all(spread, AXES, 0, 0, tiled=True)
     inverse = 1.0 / jnp.sum(gathered, axis=0)[0, 0]
-    return cam_out[0] + inverse * cam_out[1], land_base + inverse * land_slope
+    land = land_base + inverse * land_slope
+    return cam_out[0] + inverse * cam_out[1], jnp.transpose(land, (1, 0, 2))
 
 
 def solution(mesh):

time: 83.5 us -> 61.1 us (0.73)
  waiting for transfers between devices: 31.2 us -> 18.9 us
  local copies, waits for them, and re-layouts: 7.94 us -> 3.3 us
  Pallas kernels: 11.1 us -> 8.62 us
  blocking collectives: 12.6 us -> 10.2 us
  other arithmetic: 2.82 us -> 1.32 us
  starting transfers between devices: 16.5 us -> 17.4 us
    ppermute x10 -> x14, waiting for transfers between devices: 31.2 us -> 18.9 us  [exchange(): lax.ppermute(x, AXES, [(i, i ^ mask) for i in range(n_dev)])]
    unnamed x22 -> x5, local copies, waits for them, and re-layouts: 5.9 us -> 2.02 us
    all_to_all x1, blocking collectives: 12.6 us -> 10.2 us  [per_device(): gathered = lax.all_to_all(spread, AXES, 0, 0, tiled=True)]
    add x12 -> x5, other arithmetic: 2.05 us -> 0.7 us  [the longest x1 0.61 us: per_device(): return (cam_out[0] + inverse * cam_out[1], jnp.transpose(land, (1, 0, 2)))]
    pallas_call x1, Pallas kernels: 3.69 us -> 2.66 us  [per_device(): pl.pallas_call(functools.partial(second_kernel, n_row, n_col, cams), out_...]
    pallas_call x1, Pallas kernels: 3.16 us -> 2.15 us  [per_device(): pl.pallas_call(functools.partial(first_kernel, n_row, n_col, cams), out_s...]
    ppermute x10 -> x14, starting transfers between devices: 16.5 us -> 17.4 us  [exchange(): lax.ppermute(x, AXES, [(i, i ^ mask) for i in range(n_dev)])]
  transfers between devices with their start and end apart: 10 -> 14, of which waited for: 10 -> 12; matrix products, arithmetic and copies ran while one was open for 0% -> 0% of each run, Pallas kernels for 0% -> 0%
where the time goes in v2:
time: 61.1 us; the launch traced here: 60.6 us
  waiting for transfers between devices  18.9 us (31%)
  starting transfers between devices  17.4 us (28%)
  blocking collectives  10.2 us (17%)
  Pallas kernels  8.62 us (14%)
  local copies, waits for them, and re-layouts  3.3 us (5%)
  other arithmetic  1.32 us (2%)
  between operations  0.77 us (1%)
    ppermute x14, waiting for transfers between devices, exchange(): lax.ppermute(x, AXES, [(i, i ^ mask) for i in range(n_dev)])  18.9 us
    ppermute x14, starting transfers between devices, exchange(): lax.ppermute(x, AXES, [(i, i ^ mask) for i in range(n_dev)])  17.4 us
    all_to_all x1, blocking collectives, per_device(): gathered = lax.all_to_all(spread, AXES, 0, 0, tiled=True)  10.2 us
    pallas_call x1, Pallas kernels, per_device(): pl.pallas_call(functools.partial(build_kernel, n_row, n_col, cams), out_s...  3.55 us
    pallas_call x1, Pallas kernels, per_device(): pl.pallas_call(functools.partial(second_kernel, n_row, n_col, cams), out_...  2.66 us
    pallas_call x1, Pallas kernels, per_device(): pl.pallas_call(functools.partial(first_kernel, n_row, n_col, cams), out_s...  2.15 us
    unnamed x5, local copies, waits for them, and re-layouts  2.02 us
    reshape x1, local copies, waits for them, and re-layouts, per_device(): cam_damp.reshape(1, shard)  1.27 us
  transfers between devices with their start and end apart: 14, of which 12 were waited for; matrix products, arithmetic and copies ran while one was open for 0% of the time, Pallas kernels for 0%

profile of v2, /device:TPU:0, one launch (start us, length us, event | category | flops | bytes accessed | tf_op | source)
XLA Modules:
  0.0 60.6 jit_solution(3097343638613126498)
XLA Ops:
  0.6 1.3 %reshape.16.damp_ref = f32[1,576]{1,0:T(1,128)} reshape(f32[576]{0:T(1024)} %param.13) | data formatting | bytes 4608 | tf_op jit(solution)/shard_map/reshape | solution.py:369
  1.9 1.3 %copy.14 = f32[4,2,512]{2,0,1:T(4,128)} copy(f32[4,2,512]{2,1,0:T(2,128)} %param.9) | data formatting | bytes 32768 | tf_op args[2]
  3.2 3.6 %shard_map.86 = (f32[2,7,8,128]{3,2,1,0:T(8,128)S(1)}, f32[4,2,16,512]{3,2,1,0:T(8,128)S(1)}, f32[4,8,512]{2,1,0:T(8,128)S(1)}, f32[4,16,128]{2,1,0:T(8,128)S(1)}, f32[16,128]{1,0:T(8,128)S(1)}) custom-call(s32[2,4]{1,0:T(2,128)} %bitcast.18, f32[18,4,512]{2,1,0:T(4,128)} %bitcast.14, f32[6,4,512]{2,1,0:T(4,128)} %bitcast.17, f32[2,4,512]{2,1,0:T(4,128)} %bitcast.15, ...), custom_call_target="tpu_custom_call" | custom-call | tf_op jit(solution)/shard_map/pallas_call | solution.py:357
  6.8 5.1 %collective-permute-start.2 = (f32[2,7,8,128]{3,2,1,0:T(8,128)S(1)}, f32[2,7,8,128]{3,2,1,0:T(8,128)S(1)}, u32[]{:S(2)}, u32[]{:S(2)}) collective-permute-start(f32[2,7,8,128]{3,2,1,0:T(8,128)S(1)} %get-tuple-element.13.refs_0_), channel_id=1, source_target_pairs={{0,24},{1,25},{2,26},{3,27},{4,28},{5,29},{6,30},{7,31},{8,16},{9,... | collective-permute-start | bytes 172040 | tf_op jit(solution)/shard_map/ppermute | solution.py:310
  11.9 0.6 %collective-permute-start = (f32[2,7,8,128]{3,2,1,0:T(8,128)S(1)}, f32[2,7,8,128]{3,2,1,0:T(8,128)S(1)}, u32[]{:S(2)}, u32[]{:S(2)}) collective-permute-start(f32[2,7,8,128]{3,2,1,0:T(8,128)S(1)} %get-tuple-element.13.refs_0_), channel_id=1, source_target_pairs={{0,8},{1,9},{2,10},{3,11},{4,12},{5,13},{6,14},{7,15},{8,0},{9,1},... | collective-permute-start | bytes 172040 | tf_op jit(solution)/shard_map/ppermute | solution.py:310
  12.5 1.8 %collective-permute-done.2.refs_3_ = f32[2,7,8,128]{3,2,1,0:T(8,128)S(1)} collective-permute-done((f32[2,7,8,128]{3,2,1,0:T(8,128)S(1)}, f32[2,7,8,128]{3,2,1,0:T(8,128)S(1)}, u32[]{:S(2)}, u32[]{:S(2)}) %collective-permute-start.2) | collective-permute-done | bytes 57376 | tf_op jit(solution)/shard_map/ppermute | solution.py:310
  14.3 2.7 %collective-permute-done.1.refs_2_ = f32[2,7,8,128]{3,2,1,0:T(8,128)S(1)} collective-permute-done((f32[2,7,8,128]{3,2,1,0:T(8,128)S(1)}, f32[2,7,8,128]{3,2,1,0:T(8,128)S(1)}, u32[]{:S(2)}, u32[]{:S(2)}) %collective-permute-start.1) | collective-permute-done | bytes 57376 | tf_op jit(solution)/shard_map/ppermute | solution.py:310
  17.1 2.5 %collective-permute-start.5 = (f32[2,18,8,128]{3,2,1,0:T(8,128)S(1)}, f32[2,18,8,128]{3,2,1,0:T(8,128)S(1)}, u32[]{:S(2)}, u32[]{:S(2)}) collective-permute-start(f32[2,18,8,128]{3,2,1,0:T(8,128)S(1)} %shard_map.87), channel_id=1, source_target_pairs={{0,6},{1,7},{2,4},{3,5},{4,2},{5,3},{6,0},{7,1},{8,14},{9,15},{10,... | collective-permute-start | bytes 442376 | tf_op jit(solution)/shard_map/ppermute | solution.py:310
  20.7 3.5 %collective-permute-done.5 = f32[2,18,8,128]{3,2,1,0:T(8,128)S(1)} collective-permute-done((f32[2,18,8,128]{3,2,1,0:T(8,128)S(1)}, f32[2,18,8,128]{3,2,1,0:T(8,128)S(1)}, u32[]{:S(2)}, u32[]{:S(2)}) %collective-permute-start.5) | collective-permute-done | bytes 147488 | tf_op jit(solution)/shard_map/ppermute | solution.py:310
  24.2 2.0 %collective-permute-done.4 = f32[2,18,8,128]{3,2,1,0:T(8,128)S(1)} collective-permute-done((f32[2,18,8,128]{3,2,1,0:T(8,128)S(1)}, f32[2,18,8,128]{3,2,1,0:T(8,128)S(1)}, u32[]{:S(2)}, u32[]{:S(2)}) %collective-permute-start.4) | collective-permute-done | bytes 147488 | tf_op jit(solution)/shard_map/ppermute | solution.py:310
  26.4 1.4 %collective-permute-done.6 = f32[2,18,8,128]{3,2,1,0:T(8,128)S(1)} collective-permute-done((f32[2,18,8,128]{3,2,1,0:T(8,128)S(1)}, f32[2,18,8,128]{3,2,1,0:T(8,128)S(1)}, u32[]{:S(2)}, u32[]{:S(2)}) %collective-permute-start.6) | collective-permute-done | bytes 147488 | tf_op jit(solution)/shard_map/ppermute | solution.py:310
  27.8 0.7 %copy-done = s32[4,512]{1,0:T(4,128)S(1)} copy-done((s32[4,512]{1,0:T(4,128)S(1)}, s32[4,512]{1,0:T(4,128)}, u32[]{:S(2)}) %copy-start) | copy-done | bytes 8216
  28.5 2.1 %shard_map.88 = (f32[1,7,8,128]{3,2,1,0:T(8,128)S(1)}, f32[4,8,128]{2,1,0:T(8,128)S(1)}) custom-call(s32[2,4]{1,0:T(2,128)} %bitcast.19, f32[2,18,8,128]{3,2,1,0:T(8,128)S(1)} %add.36.sums_ref, f32[4,2,16,512]{3,2,1,0:T(8,128)S(1)} %get-tuple-element.14.jac_ref, s32[4,512]{1,0:T(4,128)S(1)} %copy-done, s32[4,512]{1,0:T(4,128)S(1)} %copy-done.1, ...), custom_call_target="tpu_custom_call" | custom-call | tf_op jit(solution)/shard_map/pallas_call | solution.py:373
  30.6 2.1 %collective-permute-start.9 = (f32[1,7,8,128]{3,2,1,0:T(8,128)S(1)}, f32[1,7,8,128]{3,2,1,0:T(8,128)S(1)}, u32[]{:S(2)}, u32[]{:S(2)}) collective-permute-start(f32[1,7,8,128]{3,2,1,0:T(8,128)S(1)} %get-tuple-element.18.refs_0_), channel_id=1, source_target_pairs={{0,24},{1,25},{2,26},{3,27},{4,28},{5,29},{6,30},{7,31},{8,16},{9,... | collective-permute-start | bytes 86024 | tf_op jit(solution)/shard_map/ppermute | solution.py:310
  32.7 2.3 %collective-permute-start.7 = (f32[1,7,8,128]{3,2,1,0:T(8,128)S(1)}, f32[1,7,8,128]{3,2,1,0:T(8,128)S(1)}, u32[]{:S(2)}, u32[]{:S(2)}) collective-permute-start(f32[1,7,8,128]{3,2,1,0:T(8,128)S(1)} %get-tuple-element.18.refs_0_), channel_id=1, source_target_pairs={{0,8},{1,9},{2,10},{3,11},{4,12},{5,13},{6,14},{7,15},{8,0},{9,1},... | collective-permute-start | bytes 86024 | tf_op jit(solution)/shard_map/ppermute | solution.py:310
  35.1 1.3 %collective-permute-done.9.refs_3_ = f32[1,7,8,128]{3,2,1,0:T(8,128)S(1)} collective-permute-done((f32[1,7,8,128]{3,2,1,0:T(8,128)S(1)}, f32[1,7,8,128]{3,2,1,0:T(8,128)S(1)}, u32[]{:S(2)}, u32[]{:S(2)}) %collective-permute-start.9) | collective-permute-done | bytes 28704 | tf_op jit(solution)/shard_map/ppermute | solution.py:310
  36.4 1.1 %collective-permute-done.8.refs_2_ = f32[1,7,8,128]{3,2,1,0:T(8,128)S(1)} collective-permute-done((f32[1,7,8,128]{3,2,1,0:T(8,128)S(1)}, f32[1,7,8,128]{3,2,1,0:T(8,128)S(1)}, u32[]{:S(2)}, u32[]{:S(2)}) %collective-permute-start.8) | collective-permute-done | bytes 28704 | tf_op jit(solution)/shard_map/ppermute | solution.py:310
  37.6 1.8 %collective-permute-start.12 = (f32[1,18,8,128]{3,2,1,0:T(8,128)S(1)}, f32[1,18,8,128]{3,2,1,0:T(8,128)S(1)}, u32[]{:S(2)}, u32[]{:S(2)}) collective-permute-start(f32[1,18,8,128]{3,2,1,0:T(8,128)S(1)} %shard_map.89), channel_id=1, source_target_pairs={{0,6},{1,7},{2,4},{3,5},{4,2},{5,3},{6,0},{7,1},{8,14},{9,15},{10,... | collective-permute-start | bytes 221192 | tf_op jit(solution)/shard_map/ppermute | solution.py:310
  39.4 1.3 %collective-permute-start.11 = (f32[1,18,8,128]{3,2,1,0:T(8,128)S(1)}, f32[1,18,8,128]{3,2,1,0:T(8,128)S(1)}, u32[]{:S(2)}, u32[]{:S(2)}) collective-permute-start(f32[1,18,8,128]{3,2,1,0:T(8,128)S(1)} %shard_map.89), channel_id=1, source_target_pairs={{0,2},{1,3},{2,0},{3,1},{4,6},{5,7},{6,4},{7,5},{8,10},{9,11},{10,... | collective-permute-start | bytes 221192 | tf_op jit(solution)/shard_map/ppermute | solution.py:310
  41.2 2.5 %collective-permute-done.12 = f32[1,18,8,128]{3,2,1,0:T(8,128)S(1)} collective-permute-done((f32[1,18,8,128]{3,2,1,0:T(8,128)S(1)}, f32[1,18,8,128]{3,2,1,0:T(8,128)S(1)}, u32[]{:S(2)}, u32[]{:S(2)}) %collective-permute-start.12) | collective-permute-done | bytes 73760 | tf_op jit(solution)/shard_map/ppermute | solution.py:310
  44.1 0.9 %collective-permute-done.10 = f32[1,18,8,128]{3,2,1,0:T(8,128)S(1)} collective-permute-done((f32[1,18,8,128]{3,2,1,0:T(8,128)S(1)}, f32[1,18,8,128]{3,2,1,0:T(8,128)S(1)}, u32[]{:S(2)}, u32[]{:S(2)}) %collective-permute-start.10) | collective-permute-done | bytes 73760 | tf_op jit(solution)/shard_map/ppermute | solution.py:310
  45.1 1.3 %collective-permute-done.13 = f32[1,18,8,128]{3,2,1,0:T(8,128)S(1)} collective-permute-done((f32[1,18,8,128]{3,2,1,0:T(8,128)S(1)}, f32[1,18,8,128]{3,2,1,0:T(8,128)S(1)}, u32[]{:S(2)}, u32[]{:S(2)}) %collective-permute-start.13) | collective-permute-done | bytes 73760 | tf_op jit(solution)/shard_map/ppermute | solution.py:310
  46.4 2.7 %shard_map.90 = (f32[8,128]{1,0:T(8,128)S(1)}, f32[2,576]{1,0:T(2,128)S(1)}, f32[3,4,128]{2,1,0:T(4,128)S(1)}, f32[3,4,128]{2,1,0:T(4,128)S(1)}) custom-call(s32[2,4]{1,0:T(2,128)} %bitcast.20, f32[2,18,8,128]{3,2,1,0:T(8,128)S(1)} %add.36.sums_ref, f32[1,18,8,128]{3,2,1,0:T(8,128)S(1)} %add.40.image_ref, f32[4,2,16,512]{3,2,1,0:T(8,128)S(1)} %get-tuple-element.14.jac_ref, ...), custom_call_target="tpu_custom_call" | custom-call | tf_op jit(solution)/shard_map/pallas_call | solution.py:383
  49.1 10.2 %all_to_all.5 = f32[32,1,128]{2,1,0:T(1,128)S(1)} all-to-all(f32[32,1,128]{2,1,0:T(1,128)S(1)} %broadcast_in_dim.9), channel_id=1, replica_groups=mesh['row'=8,'col'=4] {'row','col'}, dimensions={0} | all-to-all | bytes 32768 | tf_op jit(solution)/shard_map/all_to_all | solution.py:392
  (25 shorter events, 3.8 us)
Async XLA Ops:
  6.8 7.5 %collective-permute-start.2 = (f32[2,7,8,128]{3,2,1,0:T(8,128)S(1)}, f32[2,7,8,128]{3,2,1,0:T(8,128)S(1)}, u32[]{:S(2)}, u32[]{:S(2)}) collective-permute-start(f32[2,7,8,128]{3,2,1,0:T(8,128)S(1)} %get-tuple-element.13.refs_0_), channel_id=1, source_target_pairs={{0,24},{1,25},{2,26},{3,27},{4,28},{5,29},{6,30},{7,31},{8,16},{9,... | collective-permute-start | bytes 172040 | tf_op jit(solution)/shard_map/ppermute | solution.py:310
  11.9 5.1 %collective-permute-start.1 = (f32[2,7,8,128]{3,2,1,0:T(8,128)S(1)}, f32[2,7,8,128]{3,2,1,0:T(8,128)S(1)}, u32[]{:S(2)}, u32[]{:S(2)}) collective-permute-start(f32[2,7,8,128]{3,2,1,0:T(8,128)S(1)} %get-tuple-element.13.refs_0_), channel_id=1, source_target_pairs={{0,16},{1,17},{2,18},{3,19},{4,20},{5,21},{6,22},{7,23},{8,24},{9,... | collective-permute-start | bytes 172040 | tf_op jit(solution)/shard_map/ppermute | solution.py:310
  11.9 5.1 %collective-permute-start = (f32[2,7,8,128]{3,2,1,0:T(8,128)S(1)}, f32[2,7,8,128]{3,2,1,0:T(8,128)S(1)}, u32[]{:S(2)}, u32[]{:S(2)}) collective-permute-start(f32[2,7,8,128]{3,2,1,0:T(8,128)S(1)} %get-tuple-element.13.refs_0_), channel_id=1, source_target_pairs={{0,8},{1,9},{2,10},{3,11},{4,12},{5,13},{6,14},{7,15},{8,0},{9,1},... | collective-permute-start | bytes 172040 | tf_op jit(solution)/shard_map/ppermute | solution.py:310
  17.1 7.0 %collective-permute-start.5 = (f32[2,18,8,128]{3,2,1,0:T(8,128)S(1)}, f32[2,18,8,128]{3,2,1,0:T(8,128)S(1)}, u32[]{:S(2)}, u32[]{:S(2)}) collective-permute-start(f32[2,18,8,128]{3,2,1,0:T(8,128)S(1)} %shard_map.87), channel_id=1, source_target_pairs={{0,6},{1,7},{2,4},{3,5},{4,2},{5,3},{6,0},{7,1},{8,14},{9,15},{10,... | collective-permute-start | bytes 442376 | tf_op jit(solution)/shard_map/ppermute | solution.py:310
  19.7 6.5 %collective-permute-start.4 = (f32[2,18,8,128]{3,2,1,0:T(8,128)S(1)}, f32[2,18,8,128]{3,2,1,0:T(8,128)S(1)}, u32[]{:S(2)}, u32[]{:S(2)}) collective-permute-start(f32[2,18,8,128]{3,2,1,0:T(8,128)S(1)} %shard_map.87), channel_id=1, source_target_pairs={{0,2},{1,3},{2,0},{3,1},{4,6},{5,7},{6,4},{7,5},{8,10},{9,11},{10,... | collective-permute-start | bytes 442376 | tf_op jit(solution)/shard_map/ppermute | solution.py:310
  20.2 6.1 %collective-permute-start.3 = (f32[2,18,8,128]{3,2,1,0:T(8,128)S(1)}, f32[2,18,8,128]{3,2,1,0:T(8,128)S(1)}, u32[]{:S(2)}, u32[]{:S(2)}) collective-permute-start(f32[2,18,8,128]{3,2,1,0:T(8,128)S(1)} %shard_map.87), channel_id=1, source_target_pairs={{0,4},{1,5},{2,6},{3,7},{4,0},{5,1},{6,2},{7,3},{8,12},{9,13},{10,... | collective-permute-start | bytes 442376 | tf_op jit(solution)/shard_map/ppermute | solution.py:310
  26.3 1.4 %collective-permute-start.6 = (f32[2,18,8,128]{3,2,1,0:T(8,128)S(1)}, f32[2,18,8,128]{3,2,1,0:T(8,128)S(1)}, u32[]{:S(2)}, u32[]{:S(2)}) collective-permute-start(f32[2,18,8,128]{3,2,1,0:T(8,128)S(1)} %add_add_fusion), channel_id=1, source_target_pairs={{0,1},{1,0},{2,3},{3,2},{4,5},{5,4},{6,7},{7,6},{8,9},{9,8},{10,11... | collective-permute-start | bytes 442376 | tf_op jit(solution)/shard_map/ppermute | solution.py:310
  27.8 0.7 %copy-start = (s32[4,512]{1,0:T(4,128)S(1)}, s32[4,512]{1,0:T(4,128)}, u32[]{:S(2)}) copy-start(s32[4,512]{1,0:T(4,128)} %ocam_ref.5) | copy-start | bytes 24580
  27.8 0.7 %copy-start.1 = (s32[4,512]{1,0:T(4,128)S(1)}, s32[4,512]{1,0:T(4,128)}, u32[]{:S(2)}) copy-start(s32[4,512]{1,0:T(4,128)} %oland_ref.5) | copy-start | bytes 24580
  30.6 5.7 %collective-permute-start.9 = (f32[1,7,8,128]{3,2,1,0:T(8,128)S(1)}, f32[1,7,8,128]{3,2,1,0:T(8,128)S(1)}, u32[]{:S(2)}, u32[]{:S(2)}) collective-permute-start(f32[1,7,8,128]{3,2,1,0:T(8,128)S(1)} %get-tuple-element.18.refs_0_), channel_id=1, source_target_pairs={{0,24},{1,25},{2,26},{3,27},{4,28},{5,29},{6,30},{7,31},{8,16},{9,... | collective-permute-start | bytes 86024 | tf_op jit(solution)/shard_map/ppermute | solution.py:310
  32.7 4.8 %collective-permute-start.8 = (f32[1,7,8,128]{3,2,1,0:T(8,128)S(1)}, f32[1,7,8,128]{3,2,1,0:T(8,128)S(1)}, u32[]{:S(2)}, u32[]{:S(2)}) collective-permute-start(f32[1,7,8,128]{3,2,1,0:T(8,128)S(1)} %get-tuple-element.18.refs_0_), channel_id=1, source_target_pairs={{0,16},{1,17},{2,18},{3,19},{4,20},{5,21},{6,22},{7,23},{8,24},{9,... | collective-permute-start | bytes 86024 | tf_op jit(solution)/shard_map/ppermute | solution.py:310
  32.7 4.8 %collective-permute-start.7 = (f32[1,7,8,128]{3,2,1,0:T(8,128)S(1)}, f32[1,7,8,128]{3,2,1,0:T(8,128)S(1)}, u32[]{:S(2)}, u32[]{:S(2)}) collective-permute-start(f32[1,7,8,128]{3,2,1,0:T(8,128)S(1)} %get-tuple-element.18.refs_0_), channel_id=1, source_target_pairs={{0,8},{1,9},{2,10},{3,11},{4,12},{5,13},{6,14},{7,15},{8,0},{9,1},... | collective-permute-start | bytes 86024 | tf_op jit(solution)/shard_map/ppermute | solution.py:310
  37.6 6.1 %collective-permute-start.12 = (f32[1,18,8,128]{3,2,1,0:T(8,128)S(1)}, f32[1,18,8,128]{3,2,1,0:T(8,128)S(1)}, u32[]{:S(2)}, u32[]{:S(2)}) collective-permute-start(f32[1,18,8,128]{3,2,1,0:T(8,128)S(1)} %shard_map.89), channel_id=1, source_target_pairs={{0,6},{1,7},{2,4},{3,5},{4,2},{5,3},{6,0},{7,1},{8,14},{9,15},{10,... | collective-permute-start | bytes 221192 | tf_op jit(solution)/shard_map/ppermute | solution.py:310
  39.4 4.7 %collective-permute-start.11 = (f32[1,18,8,128]{3,2,1,0:T(8,128)S(1)}, f32[1,18,8,128]{3,2,1,0:T(8,128)S(1)}, u32[]{:S(2)}, u32[]{:S(2)}) collective-permute-start(f32[1,18,8,128]{3,2,1,0:T(8,128)S(1)} %shard_map.89), channel_id=1, source_target_pairs={{0,2},{1,3},{2,0},{3,1},{4,6},{5,7},{6,4},{7,5},{8,10},{9,11},{10,... | collective-permute-start | bytes 221192 | tf_op jit(solution)/shard_map/ppermute | solution.py:310
  40.7 4.4 %collective-permute-start.10 = (f32[1,18,8,128]{3,2,1,0:T(8,128)S(1)}, f32[1,18,8,128]{3,2,1,0:T(8,128)S(1)}, u32[]{:S(2)}, u32[]{:S(2)}) collective-permute-start(f32[1,18,8,128]{3,2,1,0:T(8,128)S(1)} %shard_map.89), channel_id=1, source_target_pairs={{0,4},{1,5},{2,6},{3,7},{4,0},{5,1},{6,2},{7,3},{8,12},{9,13},{10,... | collective-permute-start | bytes 221192 | tf_op jit(solution)/shard_map/ppermute | solution.py:310
  45.1 1.3 %collective-permute-start.13 = (f32[1,18,8,128]{3,2,1,0:T(8,128)S(1)}, f32[1,18,8,128]{3,2,1,0:T(8,128)S(1)}, u32[]{:S(2)}, u32[]{:S(2)}) collective-permute-start(f32[1,18,8,128]{3,2,1,0:T(8,128)S(1)} %add_add_fusion.1), channel_id=1, source_target_pairs={{0,1},{1,0},{2,3},{3,2},{4,5},{5,4},{6,7},{7,6},{8,9},{9,8},{10,11... | collective-permute-start | bytes 221192 | tf_op jit(solution)/shard_map/ppermute | solution.py:310

commit v3 on v2

--- a/solution.py
+++ b/solution.py
@@ -31,12 +31,21 @@
     return (y[2 * n :] + y[n : 2 * n]) + y[:n]
 
 
-def onehot(index_row, size):
-    ids = lax.broadcasted_iota(jnp.int32, (size, index_row.shape[1]), 0)
-    return jnp.where(ids == index_row, 1.0, 0.0).astype(jnp.bfloat16)
+def onehot(index_column, lanes):
+    return jnp.where(index_column == lanes, 1.0, 0.0).astype(jnp.bfloat16)
+
+
+def take_lanes(x, index_row):
+    pieces = []
+    for start in range(0, index_row.shape[1], LANES):
+        index = jnp.broadcast_to(index_row[:, start : start + LANES], x.shape)
+        pieces.append(jnp.take_along_axis(x, index, axis=1, mode="promise_in_bounds"))
+    return jnp.concatenate(pieces, axis=1)
 
 
 def pad_rows(x, rows):
+    if x.shape[0] == rows:
+        return x
     return jnp.concatenate([x, jnp.zeros((rows - x.shape[0], x.shape[1]), x.dtype)], axis=0)
 
 
@@ -129,44 +138,49 @@
     return start // LANES, start % LANES
 
 
-def build_kernel(n_row, n_col, cams, pairs_ref, cam_ref, land_ref, resid_ref, ocam_ref, oland_ref, damp_ref, part_ref, jac_ref, m_ref, fac_ref, damp_tile_ref):
+def build_kernel(n_row, n_col, cams, pairs_ref, cam_ref, land_ref, resid_ref, ocam_ref, oland_ref, damp_ref, part_ref, jac_ref, cam_hot_ref, land_hot_ref, index_ref, m_ref, fac_ref, damp_tile_ref):
     groups = cams // CAM
     row_tiles = cams // n_row // LANES
     tiles = row_tiles + cams // n_col // LANES
     count, obs = ocam_ref.shape
-    shard = damp_ref.shape[1]
+    shard = damp_ref.shape[0]
     part_ref[...] = jnp.zeros(part_ref.shape, jnp.float32)
     rhs_ref, diag_ref = part_ref.at[0], part_ref.at[1]
 
     own_tile, own_lane = own_place(n_row, n_col, cams)
-    spread = jnp.where(param_mask(shard), damp_ref[...], 0.0)
+    spread = jnp.where(param_mask(shard), damp_ref[...].reshape(1, shard), 0.0)
     damp_tile = dot3(spread, shard_select(shard, own_lane), NN)
     damp_tile_ref[...] = damp_tile
     add_tile(diag_ref, tiles, own_tile, damp_tile)
 
-    key = ocam_ref[...] * LM + oland_ref[...]
-    key = jnp.concatenate([key.astype(jnp.float32), jnp.full((8 - count, obs), -1.0, jnp.float32)], axis=0)
-    key_t = jnp.transpose(key)
+    index_ref[0] = ocam_ref[...]
+    index_ref[1] = oland_ref[...]
+    rows = jnp.concatenate([ocam_ref[...], oland_ref[...]], axis=0).astype(jnp.float32)
+    columns = jnp.transpose(pad_rows(rows, (2 * count + 7) // 8 * 8))
+    key = rows[:count] * float(LM) + rows[count:]
+    lanes = lax.broadcasted_iota(jnp.int32, (obs, LANES), 1).astype(jnp.float32)
 
     for k in range(count):
-        cam_hot = onehot(ocam_ref[k : k + 1, :], 2 * CAM)
-        land_hot = onehot(oland_ref[k : k + 1, :], LM)
+        cam_column, land_column = columns[:, k : k + 1], columns[:, count + k : count + k + 1]
+        cam_hot, land_hot = onehot(cam_column, lanes), onehot(land_column, lanes)
+        cam_hot_ref[k] = cam_hot
+        land_hot_ref[k] = land_hot
         lj = [land_ref[i, k : k + 1, :] for i in range(6)]
-        e0, e1 = resid_ref[0, k : k + 1, :], resid_ref[1, k : k + 1, :]
+        e0, e1 = resid_ref[k, 0:1, :], resid_ref[k, 1:2, :]
 
         def outer(i, j):
             return lj[i] * lj[j] + lj[3 + i] * lj[3 + j]
 
         entries = [outer(0, 0), outer(0, 1), outer(0, 2), outer(1, 1), outer(1, 2), outer(2, 2)]
         entries += [lj[b] * e0 + lj[3 + b] * e1 for b in range(3)]
-        sums = row_list(dot3(stack_rows(entries, 16), land_hot, NT), 9)
+        sums = row_list(dot3(stack_rows(entries, 16), land_hot, NN), 9)
         factor = cholesky_three(
             sums[0] + DAMPING, sums[1], sums[2], sums[3] + DAMPING, sums[4], sums[5] + DAMPING
         )
         tvec = lower_solve(factor, sums[6], sums[7], sums[8])
         land_values = stack_rows(list(factor) + list(tvec), 16)
         fac_ref[k] = land_values
-        at_obs = row_list(dot3(land_values, land_hot, NN), 9)
+        at_obs = row_list(take_lanes(land_values, oland_ref[k : k + 1, :]), 9)
         m0 = lower_solve(at_obs, lj[0], lj[1], lj[2])
         m1 = lower_solve(at_obs, lj[3], lj[4], lj[5])
         m_ref[k] = stack_rows(m0 + m1, 8)
@@ -178,33 +192,31 @@
         jac_ref[k, 1] = j1
         rhs = j0 * w0 + j1 * w1
         coupled = jnp.concatenate([j0 * m0[b] + j1 * m1[b] for b in range(3)], axis=0)
-        same = jnp.where(key_t[:, k : k + 1] == key[k : k + 1, :], 1.0, 0.0).astype(jnp.bfloat16)
+        same = onehot(cam_column * float(LM) + land_column, key[k : k + 1, :])
         prod = coupled * dot3(coupled, same, NN)
         diag = j0 * j0 + j1 * j1 - (prod[0:16] + prod[16:32] + prod[32:48])
-        both = dot3(jnp.concatenate([rhs, diag], axis=0), cam_hot, NT)
+        both = dot3(jnp.concatenate([rhs, diag], axis=0), cam_hot, NN)
         spot = place(pairs_ref, k, n_row, n_col, groups)
         scatter_pair(both[:16], rhs_ref, tiles, row_tiles, spot)
         scatter_pair(both[16:], diag_ref, tiles, row_tiles, spot)
 
 
-def half_product(k, p_ref, pairs_ref, jac_ref, ocam_ref, oland_ref, m_ref):
+def half_product(k, p_ref, pairs_ref, jac_ref, land_hot_ref, index_ref, m_ref):
     cams_tiles = p_ref.shape[0] * 8 // 9
     first, second = pairs_ref[0, k], pairs_ref[1, k]
     p_first = to_first(load_tile(p_ref, cams_tiles, first // 2), first % 2)
     p_second = to_second(load_tile(p_ref, cams_tiles, second // 2), second % 2)
     p_here = jnp.where(lane_ids(16) < CAM, p_first, p_second)
-    cam_hot = onehot(ocam_ref[k : k + 1, :], 2 * CAM)
-    land_hot = onehot(oland_ref[k : k + 1, :], LM)
-    at_obs = dot3(p_here, cam_hot, NN)
+    at_obs = take_lanes(p_here, index_ref[0, k : k + 1, :])
     u0 = jnp.sum(jac_ref[k, 0] * at_obs, axis=0, keepdims=True)
     u1 = jnp.sum(jac_ref[k, 1] * at_obs, axis=0, keepdims=True)
     m = [m_ref[k, i : i + 1, :] for i in range(6)]
     y = [m[b] * u0 + m[3 + b] * u1 for b in range(3)]
-    y_land = dot3(stack_rows(y, 16), land_hot, NT)
-    return cam_hot, land_hot, u0, u1, m, y_land
-
-
-def first_kernel(n_row, n_col, cams, pairs_ref, sums_ref, jac_ref, ocam_ref, oland_ref, m_ref, fac_ref, damp_tile_ref, parts_ref, back_ref, p_ref):
+    y_land = dot3(stack_rows(y, 16), land_hot_ref[k], NN)
+    return u0, u1, m, y_land
+
+
+def first_kernel(n_row, n_col, cams, pairs_ref, sums_ref, jac_ref, cam_hot_ref, land_hot_ref, index_ref, m_ref, fac_ref, damp_tile_ref, parts_ref, back_ref, p_ref):
     part_ref = parts_ref.at[0]
     groups = cams // CAM
     row_tiles = cams // n_row // LANES
@@ -217,16 +229,16 @@
     own = load_tile(p_ref, cams // LANES, whole_tile)
     add_tile(part_ref, tiles, own_tile, own * damp_tile_ref[...])
     for k in range(count):
-        cam_hot, land_hot, u0, u1, m, y_land = half_product(k, p_ref, pairs_ref, jac_ref, ocam_ref, oland_ref, m_ref)
+        u0, u1, m, y_land = half_product(k, p_ref, pairs_ref, jac_ref, land_hot_ref, index_ref, m_ref)
         factor = row_list(fac_ref[k], 9)
         solved = upper_solve(factor, y_land[0:1], y_land[1:2], y_land[2:3])
         from_t = upper_solve(factor, factor[6], factor[7], factor[8])
         back_ref[k] = stack_rows(solved + from_t, 8)
-        y_obs = row_list(dot3(y_land, land_hot, NN), 3)
+        y_obs = row_list(take_lanes(y_land[:8], index_ref[1, k : k + 1, :]), 3)
         v0 = u0 - (m[0] * y_obs[0] + m[1] * y_obs[1] + m[2] * y_obs[2])
         v1 = u1 - (m[3] * y_obs[0] + m[4] * y_obs[1] + m[5] * y_obs[2])
         image = jac_ref[k, 0] * v0 + jac_ref[k, 1] * v1
-        image = dot3(image, cam_hot, NT)
+        image = dot3(image, cam_hot_ref[k], NN)
         scatter_pair(image, part_ref, tiles, row_tiles, place(pairs_ref, k, n_row, n_col, groups))
 
 
@@ -235,7 +247,7 @@
     return jnp.sum(jnp.sum(x, axis=0, keepdims=True), axis=1, keepdims=True)
 
 
-def second_kernel(n_row, n_col, cams, pairs_ref, sums_ref, image_ref, jac_ref, ocam_ref, oland_ref, m_ref, fac_ref, damp_tile_ref, back_ref, energy_ref, cam_out_ref, land_base_ref, land_slope_ref, p_ref, d_ref):
+def second_kernel(n_row, n_col, cams, pairs_ref, sums_ref, image_ref, jac_ref, land_hot_ref, index_ref, m_ref, fac_ref, damp_tile_ref, back_ref, energy_ref, cam_out_ref, land_base_ref, land_slope_ref, p_ref, d_ref):
     row_tiles = cams // n_row // LANES
     count = jac_ref.shape[0]
     shard = cam_out_ref.shape[1]
@@ -266,13 +278,13 @@
     cam_out_ref[1:2, :] = norm_next * flat_second
 
     for k in range(count):
-        _, land_hot, u0, u1, m, y_land = half_product(k, d_ref, pairs_ref, jac_ref, ocam_ref, oland_ref, m_ref)
+        u0, u1, m, y_land = half_product(k, d_ref, pairs_ref, jac_ref, land_hot_ref, index_ref, m_ref)
         factor = row_list(fac_ref[k], 9)
         solved = upper_solve(factor, y_land[0:1], y_land[1:2], y_land[2:3])
         for b in range(3):
             land_base_ref[b, k : k + 1, :] = -(back_ref[k, 3 + b : 4 + b, :] + alpha * back_ref[k, b : b + 1, :])
             land_slope_ref[b, k : k + 1, :] = -norm_next * solved[b]
-        y_obs = row_list(dot3(y_land, land_hot, NN), 3)
+        y_obs = row_list(take_lanes(y_land[:8], index_ref[1, k : k + 1, :]), 3)
         v0 = u0 - (m[0] * y_obs[0] + m[1] * y_obs[1] + m[2] * y_obs[2])
         v1 = u1 - (m[3] * y_obs[0] + m[4] * y_obs[1] + m[5] * y_obs[2])
         energy = energy + jnp.sum(u0 * v0 + u1 * v1, axis=1, keepdims=True)
@@ -304,6 +316,12 @@
             total = total + part
         for i in range(col_tiles):
             add(col * col_tiles + i, row_tiles + i, total)
+
+
+def last_kernel(energy_ref, cam_ref, land_base_ref, land_slope_ref, cam_out_ref, land_out_ref):
+    inverse = 1.0 / jnp.sum(energy_ref[...], axis=0)[:, 0:1]
+    cam_out_ref[...] = (cam_ref[0:1, :] + inverse * cam_ref[1:2, :]).reshape(cam_out_ref.shape)
+    land_out_ref[...] = land_base_ref[...] + inverse[None] * land_slope_ref[...]
 
 
 def exchange(x, masks, n_dev):
@@ -354,45 +372,49 @@
                 x = x + y
         return x
 
-    part, jac, m, fac, damp_tile = pl.pallas_call(
+    hot = pltpu.VMEM((count, obs, LANES), jnp.bfloat16)
+    part, jac, cam_hot, land_hot, index, m, fac, damp_tile = pl.pallas_call(
         functools.partial(build_kernel, n_row, n_col, cams),
-        out_shape=(shape(2, part_tiles, 8, LANES), shape(count, 2, 16, obs), shape(count, 8, obs), shape(count, 16, LM), shape(16, LANES)),
+        out_shape=(shape(2, part_tiles, 8, LANES), shape(count, 2, 16, obs), hot, hot, pltpu.VMEM((2, count, obs), jnp.int32), shape(count, 8, obs), shape(count, 16, LM), shape(16, LANES)),
         in_specs=[smem] + [vmem] * 6,
-        out_specs=(vmem,) * 5,
+        out_specs=(vmem,) * 8,
     )(
         pairs.T,
         jnp.transpose(cam_jac, (1, 0, 2)),
         jnp.transpose(land_jac, (1, 0, 2)),
-        jnp.transpose(resid, (1, 0, 2)),
+        resid,
         obs_cam,
         obs_land,
-        cam_damp.reshape(1, shard),
+        cam_damp,
     )
     sums = all_reduce(part)
 
     image, back = pl.pallas_call(
         functools.partial(first_kernel, n_row, n_col, cams),
         out_shape=(shape(1, part_tiles, 8, LANES), shape(count, 8, LM)),
-        in_specs=[smem] + [vmem] * 7,
+        in_specs=[smem] + [vmem] * 8,
         out_specs=(vmem,) * 2,
         scratch_shapes=[pltpu.VMEM((whole_packed, 8, LANES), f32)],
-    )(pairs.T, *map(in_vmem, (sums, jac, obs_cam, obs_land, m, fac, damp_tile)))
+    )(pairs.T, *map(in_vmem, (sums, jac, cam_hot, land_hot, index, m, fac, damp_tile)))
 
     image = all_reduce(image)
 
     energy, cam_out, land_base, land_slope = pl.pallas_call(
         functools.partial(second_kernel, n_row, n_col, cams),
-        out_shape=(shape(8, LANES), shape(2, shard), shape(3, count, LM), shape(3, count, LM)),
+        out_shape=(shape(n_dev, 1, LANES), shape(2, shard), shape(3, count, LM), shape(3, count, LM)),
         in_specs=[smem] + [vmem] * 9,
         out_specs=(vmem,) * 4,
         scratch_shapes=[pltpu.VMEM((whole_packed, 8, LANES), f32)] * 2,
-    )(pairs.T, *map(in_vmem, (sums, image, jac, obs_cam, obs_land, m, fac, damp_tile, back)))
-
-    spread = jnp.broadcast_to(energy[0:1][None], (n_dev, 1, LANES))
-    gathered = lax.all_to_all(spread, AXES, 0, 0, tiled=True)
-    inverse = 1.0 / jnp.sum(gathered, axis=0)[0, 0]
-    land = land_base + inverse * land_slope
-    return cam_out[0] + inverse * cam_out[1], jnp.transpose(land, (1, 0, 2))
+    )(pairs.T, *map(in_vmem, (sums, image, jac, land_hot, index, m, fac, damp_tile, back)))
+
+    gathered = lax.all_to_all(energy, AXES, 0, 0, tiled=True)
+    cam_step, land_step = pl.pallas_call(
+        last_kernel,
+        out_shape=(jax.ShapeDtypeStruct((shard,), f32), jax.ShapeDtypeStruct((3, count, LM), f32)),
+        in_specs=[vmem] * 4,
+        out_specs=(vmem,) * 2,
+    )(*map(in_vmem, (gathered, cam_out, land_base, land_slope)))
+    return cam_step, jnp.transpose(land_step, (1, 0, 2))
 
 
 def solution(mesh):

time: 61.1 us -> 55.8 us (0.913)
  local copies, waits for them, and re-layouts: 3.3 us -> 0 us
  other arithmetic: 1.32 us -> 0.1 us
    unnamed x5 -> x0, local copies, waits for them, and re-layouts: 2.02 us -> none
    reshape x1 -> x0, local copies, waits for them, and re-layouts: 1.27 us -> none  [per_device(): cam_damp.reshape(1, shard)]
    pallas_call x1, Pallas kernels: 2.66 us -> 1.56 us  [per_device(): pl.pallas_call(functools.partial(second_kernel, n_row, n_col, cams), out_...]
    pallas_call x0 -> x1, Pallas kernels: none -> 0.69 us  [per_device(): pl.pallas_call(last_kernel, out_shape=(jax.ShapeDtypeStruct((shard,), f32...]
where the time goes in v3:
time: 55.8 us; the launch traced here: 55.6 us
  waiting for transfers between devices  19 us (34%)
  starting transfers between devices  17.4 us (31%)
  blocking collectives  10.2 us (18%)
  Pallas kernels  8.26 us (15%)
  between operations  0.69 us (1%)
    ppermute x14, waiting for transfers between devices, exchange(): lax.ppermute(x, AXES, [(i, i ^ mask) for i in range(n_dev)])  19 us
    ppermute x14, starting transfers between devices, exchange(): lax.ppermute(x, AXES, [(i, i ^ mask) for i in range(n_dev)])  17.4 us
    all_to_all x1, blocking collectives, per_device(): gathered = lax.all_to_all(energy, AXES, 0, 0, tiled=True)  10.2 us
    pallas_call x1, Pallas kernels, per_device(): pl.pallas_call(functools.partial(build_kernel, n_row, n_col, cams), out_s...  3.67 us
    pallas_call x1, Pallas kernels, per_device(): pl.pallas_call(functools.partial(first_kernel, n_row, n_col, cams), out_s...  2.07 us
    pallas_call x1, Pallas kernels, per_device(): pl.pallas_call(functools.partial(second_kernel, n_row, n_col, cams), out_...  1.56 us
  transfers between devices with their start and end apart: 14, of which 12 were waited for; matrix products, arithmetic and copies ran while one was open for 0% of the time, Pallas kernels for 0%

profile of v3, /device:TPU:0, one launch (start us, length us, event | category | flops | bytes accessed | tf_op | source)
XLA Modules:
  0.0 55.6 jit_solution(11404182469202194972)
XLA Ops:
  0.6 3.7 %shard_map.86 = (f32[2,7,8,128]{3,2,1,0:T(8,128)S(1)}, f32[4,2,16,512]{3,2,1,0:T(8,128)S(1)}, bf16[4,512,128]{2,1,0:T(8,128)(2,1)S(1)}, bf16[4,512,128]{2,1,0:T(...) custom-call(s32[2,4]{1,0:T(2,128)} %bitcast.6, ...), custom_call_target="tpu_custom_call" | custom-call | tf_op jit(solution)/shard_map/pallas_call | solution.py:376
  4.3 5.1 %collective-permute-start.2 = (f32[2,7,8,128]{3,2,1,0:T(8,128)S(1)}, f32[2,7,8,128]{3,2,1,0:T(8,128)S(1)}, u32[]{:S(2)}, u32[]{:S(2)}) collective-permute-start(f32[2,7,8,128]{3,2,1,0:T(8,128)S(1)} %get-tuple-element.18.refs_0_), channel_id=1, source_target_pairs={{0,24},{1,25},{2,26},{3,27},{4,28},{5,29},{6,30},{7,31},{8,16},{9,... | collective-permute-start | bytes 172040 | tf_op jit(solution)/shard_map/ppermute | solution.py:328
  9.4 0.6 %collective-permute-start = (f32[2,7,8,128]{3,2,1,0:T(8,128)S(1)}, f32[2,7,8,128]{3,2,1,0:T(8,128)S(1)}, u32[]{:S(2)}, u32[]{:S(2)}) collective-permute-start(f32[2,7,8,128]{3,2,1,0:T(8,128)S(1)} %get-tuple-element.18.refs_0_), channel_id=1, source_target_pairs={{0,8},{1,9},{2,10},{3,11},{4,12},{5,13},{6,14},{7,15},{8,0},{9,1},... | collective-permute-start | bytes 172040 | tf_op jit(solution)/shard_map/ppermute | solution.py:328
  10.1 1.8 %collective-permute-done.2.refs_3_ = f32[2,7,8,128]{3,2,1,0:T(8,128)S(1)} collective-permute-done((f32[2,7,8,128]{3,2,1,0:T(8,128)S(1)}, f32[2,7,8,128]{3,2,1,0:T(8,128)S(1)}, u32[]{:S(2)}, u32[]{:S(2)}) %collective-permute-start.2) | collective-permute-done | bytes 57376 | tf_op jit(solution)/shard_map/ppermute | solution.py:328
  11.8 2.7 %collective-permute-done.1.refs_2_ = f32[2,7,8,128]{3,2,1,0:T(8,128)S(1)} collective-permute-done((f32[2,7,8,128]{3,2,1,0:T(8,128)S(1)}, f32[2,7,8,128]{3,2,1,0:T(8,128)S(1)}, u32[]{:S(2)}, u32[]{:S(2)}) %collective-permute-start.1) | collective-permute-done | bytes 57376 | tf_op jit(solution)/shard_map/ppermute | solution.py:328
  14.7 2.5 %collective-permute-start.5 = (f32[2,18,8,128]{3,2,1,0:T(8,128)S(1)}, f32[2,18,8,128]{3,2,1,0:T(8,128)S(1)}, u32[]{:S(2)}, u32[]{:S(2)}) collective-permute-start(f32[2,18,8,128]{3,2,1,0:T(8,128)S(1)} %shard_map.87), channel_id=1, source_target_pairs={{0,6},{1,7},{2,4},{3,5},{4,2},{5,3},{6,0},{7,1},{8,14},{9,15},{10,... | collective-permute-start | bytes 442376 | tf_op jit(solution)/shard_map/ppermute | solution.py:328
  17.2 0.5 collective-permute-start.4
  17.7 0.5 collective-permute-start.3
  18.2 3.5 %collective-permute-done.5 = f32[2,18,8,128]{3,2,1,0:T(8,128)S(1)} collective-permute-done((f32[2,18,8,128]{3,2,1,0:T(8,128)S(1)}, f32[2,18,8,128]{3,2,1,0:T(8,128)S(1)}, u32[]{:S(2)}, u32[]{:S(2)}) %collective-permute-start.5) | collective-permute-done | bytes 147488 | tf_op jit(solution)/shard_map/ppermute | solution.py:328
  21.7 2.0 %collective-permute-done.4 = f32[2,18,8,128]{3,2,1,0:T(8,128)S(1)} collective-permute-done((f32[2,18,8,128]{3,2,1,0:T(8,128)S(1)}, f32[2,18,8,128]{3,2,1,0:T(8,128)S(1)}, u32[]{:S(2)}, u32[]{:S(2)}) %collective-permute-start.4) | collective-permute-done | bytes 147488 | tf_op jit(solution)/shard_map/ppermute | solution.py:328
  23.9 1.4 %collective-permute-done.6 = f32[2,18,8,128]{3,2,1,0:T(8,128)S(1)} collective-permute-done((f32[2,18,8,128]{3,2,1,0:T(8,128)S(1)}, f32[2,18,8,128]{3,2,1,0:T(8,128)S(1)}, u32[]{:S(2)}, u32[]{:S(2)}) %collective-permute-start.6) | collective-permute-done | bytes 147488 | tf_op jit(solution)/shard_map/ppermute | solution.py:328
  25.3 2.1 %shard_map.88 = (f32[1,7,8,128]{3,2,1,0:T(8,128)S(1)}, f32[4,8,128]{2,1,0:T(8,128)S(1)}) custom-call(s32[2,4]{1,0:T(2,128)} %bitcast.7, f32[2,18,8,128]{3,2,1,0:T(8,128)S(1)} %add.27.sums_ref, f32[4,2,16,512]{3,2,1,0:T(8,128)S(1)} %get-tuple-element.19.jac_ref, bf16[4,512,128]{2,1,0:T(8,128)(2,1)S(1)} %get-tuple-element.20.cam_hot_ref, ...), custom_call_target="tpu_custom_call" | custom-call | tf_op jit(solution)/shard_map/pallas_call | solution.py:392
  27.4 2.1 %collective-permute-start.9 = (f32[1,7,8,128]{3,2,1,0:T(8,128)S(1)}, f32[1,7,8,128]{3,2,1,0:T(8,128)S(1)}, u32[]{:S(2)}, u32[]{:S(2)}) collective-permute-start(f32[1,7,8,128]{3,2,1,0:T(8,128)S(1)} %get-tuple-element.26.refs_0_), channel_id=1, source_target_pairs={{0,24},{1,25},{2,26},{3,27},{4,28},{5,29},{6,30},{7,31},{8,16},{9,... | collective-permute-start | bytes 86024 | tf_op jit(solution)/shard_map/ppermute | solution.py:328
  29.5 2.3 %collective-permute-start.7 = (f32[1,7,8,128]{3,2,1,0:T(8,128)S(1)}, f32[1,7,8,128]{3,2,1,0:T(8,128)S(1)}, u32[]{:S(2)}, u32[]{:S(2)}) collective-permute-start(f32[1,7,8,128]{3,2,1,0:T(8,128)S(1)} %get-tuple-element.26.refs_0_), channel_id=1, source_target_pairs={{0,8},{1,9},{2,10},{3,11},{4,12},{5,13},{6,14},{7,15},{8,0},{9,1},... | collective-permute-start | bytes 86024 | tf_op jit(solution)/shard_map/ppermute | solution.py:328
  31.8 1.3 %collective-permute-done.9.refs_3_ = f32[1,7,8,128]{3,2,1,0:T(8,128)S(1)} collective-permute-done((f32[1,7,8,128]{3,2,1,0:T(8,128)S(1)}, f32[1,7,8,128]{3,2,1,0:T(8,128)S(1)}, u32[]{:S(2)}, u32[]{:S(2)}) %collective-permute-start.9) | collective-permute-done | bytes 28704 | tf_op jit(solution)/shard_map/ppermute | solution.py:328
  33.1 1.1 %collective-permute-done.8.refs_2_ = f32[1,7,8,128]{3,2,1,0:T(8,128)S(1)} collective-permute-done((f32[1,7,8,128]{3,2,1,0:T(8,128)S(1)}, f32[1,7,8,128]{3,2,1,0:T(8,128)S(1)}, u32[]{:S(2)}, u32[]{:S(2)}) %collective-permute-start.8) | collective-permute-done | bytes 28704 | tf_op jit(solution)/shard_map/ppermute | solution.py:328
  34.4 1.8 %collective-permute-start.12 = (f32[1,18,8,128]{3,2,1,0:T(8,128)S(1)}, f32[1,18,8,128]{3,2,1,0:T(8,128)S(1)}, u32[]{:S(2)}, u32[]{:S(2)}) collective-permute-start(f32[1,18,8,128]{3,2,1,0:T(8,128)S(1)} %shard_map.89), channel_id=1, source_target_pairs={{0,6},{1,7},{2,4},{3,5},{4,2},{5,3},{6,0},{7,1},{8,14},{9,15},{10,... | collective-permute-start | bytes 221192 | tf_op jit(solution)/shard_map/ppermute | solution.py:328
  36.1 1.3 %collective-permute-start.11 = (f32[1,18,8,128]{3,2,1,0:T(8,128)S(1)}, f32[1,18,8,128]{3,2,1,0:T(8,128)S(1)}, u32[]{:S(2)}, u32[]{:S(2)}) collective-permute-start(f32[1,18,8,128]{3,2,1,0:T(8,128)S(1)} %shard_map.89), channel_id=1, source_target_pairs={{0,2},{1,3},{2,0},{3,1},{4,6},{5,7},{6,4},{7,5},{8,10},{9,11},{10,... | collective-permute-start | bytes 221192 | tf_op jit(solution)/shard_map/ppermute | solution.py:328
  37.9 2.5 %collective-permute-done.12 = f32[1,18,8,128]{3,2,1,0:T(8,128)S(1)} collective-permute-done((f32[1,18,8,128]{3,2,1,0:T(8,128)S(1)}, f32[1,18,8,128]{3,2,1,0:T(8,128)S(1)}, u32[]{:S(2)}, u32[]{:S(2)}) %collective-permute-start.12) | collective-permute-done | bytes 73760 | tf_op jit(solution)/shard_map/ppermute | solution.py:328
  40.9 0.9 %collective-permute-done.10 = f32[1,18,8,128]{3,2,1,0:T(8,128)S(1)} collective-permute-done((f32[1,18,8,128]{3,2,1,0:T(8,128)S(1)}, f32[1,18,8,128]{3,2,1,0:T(8,128)S(1)}, u32[]{:S(2)}, u32[]{:S(2)}) %collective-permute-start.10) | collective-permute-done | bytes 73760 | tf_op jit(solution)/shard_map/ppermute | solution.py:328
  41.9 1.3 %collective-permute-done.13 = f32[1,18,8,128]{3,2,1,0:T(8,128)S(1)} collective-permute-done((f32[1,18,8,128]{3,2,1,0:T(8,128)S(1)}, f32[1,18,8,128]{3,2,1,0:T(8,128)S(1)}, u32[]{:S(2)}, u32[]{:S(2)}) %collective-permute-start.13) | collective-permute-done | bytes 73760 | tf_op jit(solution)/shard_map/ppermute | solution.py:328
  43.2 1.6 %shard_map.90 = (f32[32,1,128]{2,1,0:T(1,128)S(1)}, f32[2,576]{1,0:T(2,128)S(1)}, f32[3,4,128]{2,1,0:T(4,128)S(1)}, f32[3,4,128]{2,1,0:T(4,128)S(1)}) custom-call(s32[2,4]{1,0:T(2,128)} %bitcast.8, f32[2,18,8,128]{3,2,1,0:T(8,128)S(1)} %add.27.sums_ref, f32[1,18,8,128]{3,2,1,0:T(8,128)S(1)} %add.31.image_ref, ...), custom_call_target="tpu_custom_call" | custom-call | tf_op jit(solution)/shard_map/pallas_call | solution.py:402
  44.7 10.2 %all_to_all.5.energy_ref = f32[32,1,128]{2,1,0:T(1,128)S(1)} all-to-all(f32[32,1,128]{2,1,0:T(1,128)S(1)} %get-tuple-element.28), channel_id=1, replica_groups=mesh['row'=8,'col'=4] {'row','col'}, dimensions={0} | all-to-all | bytes 32768 | tf_op jit(solution)/shard_map/all_to_all | solution.py:410
  54.9 0.7 %shard_map.91 = (f32[576]{0:T(1024)}, f32[3,4,128]{2,1,0:T(4,128)}) custom-call(f32[32,1,128]{2,1,0:T(1,128)S(1)} %all_to_all.5.energy_ref, f32[2,576]{1,0:T(2,128)S(1)} %get-tuple-element.29.cam_ref, f32[3,4,128]{2,1,0:T(4,128)S(1)} %get-tuple-element.30.land_base_ref, f32[3,4,128]{2,1,0:T(4,128)S(1)} %get-tuple-element.31.land_slope_ref), custom_call_target="tpu_custom_call" | custom-call | tf_op jit(solution)/shard_map/pallas_call | solution.py:411
  (15 shorter events, 1.5 us)
Async XLA Ops:
  4.3 7.5 %collective-permute-start.2 = (f32[2,7,8,128]{3,2,1,0:T(8,128)S(1)}, f32[2,7,8,128]{3,2,1,0:T(8,128)S(1)}, u32[]{:S(2)}, u32[]{:S(2)}) collective-permute-start(f32[2,7,8,128]{3,2,1,0:T(8,128)S(1)} %get-tuple-element.18.refs_0_), channel_id=1, source_target_pairs={{0,24},{1,25},{2,26},{3,27},{4,28},{5,29},{6,30},{7,31},{8,16},{9,... | collective-permute-start | bytes 172040 | tf_op jit(solution)/shard_map/ppermute | solution.py:328
  9.4 5.1 %collective-permute-start.1 = (f32[2,7,8,128]{3,2,1,0:T(8,128)S(1)}, f32[2,7,8,128]{3,2,1,0:T(8,128)S(1)}, u32[]{:S(2)}, u32[]{:S(2)}) collective-permute-start(f32[2,7,8,128]{3,2,1,0:T(8,128)S(1)} %get-tuple-element.18.refs_0_), channel_id=1, source_target_pairs={{0,16},{1,17},{2,18},{3,19},{4,20},{5,21},{6,22},{7,23},{8,24},{9,... | collective-permute-start | bytes 172040 | tf_op jit(solution)/shard_map/ppermute | solution.py:328
  9.4 5.1 %collective-permute-start = (f32[2,7,8,128]{3,2,1,0:T(8,128)S(1)}, f32[2,7,8,128]{3,2,1,0:T(8,128)S(1)}, u32[]{:S(2)}, u32[]{:S(2)}) collective-permute-start(f32[2,7,8,128]{3,2,1,0:T(8,128)S(1)} %get-tuple-element.18.refs_0_), channel_id=1, source_target_pairs={{0,8},{1,9},{2,10},{3,11},{4,12},{5,13},{6,14},{7,15},{8,0},{9,1},... | collective-permute-start | bytes 172040 | tf_op jit(solution)/shard_map/ppermute | solution.py:328
  14.7 7.0 %collective-permute-start.5 = (f32[2,18,8,128]{3,2,1,0:T(8,128)S(1)}, f32[2,18,8,128]{3,2,1,0:T(8,128)S(1)}, u32[]{:S(2)}, u32[]{:S(2)}) collective-permute-start(f32[2,18,8,128]{3,2,1,0:T(8,128)S(1)} %shard_map.87), channel_id=1, source_target_pairs={{0,6},{1,7},{2,4},{3,5},{4,2},{5,3},{6,0},{7,1},{8,14},{9,15},{10,... | collective-permute-start | bytes 442376 | tf_op jit(solution)/shard_map/ppermute | solution.py:328
  17.2 6.5 %collective-permute-start.4 = (f32[2,18,8,128]{3,2,1,0:T(8,128)S(1)}, f32[2,18,8,128]{3,2,1,0:T(8,128)S(1)}, u32[]{:S(2)}, u32[]{:S(2)}) collective-permute-start(f32[2,18,8,128]{3,2,1,0:T(8,128)S(1)} %shard_map.87), channel_id=1, source_target_pairs={{0,2},{1,3},{2,0},{3,1},{4,6},{5,7},{6,4},{7,5},{8,10},{9,11},{10,... | collective-permute-start | bytes 442376 | tf_op jit(solution)/shard_map/ppermute | solution.py:328
  17.7 6.1 %collective-permute-start.3 = (f32[2,18,8,128]{3,2,1,0:T(8,128)S(1)}, f32[2,18,8,128]{3,2,1,0:T(8,128)S(1)}, u32[]{:S(2)}, u32[]{:S(2)}) collective-permute-start(f32[2,18,8,128]{3,2,1,0:T(8,128)S(1)} %shard_map.87), channel_id=1, source_target_pairs={{0,4},{1,5},{2,6},{3,7},{4,0},{5,1},{6,2},{7,3},{8,12},{9,13},{10,... | collective-permute-start | bytes 442376 | tf_op jit(solution)/shard_map/ppermute | solution.py:328
  23.9 1.4 %collective-permute-start.6 = (f32[2,18,8,128]{3,2,1,0:T(8,128)S(1)}, f32[2,18,8,128]{3,2,1,0:T(8,128)S(1)}, u32[]{:S(2)}, u32[]{:S(2)}) collective-permute-start(f32[2,18,8,128]{3,2,1,0:T(8,128)S(1)} %add_add_fusion), channel_id=1, source_target_pairs={{0,1},{1,0},{2,3},{3,2},{4,5},{5,4},{6,7},{7,6},{8,9},{9,8},{10,11... | collective-permute-start | bytes 442376 | tf_op jit(solution)/shard_map/ppermute | solution.py:328
  27.4 5.7 %collective-permute-start.9 = (f32[1,7,8,128]{3,2,1,0:T(8,128)S(1)}, f32[1,7,8,128]{3,2,1,0:T(8,128)S(1)}, u32[]{:S(2)}, u32[]{:S(2)}) collective-permute-start(f32[1,7,8,128]{3,2,1,0:T(8,128)S(1)} %get-tuple-element.26.refs_0_), channel_id=1, source_target_pairs={{0,24},{1,25},{2,26},{3,27},{4,28},{5,29},{6,30},{7,31},{8,16},{9,... | collective-permute-start | bytes 86024 | tf_op jit(solution)/shard_map/ppermute | solution.py:328
  29.5 4.8 %collective-permute-start.8 = (f32[1,7,8,128]{3,2,1,0:T(8,128)S(1)}, f32[1,7,8,128]{3,2,1,0:T(8,128)S(1)}, u32[]{:S(2)}, u32[]{:S(2)}) collective-permute-start(f32[1,7,8,128]{3,2,1,0:T(8,128)S(1)} %get-tuple-element.26.refs_0_), channel_id=1, source_target_pairs={{0,16},{1,17},{2,18},{3,19},{4,20},{5,21},{6,22},{7,23},{8,24},{9,... | collective-permute-start | bytes 86024 | tf_op jit(solution)/shard_map/ppermute | solution.py:328
  29.5 4.8 %collective-permute-start.7 = (f32[1,7,8,128]{3,2,1,0:T(8,128)S(1)}, f32[1,7,8,128]{3,2,1,0:T(8,128)S(1)}, u32[]{:S(2)}, u32[]{:S(2)}) collective-permute-start(f32[1,7,8,128]{3,2,1,0:T(8,128)S(1)} %get-tuple-element.26.refs_0_), channel_id=1, source_target_pairs={{0,8},{1,9},{2,10},{3,11},{4,12},{5,13},{6,14},{7,15},{8,0},{9,1},... | collective-permute-start | bytes 86024 | tf_op jit(solution)/shard_map/ppermute | solution.py:328
  34.4 6.1 %collective-permute-start.12 = (f32[1,18,8,128]{3,2,1,0:T(8,128)S(1)}, f32[1,18,8,128]{3,2,1,0:T(8,128)S(1)}, u32[]{:S(2)}, u32[]{:S(2)}) collective-permute-start(f32[1,18,8,128]{3,2,1,0:T(8,128)S(1)} %shard_map.89), channel_id=1, source_target_pairs={{0,6},{1,7},{2,4},{3,5},{4,2},{5,3},{6,0},{7,1},{8,14},{9,15},{10,... | collective-permute-start | bytes 221192 | tf_op jit(solution)/shard_map/ppermute | solution.py:328
  36.1 4.7 %collective-permute-start.11 = (f32[1,18,8,128]{3,2,1,0:T(8,128)S(1)}, f32[1,18,8,128]{3,2,1,0:T(8,128)S(1)}, u32[]{:S(2)}, u32[]{:S(2)}) collective-permute-start(f32[1,18,8,128]{3,2,1,0:T(8,128)S(1)} %shard_map.89), channel_id=1, source_target_pairs={{0,2},{1,3},{2,0},{3,1},{4,6},{5,7},{6,4},{7,5},{8,10},{9,11},{10,... | collective-permute-start | bytes 221192 | tf_op jit(solution)/shard_map/ppermute | solution.py:328
  37.5 4.4 %collective-permute-start.10 = (f32[1,18,8,128]{3,2,1,0:T(8,128)S(1)}, f32[1,18,8,128]{3,2,1,0:T(8,128)S(1)}, u32[]{:S(2)}, u32[]{:S(2)}) collective-permute-start(f32[1,18,8,128]{3,2,1,0:T(8,128)S(1)} %shard_map.89), channel_id=1, source_target_pairs={{0,4},{1,5},{2,6},{3,7},{4,0},{5,1},{6,2},{7,3},{8,12},{9,13},{10,... | collective-permute-start | bytes 221192 | tf_op jit(solution)/shard_map/ppermute | solution.py:328
  41.8 1.3 %collective-permute-start.13 = (f32[1,18,8,128]{3,2,1,0:T(8,128)S(1)}, f32[1,18,8,128]{3,2,1,0:T(8,128)S(1)}, u32[]{:S(2)}, u32[]{:S(2)}) collective-permute-start(f32[1,18,8,128]{3,2,1,0:T(8,128)S(1)} %add_add_fusion.1), channel_id=1, source_target_pairs={{0,1},{1,0},{2,3},{3,2},{4,5},{5,4},{6,7},{7,6},{8,9},{9,8},{10,11... | collective-permute-start | bytes 221192 | tf_op jit(solution)/shard_map/ppermute | solution.py:328

commit v4 on v3

--- a/solution.py
+++ b/solution.py
@@ -51,6 +51,8 @@
 
 def stack_rows(rows, total):
     rows = list(rows)
+    if len(rows) == total:
+        return jnp.concatenate(rows, axis=0)
     rows.append(jnp.zeros((total - len(rows), rows[0].shape[1]), jnp.float32))
     return jnp.concatenate(rows, axis=0)
 
@@ -100,11 +102,6 @@
     return jnp.concatenate([ref[t], ninth, jnp.zeros((7, LANES), jnp.float32)], axis=0)
 
 
-def add_tile(ref, tiles, t, value):
-    ref[t] += value[:8]
-    ref[tiles + t // 8, pl.ds(t % 8, 1), :] += value[8:9]
-
-
 def shard_select(shard, lane_offset):
     entry = lax.broadcasted_iota(jnp.int32, (shard, LANES), 0)
     start = 9 * (lax.broadcasted_iota(jnp.int32, (shard, LANES), 1) - lane_offset)
@@ -125,11 +122,24 @@
     return first // 2, first % 2, second // 2, second % 2
 
 
-def scatter_pair(value, ref, tiles, row_tiles, spot):
-    t_first, h_first, t_second, h_second = spot
-    lower = lane_ids(value.shape[0]) < CAM
-    add_tile(ref, tiles, t_first, to_first(jnp.where(lower, value, 0.0), h_first))
-    add_tile(ref, tiles, row_tiles + t_second, to_second(jnp.where(lower, 0.0, value), h_second))
+def write_parts(ref, row_tiles, tiles, spots, values, extra=None):
+    rows = values[0].shape[0]
+    lower = lane_ids(rows) < CAM
+    firsts = [to_first(jnp.where(lower, v, 0.0), spot[1]) for v, spot in zip(values, spots)]
+    seconds = [to_second(jnp.where(lower, 0.0, v), spot[3]) for v, spot in zip(values, spots)]
+    ninths = []
+    for t in range(tiles):
+        if t < row_tiles:
+            items = [(spot[0] == t, v) for v, spot in zip(firsts, spots)]
+            if extra is not None:
+                items.append((extra[0] == t, extra[1]))
+        else:
+            items = [(spot[2] == t - row_tiles, v) for v, spot in zip(seconds, spots)]
+        total = sum(jnp.where(here, v, 0.0) for here, v in items)
+        ref[t] = total[:8]
+        ninths.append(total[8:9])
+    for start in range(0, tiles, 8):
+        ref[tiles + start // 8] = stack_rows(ninths[start : start + 8], 8)
 
 
 def own_place(n_row, n_col, cams):
@@ -143,15 +153,8 @@
     row_tiles = cams // n_row // LANES
     tiles = row_tiles + cams // n_col // LANES
     count, obs = ocam_ref.shape
+    each = range(count)
     shard = damp_ref.shape[0]
-    part_ref[...] = jnp.zeros(part_ref.shape, jnp.float32)
-    rhs_ref, diag_ref = part_ref.at[0], part_ref.at[1]
-
-    own_tile, own_lane = own_place(n_row, n_col, cams)
-    spread = jnp.where(param_mask(shard), damp_ref[...].reshape(1, shard), 0.0)
-    damp_tile = dot3(spread, shard_select(shard, own_lane), NN)
-    damp_tile_ref[...] = damp_tile
-    add_tile(diag_ref, tiles, own_tile, damp_tile)
 
     index_ref[0] = ocam_ref[...]
     index_ref[1] = oland_ref[...]
@@ -159,87 +162,113 @@
     columns = jnp.transpose(pad_rows(rows, (2 * count + 7) // 8 * 8))
     key = rows[:count] * float(LM) + rows[count:]
     lanes = lax.broadcasted_iota(jnp.int32, (obs, LANES), 1).astype(jnp.float32)
-
-    for k in range(count):
-        cam_column, land_column = columns[:, k : k + 1], columns[:, count + k : count + k + 1]
-        cam_hot, land_hot = onehot(cam_column, lanes), onehot(land_column, lanes)
-        cam_hot_ref[k] = cam_hot
-        land_hot_ref[k] = land_hot
-        lj = [land_ref[i, k : k + 1, :] for i in range(6)]
-        e0, e1 = resid_ref[k, 0:1, :], resid_ref[k, 1:2, :]
+    cam_columns = [columns[:, k : k + 1] for k in each]
+    land_columns = [columns[:, count + k : count + k + 1] for k in each]
+    for k in each:
+        land_hot_ref[k] = onehot(land_columns[k], lanes)
+
+    lj = [[land_ref[i, k : k + 1, :] for i in range(6)] for k in each]
+    e0 = [resid_ref[k, 0:1, :] for k in each]
+    e1 = [resid_ref[k, 1:2, :] for k in each]
+    sums = []
+    for k in each:
 
         def outer(i, j):
-            return lj[i] * lj[j] + lj[3 + i] * lj[3 + j]
+            return lj[k][i] * lj[k][j] + lj[k][3 + i] * lj[k][3 + j]
 
         entries = [outer(0, 0), outer(0, 1), outer(0, 2), outer(1, 1), outer(1, 2), outer(2, 2)]
-        entries += [lj[b] * e0 + lj[3 + b] * e1 for b in range(3)]
-        sums = row_list(dot3(stack_rows(entries, 16), land_hot, NN), 9)
-        factor = cholesky_three(
-            sums[0] + DAMPING, sums[1], sums[2], sums[3] + DAMPING, sums[4], sums[5] + DAMPING
-        )
-        tvec = lower_solve(factor, sums[6], sums[7], sums[8])
-        land_values = stack_rows(list(factor) + list(tvec), 16)
+        entries += [lj[k][b] * e0[k] + lj[k][3 + b] * e1[k] for b in range(3)]
+        sums.append(dot3(stack_rows(entries, 16), land_hot_ref[k], NN))
+    total = [jnp.concatenate([sums[k][i : i + 1] for k in each], axis=0) for i in range(9)]
+    factor = cholesky_three(
+        total[0] + DAMPING, total[1], total[2], total[3] + DAMPING, total[4], total[5] + DAMPING
+    )
+    land_rows = list(factor) + list(lower_solve(factor, total[6], total[7], total[8]))
+    for k in each:
+        cam_hot_ref[k] = onehot(cam_columns[k], lanes)
+        jac_ref[k, 0] = pad_rows(cam_ref[0:9, k, :], 16)
+        jac_ref[k, 1] = pad_rows(cam_ref[9:18, k, :], 16)
+    ms, ws = [], []
+    for k in each:
+        land_values = stack_rows([row[k : k + 1] for row in land_rows], 16)
         fac_ref[k] = land_values
         at_obs = row_list(take_lanes(land_values, oland_ref[k : k + 1, :]), 9)
-        m0 = lower_solve(at_obs, lj[0], lj[1], lj[2])
-        m1 = lower_solve(at_obs, lj[3], lj[4], lj[5])
+        m0 = lower_solve(at_obs, lj[k][0], lj[k][1], lj[k][2])
+        m1 = lower_solve(at_obs, lj[k][3], lj[k][4], lj[k][5])
         m_ref[k] = stack_rows(m0 + m1, 8)
-        w0 = m0[0] * at_obs[6] + m0[1] * at_obs[7] + m0[2] * at_obs[8] - e0
-        w1 = m1[0] * at_obs[6] + m1[1] * at_obs[7] + m1[2] * at_obs[8] - e1
-        j0 = pad_rows(cam_ref[0:9, k, :], 16)
-        j1 = pad_rows(cam_ref[9:18, k, :], 16)
-        jac_ref[k, 0] = j0
-        jac_ref[k, 1] = j1
-        rhs = j0 * w0 + j1 * w1
+        ms.append((m0, m1))
+        w0 = m0[0] * at_obs[6] + m0[1] * at_obs[7] + m0[2] * at_obs[8] - e0[k]
+        w1 = m1[0] * at_obs[6] + m1[1] * at_obs[7] + m1[2] * at_obs[8] - e1[k]
+        ws.append((w0, w1))
+    both = []
+    for k in each:
+        j0, j1 = jac_ref[k, 0], jac_ref[k, 1]
+        m0, m1 = ms[k]
         coupled = jnp.concatenate([j0 * m0[b] + j1 * m1[b] for b in range(3)], axis=0)
-        same = onehot(cam_column * float(LM) + land_column, key[k : k + 1, :])
+        same = onehot(cam_columns[k] * float(LM) + land_columns[k], key[k : k + 1, :])
         prod = coupled * dot3(coupled, same, NN)
         diag = j0 * j0 + j1 * j1 - (prod[0:16] + prod[16:32] + prod[32:48])
-        both = dot3(jnp.concatenate([rhs, diag], axis=0), cam_hot, NN)
-        spot = place(pairs_ref, k, n_row, n_col, groups)
-        scatter_pair(both[:16], rhs_ref, tiles, row_tiles, spot)
-        scatter_pair(both[16:], diag_ref, tiles, row_tiles, spot)
-
-
-def half_product(k, p_ref, pairs_ref, jac_ref, land_hot_ref, index_ref, m_ref):
+        rhs = j0 * ws[k][0] + j1 * ws[k][1]
+        both.append(dot3(jnp.concatenate([rhs, diag], axis=0), cam_hot_ref[k], NN))
+
+    own_tile, own_lane = own_place(n_row, n_col, cams)
+    spread = jnp.where(param_mask(shard), damp_ref[...].reshape(1, shard), 0.0)
+    damp_tile = dot3(spread, shard_select(shard, own_lane), NN)
+    damp_tile_ref[...] = damp_tile
+    spots = [place(pairs_ref, k, n_row, n_col, groups) for k in each]
+    write_parts(part_ref.at[0], row_tiles, tiles, spots, [x[:16] for x in both])
+    write_parts(part_ref.at[1], row_tiles, tiles, spots, [x[16:] for x in both], (own_tile, damp_tile))
+
+
+def half_product(p_ref, pairs_ref, jac_ref, land_hot_ref, index_ref, m_ref):
+    each = range(jac_ref.shape[0])
     cams_tiles = p_ref.shape[0] * 8 // 9
-    first, second = pairs_ref[0, k], pairs_ref[1, k]
-    p_first = to_first(load_tile(p_ref, cams_tiles, first // 2), first % 2)
-    p_second = to_second(load_tile(p_ref, cams_tiles, second // 2), second % 2)
-    p_here = jnp.where(lane_ids(16) < CAM, p_first, p_second)
-    at_obs = take_lanes(p_here, index_ref[0, k : k + 1, :])
-    u0 = jnp.sum(jac_ref[k, 0] * at_obs, axis=0, keepdims=True)
-    u1 = jnp.sum(jac_ref[k, 1] * at_obs, axis=0, keepdims=True)
-    m = [m_ref[k, i : i + 1, :] for i in range(6)]
-    y = [m[b] * u0 + m[3 + b] * u1 for b in range(3)]
-    y_land = dot3(stack_rows(y, 16), land_hot_ref[k], NN)
-    return u0, u1, m, y_land
-
-
-def first_kernel(n_row, n_col, cams, pairs_ref, sums_ref, jac_ref, cam_hot_ref, land_hot_ref, index_ref, m_ref, fac_ref, damp_tile_ref, parts_ref, back_ref, p_ref):
-    part_ref = parts_ref.at[0]
+    lower = lane_ids(16) < CAM
+    u, m, y_land = [], [], []
+    for k in each:
+        first, second = pairs_ref[0, k], pairs_ref[1, k]
+        p_first = to_first(load_tile(p_ref, cams_tiles, first // 2), first % 2)
+        p_second = to_second(load_tile(p_ref, cams_tiles, second // 2), second % 2)
+        at_obs = take_lanes(jnp.where(lower, p_first, p_second), index_ref[0, k : k + 1, :])
+        u.append([jnp.sum(jac_ref[k, r] * at_obs, axis=0, keepdims=True) for r in range(2)])
+    for k in each:
+        m.append([m_ref[k, i : i + 1, :] for i in range(6)])
+        y = [m[k][b] * u[k][0] + m[k][3 + b] * u[k][1] for b in range(3)]
+        y_land.append(dot3(stack_rows(y, 16), land_hot_ref[k], NN)[:8])
+    return u, m, y_land
+
+
+def reduced_rows(u, m, y_land, index_ref):
+    out = []
+    for k in range(len(u)):
+        y = row_list(take_lanes(y_land[k], index_ref[1, k : k + 1, :]), 3)
+        out.append([u[k][r] - (m[k][3 * r] * y[0] + m[k][3 * r + 1] * y[1] + m[k][3 * r + 2] * y[2]) for r in range(2)])
+    return out
+
+
+def back_solve(fac_ref, k, rows):
+    factor = row_list(fac_ref[k], 9)
+    return upper_solve(factor, *rows), factor
+
+
+def first_kernel(n_row, n_col, cams, pairs_ref, sums_ref, jac_ref, cam_hot_ref, land_hot_ref, index_ref, m_ref, fac_ref, damp_tile_ref, part_ref, back_ref, p_ref):
     groups = cams // CAM
     row_tiles = cams // n_row // LANES
     tiles = row_tiles + cams // n_col // LANES
-    count = jac_ref.shape[0]
+    each = range(jac_ref.shape[0])
     p_ref[...] = sums_ref[0] * (1.0 / sums_ref[1])
-    part_ref[...] = jnp.zeros(part_ref.shape, jnp.float32)
     own_tile, _ = own_place(n_row, n_col, cams)
     whole_tile = lax.axis_index("row") * row_tiles + own_tile
-    own = load_tile(p_ref, cams // LANES, whole_tile)
-    add_tile(part_ref, tiles, own_tile, own * damp_tile_ref[...])
-    for k in range(count):
-        u0, u1, m, y_land = half_product(k, p_ref, pairs_ref, jac_ref, land_hot_ref, index_ref, m_ref)
-        factor = row_list(fac_ref[k], 9)
-        solved = upper_solve(factor, y_land[0:1], y_land[1:2], y_land[2:3])
+    own = load_tile(p_ref, cams // LANES, whole_tile) * damp_tile_ref[...]
+    u, m, y_land = half_product(p_ref, pairs_ref, jac_ref, land_hot_ref, index_ref, m_ref)
+    v = reduced_rows(u, m, y_land, index_ref)
+    images = [dot3(jac_ref[k, 0] * v[k][0] + jac_ref[k, 1] * v[k][1], cam_hot_ref[k], NN) for k in each]
+    for k in each:
+        solved, factor = back_solve(fac_ref, k, row_list(y_land[k], 3))
         from_t = upper_solve(factor, factor[6], factor[7], factor[8])
         back_ref[k] = stack_rows(solved + from_t, 8)
-        y_obs = row_list(take_lanes(y_land[:8], index_ref[1, k : k + 1, :]), 3)
-        v0 = u0 - (m[0] * y_obs[0] + m[1] * y_obs[1] + m[2] * y_obs[2])
-        v1 = u1 - (m[3] * y_obs[0] + m[4] * y_obs[1] + m[5] * y_obs[2])
-        image = jac_ref[k, 0] * v0 + jac_ref[k, 1] * v1
-        image = dot3(image, cam_hot_ref[k], NN)
-        scatter_pair(image, part_ref, tiles, row_tiles, place(pairs_ref, k, n_row, n_col, groups))
+    spots = [place(pairs_ref, k, n_row, n_col, groups) for k in each]
+    write_parts(part_ref.at[0], row_tiles, tiles, spots, images, (own_tile, own))
 
 
 def total_sum(x):
@@ -277,17 +306,15 @@
     cam_out_ref[0:1, :] = alpha * flat_first
     cam_out_ref[1:2, :] = norm_next * flat_second
 
+    u, m, y_land = half_product(d_ref, pairs_ref, jac_ref, land_hot_ref, index_ref, m_ref)
+    v = reduced_rows(u, m, y_land, index_ref)
+    by_obs = sum(u[k][0] * v[k][0] + u[k][1] * v[k][1] for k in range(count))
+    energy = energy + jnp.sum(by_obs, axis=1, keepdims=True)
     for k in range(count):
-        u0, u1, m, y_land = half_product(k, d_ref, pairs_ref, jac_ref, land_hot_ref, index_ref, m_ref)
-        factor = row_list(fac_ref[k], 9)
-        solved = upper_solve(factor, y_land[0:1], y_land[1:2], y_land[2:3])
+        solved, _ = back_solve(fac_ref, k, row_list(y_land[k], 3))
         for b in range(3):
             land_base_ref[b, k : k + 1, :] = -(back_ref[k, 3 + b : 4 + b, :] + alpha * back_ref[k, b : b + 1, :])
             land_slope_ref[b, k : k + 1, :] = -norm_next * solved[b]
-        y_obs = row_list(take_lanes(y_land[:8], index_ref[1, k : k + 1, :]), 3)
-        v0 = u0 - (m[0] * y_obs[0] + m[1] * y_obs[1] + m[2] * y_obs[2])
-        v1 = u1 - (m[3] * y_obs[0] + m[4] * y_obs[1] + m[5] * y_obs[2])
-        energy = energy + jnp.sum(u0 * v0 + u1 * v1, axis=1, keepdims=True)
     energy_ref[...] = jnp.broadcast_to(energy, energy_ref.shape)
 
 

time: 55.8 us -> 54.7 us (0.980)
  Pallas kernels: 8.26 us -> 7.12 us
    pallas_call x1, Pallas kernels: 2.07 us -> 1.47 us  [per_device(): pl.pallas_call(functools.partial(first_kernel, n_row, n_col, cams), out_s...]
where the time goes in v4:
time: 54.7 us; the launch traced here: 54.5 us
  waiting for transfers between devices  19 us (35%)
  starting transfers between devices  17.5 us (32%)
  blocking collectives  10.1 us (18%)
  Pallas kernels  7.12 us (13%)
  between operations  0.69 us (1%)
    ppermute x14, waiting for transfers between devices, exchange(): lax.ppermute(x, AXES, [(i, i ^ mask) for i in range(n_dev)])  19 us
    ppermute x14, starting transfers between devices, exchange(): lax.ppermute(x, AXES, [(i, i ^ mask) for i in range(n_dev)])  17.5 us
    all_to_all x1, blocking collectives, per_device(): gathered = lax.all_to_all(energy, AXES, 0, 0, tiled=True)  10.1 us
    pallas_call x1, Pallas kernels, per_device(): pl.pallas_call(functools.partial(build_kernel, n_row, n_col, cams), out_s...  3.14 us
    pallas_call x1, Pallas kernels, per_device(): pl.pallas_call(functools.partial(second_kernel, n_row, n_col, cams), out_...  1.56 us
    pallas_call x1, Pallas kernels, per_device(): pl.pallas_call(functools.partial(first_kernel, n_row, n_col, cams), out_s...  1.47 us
  transfers between devices with their start and end apart: 14, of which 12 were waited for; matrix products, arithmetic and copies ran while one was open for 0% of the time, Pallas kernels for 0%

profile of v4, /device:TPU:0, one launch (start us, length us, event | category | flops | bytes accessed | tf_op | source)
XLA Modules:
  0.0 54.5 jit_solution(5610529943148402151)
XLA Ops:
  0.6 3.1 %shard_map.86 = (f32[2,7,8,128]{3,2,1,0:T(8,128)S(1)}, f32[4,2,16,512]{3,2,1,0:T(8,128)S(1)}, bf16[4,512,128]{2,1,0:T(8,128)(2,1)S(1)}, bf16[4,512,128]{2,1,0:T(...) custom-call(s32[2,4]{1,0:T(2,128)} %bitcast.6, ...), custom_call_target="tpu_custom_call" | custom-call | tf_op jit(solution)/shard_map/pallas_call | solution.py:403
  3.8 5.1 %collective-permute-start.2 = (f32[2,7,8,128]{3,2,1,0:T(8,128)S(1)}, f32[2,7,8,128]{3,2,1,0:T(8,128)S(1)}, u32[]{:S(2)}, u32[]{:S(2)}) collective-permute-start(f32[2,7,8,128]{3,2,1,0:T(8,128)S(1)} %get-tuple-element.18.refs_0_), channel_id=1, source_target_pairs={{0,24},{1,25},{2,26},{3,27},{4,28},{5,29},{6,30},{7,31},{8,16},{9,... | collective-permute-start | bytes 172040 | tf_op jit(solution)/shard_map/ppermute | solution.py:355
  8.9 0.6 %collective-permute-start = (f32[2,7,8,128]{3,2,1,0:T(8,128)S(1)}, f32[2,7,8,128]{3,2,1,0:T(8,128)S(1)}, u32[]{:S(2)}, u32[]{:S(2)}) collective-permute-start(f32[2,7,8,128]{3,2,1,0:T(8,128)S(1)} %get-tuple-element.18.refs_0_), channel_id=1, source_target_pairs={{0,8},{1,9},{2,10},{3,11},{4,12},{5,13},{6,14},{7,15},{8,0},{9,1},... | collective-permute-start | bytes 172040 | tf_op jit(solution)/shard_map/ppermute | solution.py:355
  9.5 1.8 %collective-permute-done.2.refs_3_ = f32[2,7,8,128]{3,2,1,0:T(8,128)S(1)} collective-permute-done((f32[2,7,8,128]{3,2,1,0:T(8,128)S(1)}, f32[2,7,8,128]{3,2,1,0:T(8,128)S(1)}, u32[]{:S(2)}, u32[]{:S(2)}) %collective-permute-start.2) | collective-permute-done | bytes 57376 | tf_op jit(solution)/shard_map/ppermute | solution.py:355
  11.3 2.7 %collective-permute-done.1.refs_2_ = f32[2,7,8,128]{3,2,1,0:T(8,128)S(1)} collective-permute-done((f32[2,7,8,128]{3,2,1,0:T(8,128)S(1)}, f32[2,7,8,128]{3,2,1,0:T(8,128)S(1)}, u32[]{:S(2)}, u32[]{:S(2)}) %collective-permute-start.1) | collective-permute-done | bytes 57376 | tf_op jit(solution)/shard_map/ppermute | solution.py:355
  14.1 2.6 %collective-permute-start.5 = (f32[2,18,8,128]{3,2,1,0:T(8,128)S(1)}, f32[2,18,8,128]{3,2,1,0:T(8,128)S(1)}, u32[]{:S(2)}, u32[]{:S(2)}) collective-permute-start(f32[2,18,8,128]{3,2,1,0:T(8,128)S(1)} %shard_map.87), channel_id=1, source_target_pairs={{0,6},{1,7},{2,4},{3,5},{4,2},{5,3},{6,0},{7,1},{8,14},{9,15},{10,... | collective-permute-start | bytes 442376 | tf_op jit(solution)/shard_map/ppermute | solution.py:355
  16.7 0.5 collective-permute-start.4
  17.2 0.5 collective-permute-start.3
  17.7 3.5 %collective-permute-done.5 = f32[2,18,8,128]{3,2,1,0:T(8,128)S(1)} collective-permute-done((f32[2,18,8,128]{3,2,1,0:T(8,128)S(1)}, f32[2,18,8,128]{3,2,1,0:T(8,128)S(1)}, u32[]{:S(2)}, u32[]{:S(2)}) %collective-permute-start.5) | collective-permute-done | bytes 147488 | tf_op jit(solution)/shard_map/ppermute | solution.py:355
  21.1 2.0 %collective-permute-done.4 = f32[2,18,8,128]{3,2,1,0:T(8,128)S(1)} collective-permute-done((f32[2,18,8,128]{3,2,1,0:T(8,128)S(1)}, f32[2,18,8,128]{3,2,1,0:T(8,128)S(1)}, u32[]{:S(2)}, u32[]{:S(2)}) %collective-permute-start.4) | collective-permute-done | bytes 147488 | tf_op jit(solution)/shard_map/ppermute | solution.py:355
  23.4 1.4 %collective-permute-done.6 = f32[2,18,8,128]{3,2,1,0:T(8,128)S(1)} collective-permute-done((f32[2,18,8,128]{3,2,1,0:T(8,128)S(1)}, f32[2,18,8,128]{3,2,1,0:T(8,128)S(1)}, u32[]{:S(2)}, u32[]{:S(2)}) %collective-permute-start.6) | collective-permute-done | bytes 147488 | tf_op jit(solution)/shard_map/ppermute | solution.py:355
  24.8 1.5 %shard_map.88 = (f32[1,7,8,128]{3,2,1,0:T(8,128)S(1)}, f32[4,8,128]{2,1,0:T(8,128)S(1)}) custom-call(s32[2,4]{1,0:T(2,128)} %bitcast.7, f32[2,18,8,128]{3,2,1,0:T(8,128)S(1)} %add.27.sums_ref, f32[4,2,16,512]{3,2,1,0:T(8,128)S(1)} %get-tuple-element.19.jac_ref, bf16[4,512,128]{2,1,0:T(8,128)(2,1)S(1)} %get-tuple-element.20.cam_hot_ref, ...), custom_call_target="tpu_custom_call" | custom-call | tf_op jit(solution)/shard_map/pallas_call | solution.py:419
  26.3 2.1 %collective-permute-start.9 = (f32[1,7,8,128]{3,2,1,0:T(8,128)S(1)}, f32[1,7,8,128]{3,2,1,0:T(8,128)S(1)}, u32[]{:S(2)}, u32[]{:S(2)}) collective-permute-start(f32[1,7,8,128]{3,2,1,0:T(8,128)S(1)} %get-tuple-element.26.refs_0_), channel_id=1, source_target_pairs={{0,24},{1,25},{2,26},{3,27},{4,28},{5,29},{6,30},{7,31},{8,16},{9,... | collective-permute-start | bytes 86024 | tf_op jit(solution)/shard_map/ppermute | solution.py:355
  28.4 2.3 %collective-permute-start.7 = (f32[1,7,8,128]{3,2,1,0:T(8,128)S(1)}, f32[1,7,8,128]{3,2,1,0:T(8,128)S(1)}, u32[]{:S(2)}, u32[]{:S(2)}) collective-permute-start(f32[1,7,8,128]{3,2,1,0:T(8,128)S(1)} %get-tuple-element.26.refs_0_), channel_id=1, source_target_pairs={{0,8},{1,9},{2,10},{3,11},{4,12},{5,13},{6,14},{7,15},{8,0},{9,1},... | collective-permute-start | bytes 86024 | tf_op jit(solution)/shard_map/ppermute | solution.py:355
  30.7 1.3 %collective-permute-done.9.refs_3_ = f32[1,7,8,128]{3,2,1,0:T(8,128)S(1)} collective-permute-done((f32[1,7,8,128]{3,2,1,0:T(8,128)S(1)}, f32[1,7,8,128]{3,2,1,0:T(8,128)S(1)}, u32[]{:S(2)}, u32[]{:S(2)}) %collective-permute-start.9) | collective-permute-done | bytes 28704 | tf_op jit(solution)/shard_map/ppermute | solution.py:355
  32.0 1.1 %collective-permute-done.8.refs_2_ = f32[1,7,8,128]{3,2,1,0:T(8,128)S(1)} collective-permute-done((f32[1,7,8,128]{3,2,1,0:T(8,128)S(1)}, f32[1,7,8,128]{3,2,1,0:T(8,128)S(1)}, u32[]{:S(2)}, u32[]{:S(2)}) %collective-permute-start.8) | collective-permute-done | bytes 28704 | tf_op jit(solution)/shard_map/ppermute | solution.py:355
  33.2 1.8 %collective-permute-start.12 = (f32[1,18,8,128]{3,2,1,0:T(8,128)S(1)}, f32[1,18,8,128]{3,2,1,0:T(8,128)S(1)}, u32[]{:S(2)}, u32[]{:S(2)}) collective-permute-start(f32[1,18,8,128]{3,2,1,0:T(8,128)S(1)} %shard_map.89), channel_id=1, source_target_pairs={{0,6},{1,7},{2,4},{3,5},{4,2},{5,3},{6,0},{7,1},{8,14},{9,15},{10,... | collective-permute-start | bytes 221192 | tf_op jit(solution)/shard_map/ppermute | solution.py:355
  35.0 1.3 %collective-permute-start.11 = (f32[1,18,8,128]{3,2,1,0:T(8,128)S(1)}, f32[1,18,8,128]{3,2,1,0:T(8,128)S(1)}, u32[]{:S(2)}, u32[]{:S(2)}) collective-permute-start(f32[1,18,8,128]{3,2,1,0:T(8,128)S(1)} %shard_map.89), channel_id=1, source_target_pairs={{0,2},{1,3},{2,0},{3,1},{4,6},{5,7},{6,4},{7,5},{8,10},{9,11},{10,... | collective-permute-start | bytes 221192 | tf_op jit(solution)/shard_map/ppermute | solution.py:355
  36.8 2.5 %collective-permute-done.12 = f32[1,18,8,128]{3,2,1,0:T(8,128)S(1)} collective-permute-done((f32[1,18,8,128]{3,2,1,0:T(8,128)S(1)}, f32[1,18,8,128]{3,2,1,0:T(8,128)S(1)}, u32[]{:S(2)}, u32[]{:S(2)}) %collective-permute-start.12) | collective-permute-done | bytes 73760 | tf_op jit(solution)/shard_map/ppermute | solution.py:355
  39.7 1.0 %collective-permute-done.10 = f32[1,18,8,128]{3,2,1,0:T(8,128)S(1)} collective-permute-done((f32[1,18,8,128]{3,2,1,0:T(8,128)S(1)}, f32[1,18,8,128]{3,2,1,0:T(8,128)S(1)}, u32[]{:S(2)}, u32[]{:S(2)}) %collective-permute-start.10) | collective-permute-done | bytes 73760 | tf_op jit(solution)/shard_map/ppermute | solution.py:355
  40.8 1.3 %collective-permute-done.13 = f32[1,18,8,128]{3,2,1,0:T(8,128)S(1)} collective-permute-done((f32[1,18,8,128]{3,2,1,0:T(8,128)S(1)}, f32[1,18,8,128]{3,2,1,0:T(8,128)S(1)}, u32[]{:S(2)}, u32[]{:S(2)}) %collective-permute-start.13) | collective-permute-done | bytes 73760 | tf_op jit(solution)/shard_map/ppermute | solution.py:355
  42.1 1.6 %shard_map.90 = (f32[32,1,128]{2,1,0:T(1,128)S(1)}, f32[2,576]{1,0:T(2,128)S(1)}, f32[3,4,128]{2,1,0:T(4,128)S(1)}, f32[3,4,128]{2,1,0:T(4,128)S(1)}) custom-call(s32[2,4]{1,0:T(2,128)} %bitcast.8, f32[2,18,8,128]{3,2,1,0:T(8,128)S(1)} %add.27.sums_ref, f32[1,18,8,128]{3,2,1,0:T(8,128)S(1)} %add.31.image_ref, ...), custom_call_target="tpu_custom_call" | custom-call | tf_op jit(solution)/shard_map/pallas_call | solution.py:429
  43.6 10.1 %all_to_all.5.energy_ref = f32[32,1,128]{2,1,0:T(1,128)S(1)} all-to-all(f32[32,1,128]{2,1,0:T(1,128)S(1)} %get-tuple-element.28), channel_id=1, replica_groups=mesh['row'=8,'col'=4] {'row','col'}, dimensions={0} | all-to-all | bytes 32768 | tf_op jit(solution)/shard_map/all_to_all | solution.py:437
  53.8 0.7 %shard_map.91 = (f32[576]{0:T(1024)}, f32[3,4,128]{2,1,0:T(4,128)}) custom-call(f32[32,1,128]{2,1,0:T(1,128)S(1)} %all_to_all.5.energy_ref, f32[2,576]{1,0:T(2,128)S(1)} %get-tuple-element.29.cam_ref, f32[3,4,128]{2,1,0:T(4,128)S(1)} %get-tuple-element.30.land_base_ref, f32[3,4,128]{2,1,0:T(4,128)S(1)} %get-tuple-element.31.land_slope_ref), custom_call_target="tpu_custom_call" | custom-call | tf_op jit(solution)/shard_map/pallas_call | solution.py:438
  (15 shorter events, 1.5 us)
Async XLA Ops:
  3.8 7.5 %collective-permute-start.2 = (f32[2,7,8,128]{3,2,1,0:T(8,128)S(1)}, f32[2,7,8,128]{3,2,1,0:T(8,128)S(1)}, u32[]{:S(2)}, u32[]{:S(2)}) collective-permute-start(f32[2,7,8,128]{3,2,1,0:T(8,128)S(1)} %get-tuple-element.18.refs_0_), channel_id=1, source_target_pairs={{0,24},{1,25},{2,26},{3,27},{4,28},{5,29},{6,30},{7,31},{8,16},{9,... | collective-permute-start | bytes 172040 | tf_op jit(solution)/shard_map/ppermute | solution.py:355
  8.9 5.1 %collective-permute-start.1 = (f32[2,7,8,128]{3,2,1,0:T(8,128)S(1)}, f32[2,7,8,128]{3,2,1,0:T(8,128)S(1)}, u32[]{:S(2)}, u32[]{:S(2)}) collective-permute-start(f32[2,7,8,128]{3,2,1,0:T(8,128)S(1)} %get-tuple-element.18.refs_0_), channel_id=1, source_target_pairs={{0,16},{1,17},{2,18},{3,19},{4,20},{5,21},{6,22},{7,23},{8,24},{9,... | collective-permute-start | bytes 172040 | tf_op jit(solution)/shard_map/ppermute | solution.py:355
  8.9 5.1 %collective-permute-start = (f32[2,7,8,128]{3,2,1,0:T(8,128)S(1)}, f32[2,7,8,128]{3,2,1,0:T(8,128)S(1)}, u32[]{:S(2)}, u32[]{:S(2)}) collective-permute-start(f32[2,7,8,128]{3,2,1,0:T(8,128)S(1)} %get-tuple-element.18.refs_0_), channel_id=1, source_target_pairs={{0,8},{1,9},{2,10},{3,11},{4,12},{5,13},{6,14},{7,15},{8,0},{9,1},... | collective-permute-start | bytes 172040 | tf_op jit(solution)/shard_map/ppermute | solution.py:355
  14.1 7.0 %collective-permute-start.5 = (f32[2,18,8,128]{3,2,1,0:T(8,128)S(1)}, f32[2,18,8,128]{3,2,1,0:T(8,128)S(1)}, u32[]{:S(2)}, u32[]{:S(2)}) collective-permute-start(f32[2,18,8,128]{3,2,1,0:T(8,128)S(1)} %shard_map.87), channel_id=1, source_target_pairs={{0,6},{1,7},{2,4},{3,5},{4,2},{5,3},{6,0},{7,1},{8,14},{9,15},{10,... | collective-permute-start | bytes 442376 | tf_op jit(solution)/shard_map/ppermute | solution.py:355
  16.7 6.5 %collective-permute-start.4 = (f32[2,18,8,128]{3,2,1,0:T(8,128)S(1)}, f32[2,18,8,128]{3,2,1,0:T(8,128)S(1)}, u32[]{:S(2)}, u32[]{:S(2)}) collective-permute-start(f32[2,18,8,128]{3,2,1,0:T(8,128)S(1)} %shard_map.87), channel_id=1, source_target_pairs={{0,2},{1,3},{2,0},{3,1},{4,6},{5,7},{6,4},{7,5},{8,10},{9,11},{10,... | collective-permute-start | bytes 442376 | tf_op jit(solution)/shard_map/ppermute | solution.py:355
  17.2 6.1 %collective-permute-start.3 = (f32[2,18,8,128]{3,2,1,0:T(8,128)S(1)}, f32[2,18,8,128]{3,2,1,0:T(8,128)S(1)}, u32[]{:S(2)}, u32[]{:S(2)}) collective-permute-start(f32[2,18,8,128]{3,2,1,0:T(8,128)S(1)} %shard_map.87), channel_id=1, source_target_pairs={{0,4},{1,5},{2,6},{3,7},{4,0},{5,1},{6,2},{7,3},{8,12},{9,13},{10,... | collective-permute-start | bytes 442376 | tf_op jit(solution)/shard_map/ppermute | solution.py:355
  23.3 1.4 %collective-permute-start.6 = (f32[2,18,8,128]{3,2,1,0:T(8,128)S(1)}, f32[2,18,8,128]{3,2,1,0:T(8,128)S(1)}, u32[]{:S(2)}, u32[]{:S(2)}) collective-permute-start(f32[2,18,8,128]{3,2,1,0:T(8,128)S(1)} %add_add_fusion), channel_id=1, source_target_pairs={{0,1},{1,0},{2,3},{3,2},{4,5},{5,4},{6,7},{7,6},{8,9},{9,8},{10,11... | collective-permute-start | bytes 442376 | tf_op jit(solution)/shard_map/ppermute | solution.py:355
  26.3 5.8 %collective-permute-start.9 = (f32[1,7,8,128]{3,2,1,0:T(8,128)S(1)}, f32[1,7,8,128]{3,2,1,0:T(8,128)S(1)}, u32[]{:S(2)}, u32[]{:S(2)}) collective-permute-start(f32[1,7,8,128]{3,2,1,0:T(8,128)S(1)} %get-tuple-element.26.refs_0_), channel_id=1, source_target_pairs={{0,24},{1,25},{2,26},{3,27},{4,28},{5,29},{6,30},{7,31},{8,16},{9,... | collective-permute-start | bytes 86024 | tf_op jit(solution)/shard_map/ppermute | solution.py:355
  28.4 4.8 %collective-permute-start.8 = (f32[1,7,8,128]{3,2,1,0:T(8,128)S(1)}, f32[1,7,8,128]{3,2,1,0:T(8,128)S(1)}, u32[]{:S(2)}, u32[]{:S(2)}) collective-permute-start(f32[1,7,8,128]{3,2,1,0:T(8,128)S(1)} %get-tuple-element.26.refs_0_), channel_id=1, source_target_pairs={{0,16},{1,17},{2,18},{3,19},{4,20},{5,21},{6,22},{7,23},{8,24},{9,... | collective-permute-start | bytes 86024 | tf_op jit(solution)/shard_map/ppermute | solution.py:355
  28.4 4.8 %collective-permute-start.7 = (f32[1,7,8,128]{3,2,1,0:T(8,128)S(1)}, f32[1,7,8,128]{3,2,1,0:T(8,128)S(1)}, u32[]{:S(2)}, u32[]{:S(2)}) collective-permute-start(f32[1,7,8,128]{3,2,1,0:T(8,128)S(1)} %get-tuple-element.26.refs_0_), channel_id=1, source_target_pairs={{0,8},{1,9},{2,10},{3,11},{4,12},{5,13},{6,14},{7,15},{8,0},{9,1},... | collective-permute-start | bytes 86024 | tf_op jit(solution)/shard_map/ppermute | solution.py:355
  33.2 6.1 %collective-permute-start.12 = (f32[1,18,8,128]{3,2,1,0:T(8,128)S(1)}, f32[1,18,8,128]{3,2,1,0:T(8,128)S(1)}, u32[]{:S(2)}, u32[]{:S(2)}) collective-permute-start(f32[1,18,8,128]{3,2,1,0:T(8,128)S(1)} %shard_map.89), channel_id=1, source_target_pairs={{0,6},{1,7},{2,4},{3,5},{4,2},{5,3},{6,0},{7,1},{8,14},{9,15},{10,... | collective-permute-start | bytes 221192 | tf_op jit(solution)/shard_map/ppermute | solution.py:355
  35.0 4.7 %collective-permute-start.11 = (f32[1,18,8,128]{3,2,1,0:T(8,128)S(1)}, f32[1,18,8,128]{3,2,1,0:T(8,128)S(1)}, u32[]{:S(2)}, u32[]{:S(2)}) collective-permute-start(f32[1,18,8,128]{3,2,1,0:T(8,128)S(1)} %shard_map.89), channel_id=1, source_target_pairs={{0,2},{1,3},{2,0},{3,1},{4,6},{5,7},{6,4},{7,5},{8,10},{9,11},{10,... | collective-permute-start | bytes 221192 | tf_op jit(solution)/shard_map/ppermute | solution.py:355
  36.4 4.4 %collective-permute-start.10 = (f32[1,18,8,128]{3,2,1,0:T(8,128)S(1)}, f32[1,18,8,128]{3,2,1,0:T(8,128)S(1)}, u32[]{:S(2)}, u32[]{:S(2)}) collective-permute-start(f32[1,18,8,128]{3,2,1,0:T(8,128)S(1)} %shard_map.89), channel_id=1, source_target_pairs={{0,4},{1,5},{2,6},{3,7},{4,0},{5,1},{6,2},{7,3},{8,12},{9,13},{10,... | collective-permute-start | bytes 221192 | tf_op jit(solution)/shard_map/ppermute | solution.py:355
  40.7 1.3 %collective-permute-start.13 = (f32[1,18,8,128]{3,2,1,0:T(8,128)S(1)}, f32[1,18,8,128]{3,2,1,0:T(8,128)S(1)}, u32[]{:S(2)}, u32[]{:S(2)}) collective-permute-start(f32[1,18,8,128]{3,2,1,0:T(8,128)S(1)} %add_add_fusion.1), channel_id=1, source_target_pairs={{0,1},{1,0},{2,3},{3,2},{4,5},{5,4},{6,7},{7,6},{8,9},{9,8},{10,11... | collective-permute-start | bytes 221192 | tf_op jit(solution)/shard_map/ppermute | solution.py:355

commit v5 on v4

v5 whole, which is shorter than its diff:
```python
import functools

import jax
import jax.numpy as jnp
from jax import lax
from jax.experimental import pallas as pl
from jax.experimental.pallas import tpu as pltpu
from jax.sharding import PartitionSpec as P

CAM = 64
LM = 128
LANES = 128
AXES = ("row", "col")
DAMPING = 1.0

NN = (((1,), (0,)), ((), ()))
NT = (((1,), (1,)), ((), ()))


def split3(x):
    hi = x.astype(jnp.bfloat16)
    rest = x - hi.astype(jnp.float32)
    mid = rest.astype(jnp.bfloat16)
    low = (rest - mid.astype(jnp.float32)).astype(jnp.bfloat16)
    return jnp.concatenate([hi, mid, low], axis=0)


def dot3(x, exact, dims):
    n = x.shape[0]
    y = lax.dot_general(split3(x), exact, dims, preferred_element_type=jnp.float32)
    return (y[2 * n :] + y[n : 2 * n]) + y[:n]


def onehot(index_column, lanes):
    return jnp.where(index_column == lanes, jnp.bfloat16(1), jnp.bfloat16(0))


def take_lanes(x, index_row):
    pieces = []
    for start in range(0, index_row.shape[1], LANES):
        index = jnp.broadcast_to(index_row[:, start : start + LANES], x.shape)
        pieces.append(jnp.take_along_axis(x, index, axis=1, mode="promise_in_bounds"))
    return jnp.concatenate(pieces, axis=1)


def pad_rows(x, rows):
    if x.shape[0] == rows:
        return x
    return jnp.concatenate([x, jnp.zeros((rows - x.shape[0], x.shape[1]), x.dtype)], axis=0)


def stack_rows(rows, total):
    rows = list(rows)
    if len(rows) == total:
        return jnp.concatenate(rows, axis=0)
    rows.append(jnp.zeros((total - len(rows), rows[0].shape[1]), jnp.float32))
    return jnp.concatenate(rows, axis=0)


def cholesky_three(v00, v01, v02, v11, v12, v22):
    inv_first = 1.0 / jnp.sqrt(v00)
    low_one = v01 * inv_first
    low_two = v02 * inv_first
    inv_second = 1.0 / jnp.sqrt(v11 - low_one * low_one)
    low_three = (v12 - low_two * low_one) * inv_second
    inv_third = 1.0 / jnp.sqrt(v22 - low_two * low_two - low_three * low_three)
    return (inv_first, low_one, low_two, inv_second, low_three, inv_third)


def lower_solve(factor, first, second, third):
    out_one = first * factor[0]
    out_two = (second - factor[1] * out_one) * factor[3]
    out_three = (third - factor[2] * out_one - factor[4] * out_two) * factor[5]
    return (out_one, out_two, out_three)


def upper_solve(factor, first, second, third):
    out_three = third * factor[5]
    out_two = (second - factor[4] * out_three) * factor[3]
    out_one = (first - factor[1] * out_two - factor[2] * out_three) * factor[0]
    return (out_one, out_two, out_three)


def row_list(x, count):
    return [x[i : i + 1] for i in range(count)]


def lane_ids(rows):
    return lax.broadcasted_iota(jnp.int32, (rows, LANES), 1)


def to_first(x, half):
    return pltpu.roll(x, half * CAM, 1)


def to_second(x, half):
    return pltpu.roll(x, (1 - half) * CAM, 1)


def packed(tiles):
    return tiles + tiles // 8 + 1


def load_tile(ref, tiles, t):
    ninth = ref[tiles + t // 8, pl.ds(t % 8, 1), :]
    return jnp.concatenate([ref[t], ninth, jnp.zeros((7, LANES), jnp.float32)], axis=0)


def write_ninths(ref, tiles, rows, sums=None):
    rows = list(rows) + [jnp.zeros((1, LANES), jnp.float32) if sums is None else sums]
    for start in range(0, len(rows), 8):
        ref[tiles + start // 8] = stack_rows(rows[start : start + 8], 8)


def shard_select(shard, lane_offset):
    entry = lax.broadcasted_iota(jnp.int32, (shard, LANES), 0)
    start = 9 * (lax.broadcasted_iota(jnp.int32, (shard, LANES), 1) - lane_offset)
    inside = (entry >= start) & (entry < start + 9)
    return jnp.where(inside, 1.0, 0.0).astype(jnp.bfloat16)


def param_mask(shard):
    entry = lax.broadcasted_iota(jnp.int32, (16, shard), 1).astype(jnp.float32)
    camera = jnp.floor((entry + 0.5) * (1.0 / 9.0))
    param = entry - 9.0 * camera
    return param == lax.broadcasted_iota(jnp.int32, (16, shard), 0).astype(jnp.float32)


def place(pairs_ref, k, n_row, n_col, groups):
    first = pairs_ref[0, k] - lax.axis_index("row") * (groups // n_row)
    second = pairs_ref[1, k] - lax.axis_index("col") * (groups // n_col)
    return first // 2, first % 2, second // 2, second % 2


def read_spots(spots_ref):
    return [[spots_ref[i, k] for i in range(4)] for k in range(spots_ref.shape[1])]


def write_parts(ref, row_tiles, tiles, spots, values, extra=None, sums=None):
    lower = lane_ids(values[0].shape[0]) < CAM
    firsts = [to_first(jnp.where(lower, v, 0.0), spot[1]) for v, spot in zip(values, spots)]
    seconds = [to_second(jnp.where(lower, 0.0, v), spot[3]) for v, spot in zip(values, spots)]
    ninths = []
    for t in range(tiles):
        if t < row_tiles:
            items = [(spot[0] == t, v) for v, spot in zip(firsts, spots)]
            if extra is not None:
                items.append((extra[0] == t, extra[1]))
        else:
            items = [(spot[2] == t - row_tiles, v) for v, spot in zip(seconds, spots)]
        total = sum(jnp.where(here, v, 0.0) for here, v in items)
        ref[t] = total[:8]
        ninths.append(total[8:9])
    write_ninths(ref, tiles, ninths, sums)


def own_place(n_row, n_col, cams):
    shard_cams = cams // (n_row * n_col)
    start = lax.axis_index("col") * shard_cams
    return start // LANES, start % LANES


def build_kernel(n_row, n_col, cams, pairs_ref, cam_ref, land_ref, resid_ref, ocam_ref, oland_ref, damp_ref, part_ref, jac_ref, cam_hot_ref, land_hot_ref, index_ref, m_ref, fac_ref, damp_tile_ref, select_ref, spots_ref):
    groups = cams // CAM
    row_tiles = cams // n_row // LANES
    tiles = row_tiles + cams // n_col // LANES
    count, obs = ocam_ref.shape
    each = range(count)
    shard = damp_ref.shape[0]

    index_ref[0] = ocam_ref[...]
    index_ref[1] = oland_ref[...]
    rows = jnp.concatenate([ocam_ref[...], oland_ref[...]], axis=0).astype(jnp.float32)
    columns = jnp.transpose(pad_rows(rows, (2 * count + 7) // 8 * 8)).astype(jnp.int32)
    key = (ocam_ref[...] * LM + oland_ref[...]).astype(jnp.int16)
    lanes = lax.broadcasted_iota(jnp.int32, (obs, LANES), 1).astype(jnp.int16)
    cam_columns = [columns[:, k : k + 1] for k in each]
    land_columns = [columns[:, count + k : count + k + 1] for k in each]
    for k in each:
        land_hot_ref[k] = onehot(land_columns[k].astype(jnp.int16), lanes)

    lj = [[land_ref[i, k : k + 1, :] for i in range(6)] for k in each]
    e0 = [resid_ref[k, 0:1, :] for k in each]
    e1 = [resid_ref[k, 1:2, :] for k in each]
    sums = []
    for k in each:

        def outer(i, j):
            return lj[k][i] * lj[k][j] + lj[k][3 + i] * lj[k][3 + j]

        entries = [outer(0, 0), outer(0, 1), outer(0, 2), outer(1, 1), outer(1, 2), outer(2, 2)]
        entries += [lj[k][b] * e0[k] + lj[k][3 + b] * e1[k] for b in range(3)]
        sums.append(dot3(stack_rows(entries, 16), land_hot_ref[k], NN))
    total = [jnp.concatenate([sums[k][i : i + 1] for k in each], axis=0) for i in range(9)]
    factor = cholesky_three(
        total[0] + DAMPING, total[1], total[2], total[3] + DAMPING, total[4], total[5] + DAMPING
    )
    land_rows = list(factor) + list(lower_solve(factor, total[6], total[7], total[8]))
    for k in each:
        cam_hot_ref[k] = onehot(cam_columns[k].astype(jnp.int16), lanes)
        jac_ref[k, 0] = pad_rows(cam_ref[0:9, k, :], 16)
        jac_ref[k, 1] = pad_rows(cam_ref[9:18, k, :], 16)
    ms, ws = [], []
    for k in each:
        land_values = stack_rows([row[k : k + 1] for row in land_rows], 16)
        fac_ref[k] = land_values
        at_obs = row_list(take_lanes(land_values, oland_ref[k : k + 1, :]), 9)
        m0 = lower_solve(at_obs, lj[k][0], lj[k][1], lj[k][2])
        m1 = lower_solve(at_obs, lj[k][3], lj[k][4], lj[k][5])
        m_ref[k] = stack_rows(m0 + m1, 8)
        ms.append((m0, m1))
        w0 = m0[0] * at_obs[6] + m0[1] * at_obs[7] + m0[2] * at_obs[8] - e0[k]
        w1 = m1[0] * at_obs[6] + m1[1] * at_obs[7] + m1[2] * at_obs[8] - e1[k]
        ws.append((w0, w1))
    both = []
    for k in each:
        j0, j1 = jac_ref[k, 0], jac_ref[k, 1]
        m0, m1 = ms[k]
        coupled = jnp.concatenate([j0 * m0[b] + j1 * m1[b] for b in range(3)], axis=0)
        same = onehot((cam_columns[k] * LM + land_columns[k]).astype(jnp.int16), key[k : k + 1, :])
        prod = coupled * dot3(coupled, same, NN)
        diag = j0 * j0 + j1 * j1 - (prod[0:16] + prod[16:32] + prod[32:48])
        rhs = j0 * ws[k][0] + j1 * ws[k][1]
        both.append(dot3(jnp.concatenate([rhs, diag], axis=0), cam_hot_ref[k], NN))

    own_tile, own_lane = own_place(n_row, n_col, cams)
    spread = jnp.where(param_mask(shard), damp_ref[...].reshape(1, shard), 0.0)
    select = shard_select(shard, own_lane)
    select_ref[...] = select
    damp_tile = dot3(spread, select, NN)
    damp_tile_ref[...] = damp_tile
    spots = [place(pairs_ref, k, n_row, n_col, groups) for k in each]
    for k in each:
        for i in range(4):
            spots_ref[i, k] = spots[k][i]
    write_parts(part_ref.at[0], row_tiles, tiles, spots, [x[:16] for x in both])
    write_parts(part_ref.at[1], row_tiles, tiles, spots, [x[16:] for x in both], (own_tile, damp_tile))


def half_product(p_ref, row_tiles, tiles, spots, jac_ref, land_hot_ref, index_ref, m_ref):
    each = range(jac_ref.shape[0])
    lower = lane_ids(16) < CAM
    u, m, y_land = [], [], []
    for k in each:
        t_first, h_first, t_second, h_second = spots[k]
        p_first = to_first(load_tile(p_ref, tiles, t_first), h_first)
        p_second = to_second(load_tile(p_ref, tiles, row_tiles + t_second), h_second)
        at_obs = take_lanes(jnp.where(lower, p_first, p_second), index_ref[0, k : k + 1, :])
        u.append([jnp.sum(jac_ref[k, r] * at_obs, axis=0, keepdims=True) for r in range(2)])
    for k in each:
        m.append([m_ref[k, i : i + 1, :] for i in range(6)])
        y = [m[k][b] * u[k][0] + m[k][3 + b] * u[k][1] for b in range(3)]
        y_land.append(dot3(stack_rows(y, 16), land_hot_ref[k], NN)[:8])
    return u, m, y_land


def reduced_rows(u, m, y_land, index_ref):
    out = []
    for k in range(len(u)):
        y = row_list(take_lanes(y_land[k], index_ref[1, k : k + 1, :]), 3)
        out.append([u[k][r] - (m[k][3 * r] * y[0] + m[k][3 * r + 1] * y[1] + m[k][3 * r + 2] * y[2]) for r in range(2)])
    return out


def back_solve(fac_ref, k, rows):
    factor = row_list(fac_ref[k], 9)
    return upper_solve(factor, *rows), factor


def total_sum(x):
    return jnp.sum(jnp.sum(x, axis=0, keepdims=True), axis=1, keepdims=True)


def own_lanes(own_lane, shard_cams):
    ids = lane_ids(16)
    return (ids >= own_lane) & (ids < own_lane + shard_cams)


def in_lanes(values):
    ids = lane_ids(1)
    row = jnp.zeros((1, LANES), jnp.float32)
    for lane, value in enumerate(values):
        row = jnp.where(ids == lane, value, row)
    return row


def energy_sum(u, v):
    return total_sum(sum(u[k][r] * v[k][r] for k in range(len(u)) for r in range(2)))


def first_kernel(n_row, n_col, cams, spots_ref, mine_ref, other_ref, jac_ref, cam_hot_ref, land_hot_ref, index_ref, m_ref, fac_ref, damp_tile_ref, part_ref, back_ref, p_ref, right_ref):
    row_tiles = cams // n_row // LANES
    tiles = row_tiles + cams // n_col // LANES
    each = range(jac_ref.shape[0])
    right = mine_ref[0] + other_ref[0]
    right_ref[...] = right
    p_ref[...] = right * (1.0 / (mine_ref[1] + other_ref[1]))
    spots = read_spots(spots_ref)
    u, m, y_land = half_product(p_ref, row_tiles, tiles, spots, jac_ref, land_hot_ref, index_ref, m_ref)
    v = reduced_rows(u, m, y_land, index_ref)
    images = [dot3(jac_ref[k, 0] * v[k][0] + jac_ref[k, 1] * v[k][1], cam_hot_ref[k], NN) for k in each]
    own_tile, own_lane = own_place(n_row, n_col, cams)
    own = load_tile(p_ref, tiles, own_tile)
    damped = own * damp_tile_ref[...]
    mask = own_lanes(own_lane, cams // (n_row * n_col))
    norm_now = total_sum(jnp.where(mask, own * load_tile(right_ref, tiles, own_tile), 0.0))
    energy = energy_sum(u, v) + total_sum(own * damped)
    for k in each:
        solved, factor = back_solve(fac_ref, k, row_list(y_land[k], 3))
        from_t = upper_solve(factor, factor[6], factor[7], factor[8])
        for b in range(3):
            back_ref[0, b, k : k + 1, :] = from_t[b]
            back_ref[1, b, k : k + 1, :] = solved[b]
    write_parts(part_ref.at[0], row_tiles, tiles, spots, images, (own_tile, damped), in_lanes([norm_now, energy]))


def second_kernel(n_row, n_col, cams, spots_ref, mine_ref, other_ref, image_mine_ref, image_other_ref, jac_ref, land_hot_ref, index_ref, m_ref, fac_ref, damp_tile_ref, select_ref, sums_ref, known_ref, cam_ref, solved_ref, p_ref, scratch_ref):
    row_tiles = cams // n_row // LANES
    tiles = row_tiles + cams // n_col // LANES
    each = range(jac_ref.shape[0])
    shard = cam_ref.shape[1]
    image = image_mine_ref[0] + image_other_ref[0]
    sums = image[tiles + tiles // 8, tiles % 8 : tiles % 8 + 1]
    norm_now, energy_now = sums[:, 0:1], sums[:, 1:2]
    alpha = norm_now / energy_now
    for i, value in enumerate((1.0 / norm_now, energy_now, alpha)):
        known_ref[i : i + 1, :] = jnp.broadcast_to(value, (1, LANES))
    right = mine_ref[0] + other_ref[0]
    precond = 1.0 / (mine_ref[1] + other_ref[1])
    residual = right - alpha * image
    p_ref[...] = precond * residual
    scratch_ref[0] = right * precond
    scratch_ref[1] = residual
    scratch_ref[2] = image
    spots = read_spots(spots_ref)
    u, m, y_land = half_product(p_ref, row_tiles, tiles, spots, jac_ref, land_hot_ref, index_ref, m_ref)
    v = reduced_rows(u, m, y_land, index_ref)

    own_tile, own_lane = own_place(n_row, n_col, cams)
    own = load_tile(p_ref, tiles, own_tile)
    own_start, own_residual, own_image = [load_tile(scratch_ref.at[i], tiles, own_tile) for i in range(3)]
    flat = dot3(jnp.concatenate([own_start, own], axis=0), select_ref[...], NT)
    params = param_mask(shard)
    for i in range(2):
        cam_ref[i : i + 1, :] = jnp.sum(jnp.where(params, flat[16 * i : 16 * i + 16], 0.0), axis=0, keepdims=True)
    mask = own_lanes(own_lane, cams // (n_row * n_col))
    norm_next = total_sum(jnp.where(mask, own * own_residual, 0.0))
    cross = total_sum(jnp.where(mask, own * own_image, 0.0))
    energy = energy_sum(u, v) + total_sum(own * own * damp_tile_ref[...])
    sums_ref[...] = jnp.broadcast_to(in_lanes([energy, norm_next, cross])[None], sums_ref.shape)
    for k in each:
        solved, _ = back_solve(fac_ref, k, row_list(y_land[k], 3))
        for b in range(3):
            solved_ref[b, k : k + 1, :] = solved[b]


def last_kernel(sums_ref, known_ref, cam_ref, back_ref, solved_ref, cam_out_ref, land_out_ref):
    sums = jnp.sum(sums_ref[...], axis=0)
    energy, norm_next, cross = [jnp.broadcast_to(sums[:, i : i + 1], (1, LANES)) for i in range(3)]
    inverse_now, energy_now, alpha = [known_ref[i : i + 1, :] for i in range(3)]
    beta = norm_next * inverse_now
    slope = norm_next / (energy + beta * (2.0 * cross + beta * energy_now))
    first = alpha + slope * beta
    shard = cam_ref.shape[1]
    repeats = (shard + LANES - 1) // LANES
    first_wide, slope_wide = [jnp.concatenate([x] * repeats, axis=1)[:, :shard] for x in (first, slope)]
    cam_step = first_wide * cam_ref[0:1, :] + slope_wide * cam_ref[1:2, :]
    cam_out_ref[...] = cam_step.reshape(cam_out_ref.shape)
    land_out_ref[...] = -(back_ref[0] + first[None] * back_ref[1] + slope[None] * solved_ref[...])


def spread_kernel(n_row, n_col, cams, radix, masks, *refs):
    part_refs, out_refs, (whole_ref, ninth_ref) = refs[:radix], refs[radix:-2], refs[-2:]
    row_tiles = cams // n_row // LANES
    col_tiles = cams // n_col // LANES
    tiles = row_tiles + col_tiles
    sent = row_tiles + 2 * col_tiles
    row, col = lax.axis_index("row"), lax.axis_index("col")
    for v in range(whole_ref.shape[0]):
        parts = [ref[v] for ref in part_refs]
        total = parts[0]
        for part in parts[1:]:
            total = total + part
        sums = total[tiles + tiles // 8, tiles % 8 : tiles % 8 + 1]
        whole_ref[v] = jnp.zeros(whole_ref.shape[1:], jnp.float32)
        ninth_ref[v] = jnp.zeros(ninth_ref.shape[1:], jnp.float32)
        for i in range(col_tiles):
            t = row_tiles + i
            whole_ref[v, col * col_tiles + i] = total[t]
            ninth_ref[v, pl.ds(col * col_tiles + i, 1), :] = total[tiles + t // 8, t % 8 : t % 8 + 1]
        for digit, part in enumerate(parts):
            start = (row ^ (digit * (n_row // radix))) * row_tiles
            for i in range(row_tiles):
                whole_ref[v, start + i] += part[i]
                ninth_ref[v, pl.ds(start + i, 1), :] += part[tiles + i // 8, i % 8 : i % 8 + 1]
        for mask, out_ref in zip(masks, out_refs):
            col_start = ((col ^ (mask % n_col)) // 2) * (2 * col_tiles)
            row_start = (row ^ (mask // n_col)) * row_tiles
            places = [col_start + i for i in range(2 * col_tiles)] + [row_start + i for i in range(row_tiles)]
            for i, t in enumerate(places):
                out_ref[v, i] = whole_ref[v, t]
            write_ninths(out_ref.at[v], sent, [ninth_ref[v, pl.ds(t, 1), :] for t in places], sums)


def pair_kernel(n_row, n_col, cams, *refs):
    in_refs, (mine_ref, other_ref) = refs[:-2], refs[-2:]
    row_tiles = cams // n_row // LANES
    col_tiles = cams // n_col // LANES
    tiles = row_tiles + col_tiles
    sent = row_tiles + 2 * col_tiles
    core = lax.axis_index("col") % 2
    for v in range(mine_ref.shape[0]):
        total = in_refs[0][v]
        for ref in in_refs[1:]:
            total = total + ref[v]

        def ninth(i):
            return total[sent + i // 8, i % 8 : i % 8 + 1]

        sums = ninth(sent)
        rows = range(2 * col_tiles, sent)
        lower = [(total[i], ninth(i)) for i in range(col_tiles)]
        upper = [(total[i], ninth(i)) for i in range(col_tiles, 2 * col_tiles)]
        for out_ref, first in ((mine_ref, core == 0), (other_ref, core == 1)):
            ninths = []
            for i, t in enumerate(rows):
                out_ref[v, i] = total[t]
                ninths.append(ninth(t))
            for i in range(col_tiles):
                out_ref[v, row_tiles + i] = jnp.where(first, lower[i][0], upper[i][0])
                ninths.append(jnp.where(first, lower[i][1], upper[i][1]))
            write_ninths(out_ref.at[v], tiles, ninths, sums)


def exchange(x, masks, n_dev):
    return [lax.ppermute(x, AXES, [(i, i ^ mask) for i in range(n_dev)]) for mask in masks]


def in_vmem(x):
    return pltpu.with_memory_space_constraint(x, pltpu.VMEM)


def per_device(n_row, n_col, cam_jac, land_jac, resid, obs_cam, obs_land, pairs, cam_damp):
    f32 = jnp.float32
    count, _, obs = cam_jac.shape
    shard = cam_damp.shape[0]
    n_dev = n_row * n_col
    cams = shard * n_dev // 9
    row_tiles = cams // n_row // LANES
    col_tiles = cams // n_col // LANES
    tiles = row_tiles + col_tiles
    sent = row_tiles + 2 * col_tiles
    vmem = pl.BlockSpec(memory_space=pltpu.VMEM)
    smem = pl.BlockSpec(memory_space=pltpu.SMEM)

    def shape(*dims):
        return pltpu.VMEM(dims, f32)

    radix = min(n_row, 4)
    low = n_row // radix
    lead = [digit * low * n_col for digit in range(1, radix)]
    middle = [x * n_col + y * 2 for x in range(low) for y in range(n_col // 2)]
    middle = middle[:1] + middle[:0:-1]

    def call(kernel, operands, out_shape, scratch=(), whole=(n_row, n_col, cams), specs=None, out_specs=None):
        return pl.pallas_call(
            functools.partial(kernel, *whole),
            out_shape=out_shape,
            in_specs=specs or [vmem] * len(operands),
            out_specs=out_specs or jax.tree.map(lambda _: vmem, out_shape),
            scratch_shapes=scratch,
        )(*operands)

    def all_reduce(part):
        vectors = part.shape[0]
        pieces = [part] + exchange(part, lead, n_dev)
        to_send = call(
            spread_kernel,
            tuple(map(in_vmem, pieces)),
            (shape(vectors, packed(sent), 8, LANES),) * len(middle),
            (pltpu.VMEM((vectors, cams // LANES, 8, LANES), f32), pltpu.VMEM((vectors, cams // LANES, LANES), f32)),
            (n_row, n_col, cams, radix, tuple(middle)),
        )
        got = [to_send[0]] + [exchange(x, [mask], n_dev)[0] for x, mask in zip(to_send[1:], middle[1:])]
        mine, other = call(pair_kernel, tuple(map(in_vmem, got)), (shape(vectors, packed(tiles), 8, LANES),) * 2)
        return in_vmem(mine), in_vmem(exchange(other, [1], n_dev)[0])

    hot = pltpu.VMEM((count, obs, LANES), jnp.bfloat16)
    part, jac, cam_hot, land_hot, index, m, fac, damp_tile, select, spots = call(
        build_kernel,
        (
            pairs.T,
            jnp.transpose(cam_jac, (1, 0, 2)),
            jnp.transpose(land_jac, (1, 0, 2)),
            resid,
            obs_cam,
            obs_land,
            cam_damp,
        ),
        (
            shape(2, packed(tiles), 8, LANES),
            shape(count, 2, 16, obs),
            hot,
            hot,
            pltpu.VMEM((2, count, obs), jnp.int32),
            shape(count, 8, obs),
            shape(count, 16, LM),
            shape(16, LANES),
            pltpu.VMEM((shard, LANES), jnp.bfloat16),
            pltpu.SMEM((4, count), jnp.int32),
        ),
        specs=[smem] + [vmem] * 6,
        out_specs=(vmem,) * 9 + (smem,),
    )
    sums = all_reduce(part)
    jac, cam_hot, land_hot, index, m, fac, damp_tile, select = map(
        in_vmem, (jac, cam_hot, land_hot, index, m, fac, damp_tile, select)
    )
    spots = pltpu.with_memory_space_constraint(spots, pltpu.SMEM)
    vector = pltpu.VMEM((packed(tiles), 8, LANES), f32)
    part, back = call(
        first_kernel,
        (spots, *sums, jac, cam_hot, land_hot, index, m, fac, damp_tile),
        (shape(1, packed(tiles), 8, LANES), shape(2, 3, count, LM)),
        (vector, vector),
        specs=[smem] + [vmem] * 9,
    )
    image = all_reduce(part)
    partial, known, cam_flat, solved = call(
        second_kernel,
        (spots, *sums, *image, jac, land_hot, index, m, fac, damp_tile, select),
        (shape(n_dev, 1, LANES), shape(8, LANES), shape(2, shard), shape(3, count, LM)),
        (vector, pltpu.VMEM((3, packed(tiles), 8, LANES), f32)),
        specs=[smem] + [vmem] * 11,
    )
    gathered = lax.all_to_all(partial, AXES, 0, 0, tiled=True)
    cam_step, land_step = call(
        last_kernel,
        tuple(map(in_vmem, (gathered, known, cam_flat, back, solved))),
        (jax.ShapeDtypeStruct((shard,), f32), jax.ShapeDtypeStruct((3, count, LM), f32)),
        whole=(),
    )
    return cam_step, jnp.transpose(land_step, (1, 0, 2))


def solution(mesh):
    n_row, n_col = mesh.shape["row"], mesh.shape["col"]
    both = P(AXES)
    in_specs = (P(AXES, None, None),) * 3 + (P(AXES, None),) * 3 + (both,)
    out_specs = (both, P(AXES, None, None))
    return jax.shard_map(
        functools.partial(per_device, n_row, n_col),
        mesh=mesh,
        in_specs=in_specs,
        out_specs=out_specs,
        check_vma=False,
    )
```

time: 54.7 us -> 51.4 us (0.940)
  waiting for transfers between devices: 19 us -> 16.5 us
  Pallas kernels: 7.12 us -> 5.31 us
  blocking collectives: 10.1 us -> 11.2 us
    ppermute x14, waiting for transfers between devices: 19 us -> 16.5 us  [exchange(): lax.ppermute(x, AXES, [(i, i ^ mask) for i in range(n_dev)])]
    pallas_call x6 -> x8, Pallas kernels: 7.12 us -> 5.31 us  [call(): pl.pallas_call(functools.partial(kernel, *whole), out_shape=out_shape, in...]
    all_to_all x1, blocking collectives: 10.1 us -> 11.2 us  [per_device(): gathered = lax.all_to_all(partial, AXES, 0, 0, tiled=True)]
where the time goes in v5:
time: 51.4 us; the launch traced here: 51.2 us
  starting transfers between devices  17.5 us (34%)
  waiting for transfers between devices  16.5 us (32%)
  blocking collectives  11.2 us (22%)
  Pallas kernels  5.31 us (10%)
  between operations  0.7 us (1%)
    ppermute x14, starting transfers between devices, exchange(): lax.ppermute(x, AXES, [(i, i ^ mask) for i in range(n_dev)])  17.5 us
    ppermute x14, waiting for transfers between devices, exchange(): lax.ppermute(x, AXES, [(i, i ^ mask) for i in range(n_dev)])  16.5 us
    all_to_all x1, blocking collectives, per_device(): gathered = lax.all_to_all(partial, AXES, 0, 0, tiled=True)  11.2 us
    pallas_call x8, Pallas kernels, call(): pl.pallas_call(functools.partial(kernel, *whole), out_shape=out_shape, in...  5.31 us
  transfers between devices with their start and end apart: 14, of which 12 were waited for; matrix products, arithmetic and copies ran while one was open for 0% of the time, Pallas kernels for 0%

profile of v5, /device:TPU:0, one launch (start us, length us, event | category | flops | bytes accessed | tf_op | source)
XLA Modules:
  0.0 51.2 jit_solution(4250781629337860038)
XLA Ops:
  0.6 2.9 %shard_map.86 = (f32[2,7,8,128]{3,2,1,0:T(8,128)S(1)}, f32[4,2,16,512]{3,2,1,0:T(8,128)S(1)}, bf16[4,512,128]{2,1,0:T(8,128)(2,1)S(1)}, bf16[4,512,128]{2,1,0:T(...) custom-call(s32[2,4]{1,0:T(2,128)} %bitcast.6, ...), custom_call_target="tpu_custom_call" | custom-call | tf_op jit(solution)/shard_map/pallas_call | solution.py:466
  3.6 5.1 %collective-permute-start.2 = (f32[2,7,8,128]{3,2,1,0:T(8,128)S(1)}, f32[2,7,8,128]{3,2,1,0:T(8,128)S(1)}, u32[]{:S(2)}, u32[]{:S(2)}) collective-permute-start(f32[2,7,8,128]{3,2,1,0:T(8,128)S(1)} %get-tuple-element.33.refs_0_), channel_id=1, source_target_pairs={{0,24},{1,25},{2,26},{3,27},{4,28},{5,29},{6,30},{7,31},{8,16},{9,... | collective-permute-start | bytes 172040 | tf_op jit(solution)/shard_map/ppermute | solution.py:436
  8.7 0.6 %collective-permute-start = (f32[2,7,8,128]{3,2,1,0:T(8,128)S(1)}, f32[2,7,8,128]{3,2,1,0:T(8,128)S(1)}, u32[]{:S(2)}, u32[]{:S(2)}) collective-permute-start(f32[2,7,8,128]{3,2,1,0:T(8,128)S(1)} %get-tuple-element.33.refs_0_), channel_id=1, source_target_pairs={{0,8},{1,9},{2,10},{3,11},{4,12},{5,13},{6,14},{7,15},{8,0},{9,1},... | collective-permute-start | bytes 172040 | tf_op jit(solution)/shard_map/ppermute | solution.py:436
  9.3 1.8 %collective-permute-done.2.refs_3_ = f32[2,7,8,128]{3,2,1,0:T(8,128)S(1)} collective-permute-done((f32[2,7,8,128]{3,2,1,0:T(8,128)S(1)}, f32[2,7,8,128]{3,2,1,0:T(8,128)S(1)}, u32[]{:S(2)}, u32[]{:S(2)}) %collective-permute-start.2) | collective-permute-done | bytes 57376 | tf_op jit(solution)/shard_map/ppermute | solution.py:436
  11.1 2.7 %collective-permute-done.1.refs_2_ = f32[2,7,8,128]{3,2,1,0:T(8,128)S(1)} collective-permute-done((f32[2,7,8,128]{3,2,1,0:T(8,128)S(1)}, f32[2,7,8,128]{3,2,1,0:T(8,128)S(1)}, u32[]{:S(2)}, u32[]{:S(2)}) %collective-permute-start.1) | collective-permute-done | bytes 57376 | tf_op jit(solution)/shard_map/ppermute | solution.py:436
  13.9 2.5 %collective-permute-start.3 = (f32[2,12,8,128]{3,2,1,0:T(8,128)S(1)}, f32[2,12,8,128]{3,2,1,0:T(8,128)S(1)}, u32[]{:S(2)}, u32[]{:S(2)}) collective-permute-start(f32[2,12,8,128]{3,2,1,0:T(8,128)S(1)} %get-tuple-element.35), channel_id=1, source_target_pairs={{0,6},{1,7},{2,4},{3,5},{4,2},{5,3},{6,0},{7,1},{8,14},{9,15},{10,... | collective-permute-start | bytes 294920 | tf_op jit(solution)/shard_map/ppermute | solution.py:436
  17.4 2.6 %collective-permute-done.3.refs_1_ = f32[2,12,8,128]{3,2,1,0:T(8,128)S(1)} collective-permute-done((f32[2,12,8,128]{3,2,1,0:T(8,128)S(1)}, f32[2,12,8,128]{3,2,1,0:T(8,128)S(1)}, u32[]{:S(2)}, u32[]{:S(2)}) %collective-permute-start.3) | collective-permute-done | bytes 98336 | tf_op jit(solution)/shard_map/ppermute | solution.py:436
  20.0 1.1 %collective-permute-done.4.refs_2_ = f32[2,12,8,128]{3,2,1,0:T(8,128)S(1)} collective-permute-done((f32[2,12,8,128]{3,2,1,0:T(8,128)S(1)}, f32[2,12,8,128]{3,2,1,0:T(8,128)S(1)}, u32[]{:S(2)}, u32[]{:S(2)}) %collective-permute-start.4) | collective-permute-done | bytes 98336 | tf_op jit(solution)/shard_map/ppermute | solution.py:436
  21.7 1.2 %collective-permute-done.6.other_ref = f32[2,7,8,128]{3,2,1,0:T(8,128)S(1)} collective-permute-done((f32[2,7,8,128]{3,2,1,0:T(8,128)S(1)}, f32[2,7,8,128]{3,2,1,0:T(8,128)S(1)}, u32[]{:S(2)}, u32[]{:S(2)}) %collective-permute-start.6) | collective-permute-done | bytes 57376 | tf_op jit(solution)/shard_map/ppermute | solution.py:436
  22.9 0.7 %shard_map.89 = (f32[1,7,8,128]{3,2,1,0:T(8,128)S(1)}, f32[2,3,4,128]{3,2,1,0:T(4,128)S(1)}) custom-call(s32[4,4]{1,0:T(4,128)S(4)} %get-tuple-element.32.spots_ref, f32[2,7,8,128]{3,2,1,0:T(8,128)S(1)} %get-tuple-element.38.mine_ref, f32[2,7,8,128]{3,2,1,0:T(8,128)S(1)} %collective-permute-done.6.other_ref, ...), custom_call_target="tpu_custom_call" | custom-call | tf_op jit(solution)/shard_map/pallas_call | solution.py:466
  23.6 2.7 %collective-permute-start.9 = (f32[1,7,8,128]{3,2,1,0:T(8,128)S(1)}, f32[1,7,8,128]{3,2,1,0:T(8,128)S(1)}, u32[]{:S(2)}, u32[]{:S(2)}) collective-permute-start(f32[1,7,8,128]{3,2,1,0:T(8,128)S(1)} %get-tuple-element.47.refs_0_), channel_id=1, source_target_pairs={{0,24},{1,25},{2,26},{3,27},{4,28},{5,29},{6,30},{7,31},{8,16},{9,... | collective-permute-start | bytes 86024 | tf_op jit(solution)/shard_map/ppermute | solution.py:436
  26.3 1.8 %collective-permute-start.7 = (f32[1,7,8,128]{3,2,1,0:T(8,128)S(1)}, f32[1,7,8,128]{3,2,1,0:T(8,128)S(1)}, u32[]{:S(2)}, u32[]{:S(2)}) collective-permute-start(f32[1,7,8,128]{3,2,1,0:T(8,128)S(1)} %get-tuple-element.47.refs_0_), channel_id=1, source_target_pairs={{0,8},{1,9},{2,10},{3,11},{4,12},{5,13},{6,14},{7,15},{8,0},{9,1},... | collective-permute-start | bytes 86024 | tf_op jit(solution)/shard_map/ppermute | solution.py:436
  28.1 1.6 %collective-permute-done.9.refs_3_ = f32[1,7,8,128]{3,2,1,0:T(8,128)S(1)} collective-permute-done((f32[1,7,8,128]{3,2,1,0:T(8,128)S(1)}, f32[1,7,8,128]{3,2,1,0:T(8,128)S(1)}, u32[]{:S(2)}, u32[]{:S(2)}) %collective-permute-start.9) | collective-permute-done | bytes 28704 | tf_op jit(solution)/shard_map/ppermute | solution.py:436
  29.7 1.4 %collective-permute-done.8.refs_2_ = f32[1,7,8,128]{3,2,1,0:T(8,128)S(1)} collective-permute-done((f32[1,7,8,128]{3,2,1,0:T(8,128)S(1)}, f32[1,7,8,128]{3,2,1,0:T(8,128)S(1)}, u32[]{:S(2)}, u32[]{:S(2)}) %collective-permute-start.8) | collective-permute-done | bytes 28704 | tf_op jit(solution)/shard_map/ppermute | solution.py:436
  31.1 1.5 %collective-permute-start.10 = (f32[1,12,8,128]{3,2,1,0:T(8,128)S(1)}, f32[1,12,8,128]{3,2,1,0:T(8,128)S(1)}, u32[]{:S(2)}, u32[]{:S(2)}) collective-permute-start(f32[1,12,8,128]{3,2,1,0:T(8,128)S(1)} %get-tuple-element.49), channel_id=1, source_target_pairs={{0,6},{1,7},{2,4},{3,5},{4,2},{5,3},{6,0},{7,1},{8,14},{9,15},{10,... | collective-permute-start | bytes 147464 | tf_op jit(solution)/shard_map/ppermute | solution.py:436
  32.6 0.5 %collective-permute-start.11 = (f32[1,12,8,128]{3,2,1,0:T(8,128)S(1)}, f32[1,12,8,128]{3,2,1,0:T(8,128)S(1)}, u32[]{:S(2)}, u32[]{:S(2)}) collective-permute-start(f32[1,12,8,128]{3,2,1,0:T(8,128)S(1)} %get-tuple-element.50), channel_id=1, source_target_pairs={{0,4},{1,5},{2,6},{3,7},{4,0},{5,1},{6,2},{7,3},{8,12},{9,13},{10,... | collective-permute-start | bytes 147464 | tf_op jit(solution)/shard_map/ppermute | solution.py:436
  33.2 1.5 %collective-permute-start.12 = (f32[1,12,8,128]{3,2,1,0:T(8,128)S(1)}, f32[1,12,8,128]{3,2,1,0:T(8,128)S(1)}, u32[]{:S(2)}, u32[]{:S(2)}) collective-permute-start(f32[1,12,8,128]{3,2,1,0:T(8,128)S(1)} %get-tuple-element.51), channel_id=1, source_target_pairs={{0,2},{1,3},{2,0},{3,1},{4,6},{5,7},{6,4},{7,5},{8,10},{9,11},{10,... | collective-permute-start | bytes 147464 | tf_op jit(solution)/shard_map/ppermute | solution.py:436
  34.7 1.5 %collective-permute-done.10.refs_1_ = f32[1,12,8,128]{3,2,1,0:T(8,128)S(1)} collective-permute-done((f32[1,12,8,128]{3,2,1,0:T(8,128)S(1)}, f32[1,12,8,128]{3,2,1,0:T(8,128)S(1)}, u32[]{:S(2)}, u32[]{:S(2)}) %collective-permute-start.10) | collective-permute-done | bytes 49184 | tf_op jit(solution)/shard_map/ppermute | solution.py:436
  36.2 0.5 %collective-permute-done.11.refs_2_ = f32[1,12,8,128]{3,2,1,0:T(8,128)S(1)} collective-permute-done((f32[1,12,8,128]{3,2,1,0:T(8,128)S(1)}, f32[1,12,8,128]{3,2,1,0:T(8,128)S(1)}, u32[]{:S(2)}, u32[]{:S(2)}) %collective-permute-start.11) | collective-permute-done | bytes 49184 | tf_op jit(solution)/shard_map/ppermute | solution.py:436
  36.7 0.5 %collective-permute-done.12.refs_3_ = f32[1,12,8,128]{3,2,1,0:T(8,128)S(1)} collective-permute-done((f32[1,12,8,128]{3,2,1,0:T(8,128)S(1)}, f32[1,12,8,128]{3,2,1,0:T(8,128)S(1)}, u32[]{:S(2)}, u32[]{:S(2)}) %collective-permute-start.12) | collective-permute-done | bytes 49184 | tf_op jit(solution)/shard_map/ppermute | solution.py:436
  37.4 1.2 %collective-permute-done.13.image_other_ref = f32[1,7,8,128]{3,2,1,0:T(8,128)S(1)} collective-permute-done((f32[1,7,8,128]{3,2,1,0:T(8,128)S(1)}, f32[1,7,8,128]{3,2,1,0:T(8,128)S(1)}, u32[]{:S(2)}, u32[]{:S(2)}) %collective-permute-start.13) | collective-permute-done | bytes 28704 | tf_op jit(solution)/shard_map/ppermute | solution.py:436
  38.5 0.7 %shard_map.92 = (f32[32,1,128]{2,1,0:T(1,128)S(1)}, f32[8,128]{1,0:T(8,128)S(1)}, f32[2,576]{1,0:T(2,128)S(1)}, f32[3,4,128]{2,1,0:T(4,128)S(1)}) custom-call(s32[4,4]{1,0:T(4,128)S(4)} %get-tuple-element.32.spots_ref, f32[2,7,8,128]{3,2,1,0:T(8,128)S(1)} %get-tuple-element.38.mine_ref, f32[2,7,8,128]{3,2,1,0:T(8,128)S(1)} %collective-permute-done.6.other_ref, ...), custom_call_target="tpu_custom_call" | custom-call | tf_op jit(solution)/shard_map/pallas_call | solution.py:466
  39.3 11.2 %all_to_all.5.sums_ref = f32[32,1,128]{2,1,0:T(1,128)S(1)} all-to-all(f32[32,1,128]{2,1,0:T(1,128)S(1)} %get-tuple-element.55), channel_id=1, replica_groups=mesh['row'=8,'col'=4] {'row','col'}, dimensions={0} | all-to-all | bytes 32768 | tf_op jit(solution)/shard_map/all_to_all | solution.py:536
  50.5 0.7 %shard_map.93 = (f32[576]{0:T(1024)}, f32[3,4,128]{2,1,0:T(4,128)}) custom-call(f32[32,1,128]{2,1,0:T(1,128)S(1)} %all_to_all.5.sums_ref, f32[8,128]{1,0:T(8,128)S(1)} %get-tuple-element.56.known_ref, f32[2,576]{1,0:T(2,128)S(1)} %get-tuple-element.57.cam_ref, f32[2,3,4,128]{3,2,1,0:T(4,128)S(1)} %get-tuple-element.58.back_ref, ...), custom_call_target="tpu_custom_call" | custom-call | tf_op jit(solution)/shard_map/pallas_call | solution.py:466
  (13 shorter events, 1.8 us)
Async XLA Ops:
  3.6 7.5 %collective-permute-start.2 = (f32[2,7,8,128]{3,2,1,0:T(8,128)S(1)}, f32[2,7,8,128]{3,2,1,0:T(8,128)S(1)}, u32[]{:S(2)}, u32[]{:S(2)}) collective-permute-start(f32[2,7,8,128]{3,2,1,0:T(8,128)S(1)} %get-tuple-element.33.refs_0_), channel_id=1, source_target_pairs={{0,24},{1,25},{2,26},{3,27},{4,28},{5,29},{6,30},{7,31},{8,16},{9,... | collective-permute-start | bytes 172040 | tf_op jit(solution)/shard_map/ppermute | solution.py:436
  8.7 5.1 %collective-permute-start.1 = (f32[2,7,8,128]{3,2,1,0:T(8,128)S(1)}, f32[2,7,8,128]{3,2,1,0:T(8,128)S(1)}, u32[]{:S(2)}, u32[]{:S(2)}) collective-permute-start(f32[2,7,8,128]{3,2,1,0:T(8,128)S(1)} %get-tuple-element.33.refs_0_), channel_id=1, source_target_pairs={{0,16},{1,17},{2,18},{3,19},{4,20},{5,21},{6,22},{7,23},{8,24},{9,... | collective-permute-start | bytes 172040 | tf_op jit(solution)/shard_map/ppermute | solution.py:436
  8.7 5.1 %collective-permute-start = (f32[2,7,8,128]{3,2,1,0:T(8,128)S(1)}, f32[2,7,8,128]{3,2,1,0:T(8,128)S(1)}, u32[]{:S(2)}, u32[]{:S(2)}) collective-permute-start(f32[2,7,8,128]{3,2,1,0:T(8,128)S(1)} %get-tuple-element.33.refs_0_), channel_id=1, source_target_pairs={{0,8},{1,9},{2,10},{3,11},{4,12},{5,13},{6,14},{7,15},{8,0},{9,1},... | collective-permute-start | bytes 172040 | tf_op jit(solution)/shard_map/ppermute | solution.py:436
  13.9 6.1 %collective-permute-start.3 = (f32[2,12,8,128]{3,2,1,0:T(8,128)S(1)}, f32[2,12,8,128]{3,2,1,0:T(8,128)S(1)}, u32[]{:S(2)}, u32[]{:S(2)}) collective-permute-start(f32[2,12,8,128]{3,2,1,0:T(8,128)S(1)} %get-tuple-element.35), channel_id=1, source_target_pairs={{0,6},{1,7},{2,4},{3,5},{4,2},{5,3},{6,0},{7,1},{8,14},{9,15},{10,... | collective-permute-start | bytes 294920 | tf_op jit(solution)/shard_map/ppermute | solution.py:436
  16.4 4.7 %collective-permute-start.4 = (f32[2,12,8,128]{3,2,1,0:T(8,128)S(1)}, f32[2,12,8,128]{3,2,1,0:T(8,128)S(1)}, u32[]{:S(2)}, u32[]{:S(2)}) collective-permute-start(f32[2,12,8,128]{3,2,1,0:T(8,128)S(1)} %get-tuple-element.36), channel_id=1, source_target_pairs={{0,4},{1,5},{2,6},{3,7},{4,0},{5,1},{6,2},{7,3},{8,12},{9,13},{10,... | collective-permute-start | bytes 294920 | tf_op jit(solution)/shard_map/ppermute | solution.py:436
  16.9 4.6 %collective-permute-start.5 = (f32[2,12,8,128]{3,2,1,0:T(8,128)S(1)}, f32[2,12,8,128]{3,2,1,0:T(8,128)S(1)}, u32[]{:S(2)}, u32[]{:S(2)}) collective-permute-start(f32[2,12,8,128]{3,2,1,0:T(8,128)S(1)} %get-tuple-element.37), channel_id=1, source_target_pairs={{0,2},{1,3},{2,0},{3,1},{4,6},{5,7},{6,4},{7,5},{8,10},{9,11},{10,... | collective-permute-start | bytes 294920 | tf_op jit(solution)/shard_map/ppermute | solution.py:436
  21.6 1.3 %collective-permute-start.6 = (f32[2,7,8,128]{3,2,1,0:T(8,128)S(1)}, f32[2,7,8,128]{3,2,1,0:T(8,128)S(1)}, u32[]{:S(2)}, u32[]{:S(2)}) collective-permute-start(f32[2,7,8,128]{3,2,1,0:T(8,128)S(1)} %get-tuple-element.39), channel_id=1, source_target_pairs={{0,1},{1,0},{2,3},{3,2},{4,5},{5,4},{6,7},{7,6},{8,9},{9,8},{10,11... | collective-permute-start | bytes 172040 | tf_op jit(solution)/shard_map/ppermute | solution.py:436
  23.6 6.0 %collective-permute-start.9 = (f32[1,7,8,128]{3,2,1,0:T(8,128)S(1)}, f32[1,7,8,128]{3,2,1,0:T(8,128)S(1)}, u32[]{:S(2)}, u32[]{:S(2)}) collective-permute-start(f32[1,7,8,128]{3,2,1,0:T(8,128)S(1)} %get-tuple-element.47.refs_0_), channel_id=1, source_target_pairs={{0,24},{1,25},{2,26},{3,27},{4,28},{5,29},{6,30},{7,31},{8,16},{9,... | collective-permute-start | bytes 86024 | tf_op jit(solution)/shard_map/ppermute | solution.py:436
  26.3 4.8 %collective-permute-start.8 = (f32[1,7,8,128]{3,2,1,0:T(8,128)S(1)}, f32[1,7,8,128]{3,2,1,0:T(8,128)S(1)}, u32[]{:S(2)}, u32[]{:S(2)}) collective-permute-start(f32[1,7,8,128]{3,2,1,0:T(8,128)S(1)} %get-tuple-element.47.refs_0_), channel_id=1, source_target_pairs={{0,16},{1,17},{2,18},{3,19},{4,20},{5,21},{6,22},{7,23},{8,24},{9,... | collective-permute-start | bytes 86024 | tf_op jit(solution)/shard_map/ppermute | solution.py:436
  26.3 4.8 %collective-permute-start.7 = (f32[1,7,8,128]{3,2,1,0:T(8,128)S(1)}, f32[1,7,8,128]{3,2,1,0:T(8,128)S(1)}, u32[]{:S(2)}, u32[]{:S(2)}) collective-permute-start(f32[1,7,8,128]{3,2,1,0:T(8,128)S(1)} %get-tuple-element.47.refs_0_), channel_id=1, source_target_pairs={{0,8},{1,9},{2,10},{3,11},{4,12},{5,13},{6,14},{7,15},{8,0},{9,1},... | collective-permute-start | bytes 86024 | tf_op jit(solution)/shard_map/ppermute | solution.py:436
  31.1 5.1 %collective-permute-start.10 = (f32[1,12,8,128]{3,2,1,0:T(8,128)S(1)}, f32[1,12,8,128]{3,2,1,0:T(8,128)S(1)}, u32[]{:S(2)}, u32[]{:S(2)}) collective-permute-start(f32[1,12,8,128]{3,2,1,0:T(8,128)S(1)} %get-tuple-element.49), channel_id=1, source_target_pairs={{0,6},{1,7},{2,4},{3,5},{4,2},{5,3},{6,0},{7,1},{8,14},{9,15},{10,... | collective-permute-start | bytes 147464 | tf_op jit(solution)/shard_map/ppermute | solution.py:436
  32.6 4.1 %collective-permute-start.11 = (f32[1,12,8,128]{3,2,1,0:T(8,128)S(1)}, f32[1,12,8,128]{3,2,1,0:T(8,128)S(1)}, u32[]{:S(2)}, u32[]{:S(2)}) collective-permute-start(f32[1,12,8,128]{3,2,1,0:T(8,128)S(1)} %get-tuple-element.50), channel_id=1, source_target_pairs={{0,4},{1,5},{2,6},{3,7},{4,0},{5,1},{6,2},{7,3},{8,12},{9,13},{10,... | collective-permute-start | bytes 147464 | tf_op jit(solution)/shard_map/ppermute | solution.py:436
  33.2 4.1 %collective-permute-start.12 = (f32[1,12,8,128]{3,2,1,0:T(8,128)S(1)}, f32[1,12,8,128]{3,2,1,0:T(8,128)S(1)}, u32[]{:S(2)}, u32[]{:S(2)}) collective-permute-start(f32[1,12,8,128]{3,2,1,0:T(8,128)S(1)} %get-tuple-element.51), channel_id=1, source_target_pairs={{0,2},{1,3},{2,0},{3,1},{4,6},{5,7},{6,4},{7,5},{8,10},{9,11},{10,... | collective-permute-start | bytes 147464 | tf_op jit(solution)/shard_map/ppermute | solution.py:436
  37.3 1.3 %collective-permute-start.13 = (f32[1,7,8,128]{3,2,1,0:T(8,128)S(1)}, f32[1,7,8,128]{3,2,1,0:T(8,128)S(1)}, u32[]{:S(2)}, u32[]{:S(2)}) collective-permute-start(f32[1,7,8,128]{3,2,1,0:T(8,128)S(1)} %get-tuple-element.53), channel_id=1, source_target_pairs={{0,1},{1,0},{2,3},{3,2},{4,5},{5,4},{6,7},{7,6},{8,9},{9,8},{10,11... | collective-permute-start | bytes 86024 | tf_op jit(solution)/shard_map/ppermute | solution.py:436

commit v6 on v5

--- a/solution.py
+++ b/solution.py
@@ -191,6 +191,16 @@
         entries = [outer(0, 0), outer(0, 1), outer(0, 2), outer(1, 1), outer(1, 2), outer(2, 2)]
         entries += [lj[k][b] * e0[k] + lj[k][3 + b] * e1[k] for b in range(3)]
         sums.append(dot3(stack_rows(entries, 16), land_hot_ref[k], NN))
+    alike = []
+    for k in each:
+        for r in range(2):
+            jac_ref[k, r, 0:8, :] = cam_ref[9 * r : 9 * r + 8, k, :]
+            jac_ref[k, r, 8:16, :] = pad_rows(cam_ref[9 * r + 8 : 9 * r + 9, k, :], 8)
+        j0, j1 = jac_ref[k, 0], jac_ref[k, 1]
+        coupled = [j0[:8] * lj[k][b] + j1[:8] * lj[k][3 + b] for b in range(3)]
+        coupled.append(stack_rows([j0[8:9] * lj[k][b] + j1[8:9] * lj[k][3 + b] for b in range(3)], 8))
+        same = onehot((cam_columns[k] * LM + land_columns[k]).astype(jnp.int16), key[k : k + 1, :])
+        alike.append(dot3(jnp.concatenate(coupled, axis=0), same, NN))
     total = [jnp.concatenate([sums[k][i : i + 1] for k in each], axis=0) for i in range(9)]
     factor = cholesky_three(
         total[0] + DAMPING, total[1], total[2], total[3] + DAMPING, total[4], total[5] + DAMPING
@@ -198,8 +208,6 @@
     land_rows = list(factor) + list(lower_solve(factor, total[6], total[7], total[8]))
     for k in each:
         cam_hot_ref[k] = onehot(cam_columns[k].astype(jnp.int16), lanes)
-        jac_ref[k, 0] = pad_rows(cam_ref[0:9, k, :], 16)
-        jac_ref[k, 1] = pad_rows(cam_ref[9:18, k, :], 16)
     ms, ws = [], []
     for k in each:
         land_values = stack_rows([row[k : k + 1] for row in land_rows], 16)
@@ -208,18 +216,22 @@
         m0 = lower_solve(at_obs, lj[k][0], lj[k][1], lj[k][2])
         m1 = lower_solve(at_obs, lj[k][3], lj[k][4], lj[k][5])
         m_ref[k] = stack_rows(m0 + m1, 8)
-        ms.append((m0, m1))
+        ms.append((at_obs, m0, m1))
         w0 = m0[0] * at_obs[6] + m0[1] * at_obs[7] + m0[2] * at_obs[8] - e0[k]
         w1 = m1[0] * at_obs[6] + m1[1] * at_obs[7] + m1[2] * at_obs[8] - e1[k]
         ws.append((w0, w1))
     both = []
     for k in each:
         j0, j1 = jac_ref[k, 0], jac_ref[k, 1]
-        m0, m1 = ms[k]
-        coupled = jnp.concatenate([j0 * m0[b] + j1 * m1[b] for b in range(3)], axis=0)
-        same = onehot((cam_columns[k] * LM + land_columns[k]).astype(jnp.int16), key[k : k + 1, :])
-        prod = coupled * dot3(coupled, same, NN)
-        diag = j0 * j0 + j1 * j1 - (prod[0:16] + prod[16:32] + prod[32:48])
+        at_obs, m0, m1 = ms[k]
+        squares = []
+        for jr0, jr1, products in (
+            (j0[:8], j1[:8], [alike[k][8 * b : 8 * b + 8] for b in range(3)]),
+            (j0[8:9], j1[8:9], [alike[k][24 + b : 25 + b] for b in range(3)]),
+        ):
+            solved = lower_solve(at_obs, *products)
+            squares.append(sum((jr0 * m0[b] + jr1 * m1[b]) * solved[b] for b in range(3)))
+        diag = j0 * j0 + j1 * j1 - jnp.concatenate([squares[0], pad_rows(squares[1], 8)], axis=0)
         rhs = j0 * ws[k][0] + j1 * ws[k][1]
         both.append(dot3(jnp.concatenate([rhs, diag], axis=0), cam_hot_ref[k], NN))
 
@@ -288,13 +300,23 @@
     return total_sum(sum(u[k][r] * v[k][r] for k in range(len(u)) for r in range(2)))
 
 
-def first_kernel(n_row, n_col, cams, spots_ref, mine_ref, other_ref, jac_ref, cam_hot_ref, land_hot_ref, index_ref, m_ref, fac_ref, damp_tile_ref, part_ref, back_ref, p_ref, right_ref):
+def add_up(refs):
+    total = refs[0][...]
+    for ref in refs[1:]:
+        total = total + ref[...]
+    return total
+
+
+def first_kernel(n_row, n_col, cams, pieces, spots_ref, jac_ref, cam_hot_ref, land_hot_ref, index_ref, m_ref, fac_ref, damp_tile_ref, *refs):
+    part_ref, back_ref, right_ref, precond_ref, p_ref = refs[pieces:]
     row_tiles = cams // n_row // LANES
     tiles = row_tiles + cams // n_col // LANES
     each = range(jac_ref.shape[0])
-    right = mine_ref[0] + other_ref[0]
+    sums = add_up(refs[:pieces])
+    right, precond = sums[0], 1.0 / sums[1]
     right_ref[...] = right
-    p_ref[...] = right * (1.0 / (mine_ref[1] + other_ref[1]))
+    precond_ref[...] = precond
+    p_ref[...] = right * precond
     spots = read_spots(spots_ref)
     u, m, y_land = half_product(p_ref, row_tiles, tiles, spots, jac_ref, land_hot_ref, index_ref, m_ref)
     v = reduced_rows(u, m, y_land, index_ref)
@@ -314,19 +336,19 @@
     write_parts(part_ref.at[0], row_tiles, tiles, spots, images, (own_tile, damped), in_lanes([norm_now, energy]))
 
 
-def second_kernel(n_row, n_col, cams, spots_ref, mine_ref, other_ref, image_mine_ref, image_other_ref, jac_ref, land_hot_ref, index_ref, m_ref, fac_ref, damp_tile_ref, select_ref, sums_ref, known_ref, cam_ref, solved_ref, p_ref, scratch_ref):
+def second_kernel(n_row, n_col, cams, pieces, spots_ref, jac_ref, land_hot_ref, index_ref, m_ref, fac_ref, damp_tile_ref, select_ref, right_ref, precond_ref, *refs):
+    sums_ref, known_ref, cam_ref, solved_ref, p_ref, scratch_ref = refs[pieces:]
     row_tiles = cams // n_row // LANES
     tiles = row_tiles + cams // n_col // LANES
     each = range(jac_ref.shape[0])
     shard = cam_ref.shape[1]
-    image = image_mine_ref[0] + image_other_ref[0]
+    image = add_up(refs[:pieces])[0]
     sums = image[tiles + tiles // 8, tiles % 8 : tiles % 8 + 1]
     norm_now, energy_now = sums[:, 0:1], sums[:, 1:2]
     alpha = norm_now / energy_now
     for i, value in enumerate((1.0 / norm_now, energy_now, alpha)):
         known_ref[i : i + 1, :] = jnp.broadcast_to(value, (1, LANES))
-    right = mine_ref[0] + other_ref[0]
-    precond = 1.0 / (mine_ref[1] + other_ref[1])
+    right, precond = right_ref[...], precond_ref[...]
     residual = right - alpha * image
     p_ref[...] = precond * residual
     scratch_ref[0] = right * precond
@@ -369,66 +391,62 @@
     land_out_ref[...] = -(back_ref[0] + first[None] * back_ref[1] + slope[None] * solved_ref[...])
 
 
-def spread_kernel(n_row, n_col, cams, radix, masks, *refs):
+def core_kernel(n_row, n_col, cams, radix, *refs):
     part_refs, out_refs, (whole_ref, ninth_ref) = refs[:radix], refs[radix:-2], refs[-2:]
     row_tiles = cams // n_row // LANES
     col_tiles = cams // n_col // LANES
     tiles = row_tiles + col_tiles
-    sent = row_tiles + 2 * col_tiles
+    low = n_row // radix
     row, col = lax.axis_index("row"), lax.axis_index("col")
     for v in range(whole_ref.shape[0]):
         parts = [ref[v] for ref in part_refs]
-        total = parts[0]
-        for part in parts[1:]:
-            total = total + part
-        sums = total[tiles + tiles // 8, tiles % 8 : tiles % 8 + 1]
+        received = parts[1]
+        for part in parts[2:]:
+            received = received + part
+        row_sums = tiles + tiles // 8, tiles % 8
+        sums = (parts[0] + received)[row_sums[0], row_sums[1] : row_sums[1] + 1]
         whole_ref[v] = jnp.zeros(whole_ref.shape[1:], jnp.float32)
         ninth_ref[v] = jnp.zeros(ninth_ref.shape[1:], jnp.float32)
-        for i in range(col_tiles):
-            t = row_tiles + i
-            whole_ref[v, col * col_tiles + i] = total[t]
-            ninth_ref[v, pl.ds(col * col_tiles + i, 1), :] = total[tiles + t // 8, t % 8 : t % 8 + 1]
+        columns = [(col, parts[0]), (col ^ 1, received)]
+        for column, total in columns:
+            for i in range(col_tiles):
+                t = row_tiles + i
+                whole_ref[v, column * col_tiles + i] = total[t]
+                ninth_ref[v, pl.ds(column * col_tiles + i, 1), :] = total[tiles + t // 8, t % 8 : t % 8 + 1]
         for digit, part in enumerate(parts):
-            start = (row ^ (digit * (n_row // radix))) * row_tiles
+            start = (row ^ (digit * low)) * row_tiles
             for i in range(row_tiles):
                 whole_ref[v, start + i] += part[i]
                 ninth_ref[v, pl.ds(start + i, 1), :] += part[tiles + i // 8, i % 8 : i % 8 + 1]
-        for mask, out_ref in zip(masks, out_refs):
-            col_start = ((col ^ (mask % n_col)) // 2) * (2 * col_tiles)
-            row_start = (row ^ (mask // n_col)) * row_tiles
-            places = [col_start + i for i in range(2 * col_tiles)] + [row_start + i for i in range(row_tiles)]
+        for core, out_ref in zip((col % 2, 1 - col % 2), out_refs):
+            places = [(2 * y + 1 - core) * col_tiles + i for y in range(n_col // 2) for i in range(col_tiles)]
+            places += [(col // 2 * 2 + core) * col_tiles + i for i in range(col_tiles)]
+            places += [row // low * (low * row_tiles) + i for i in range(low * row_tiles)]
             for i, t in enumerate(places):
                 out_ref[v, i] = whole_ref[v, t]
-            write_ninths(out_ref.at[v], sent, [ninth_ref[v, pl.ds(t, 1), :] for t in places], sums)
-
-
-def pair_kernel(n_row, n_col, cams, *refs):
-    in_refs, (mine_ref, other_ref) = refs[:-2], refs[-2:]
+            write_ninths(out_ref.at[v], len(places), [ninth_ref[v, pl.ds(t, 1), :] for t in places], sums)
+
+
+def spread_kernel(n_row, n_col, cams, radix, masks, mine_ref, other_ref, *refs):
+    out_refs, total_ref = refs[:-1], refs[-1]
     row_tiles = cams // n_row // LANES
     col_tiles = cams // n_col // LANES
     tiles = row_tiles + col_tiles
-    sent = row_tiles + 2 * col_tiles
-    core = lax.axis_index("col") % 2
-    for v in range(mine_ref.shape[0]):
-        total = in_refs[0][v]
-        for ref in in_refs[1:]:
-            total = total + ref[v]
-
-        def ninth(i):
-            return total[sent + i // 8, i % 8 : i % 8 + 1]
-
-        sums = ninth(sent)
-        rows = range(2 * col_tiles, sent)
-        lower = [(total[i], ninth(i)) for i in range(col_tiles)]
-        upper = [(total[i], ninth(i)) for i in range(col_tiles, 2 * col_tiles)]
-        for out_ref, first in ((mine_ref, core == 0), (other_ref, core == 1)):
-            ninths = []
-            for i, t in enumerate(rows):
-                out_ref[v, i] = total[t]
-                ninths.append(ninth(t))
-            for i in range(col_tiles):
-                out_ref[v, row_tiles + i] = jnp.where(first, lower[i][0], upper[i][0])
-                ninths.append(jnp.where(first, lower[i][1], upper[i][1]))
+    low = n_row // radix
+    col_sent = n_col // 2 * col_tiles
+    sent = col_sent + col_tiles + low * row_tiles
+    row, col = lax.axis_index("row") % low, lax.axis_index("col") // 2
+    for v in range(total_ref.shape[0]):
+        total = mine_ref[v] + other_ref[v]
+        total_ref[v] = total
+        sums = total[sent + sent // 8, sent % 8 : sent % 8 + 1]
+        for mask, out_ref in zip(masks, out_refs):
+            row_start = col_sent + col_tiles + (row ^ (mask // n_col)) * row_tiles
+            col_start = (col ^ (mask % n_col // 2)) * col_tiles if mask else col_sent
+            places = [row_start + i for i in range(row_tiles)] + [col_start + i for i in range(col_tiles)]
+            for i, t in enumerate(places):
+                out_ref[v, i] = total_ref[v, t]
+            ninths = [total_ref[v, sent + t // 8, pl.ds(t % 8, 1), :] for t in places]
             write_ninths(out_ref.at[v], tiles, ninths, sums)
 
 
@@ -449,7 +467,6 @@
     row_tiles = cams // n_row // LANES
     col_tiles = cams // n_col // LANES
     tiles = row_tiles + col_tiles
-    sent = row_tiles + 2 * col_tiles
     vmem = pl.BlockSpec(memory_space=pltpu.VMEM)
     smem = pl.BlockSpec(memory_space=pltpu.SMEM)
 
@@ -458,9 +475,10 @@
 
     radix = min(n_row, 4)
     low = n_row // radix
-    lead = [digit * low * n_col for digit in range(1, radix)]
+    sent = n_col // 2 * col_tiles + col_tiles + low * row_tiles
+    lead = [digit * low * n_col + 1 for digit in range(1, radix)]
     middle = [x * n_col + y * 2 for x in range(low) for y in range(n_col // 2)]
-    middle = middle[:1] + middle[:0:-1]
+    middle = middle[:1] + [mask + 1 for mask in middle[:0:-1]]
 
     def call(kernel, operands, out_shape, scratch=(), whole=(n_row, n_col, cams), specs=None, out_specs=None):
         return pl.pallas_call(
@@ -474,16 +492,23 @@
     def all_reduce(part):
         vectors = part.shape[0]
         pieces = [part] + exchange(part, lead, n_dev)
+        mine, other = call(
+            core_kernel,
+            tuple(map(in_vmem, pieces)),
+            (shape(vectors, packed(sent), 8, LANES),) * 2,
+            (pltpu.VMEM((vectors, cams // LANES, 8, LANES), f32), pltpu.VMEM((vectors, cams // LANES, LANES), f32)),
+            (n_row, n_col, cams, radix),
+        )
+        (other,) = exchange(other, [1], n_dev)
         to_send = call(
             spread_kernel,
-            tuple(map(in_vmem, pieces)),
-            (shape(vectors, packed(sent), 8, LANES),) * len(middle),
-            (pltpu.VMEM((vectors, cams // LANES, 8, LANES), f32), pltpu.VMEM((vectors, cams // LANES, LANES), f32)),
+            (in_vmem(mine), in_vmem(other)),
+            (shape(vectors, packed(tiles), 8, LANES),) * len(middle),
+            (pltpu.VMEM((vectors, packed(sent), 8, LANES), f32),),
             (n_row, n_col, cams, radix, tuple(middle)),
         )
         got = [to_send[0]] + [exchange(x, [mask], n_dev)[0] for x, mask in zip(to_send[1:], middle[1:])]
-        mine, other = call(pair_kernel, tuple(map(in_vmem, got)), (shape(vectors, packed(tiles), 8, LANES),) * 2)
-        return in_vmem(mine), in_vmem(exchange(other, [1], n_dev)[0])
+        return tuple(map(in_vmem, got))
 
     hot = pltpu.VMEM((count, obs, LANES), jnp.bfloat16)
     part, jac, cam_hot, land_hot, index, m, fac, damp_tile, select, spots = call(
@@ -517,21 +542,24 @@
         in_vmem, (jac, cam_hot, land_hot, index, m, fac, damp_tile, select)
     )
     spots = pltpu.with_memory_space_constraint(spots, pltpu.SMEM)
+    pieces = len(middle)
     vector = pltpu.VMEM((packed(tiles), 8, LANES), f32)
-    part, back = call(
+    part, back, right, precond = call(
         first_kernel,
-        (spots, *sums, jac, cam_hot, land_hot, index, m, fac, damp_tile),
-        (shape(1, packed(tiles), 8, LANES), shape(2, 3, count, LM)),
-        (vector, vector),
-        specs=[smem] + [vmem] * 9,
+        (spots, jac, cam_hot, land_hot, index, m, fac, damp_tile, *sums),
+        (shape(1, packed(tiles), 8, LANES), shape(2, 3, count, LM), vector, vector),
+        (vector,),
+        (n_row, n_col, cams, pieces),
+        specs=[smem] + [vmem] * (7 + pieces),
     )
     image = all_reduce(part)
     partial, known, cam_flat, solved = call(
         second_kernel,
-        (spots, *sums, *image, jac, land_hot, index, m, fac, damp_tile, select),
+        (spots, jac, land_hot, index, m, fac, damp_tile, select, in_vmem(right), in_vmem(precond), *image),
         (shape(n_dev, 1, LANES), shape(8, LANES), shape(2, shard), shape(3, count, LM)),
         (vector, pltpu.VMEM((3, packed(tiles), 8, LANES), f32)),
-        specs=[smem] + [vmem] * 11,
+        (n_row, n_col, cams, pieces),
+        specs=[smem] + [vmem] * (9 + pieces),
     )
     gathered = lax.all_to_all(partial, AXES, 0, 0, tiled=True)
     cam_step, land_step = call(

time: 51.4 us -> 48.8 us (0.949)
  starting transfers between devices: 17.5 us -> 16 us
  blocking collectives: 11.2 us -> 10.6 us
    ppermute x14, starting transfers between devices: 17.5 us -> 16 us  [exchange(): lax.ppermute(x, AXES, [(i, i ^ mask) for i in range(n_dev)])]
    all_to_all x1, blocking collectives: 11.2 us -> 10.6 us  [per_device(): gathered = lax.all_to_all(partial, AXES, 0, 0, tiled=True)]
where the time goes in v6:
time: 48.8 us; the launch traced here: 48.6 us
  waiting for transfers between devices  16.4 us (34%)
  starting transfers between devices  16 us (33%)
  blocking collectives  10.6 us (22%)
  Pallas kernels  5 us (10%)
  between operations  0.68 us (1%)
    ppermute x14, waiting for transfers between devices, exchange(): lax.ppermute(x, AXES, [(i, i ^ mask) for i in range(n_dev)])  16.4 us
    ppermute x14, starting transfers between devices, exchange(): lax.ppermute(x, AXES, [(i, i ^ mask) for i in range(n_dev)])  16 us
    all_to_all x1, blocking collectives, per_device(): gathered = lax.all_to_all(partial, AXES, 0, 0, tiled=True)  10.6 us
    pallas_call x8, Pallas kernels, call(): pl.pallas_call(functools.partial(kernel, *whole), out_shape=out_shape, in...  5 us
  transfers between devices with their start and end apart: 14, of which 12 were waited for; matrix products, arithmetic and copies ran while one was open for 0% of the time, Pallas kernels for 0%

profile of v6, /device:TPU:0, one launch (start us, length us, event | category | flops | bytes accessed | tf_op | source)
XLA Modules:
  0.0 48.6 jit_solution(1306117675749509920)
XLA Ops:
  0.6 2.4 %shard_map.86 = (f32[2,7,8,128]{3,2,1,0:T(8,128)S(1)}, f32[4,2,16,512]{3,2,1,0:T(8,128)S(1)}, bf16[4,512,128]{2,1,0:T(8,128)(2,1)S(1)}, bf16[4,512,128]{2,1,0:T(...) custom-call(s32[2,4]{1,0:T(2,128)} %bitcast.6, ...), custom_call_target="tpu_custom_call" | custom-call | tf_op jit(solution)/shard_map/pallas_call | solution.py:484
  3.1 4.6 %collective-permute-start.2 = (f32[2,7,8,128]{3,2,1,0:T(8,128)S(1)}, f32[2,7,8,128]{3,2,1,0:T(8,128)S(1)}, u32[]{:S(2)}, u32[]{:S(2)}) collective-permute-start(f32[2,7,8,128]{3,2,1,0:T(8,128)S(1)} %get-tuple-element.43.refs_0_), channel_id=1, source_target_pairs={{0,25},{1,24},{2,27},{3,26},{4,29},{5,28},{6,31},{7,30},{8,17},{9,... | collective-permute-start | bytes 172040 | tf_op jit(solution)/shard_map/ppermute | solution.py:454
  7.6 0.9 %collective-permute-start = (f32[2,7,8,128]{3,2,1,0:T(8,128)S(1)}, f32[2,7,8,128]{3,2,1,0:T(8,128)S(1)}, u32[]{:S(2)}, u32[]{:S(2)}) collective-permute-start(f32[2,7,8,128]{3,2,1,0:T(8,128)S(1)} %get-tuple-element.43.refs_0_), channel_id=1, source_target_pairs={{0,9},{1,8},{2,11},{3,10},{4,13},{5,12},{6,15},{7,14},{8,1},{9,0},... | collective-permute-start | bytes 172040 | tf_op jit(solution)/shard_map/ppermute | solution.py:454
  8.6 1.4 %collective-permute-done.2.refs_3_ = f32[2,7,8,128]{3,2,1,0:T(8,128)S(1)} collective-permute-done((f32[2,7,8,128]{3,2,1,0:T(8,128)S(1)}, f32[2,7,8,128]{3,2,1,0:T(8,128)S(1)}, u32[]{:S(2)}, u32[]{:S(2)}) %collective-permute-start.2) | collective-permute-done | bytes 57376 | tf_op jit(solution)/shard_map/ppermute | solution.py:454
  10.0 3.4 %collective-permute-done.1.refs_2_ = f32[2,7,8,128]{3,2,1,0:T(8,128)S(1)} collective-permute-done((f32[2,7,8,128]{3,2,1,0:T(8,128)S(1)}, f32[2,7,8,128]{3,2,1,0:T(8,128)S(1)}, u32[]{:S(2)}, u32[]{:S(2)}) %collective-permute-start.1) | collective-permute-done | bytes 57376 | tf_op jit(solution)/shard_map/ppermute | solution.py:454
  13.7 1.3 %collective-permute-done.3.other_ref = f32[2,19,8,128]{3,2,1,0:T(8,128)S(1)} collective-permute-done((f32[2,19,8,128]{3,2,1,0:T(8,128)S(1)}, f32[2,19,8,128]{3,2,1,0:T(8,128)S(1)}, u32[]{:S(2)}, u32[]{:S(2)}) %collective-permute-start.3) | collective-permute-done | bytes 155680 | tf_op jit(solution)/shard_map/ppermute | solution.py:454
  15.0 2.3 %collective-permute-start.4 = (f32[2,7,8,128]{3,2,1,0:T(8,128)S(1)}, f32[2,7,8,128]{3,2,1,0:T(8,128)S(1)}, u32[]{:S(2)}, u32[]{:S(2)}) collective-permute-start(f32[2,7,8,128]{3,2,1,0:T(8,128)S(1)} %get-tuple-element.47), channel_id=1, source_target_pairs={{0,7},{1,6},{2,5},{3,4},{4,3},{5,2},{6,1},{7,0},{8,15},{9,14},{10,... | collective-permute-start | bytes 172040 | tf_op jit(solution)/shard_map/ppermute | solution.py:454
  18.1 1.8 %collective-permute-done.4.refs_1_ = f32[2,7,8,128]{3,2,1,0:T(8,128)S(1)} collective-permute-done((f32[2,7,8,128]{3,2,1,0:T(8,128)S(1)}, f32[2,7,8,128]{3,2,1,0:T(8,128)S(1)}, u32[]{:S(2)}, u32[]{:S(2)}) %collective-permute-start.4) | collective-permute-done | bytes 57376 | tf_op jit(solution)/shard_map/ppermute | solution.py:454
  19.9 1.2 %collective-permute-done.5.refs_2_ = f32[2,7,8,128]{3,2,1,0:T(8,128)S(1)} collective-permute-done((f32[2,7,8,128]{3,2,1,0:T(8,128)S(1)}, f32[2,7,8,128]{3,2,1,0:T(8,128)S(1)}, u32[]{:S(2)}, u32[]{:S(2)}) %collective-permute-start.5) | collective-permute-done | bytes 57376 | tf_op jit(solution)/shard_map/ppermute | solution.py:454
  21.7 0.8 %shard_map.89 = (f32[1,7,8,128]{3,2,1,0:T(8,128)S(1)}, f32[2,3,4,128]{3,2,1,0:T(4,128)S(1)}, f32[7,8,128]{2,1,0:T(8,128)S(1)}, f32[7,8,128]{2,1,0:T(8,128)S(1)}) custom-call(s32[4,4]{1,0:T(4,128)S(4)} %get-tuple-element.34.spots_ref, f32[4,2,16,512]{3,2,1,0:T(8,128)S(1)} %get-tuple-element.35.jac_ref, ...), custom_call_target="tpu_custom_call" | custom-call | tf_op jit(solution)/shard_map/pallas_call | solution.py:484
  22.4 2.1 %collective-permute-start.9 = (f32[1,7,8,128]{3,2,1,0:T(8,128)S(1)}, f32[1,7,8,128]{3,2,1,0:T(8,128)S(1)}, u32[]{:S(2)}, u32[]{:S(2)}) collective-permute-start(f32[1,7,8,128]{3,2,1,0:T(8,128)S(1)} %get-tuple-element.52.refs_0_), channel_id=1, source_target_pairs={{0,25},{1,24},{2,27},{3,26},{4,29},{5,28},{6,31},{7,30},{8,17},{9,... | collective-permute-start | bytes 86024 | tf_op jit(solution)/shard_map/ppermute | solution.py:454
  24.5 0.7 %collective-permute-start.8 = (f32[1,7,8,128]{3,2,1,0:T(8,128)S(1)}, f32[1,7,8,128]{3,2,1,0:T(8,128)S(1)}, u32[]{:S(2)}, u32[]{:S(2)}) collective-permute-start(f32[1,7,8,128]{3,2,1,0:T(8,128)S(1)} %get-tuple-element.52.refs_0_), channel_id=1, source_target_pairs={{0,17},{1,16},{2,19},{3,18},{4,21},{5,20},{6,23},{7,22},{8,25},{9,... | collective-permute-start | bytes 86024 | tf_op jit(solution)/shard_map/ppermute | solution.py:454
  25.2 1.2 %collective-permute-start.7 = (f32[1,7,8,128]{3,2,1,0:T(8,128)S(1)}, f32[1,7,8,128]{3,2,1,0:T(8,128)S(1)}, u32[]{:S(2)}, u32[]{:S(2)}) collective-permute-start(f32[1,7,8,128]{3,2,1,0:T(8,128)S(1)} %get-tuple-element.52.refs_0_), channel_id=1, source_target_pairs={{0,9},{1,8},{2,11},{3,10},{4,13},{5,12},{6,15},{7,14},{8,1},{9,0},... | collective-permute-start | bytes 86024 | tf_op jit(solution)/shard_map/ppermute | solution.py:454
  26.4 1.2 %collective-permute-done.9.refs_3_ = f32[1,7,8,128]{3,2,1,0:T(8,128)S(1)} collective-permute-done((f32[1,7,8,128]{3,2,1,0:T(8,128)S(1)}, f32[1,7,8,128]{3,2,1,0:T(8,128)S(1)}, u32[]{:S(2)}, u32[]{:S(2)}) %collective-permute-start.9) | collective-permute-done | bytes 28704 | tf_op jit(solution)/shard_map/ppermute | solution.py:454
  27.6 1.5 %collective-permute-done.8.refs_2_ = f32[1,7,8,128]{3,2,1,0:T(8,128)S(1)} collective-permute-done((f32[1,7,8,128]{3,2,1,0:T(8,128)S(1)}, f32[1,7,8,128]{3,2,1,0:T(8,128)S(1)}, u32[]{:S(2)}, u32[]{:S(2)}) %collective-permute-start.8) | collective-permute-done | bytes 28704 | tf_op jit(solution)/shard_map/ppermute | solution.py:454
  29.4 1.1 %collective-permute-done.10.other_ref = f32[1,19,8,128]{3,2,1,0:T(8,128)S(1)} collective-permute-done((f32[1,19,8,128]{3,2,1,0:T(8,128)S(1)}, f32[1,19,8,128]{3,2,1,0:T(8,128)S(1)}, u32[]{:S(2)}, u32[]{:S(2)}) %collective-permute-start.10) | collective-permute-done | bytes 77856 | tf_op jit(solution)/shard_map/ppermute | solution.py:454
  30.5 2.0 %collective-permute-start.11 = (f32[1,7,8,128]{3,2,1,0:T(8,128)S(1)}, f32[1,7,8,128]{3,2,1,0:T(8,128)S(1)}, u32[]{:S(2)}, u32[]{:S(2)}) collective-permute-start(f32[1,7,8,128]{3,2,1,0:T(8,128)S(1)} %get-tuple-element.56), channel_id=1, source_target_pairs={{0,7},{1,6},{2,5},{3,4},{4,3},{5,2},{6,1},{7,0},{8,15},{9,14},{10,... | collective-permute-start | bytes 86024 | tf_op jit(solution)/shard_map/ppermute | solution.py:454
  32.5 0.7 %collective-permute-start.12 = (f32[1,7,8,128]{3,2,1,0:T(8,128)S(1)}, f32[1,7,8,128]{3,2,1,0:T(8,128)S(1)}, u32[]{:S(2)}, u32[]{:S(2)}) collective-permute-start(f32[1,7,8,128]{3,2,1,0:T(8,128)S(1)} %get-tuple-element.57), channel_id=1, source_target_pairs={{0,5},{1,4},{2,7},{3,6},{4,1},{5,0},{6,3},{7,2},{8,13},{9,12},{10,... | collective-permute-start | bytes 86024 | tf_op jit(solution)/shard_map/ppermute | solution.py:454
  33.6 1.2 %collective-permute-done.11.refs_1_ = f32[1,7,8,128]{3,2,1,0:T(8,128)S(1)} collective-permute-done((f32[1,7,8,128]{3,2,1,0:T(8,128)S(1)}, f32[1,7,8,128]{3,2,1,0:T(8,128)S(1)}, u32[]{:S(2)}, u32[]{:S(2)}) %collective-permute-start.11) | collective-permute-done | bytes 28704 | tf_op jit(solution)/shard_map/ppermute | solution.py:454
  34.8 1.0 %collective-permute-done.12.refs_2_ = f32[1,7,8,128]{3,2,1,0:T(8,128)S(1)} collective-permute-done((f32[1,7,8,128]{3,2,1,0:T(8,128)S(1)}, f32[1,7,8,128]{3,2,1,0:T(8,128)S(1)}, u32[]{:S(2)}, u32[]{:S(2)}) %collective-permute-start.12) | collective-permute-done | bytes 28704 | tf_op jit(solution)/shard_map/ppermute | solution.py:454
  35.8 0.7 %collective-permute-done.13.refs_3_ = f32[1,7,8,128]{3,2,1,0:T(8,128)S(1)} collective-permute-done((f32[1,7,8,128]{3,2,1,0:T(8,128)S(1)}, f32[1,7,8,128]{3,2,1,0:T(8,128)S(1)}, u32[]{:S(2)}, u32[]{:S(2)}) %collective-permute-start.13) | collective-permute-done | bytes 28704 | tf_op jit(solution)/shard_map/ppermute | solution.py:454
  36.5 0.7 %shard_map.92 = (f32[32,1,128]{2,1,0:T(1,128)S(1)}, f32[8,128]{1,0:T(8,128)S(1)}, f32[2,576]{1,0:T(2,128)S(1)}, f32[3,4,128]{2,1,0:T(4,128)S(1)}) custom-call(s32[4,4]{1,0:T(4,128)S(4)} %get-tuple-element.34.spots_ref, f32[4,2,16,512]{3,2,1,0:T(8,128)S(1)} %get-tuple-element.35.jac_ref, bf16[4,512,128]{2,1,0:T(8,128)(2,1)S(1)} %get-tuple-element.36.land_hot_ref, ...), custom_call_target="tpu_custom_call" | custom-call | tf_op jit(solution)/shard_map/pallas_call | solution.py:484
  37.3 10.6 %all_to_all.5.sums_ref = f32[32,1,128]{2,1,0:T(1,128)S(1)} all-to-all(f32[32,1,128]{2,1,0:T(1,128)S(1)} %get-tuple-element.59), channel_id=1, replica_groups=mesh['row'=8,'col'=4] {'row','col'}, dimensions={0} | all-to-all | bytes 32768 | tf_op jit(solution)/shard_map/all_to_all | solution.py:564
  47.9 0.7 %shard_map.93 = (f32[576]{0:T(1024)}, f32[3,4,128]{2,1,0:T(4,128)}) custom-call(f32[32,1,128]{2,1,0:T(1,128)S(1)} %all_to_all.5.sums_ref, f32[8,128]{1,0:T(8,128)S(1)} %get-tuple-element.60.known_ref, f32[2,576]{1,0:T(2,128)S(1)} %get-tuple-element.61.cam_ref, f32[2,3,4,128]{3,2,1,0:T(4,128)S(1)} %get-tuple-element.62.back_ref, ...), custom_call_target="tpu_custom_call" | custom-call | tf_op jit(solution)/shard_map/pallas_call | solution.py:484
  (13 shorter events, 2.6 us)
Async XLA Ops:
  3.1 6.9 %collective-permute-start.2 = (f32[2,7,8,128]{3,2,1,0:T(8,128)S(1)}, f32[2,7,8,128]{3,2,1,0:T(8,128)S(1)}, u32[]{:S(2)}, u32[]{:S(2)}) collective-permute-start(f32[2,7,8,128]{3,2,1,0:T(8,128)S(1)} %get-tuple-element.43.refs_0_), channel_id=1, source_target_pairs={{0,25},{1,24},{2,27},{3,26},{4,29},{5,28},{6,31},{7,30},{8,17},{9,... | collective-permute-start | bytes 172040 | tf_op jit(solution)/shard_map/ppermute | solution.py:454
  7.6 5.7 %collective-permute-start.1 = (f32[2,7,8,128]{3,2,1,0:T(8,128)S(1)}, f32[2,7,8,128]{3,2,1,0:T(8,128)S(1)}, u32[]{:S(2)}, u32[]{:S(2)}) collective-permute-start(f32[2,7,8,128]{3,2,1,0:T(8,128)S(1)} %get-tuple-element.43.refs_0_), channel_id=1, source_target_pairs={{0,17},{1,16},{2,19},{3,18},{4,21},{5,20},{6,23},{7,22},{8,25},{9,... | collective-permute-start | bytes 172040 | tf_op jit(solution)/shard_map/ppermute | solution.py:454
  7.6 5.7 %collective-permute-start = (f32[2,7,8,128]{3,2,1,0:T(8,128)S(1)}, f32[2,7,8,128]{3,2,1,0:T(8,128)S(1)}, u32[]{:S(2)}, u32[]{:S(2)}) collective-permute-start(f32[2,7,8,128]{3,2,1,0:T(8,128)S(1)} %get-tuple-element.43.refs_0_), channel_id=1, source_target_pairs={{0,9},{1,8},{2,11},{3,10},{4,13},{5,12},{6,15},{7,14},{8,1},{9,0},... | collective-permute-start | bytes 172040 | tf_op jit(solution)/shard_map/ppermute | solution.py:454
  13.5 1.4 %collective-permute-start.3 = (f32[2,19,8,128]{3,2,1,0:T(8,128)S(1)}, f32[2,19,8,128]{3,2,1,0:T(8,128)S(1)}, u32[]{:S(2)}, u32[]{:S(2)}) collective-permute-start(f32[2,19,8,128]{3,2,1,0:T(8,128)S(1)} %get-tuple-element.45), channel_id=1, source_target_pairs={{0,1},{1,0},{2,3},{3,2},{4,5},{5,4},{6,7},{7,6},{8,9},{9,8},{10,11... | collective-permute-start | bytes 466952 | tf_op jit(solution)/shard_map/ppermute | solution.py:454
  15.0 4.9 %collective-permute-start.4 = (f32[2,7,8,128]{3,2,1,0:T(8,128)S(1)}, f32[2,7,8,128]{3,2,1,0:T(8,128)S(1)}, u32[]{:S(2)}, u32[]{:S(2)}) collective-permute-start(f32[2,7,8,128]{3,2,1,0:T(8,128)S(1)} %get-tuple-element.47), channel_id=1, source_target_pairs={{0,7},{1,6},{2,5},{3,4},{4,3},{5,2},{6,1},{7,0},{8,15},{9,14},{10,... | collective-permute-start | bytes 172040 | tf_op jit(solution)/shard_map/ppermute | solution.py:454
  17.3 3.8 %collective-permute-start.5 = (f32[2,7,8,128]{3,2,1,0:T(8,128)S(1)}, f32[2,7,8,128]{3,2,1,0:T(8,128)S(1)}, u32[]{:S(2)}, u32[]{:S(2)}) collective-permute-start(f32[2,7,8,128]{3,2,1,0:T(8,128)S(1)} %get-tuple-element.48), channel_id=1, source_target_pairs={{0,5},{1,4},{2,7},{3,6},{4,1},{5,0},{6,3},{7,2},{8,13},{9,12},{10,... | collective-permute-start | bytes 172040 | tf_op jit(solution)/shard_map/ppermute | solution.py:454
  17.8 3.9 %collective-permute-start.6 = (f32[2,7,8,128]{3,2,1,0:T(8,128)S(1)}, f32[2,7,8,128]{3,2,1,0:T(8,128)S(1)}, u32[]{:S(2)}, u32[]{:S(2)}) collective-permute-start(f32[2,7,8,128]{3,2,1,0:T(8,128)S(1)} %get-tuple-element.49), channel_id=1, source_target_pairs={{0,3},{1,2},{2,1},{3,0},{4,7},{5,6},{6,5},{7,4},{8,11},{9,10},{10,... | collective-permute-start | bytes 172040 | tf_op jit(solution)/shard_map/ppermute | solution.py:454
  22.4 5.2 %collective-permute-start.9 = (f32[1,7,8,128]{3,2,1,0:T(8,128)S(1)}, f32[1,7,8,128]{3,2,1,0:T(8,128)S(1)}, u32[]{:S(2)}, u32[]{:S(2)}) collective-permute-start(f32[1,7,8,128]{3,2,1,0:T(8,128)S(1)} %get-tuple-element.52.refs_0_), channel_id=1, source_target_pairs={{0,25},{1,24},{2,27},{3,26},{4,29},{5,28},{6,31},{7,30},{8,17},{9,... | collective-permute-start | bytes 86024 | tf_op jit(solution)/shard_map/ppermute | solution.py:454
  24.5 4.5 %collective-permute-start.8 = (f32[1,7,8,128]{3,2,1,0:T(8,128)S(1)}, f32[1,7,8,128]{3,2,1,0:T(8,128)S(1)}, u32[]{:S(2)}, u32[]{:S(2)}) collective-permute-start(f32[1,7,8,128]{3,2,1,0:T(8,128)S(1)} %get-tuple-element.52.refs_0_), channel_id=1, source_target_pairs={{0,17},{1,16},{2,19},{3,18},{4,21},{5,20},{6,23},{7,22},{8,25},{9,... | collective-permute-start | bytes 86024 | tf_op jit(solution)/shard_map/ppermute | solution.py:454
  25.2 3.9 %collective-permute-start.7 = (f32[1,7,8,128]{3,2,1,0:T(8,128)S(1)}, f32[1,7,8,128]{3,2,1,0:T(8,128)S(1)}, u32[]{:S(2)}, u32[]{:S(2)}) collective-permute-start(f32[1,7,8,128]{3,2,1,0:T(8,128)S(1)} %get-tuple-element.52.refs_0_), channel_id=1, source_target_pairs={{0,9},{1,8},{2,11},{3,10},{4,13},{5,12},{6,15},{7,14},{8,1},{9,0},... | collective-permute-start | bytes 86024 | tf_op jit(solution)/shard_map/ppermute | solution.py:454
  29.1 1.3 %collective-permute-start.10 = (f32[1,19,8,128]{3,2,1,0:T(8,128)S(1)}, f32[1,19,8,128]{3,2,1,0:T(8,128)S(1)}, u32[]{:S(2)}, u32[]{:S(2)}) collective-permute-start(f32[1,19,8,128]{3,2,1,0:T(8,128)S(1)} %get-tuple-element.54), channel_id=1, source_target_pairs={{0,1},{1,0},{2,3},{3,2},{4,5},{5,4},{6,7},{7,6},{8,9},{9,8},{10,11... | collective-permute-start | bytes 233480 | tf_op jit(solution)/shard_map/ppermute | solution.py:454
  30.5 4.3 %collective-permute-start.11 = (f32[1,7,8,128]{3,2,1,0:T(8,128)S(1)}, f32[1,7,8,128]{3,2,1,0:T(8,128)S(1)}, u32[]{:S(2)}, u32[]{:S(2)}) collective-permute-start(f32[1,7,8,128]{3,2,1,0:T(8,128)S(1)} %get-tuple-element.56), channel_id=1, source_target_pairs={{0,7},{1,6},{2,5},{3,4},{4,3},{5,2},{6,1},{7,0},{8,15},{9,14},{10,... | collective-permute-start | bytes 86024 | tf_op jit(solution)/shard_map/ppermute | solution.py:454
  32.5 3.3 %collective-permute-start.12 = (f32[1,7,8,128]{3,2,1,0:T(8,128)S(1)}, f32[1,7,8,128]{3,2,1,0:T(8,128)S(1)}, u32[]{:S(2)}, u32[]{:S(2)}) collective-permute-start(f32[1,7,8,128]{3,2,1,0:T(8,128)S(1)} %get-tuple-element.57), channel_id=1, source_target_pairs={{0,5},{1,4},{2,7},{3,6},{4,1},{5,0},{6,3},{7,2},{8,13},{9,12},{10,... | collective-permute-start | bytes 86024 | tf_op jit(solution)/shard_map/ppermute | solution.py:454
  33.2 3.3 %collective-permute-start.13 = (f32[1,7,8,128]{3,2,1,0:T(8,128)S(1)}, f32[1,7,8,128]{3,2,1,0:T(8,128)S(1)}, u32[]{:S(2)}, u32[]{:S(2)}) collective-permute-start(f32[1,7,8,128]{3,2,1,0:T(8,128)S(1)} %get-tuple-element.58), channel_id=1, source_target_pairs={{0,3},{1,2},{2,1},{3,0},{4,7},{5,6},{6,5},{7,4},{8,11},{9,10},{10,... | collective-permute-start | bytes 86024 | tf_op jit(solution)/shard_map/ppermute | solution.py:454

commit v7 on v6

--- a/solution.py
+++ b/solution.py
@@ -97,8 +97,8 @@
     return pltpu.roll(x, (1 - half) * CAM, 1)
 
 
-def packed(tiles):
-    return tiles + tiles // 8 + 1
+def packed(tiles, more=0):
+    return tiles + (tiles + more) // 8 + 1
 
 
 def load_tile(ref, tiles, t):
@@ -106,8 +106,8 @@
     return jnp.concatenate([ref[t], ninth, jnp.zeros((7, LANES), jnp.float32)], axis=0)
 
 
-def write_ninths(ref, tiles, rows, sums=None):
-    rows = list(rows) + [jnp.zeros((1, LANES), jnp.float32) if sums is None else sums]
+def write_ninths(ref, tiles, rows, sums=None, more=()):
+    rows = list(rows) + [jnp.zeros((1, LANES), jnp.float32) if sums is None else sums] + list(more)
     for start in range(0, len(rows), 8):
         ref[tiles + start // 8] = stack_rows(rows[start : start + 8], 8)
 
@@ -136,22 +136,26 @@
     return [[spots_ref[i, k] for i in range(4)] for k in range(spots_ref.shape[1])]
 
 
-def write_parts(ref, row_tiles, tiles, spots, values, extra=None, sums=None):
+def write_parts(ref, row_tiles, spots, values, extra=None, sums=None):
     lower = lane_ids(values[0].shape[0]) < CAM
     firsts = [to_first(jnp.where(lower, v, 0.0), spot[1]) for v, spot in zip(values, spots)]
-    seconds = [to_second(jnp.where(lower, 0.0, v), spot[3]) for v, spot in zip(values, spots)]
-    ninths = []
-    for t in range(tiles):
-        if t < row_tiles:
-            items = [(spot[0] == t, v) for v, spot in zip(firsts, spots)]
-            if extra is not None:
-                items.append((extra[0] == t, extra[1]))
-        else:
-            items = [(spot[2] == t - row_tiles, v) for v, spot in zip(seconds, spots)]
-        total = sum(jnp.where(here, v, 0.0) for here, v in items)
-        ref[t] = total[:8]
-        ninths.append(total[8:9])
-    write_ninths(ref, tiles, ninths, sums)
+    tiles = []
+    for t in range(row_tiles):
+        items = [(spot[0] == t, v) for v, spot in zip(firsts, spots)]
+        if extra is not None:
+            items.append((extra[0] == t, extra[1]))
+        tiles.append(sum(jnp.where(here, v, 0.0) for here, v in items))
+    groups = []
+    left = lane_ids(1) < CAM
+    for k in range(0, len(values), 2):
+        other = min(k + 1, len(values) - 1)
+        second = values[other] if other > k else jnp.zeros_like(values[k])
+        tiles.append(jnp.where(lower, pltpu.roll(values[k], CAM, 1), second))
+        ids = [2 * spots[i][2] + spots[i][3] for i in (k, other)]
+        groups.append(jnp.where(left, ids[0], ids[1]).astype(jnp.float32))
+    for t, tile in enumerate(tiles):
+        ref[t] = tile[:8]
+    write_ninths(ref, len(tiles), [tile[8:9] for tile in tiles], sums, groups)
 
 
 def own_place(n_row, n_col, cams):
@@ -245,8 +249,8 @@
     for k in each:
         for i in range(4):
             spots_ref[i, k] = spots[k][i]
-    write_parts(part_ref.at[0], row_tiles, tiles, spots, [x[:16] for x in both])
-    write_parts(part_ref.at[1], row_tiles, tiles, spots, [x[16:] for x in both], (own_tile, damp_tile))
+    write_parts(part_ref.at[0], row_tiles, spots, [x[:16] for x in both])
+    write_parts(part_ref.at[1], row_tiles, spots, [x[16:] for x in both], (own_tile, damp_tile))
 
 
 def half_product(p_ref, row_tiles, tiles, spots, jac_ref, land_hot_ref, index_ref, m_ref):
@@ -333,7 +337,7 @@
         for b in range(3):
             back_ref[0, b, k : k + 1, :] = from_t[b]
             back_ref[1, b, k : k + 1, :] = solved[b]
-    write_parts(part_ref.at[0], row_tiles, tiles, spots, images, (own_tile, damped), in_lanes([norm_now, energy]))
+    write_parts(part_ref.at[0], row_tiles, spots, images, (own_tile, damped), in_lanes([norm_now, energy]))
 
 
 def second_kernel(n_row, n_col, cams, pieces, spots_ref, jac_ref, land_hot_ref, index_ref, m_ref, fac_ref, damp_tile_ref, select_ref, right_ref, precond_ref, *refs):
@@ -391,28 +395,42 @@
     land_out_ref[...] = -(back_ref[0] + first[None] * back_ref[1] + slope[None] * solved_ref[...])
 
 
-def core_kernel(n_row, n_col, cams, radix, *refs):
+def column_tiles(parts, row_tiles, col_tiles, pairs):
+    tiles = row_tiles + pairs
+
+    def row(part, i):
+        return part[tiles + i // 8, i % 8 : i % 8 + 1]
+
+    halves = []
+    for part in parts:
+        for i in range(pairs):
+            t = row_tiles + i
+            value = jnp.concatenate([part[t], row(part, t), jnp.zeros((7, LANES), jnp.float32)], axis=0)
+            halves.append((row(part, tiles + 1 + i), value))
+    folded = []
+    for group in range(2 * col_tiles):
+        total = sum(jnp.where(ids == float(group), value, 0.0) for ids, value in halves)
+        folded.append(total + pltpu.roll(total, CAM, 1))
+    lower = lane_ids(16) < CAM
+    return [jnp.where(lower, folded[2 * t], folded[2 * t + 1]) for t in range(col_tiles)]
+
+
+def core_kernel(n_row, n_col, cams, radix, pairs, *refs):
     part_refs, out_refs, (whole_ref, ninth_ref) = refs[:radix], refs[radix:-2], refs[-2:]
     row_tiles = cams // n_row // LANES
     col_tiles = cams // n_col // LANES
-    tiles = row_tiles + col_tiles
+    tiles = row_tiles + pairs
     low = n_row // radix
     row, col = lax.axis_index("row"), lax.axis_index("col")
     for v in range(whole_ref.shape[0]):
         parts = [ref[v] for ref in part_refs]
-        received = parts[1]
-        for part in parts[2:]:
-            received = received + part
-        row_sums = tiles + tiles // 8, tiles % 8
-        sums = (parts[0] + received)[row_sums[0], row_sums[1] : row_sums[1] + 1]
+        sums = sum(part[tiles + tiles // 8, tiles % 8 : tiles % 8 + 1] for part in parts)
         whole_ref[v] = jnp.zeros(whole_ref.shape[1:], jnp.float32)
         ninth_ref[v] = jnp.zeros(ninth_ref.shape[1:], jnp.float32)
-        columns = [(col, parts[0]), (col ^ 1, received)]
-        for column, total in columns:
-            for i in range(col_tiles):
-                t = row_tiles + i
-                whole_ref[v, column * col_tiles + i] = total[t]
-                ninth_ref[v, pl.ds(column * col_tiles + i, 1), :] = total[tiles + t // 8, t % 8 : t % 8 + 1]
+        for column, sources in ((col, parts[:1]), (col ^ 1, parts[1:])):
+            for i, total in enumerate(column_tiles(sources, row_tiles, col_tiles, pairs)):
+                whole_ref[v, column * col_tiles + i] = total[:8]
+                ninth_ref[v, pl.ds(column * col_tiles + i, 1), :] = total[8:9]
         for digit, part in enumerate(parts):
             start = (row ^ (digit * low)) * row_tiles
             for i in range(row_tiles):
@@ -474,6 +492,8 @@
         return pltpu.VMEM(dims, f32)
 
     radix = min(n_row, 4)
+    pair_tiles = (count + 1) // 2
+    part_tiles = packed(row_tiles + pair_tiles, pair_tiles)
     low = n_row // radix
     sent = n_col // 2 * col_tiles + col_tiles + low * row_tiles
     lead = [digit * low * n_col + 1 for digit in range(1, radix)]
@@ -497,7 +517,7 @@
             tuple(map(in_vmem, pieces)),
             (shape(vectors, packed(sent), 8, LANES),) * 2,
             (pltpu.VMEM((vectors, cams // LANES, 8, LANES), f32), pltpu.VMEM((vectors, cams // LANES, LANES), f32)),
-            (n_row, n_col, cams, radix),
+            (n_row, n_col, cams, radix, pair_tiles),
         )
         (other,) = exchange(other, [1], n_dev)
         to_send = call(
@@ -523,7 +543,7 @@
             cam_damp,
         ),
         (
-            shape(2, packed(tiles), 8, LANES),
+            shape(2, part_tiles, 8, LANES),
             shape(count, 2, 16, obs),
             hot,
             hot,
@@ -547,7 +567,7 @@
     part, back, right, precond = call(
         first_kernel,
         (spots, jac, cam_hot, land_hot, index, m, fac, damp_tile, *sums),
-        (shape(1, packed(tiles), 8, LANES), shape(2, 3, count, LM), vector, vector),
+        (shape(1, part_tiles, 8, LANES), shape(2, 3, count, LM), vector, vector),
         (vector,),
         (n_row, n_col, cams, pieces),
         specs=[smem] + [vmem] * (7 + pieces),

time: 48.8 us -> 47.6 us (0.975)
  waiting for transfers between devices: 16.4 us -> 14.4 us
  starting transfers between devices: 16 us -> 16.6 us
    ppermute x14, waiting for transfers between devices: 16.4 us -> 14.4 us  [exchange(): lax.ppermute(x, AXES, [(i, i ^ mask) for i in range(n_dev)])]
    ppermute x14, starting transfers between devices: 16 us -> 16.6 us  [exchange(): lax.ppermute(x, AXES, [(i, i ^ mask) for i in range(n_dev)])]
where the time goes in v7:
time: 47.6 us; the launch traced here: 47.5 us
  starting transfers between devices  16.6 us (35%)
  waiting for transfers between devices  14.4 us (30%)
  blocking collectives  10.5 us (22%)
  Pallas kernels  5.26 us (11%)
  between operations  0.68 us (1%)
    ppermute x14, starting transfers between devices, exchange(): lax.ppermute(x, AXES, [(i, i ^ mask) for i in range(n_dev)])  16.6 us
    ppermute x14, waiting for transfers between devices, exchange(): lax.ppermute(x, AXES, [(i, i ^ mask) for i in range(n_dev)])  14.4 us
    all_to_all x1, blocking collectives, per_device(): gathered = lax.all_to_all(partial, AXES, 0, 0, tiled=True)  10.5 us
    pallas_call x8, Pallas kernels, call(): pl.pallas_call(functools.partial(kernel, *whole), out_shape=out_shape, in...  5.26 us
  transfers between devices with their start and end apart: 14, of which 12 were waited for; matrix products, arithmetic and copies ran while one was open for 0% of the time, Pallas kernels for 0%

profile of v7, /device:TPU:0, one launch (start us, length us, event | category | flops | bytes accessed | tf_op | source)
XLA Modules:
  0.0 47.5 jit_solution(17976263953457562760)
XLA Ops:
  0.6 2.4 %shard_map.86 = (f32[2,5,8,128]{3,2,1,0:T(8,128)S(1)}, f32[4,2,16,512]{3,2,1,0:T(8,128)S(1)}, bf16[4,512,128]{2,1,0:T(8,128)(2,1)S(1)}, bf16[4,512,128]{2,1,0:T(...) custom-call(s32[2,4]{1,0:T(2,128)} %bitcast.6, ...), custom_call_target="tpu_custom_call" | custom-call | tf_op jit(solution)/shard_map/pallas_call | solution.py:504
  3.0 4.6 %collective-permute-start.2 = (f32[2,5,8,128]{3,2,1,0:T(8,128)S(1)}, f32[2,5,8,128]{3,2,1,0:T(8,128)S(1)}, u32[]{:S(2)}, u32[]{:S(2)}) collective-permute-start(f32[2,5,8,128]{3,2,1,0:T(8,128)S(1)} %get-tuple-element.43.refs_0_), channel_id=1, source_target_pairs={{0,25},{1,24},{2,27},{3,26},{4,29},{5,28},{6,31},{7,30},{8,17},{9,... | collective-permute-start | bytes 122888 | tf_op jit(solution)/shard_map/ppermute | solution.py:472
  7.6 0.9 %collective-permute-start = (f32[2,5,8,128]{3,2,1,0:T(8,128)S(1)}, f32[2,5,8,128]{3,2,1,0:T(8,128)S(1)}, u32[]{:S(2)}, u32[]{:S(2)}) collective-permute-start(f32[2,5,8,128]{3,2,1,0:T(8,128)S(1)} %get-tuple-element.43.refs_0_), channel_id=1, source_target_pairs={{0,9},{1,8},{2,11},{3,10},{4,13},{5,12},{6,15},{7,14},{8,1},{9,0},... | collective-permute-start | bytes 122888 | tf_op jit(solution)/shard_map/ppermute | solution.py:472
  8.5 1.0 %collective-permute-done.2.refs_3_ = f32[2,5,8,128]{3,2,1,0:T(8,128)S(1)} collective-permute-done((f32[2,5,8,128]{3,2,1,0:T(8,128)S(1)}, f32[2,5,8,128]{3,2,1,0:T(8,128)S(1)}, u32[]{:S(2)}, u32[]{:S(2)}) %collective-permute-start.2) | collective-permute-done | bytes 40992 | tf_op jit(solution)/shard_map/ppermute | solution.py:472
  9.6 2.8 %collective-permute-done.1.refs_2_ = f32[2,5,8,128]{3,2,1,0:T(8,128)S(1)} collective-permute-done((f32[2,5,8,128]{3,2,1,0:T(8,128)S(1)}, f32[2,5,8,128]{3,2,1,0:T(8,128)S(1)}, u32[]{:S(2)}, u32[]{:S(2)}) %collective-permute-start.1) | collective-permute-done | bytes 40992 | tf_op jit(solution)/shard_map/ppermute | solution.py:472
  12.9 1.1 %collective-permute-done.3.other_ref = f32[2,19,8,128]{3,2,1,0:T(8,128)S(1)} collective-permute-done((f32[2,19,8,128]{3,2,1,0:T(8,128)S(1)}, f32[2,19,8,128]{3,2,1,0:T(8,128)S(1)}, u32[]{:S(2)}, u32[]{:S(2)}) %collective-permute-start.3) | collective-permute-done | bytes 155680 | tf_op jit(solution)/shard_map/ppermute | solution.py:472
  14.1 2.4 %collective-permute-start.4 = (f32[2,7,8,128]{3,2,1,0:T(8,128)S(1)}, f32[2,7,8,128]{3,2,1,0:T(8,128)S(1)}, u32[]{:S(2)}, u32[]{:S(2)}) collective-permute-start(f32[2,7,8,128]{3,2,1,0:T(8,128)S(1)} %get-tuple-element.47), channel_id=1, source_target_pairs={{0,7},{1,6},{2,5},{3,4},{4,3},{5,2},{6,1},{7,0},{8,15},{9,14},{10,... | collective-permute-start | bytes 172040 | tf_op jit(solution)/shard_map/ppermute | solution.py:472
  17.3 1.6 %collective-permute-done.4.refs_1_ = f32[2,7,8,128]{3,2,1,0:T(8,128)S(1)} collective-permute-done((f32[2,7,8,128]{3,2,1,0:T(8,128)S(1)}, f32[2,7,8,128]{3,2,1,0:T(8,128)S(1)}, u32[]{:S(2)}, u32[]{:S(2)}) %collective-permute-start.4) | collective-permute-done | bytes 57376 | tf_op jit(solution)/shard_map/ppermute | solution.py:472
  18.9 1.5 %collective-permute-done.5.refs_2_ = f32[2,7,8,128]{3,2,1,0:T(8,128)S(1)} collective-permute-done((f32[2,7,8,128]{3,2,1,0:T(8,128)S(1)}, f32[2,7,8,128]{3,2,1,0:T(8,128)S(1)}, u32[]{:S(2)}, u32[]{:S(2)}) %collective-permute-start.5) | collective-permute-done | bytes 57376 | tf_op jit(solution)/shard_map/ppermute | solution.py:472
  20.7 0.7 %shard_map.89 = (f32[1,5,8,128]{3,2,1,0:T(8,128)S(1)}, f32[2,3,4,128]{3,2,1,0:T(4,128)S(1)}, f32[7,8,128]{2,1,0:T(8,128)S(1)}, f32[7,8,128]{2,1,0:T(8,128)S(1)}) custom-call(s32[4,4]{1,0:T(4,128)S(4)} %get-tuple-element.34.spots_ref, f32[4,2,16,512]{3,2,1,0:T(8,128)S(1)} %get-tuple-element.35.jac_ref, ...), custom_call_target="tpu_custom_call" | custom-call | tf_op jit(solution)/shard_map/pallas_call | solution.py:504
  21.5 2.2 %collective-permute-start.9 = (f32[1,5,8,128]{3,2,1,0:T(8,128)S(1)}, f32[1,5,8,128]{3,2,1,0:T(8,128)S(1)}, u32[]{:S(2)}, u32[]{:S(2)}) collective-permute-start(f32[1,5,8,128]{3,2,1,0:T(8,128)S(1)} %get-tuple-element.52.refs_0_), channel_id=1, source_target_pairs={{0,25},{1,24},{2,27},{3,26},{4,29},{5,28},{6,31},{7,30},{8,17},{9,... | collective-permute-start | bytes 61448 | tf_op jit(solution)/shard_map/ppermute | solution.py:472
  23.7 0.5 %collective-permute-start.8 = (f32[1,5,8,128]{3,2,1,0:T(8,128)S(1)}, f32[1,5,8,128]{3,2,1,0:T(8,128)S(1)}, u32[]{:S(2)}, u32[]{:S(2)}) collective-permute-start(f32[1,5,8,128]{3,2,1,0:T(8,128)S(1)} %get-tuple-element.52.refs_0_), channel_id=1, source_target_pairs={{0,17},{1,16},{2,19},{3,18},{4,21},{5,20},{6,23},{7,22},{8,25},{9,... | collective-permute-start | bytes 61448 | tf_op jit(solution)/shard_map/ppermute | solution.py:472
  24.2 1.2 %collective-permute-start.7 = (f32[1,5,8,128]{3,2,1,0:T(8,128)S(1)}, f32[1,5,8,128]{3,2,1,0:T(8,128)S(1)}, u32[]{:S(2)}, u32[]{:S(2)}) collective-permute-start(f32[1,5,8,128]{3,2,1,0:T(8,128)S(1)} %get-tuple-element.52.refs_0_), channel_id=1, source_target_pairs={{0,9},{1,8},{2,11},{3,10},{4,13},{5,12},{6,15},{7,14},{8,1},{9,0},... | collective-permute-start | bytes 61448 | tf_op jit(solution)/shard_map/ppermute | solution.py:472
  25.5 1.1 %collective-permute-done.9.refs_3_ = f32[1,5,8,128]{3,2,1,0:T(8,128)S(1)} collective-permute-done((f32[1,5,8,128]{3,2,1,0:T(8,128)S(1)}, f32[1,5,8,128]{3,2,1,0:T(8,128)S(1)}, u32[]{:S(2)}, u32[]{:S(2)}) %collective-permute-start.9) | collective-permute-done | bytes 20512 | tf_op jit(solution)/shard_map/ppermute | solution.py:472
  26.5 1.5 %collective-permute-done.8.refs_2_ = f32[1,5,8,128]{3,2,1,0:T(8,128)S(1)} collective-permute-done((f32[1,5,8,128]{3,2,1,0:T(8,128)S(1)}, f32[1,5,8,128]{3,2,1,0:T(8,128)S(1)}, u32[]{:S(2)}, u32[]{:S(2)}) %collective-permute-start.8) | collective-permute-done | bytes 20512 | tf_op jit(solution)/shard_map/ppermute | solution.py:472
  28.2 0.4 collective-permute-start.10
  28.6 0.9 %collective-permute-done.10.other_ref = f32[1,19,8,128]{3,2,1,0:T(8,128)S(1)} collective-permute-done((f32[1,19,8,128]{3,2,1,0:T(8,128)S(1)}, f32[1,19,8,128]{3,2,1,0:T(8,128)S(1)}, u32[]{:S(2)}, u32[]{:S(2)}) %collective-permute-start.10) | collective-permute-done | bytes 77856 | tf_op jit(solution)/shard_map/ppermute | solution.py:472
  29.6 2.1 %collective-permute-start.11 = (f32[1,7,8,128]{3,2,1,0:T(8,128)S(1)}, f32[1,7,8,128]{3,2,1,0:T(8,128)S(1)}, u32[]{:S(2)}, u32[]{:S(2)}) collective-permute-start(f32[1,7,8,128]{3,2,1,0:T(8,128)S(1)} %get-tuple-element.56), channel_id=1, source_target_pairs={{0,7},{1,6},{2,5},{3,4},{4,3},{5,2},{6,1},{7,0},{8,15},{9,14},{10,... | collective-permute-start | bytes 86024 | tf_op jit(solution)/shard_map/ppermute | solution.py:472
  32.2 0.7 %collective-permute-start.13 = (f32[1,7,8,128]{3,2,1,0:T(8,128)S(1)}, f32[1,7,8,128]{3,2,1,0:T(8,128)S(1)}, u32[]{:S(2)}, u32[]{:S(2)}) collective-permute-start(f32[1,7,8,128]{3,2,1,0:T(8,128)S(1)} %get-tuple-element.58), channel_id=1, source_target_pairs={{0,3},{1,2},{2,1},{3,0},{4,7},{5,6},{6,5},{7,4},{8,11},{9,10},{10,... | collective-permute-start | bytes 86024 | tf_op jit(solution)/shard_map/ppermute | solution.py:472
  32.9 1.0 %collective-permute-done.11.refs_1_ = f32[1,7,8,128]{3,2,1,0:T(8,128)S(1)} collective-permute-done((f32[1,7,8,128]{3,2,1,0:T(8,128)S(1)}, f32[1,7,8,128]{3,2,1,0:T(8,128)S(1)}, u32[]{:S(2)}, u32[]{:S(2)}) %collective-permute-start.11) | collective-permute-done | bytes 28704 | tf_op jit(solution)/shard_map/ppermute | solution.py:472
  33.9 1.2 %collective-permute-done.12.refs_2_ = f32[1,7,8,128]{3,2,1,0:T(8,128)S(1)} collective-permute-done((f32[1,7,8,128]{3,2,1,0:T(8,128)S(1)}, f32[1,7,8,128]{3,2,1,0:T(8,128)S(1)}, u32[]{:S(2)}, u32[]{:S(2)}) %collective-permute-start.12) | collective-permute-done | bytes 28704 | tf_op jit(solution)/shard_map/ppermute | solution.py:472
  35.5 0.8 %shard_map.92 = (f32[32,1,128]{2,1,0:T(1,128)S(1)}, f32[8,128]{1,0:T(8,128)S(1)}, f32[2,576]{1,0:T(2,128)S(1)}, f32[3,4,128]{2,1,0:T(4,128)S(1)}) custom-call(s32[4,4]{1,0:T(4,128)S(4)} %get-tuple-element.34.spots_ref, f32[4,2,16,512]{3,2,1,0:T(8,128)S(1)} %get-tuple-element.35.jac_ref, bf16[4,512,128]{2,1,0:T(8,128)(2,1)S(1)} %get-tuple-element.36.land_hot_ref, ...), custom_call_target="tpu_custom_call" | custom-call | tf_op jit(solution)/shard_map/pallas_call | solution.py:504
  36.2 10.5 %all_to_all.5.sums_ref = f32[32,1,128]{2,1,0:T(1,128)S(1)} all-to-all(f32[32,1,128]{2,1,0:T(1,128)S(1)} %get-tuple-element.59), channel_id=1, replica_groups=mesh['row'=8,'col'=4] {'row','col'}, dimensions={0} | all-to-all | bytes 32768 | tf_op jit(solution)/shard_map/all_to_all | solution.py:584
  46.8 0.7 %shard_map.93 = (f32[576]{0:T(1024)}, f32[3,4,128]{2,1,0:T(4,128)}) custom-call(f32[32,1,128]{2,1,0:T(1,128)S(1)} %all_to_all.5.sums_ref, f32[8,128]{1,0:T(8,128)S(1)} %get-tuple-element.60.known_ref, f32[2,576]{1,0:T(2,128)S(1)} %get-tuple-element.61.cam_ref, f32[2,3,4,128]{3,2,1,0:T(4,128)S(1)} %get-tuple-element.62.back_ref, ...), custom_call_target="tpu_custom_call" | custom-call | tf_op jit(solution)/shard_map/pallas_call | solution.py:504
  (13 shorter events, 2.8 us)
Async XLA Ops:
  3.0 6.5 %collective-permute-start.2 = (f32[2,5,8,128]{3,2,1,0:T(8,128)S(1)}, f32[2,5,8,128]{3,2,1,0:T(8,128)S(1)}, u32[]{:S(2)}, u32[]{:S(2)}) collective-permute-start(f32[2,5,8,128]{3,2,1,0:T(8,128)S(1)} %get-tuple-element.43.refs_0_), channel_id=1, source_target_pairs={{0,25},{1,24},{2,27},{3,26},{4,29},{5,28},{6,31},{7,30},{8,17},{9,... | collective-permute-start | bytes 122888 | tf_op jit(solution)/shard_map/ppermute | solution.py:472
  7.6 4.7 %collective-permute-start.1 = (f32[2,5,8,128]{3,2,1,0:T(8,128)S(1)}, f32[2,5,8,128]{3,2,1,0:T(8,128)S(1)}, u32[]{:S(2)}, u32[]{:S(2)}) collective-permute-start(f32[2,5,8,128]{3,2,1,0:T(8,128)S(1)} %get-tuple-element.43.refs_0_), channel_id=1, source_target_pairs={{0,17},{1,16},{2,19},{3,18},{4,21},{5,20},{6,23},{7,22},{8,25},{9,... | collective-permute-start | bytes 122888 | tf_op jit(solution)/shard_map/ppermute | solution.py:472
  7.6 4.7 %collective-permute-start = (f32[2,5,8,128]{3,2,1,0:T(8,128)S(1)}, f32[2,5,8,128]{3,2,1,0:T(8,128)S(1)}, u32[]{:S(2)}, u32[]{:S(2)}) collective-permute-start(f32[2,5,8,128]{3,2,1,0:T(8,128)S(1)} %get-tuple-element.43.refs_0_), channel_id=1, source_target_pairs={{0,9},{1,8},{2,11},{3,10},{4,13},{5,12},{6,15},{7,14},{8,1},{9,0},... | collective-permute-start | bytes 122888 | tf_op jit(solution)/shard_map/ppermute | solution.py:472
  12.6 1.4 %collective-permute-start.3 = (f32[2,19,8,128]{3,2,1,0:T(8,128)S(1)}, f32[2,19,8,128]{3,2,1,0:T(8,128)S(1)}, u32[]{:S(2)}, u32[]{:S(2)}) collective-permute-start(f32[2,19,8,128]{3,2,1,0:T(8,128)S(1)} %get-tuple-element.45), channel_id=1, source_target_pairs={{0,1},{1,0},{2,3},{3,2},{4,5},{5,4},{6,7},{7,6},{8,9},{9,8},{10,11... | collective-permute-start | bytes 466952 | tf_op jit(solution)/shard_map/ppermute | solution.py:472
  14.1 4.8 %collective-permute-start.4 = (f32[2,7,8,128]{3,2,1,0:T(8,128)S(1)}, f32[2,7,8,128]{3,2,1,0:T(8,128)S(1)}, u32[]{:S(2)}, u32[]{:S(2)}) collective-permute-start(f32[2,7,8,128]{3,2,1,0:T(8,128)S(1)} %get-tuple-element.47), channel_id=1, source_target_pairs={{0,7},{1,6},{2,5},{3,4},{4,3},{5,2},{6,1},{7,0},{8,15},{9,14},{10,... | collective-permute-start | bytes 172040 | tf_op jit(solution)/shard_map/ppermute | solution.py:472
  16.5 3.9 %collective-permute-start.5 = (f32[2,7,8,128]{3,2,1,0:T(8,128)S(1)}, f32[2,7,8,128]{3,2,1,0:T(8,128)S(1)}, u32[]{:S(2)}, u32[]{:S(2)}) collective-permute-start(f32[2,7,8,128]{3,2,1,0:T(8,128)S(1)} %get-tuple-element.48), channel_id=1, source_target_pairs={{0,5},{1,4},{2,7},{3,6},{4,1},{5,0},{6,3},{7,2},{8,13},{9,12},{10,... | collective-permute-start | bytes 172040 | tf_op jit(solution)/shard_map/ppermute | solution.py:472
  16.9 3.8 %collective-permute-start.6 = (f32[2,7,8,128]{3,2,1,0:T(8,128)S(1)}, f32[2,7,8,128]{3,2,1,0:T(8,128)S(1)}, u32[]{:S(2)}, u32[]{:S(2)}) collective-permute-start(f32[2,7,8,128]{3,2,1,0:T(8,128)S(1)} %get-tuple-element.49), channel_id=1, source_target_pairs={{0,3},{1,2},{2,1},{3,0},{4,7},{5,6},{6,5},{7,4},{8,11},{9,10},{10,... | collective-permute-start | bytes 172040 | tf_op jit(solution)/shard_map/ppermute | solution.py:472
  21.5 5.1 %collective-permute-start.9 = (f32[1,5,8,128]{3,2,1,0:T(8,128)S(1)}, f32[1,5,8,128]{3,2,1,0:T(8,128)S(1)}, u32[]{:S(2)}, u32[]{:S(2)}) collective-permute-start(f32[1,5,8,128]{3,2,1,0:T(8,128)S(1)} %get-tuple-element.52.refs_0_), channel_id=1, source_target_pairs={{0,25},{1,24},{2,27},{3,26},{4,29},{5,28},{6,31},{7,30},{8,17},{9,... | collective-permute-start | bytes 61448 | tf_op jit(solution)/shard_map/ppermute | solution.py:472
  23.7 4.3 %collective-permute-start.8 = (f32[1,5,8,128]{3,2,1,0:T(8,128)S(1)}, f32[1,5,8,128]{3,2,1,0:T(8,128)S(1)}, u32[]{:S(2)}, u32[]{:S(2)}) collective-permute-start(f32[1,5,8,128]{3,2,1,0:T(8,128)S(1)} %get-tuple-element.52.refs_0_), channel_id=1, source_target_pairs={{0,17},{1,16},{2,19},{3,18},{4,21},{5,20},{6,23},{7,22},{8,25},{9,... | collective-permute-start | bytes 61448 | tf_op jit(solution)/shard_map/ppermute | solution.py:472
  24.2 3.8 %collective-permute-start.7 = (f32[1,5,8,128]{3,2,1,0:T(8,128)S(1)}, f32[1,5,8,128]{3,2,1,0:T(8,128)S(1)}, u32[]{:S(2)}, u32[]{:S(2)}) collective-permute-start(f32[1,5,8,128]{3,2,1,0:T(8,128)S(1)} %get-tuple-element.52.refs_0_), channel_id=1, source_target_pairs={{0,9},{1,8},{2,11},{3,10},{4,13},{5,12},{6,15},{7,14},{8,1},{9,0},... | collective-permute-start | bytes 61448 | tf_op jit(solution)/shard_map/ppermute | solution.py:472
  28.2 1.3 %collective-permute-start.10 = (f32[1,19,8,128]{3,2,1,0:T(8,128)S(1)}, f32[1,19,8,128]{3,2,1,0:T(8,128)S(1)}, u32[]{:S(2)}, u32[]{:S(2)}) collective-permute-start(f32[1,19,8,128]{3,2,1,0:T(8,128)S(1)} %get-tuple-element.54), channel_id=1, source_target_pairs={{0,1},{1,0},{2,3},{3,2},{4,5},{5,4},{6,7},{7,6},{8,9},{9,8},{10,11... | collective-permute-start | bytes 233480 | tf_op jit(solution)/shard_map/ppermute | solution.py:472
  29.6 4.3 %collective-permute-start.11 = (f32[1,7,8,128]{3,2,1,0:T(8,128)S(1)}, f32[1,7,8,128]{3,2,1,0:T(8,128)S(1)}, u32[]{:S(2)}, u32[]{:S(2)}) collective-permute-start(f32[1,7,8,128]{3,2,1,0:T(8,128)S(1)} %get-tuple-element.56), channel_id=1, source_target_pairs={{0,7},{1,6},{2,5},{3,4},{4,3},{5,2},{6,1},{7,0},{8,15},{9,14},{10,... | collective-permute-start | bytes 86024 | tf_op jit(solution)/shard_map/ppermute | solution.py:472
  31.8 3.3 %collective-permute-start.12 = (f32[1,7,8,128]{3,2,1,0:T(8,128)S(1)}, f32[1,7,8,128]{3,2,1,0:T(8,128)S(1)}, u32[]{:S(2)}, u32[]{:S(2)}) collective-permute-start(f32[1,7,8,128]{3,2,1,0:T(8,128)S(1)} %get-tuple-element.57), channel_id=1, source_target_pairs={{0,5},{1,4},{2,7},{3,6},{4,1},{5,0},{6,3},{7,2},{8,13},{9,12},{10,... | collective-permute-start | bytes 86024 | tf_op jit(solution)/shard_map/ppermute | solution.py:472
  32.2 3.3 %collective-permute-start.13 = (f32[1,7,8,128]{3,2,1,0:T(8,128)S(1)}, f32[1,7,8,128]{3,2,1,0:T(8,128)S(1)}, u32[]{:S(2)}, u32[]{:S(2)}) collective-permute-start(f32[1,7,8,128]{3,2,1,0:T(8,128)S(1)} %get-tuple-element.58), channel_id=1, source_target_pairs={{0,3},{1,2},{2,1},{3,0},{4,7},{5,6},{6,5},{7,4},{8,11},{9,10},{10,... | collective-permute-start | bytes 86024 | tf_op jit(solution)/shard_map/ppermute | solution.py:472

commit v8 on v7

--- a/solution.py
+++ b/solution.py
@@ -360,7 +360,6 @@
     scratch_ref[2] = image
     spots = read_spots(spots_ref)
     u, m, y_land = half_product(p_ref, row_tiles, tiles, spots, jac_ref, land_hot_ref, index_ref, m_ref)
-    v = reduced_rows(u, m, y_land, index_ref)
 
     own_tile, own_lane = own_place(n_row, n_col, cams)
     own = load_tile(p_ref, tiles, own_tile)
@@ -372,7 +371,7 @@
     mask = own_lanes(own_lane, cams // (n_row * n_col))
     norm_next = total_sum(jnp.where(mask, own * own_residual, 0.0))
     cross = total_sum(jnp.where(mask, own * own_image, 0.0))
-    energy = energy_sum(u, v) + total_sum(own * own * damp_tile_ref[...])
+    energy = energy_sum(u, u) - total_sum(sum(y[:3] * y[:3] for y in y_land)) + total_sum(own * own * damp_tile_ref[...])
     sums_ref[...] = jnp.broadcast_to(in_lanes([energy, norm_next, cross])[None], sums_ref.shape)
     for k in each:
         solved, _ = back_solve(fac_ref, k, row_list(y_land[k], 3))
@@ -415,57 +414,65 @@
     return [jnp.where(lower, folded[2 * t], folded[2 * t + 1]) for t in range(col_tiles)]
 
 
-def core_kernel(n_row, n_col, cams, radix, pairs, *refs):
-    part_refs, out_refs, (whole_ref, ninth_ref) = refs[:radix], refs[radix:-2], refs[-2:]
+def kept_tiles(n_col, row_tiles, col_tiles, middle):
+    ys = sorted({mask % n_col // 2 for mask in middle})
+    rows = sorted({mask // n_col for mask in middle})
+    return ys, rows, (len(ys) + 1) * col_tiles + len(rows) * row_tiles
+
+
+def core_kernel(n_row, n_col, cams, lead, middle, pairs, *refs):
+    part_refs, out_refs, (whole_ref, ninth_ref) = refs[: len(lead)], refs[len(lead) : -2], refs[-2:]
     row_tiles = cams // n_row // LANES
     col_tiles = cams // n_col // LANES
     tiles = row_tiles + pairs
-    low = n_row // radix
     row, col = lax.axis_index("row"), lax.axis_index("col")
+    ys, rows, sent = kept_tiles(n_col, row_tiles, col_tiles, middle)
     for v in range(whole_ref.shape[0]):
         parts = [ref[v] for ref in part_refs]
         sums = sum(part[tiles + tiles // 8, tiles % 8 : tiles % 8 + 1] for part in parts)
         whole_ref[v] = jnp.zeros(whole_ref.shape[1:], jnp.float32)
         ninth_ref[v] = jnp.zeros(ninth_ref.shape[1:], jnp.float32)
-        for column, sources in ((col, parts[:1]), (col ^ 1, parts[1:])):
+        by_column, by_row = {}, {}
+        for mask, part in zip(lead, parts):
+            by_column.setdefault(mask % n_col, []).append(part)
+            by_row.setdefault(mask // n_col, []).append(part)
+        for bits, sources in by_column.items():
             for i, total in enumerate(column_tiles(sources, row_tiles, col_tiles, pairs)):
-                whole_ref[v, column * col_tiles + i] = total[:8]
-                ninth_ref[v, pl.ds(column * col_tiles + i, 1), :] = total[8:9]
-        for digit, part in enumerate(parts):
-            start = (row ^ (digit * low)) * row_tiles
+                whole_ref[v, (col ^ bits) * col_tiles + i] = total[:8]
+                ninth_ref[v, pl.ds((col ^ bits) * col_tiles + i, 1), :] = total[8:9]
+        for bits, sources in by_row.items():
+            total = sum(sources)
+            start = (row ^ bits) * row_tiles
             for i in range(row_tiles):
-                whole_ref[v, start + i] += part[i]
-                ninth_ref[v, pl.ds(start + i, 1), :] += part[tiles + i // 8, i % 8 : i % 8 + 1]
+                whole_ref[v, start + i] += total[i]
+                ninth_ref[v, pl.ds(start + i, 1), :] += total[tiles + i // 8, i % 8 : i % 8 + 1]
         for core, out_ref in zip((col % 2, 1 - col % 2), out_refs):
-            places = [(2 * y + 1 - core) * col_tiles + i for y in range(n_col // 2) for i in range(col_tiles)]
-            places += [(col // 2 * 2 + core) * col_tiles + i for i in range(col_tiles)]
-            places += [row // low * (low * row_tiles) + i for i in range(low * row_tiles)]
+            columns = [(col // 2 ^ y) * 2 + 1 - core for y in ys] + [col // 2 * 2 + core]
+            places = [column * col_tiles + i for column in columns for i in range(col_tiles)]
+            places += [(row ^ bits) * row_tiles + i for bits in rows for i in range(row_tiles)]
             for i, t in enumerate(places):
                 out_ref[v, i] = whole_ref[v, t]
-            write_ninths(out_ref.at[v], len(places), [ninth_ref[v, pl.ds(t, 1), :] for t in places], sums)
-
-
-def spread_kernel(n_row, n_col, cams, radix, masks, mine_ref, other_ref, *refs):
-    out_refs, total_ref = refs[:-1], refs[-1]
+            write_ninths(out_ref.at[v], sent, [ninth_ref[v, pl.ds(t, 1), :] for t in places], sums)
+
+
+def spread_kernel(n_row, n_col, cams, middle, mine_ref, other_ref, *out_refs):
     row_tiles = cams // n_row // LANES
     col_tiles = cams // n_col // LANES
     tiles = row_tiles + col_tiles
-    low = n_row // radix
-    col_sent = n_col // 2 * col_tiles
-    sent = col_sent + col_tiles + low * row_tiles
-    row, col = lax.axis_index("row") % low, lax.axis_index("col") // 2
-    for v in range(total_ref.shape[0]):
+    ys, rows, sent = kept_tiles(n_col, row_tiles, col_tiles, middle)
+    for v in range(mine_ref.shape[0]):
         total = mine_ref[v] + other_ref[v]
-        total_ref[v] = total
-        sums = total[sent + sent // 8, sent % 8 : sent % 8 + 1]
-        for mask, out_ref in zip(masks, out_refs):
-            row_start = col_sent + col_tiles + (row ^ (mask // n_col)) * row_tiles
-            col_start = (col ^ (mask % n_col // 2)) * col_tiles if mask else col_sent
+
+        def ninth(t):
+            return total[sent + t // 8, t % 8 : t % 8 + 1]
+
+        for mask, out_ref in zip(middle, out_refs):
+            row_start = (len(ys) + 1) * col_tiles + rows.index(mask // n_col) * row_tiles
+            col_start = (ys.index(mask % n_col // 2) if mask else len(ys)) * col_tiles
             places = [row_start + i for i in range(row_tiles)] + [col_start + i for i in range(col_tiles)]
             for i, t in enumerate(places):
-                out_ref[v, i] = total_ref[v, t]
-            ninths = [total_ref[v, sent + t // 8, pl.ds(t % 8, 1), :] for t in places]
-            write_ninths(out_ref.at[v], tiles, ninths, sums)
+                out_ref[v, i] = total[t]
+            write_ninths(out_ref.at[v], tiles, [ninth(t) for t in places], ninth(sent))
 
 
 def exchange(x, masks, n_dev):
@@ -491,14 +498,12 @@
     def shape(*dims):
         return pltpu.VMEM(dims, f32)
 
-    radix = min(n_row, 4)
     pair_tiles = (count + 1) // 2
     part_tiles = packed(row_tiles + pair_tiles, pair_tiles)
-    low = n_row // radix
-    sent = n_col // 2 * col_tiles + col_tiles + low * row_tiles
-    lead = [digit * low * n_col + 1 for digit in range(1, radix)]
-    middle = [x * n_col + y * 2 for x in range(low) for y in range(n_col // 2)]
-    middle = middle[:1] + [mask + 1 for mask in middle[:0:-1]]
+    low = n_row // 4
+    over_z = [0] + [z * low * n_col + 1 for z in range(1, 4)]
+    over_xy = [x * n_col + y * 2 for x in range(low) for y in range(n_col // 2)]
+    over_xy = [0] + [mask + 1 for mask in over_xy[1:]]
 
     def call(kernel, operands, out_shape, scratch=(), whole=(n_row, n_col, cams), specs=None, out_specs=None):
         return pl.pallas_call(
@@ -509,23 +514,23 @@
             scratch_shapes=scratch,
         )(*operands)
 
-    def all_reduce(part):
+    def all_reduce(part, lead, middle):
         vectors = part.shape[0]
-        pieces = [part] + exchange(part, lead, n_dev)
+        sent = kept_tiles(n_col, row_tiles, col_tiles, middle)[2]
         mine, other = call(
             core_kernel,
-            tuple(map(in_vmem, pieces)),
+            tuple(map(in_vmem, [part] + exchange(part, lead[1:], n_dev))),
             (shape(vectors, packed(sent), 8, LANES),) * 2,
             (pltpu.VMEM((vectors, cams // LANES, 8, LANES), f32), pltpu.VMEM((vectors, cams // LANES, LANES), f32)),
-            (n_row, n_col, cams, radix, pair_tiles),
+            (n_row, n_col, cams, tuple(lead), tuple(middle), pair_tiles),
         )
         (other,) = exchange(other, [1], n_dev)
         to_send = call(
             spread_kernel,
             (in_vmem(mine), in_vmem(other)),
             (shape(vectors, packed(tiles), 8, LANES),) * len(middle),
-            (pltpu.VMEM((vectors, packed(sent), 8, LANES), f32),),
-            (n_row, n_col, cams, radix, tuple(middle)),
+            (),
+            (n_row, n_col, cams, tuple(middle)),
         )
         got = [to_send[0]] + [exchange(x, [mask], n_dev)[0] for x, mask in zip(to_send[1:], middle[1:])]
         return tuple(map(in_vmem, got))
@@ -557,29 +562,28 @@
         specs=[smem] + [vmem] * 6,
         out_specs=(vmem,) * 9 + (smem,),
     )
-    sums = all_reduce(part)
+    sums = all_reduce(part, over_z, over_xy[:1] + over_xy[:0:-1])
     jac, cam_hot, land_hot, index, m, fac, damp_tile, select = map(
         in_vmem, (jac, cam_hot, land_hot, index, m, fac, damp_tile, select)
     )
     spots = pltpu.with_memory_space_constraint(spots, pltpu.SMEM)
-    pieces = len(middle)
     vector = pltpu.VMEM((packed(tiles), 8, LANES), f32)
     part, back, right, precond = call(
         first_kernel,
         (spots, jac, cam_hot, land_hot, index, m, fac, damp_tile, *sums),
         (shape(1, part_tiles, 8, LANES), shape(2, 3, count, LM), vector, vector),
         (vector,),
-        (n_row, n_col, cams, pieces),
-        specs=[smem] + [vmem] * (7 + pieces),
+        (n_row, n_col, cams, len(sums)),
+        specs=[smem] + [vmem] * (7 + len(sums)),
     )
-    image = all_reduce(part)
+    image = all_reduce(part, over_z, over_xy[:1] + over_xy[:0:-1])
     partial, known, cam_flat, solved = call(
         second_kernel,
         (spots, jac, land_hot, index, m, fac, damp_tile, select, in_vmem(right), in_vmem(precond), *image),
         (shape(n_dev, 1, LANES), shape(8, LANES), shape(2, shard), shape(3, count, LM)),
         (vector, pltpu.VMEM((3, packed(tiles), 8, LANES), f32)),
-        (n_row, n_col, cams, pieces),
-        specs=[smem] + [vmem] * (9 + pieces),
+        (n_row, n_col, cams, len(image)),
+        specs=[smem] + [vmem] * (9 + len(image)),
     )
     gathered = lax.all_to_all(partial, AXES, 0, 0, tiled=True)
     cam_step, land_step = call(

time: 47.6 us -> 47.4 us (level)
  no operation moved by 1% of the time
where the time goes in v8:
time: 47.4 us; the launch traced here: 47.2 us
  starting transfers between devices  16.6 us (35%)
  waiting for transfers between devices  14.4 us (30%)
  blocking collectives  10.5 us (22%)
  Pallas kernels  5.03 us (11%)
  between operations  0.67 us (1%)
    ppermute x14, starting transfers between devices, exchange(): lax.ppermute(x, AXES, [(i, i ^ mask) for i in range(n_dev)])  16.6 us
    ppermute x14, waiting for transfers between devices, exchange(): lax.ppermute(x, AXES, [(i, i ^ mask) for i in range(n_dev)])  14.4 us
    all_to_all x1, blocking collectives, per_device(): gathered = lax.all_to_all(partial, AXES, 0, 0, tiled=True)  10.5 us
    pallas_call x8, Pallas kernels, call(): pl.pallas_call(functools.partial(kernel, *whole), out_shape=out_shape, in...  5.03 us
  transfers between devices with their start and end apart: 14, of which 12 were waited for; matrix products, arithmetic and copies ran while one was open for 0% of the time, Pallas kernels for 0%

profile of v8, /device:TPU:0, one launch (start us, length us, event | category | flops | bytes accessed | tf_op | source)
XLA Modules:
  0.0 47.2 jit_solution(6774187759245885416)
XLA Ops:
  0.6 2.4 %shard_map.86 = (f32[2,5,8,128]{3,2,1,0:T(8,128)S(1)}, f32[4,2,16,512]{3,2,1,0:T(8,128)S(1)}, bf16[4,512,128]{2,1,0:T(8,128)(2,1)S(1)}, bf16[4,512,128]{2,1,0:T(...) custom-call(s32[2,4]{1,0:T(2,128)} %bitcast.6, ...), custom_call_target="tpu_custom_call" | custom-call | tf_op jit(solution)/shard_map/pallas_call | solution.py:509
  3.0 4.6 %collective-permute-start.2 = (f32[2,5,8,128]{3,2,1,0:T(8,128)S(1)}, f32[2,5,8,128]{3,2,1,0:T(8,128)S(1)}, u32[]{:S(2)}, u32[]{:S(2)}) collective-permute-start(f32[2,5,8,128]{3,2,1,0:T(8,128)S(1)} %get-tuple-element.43.refs_0_), channel_id=1, source_target_pairs={{0,25},{1,24},{2,27},{3,26},{4,29},{5,28},{6,31},{7,30},{8,17},{9,... | collective-permute-start | bytes 122888 | tf_op jit(solution)/shard_map/ppermute | solution.py:479
  7.6 0.9 %collective-permute-start = (f32[2,5,8,128]{3,2,1,0:T(8,128)S(1)}, f32[2,5,8,128]{3,2,1,0:T(8,128)S(1)}, u32[]{:S(2)}, u32[]{:S(2)}) collective-permute-start(f32[2,5,8,128]{3,2,1,0:T(8,128)S(1)} %get-tuple-element.43.refs_0_), channel_id=1, source_target_pairs={{0,9},{1,8},{2,11},{3,10},{4,13},{5,12},{6,15},{7,14},{8,1},{9,0},... | collective-permute-start | bytes 122888 | tf_op jit(solution)/shard_map/ppermute | solution.py:479
  8.5 1.0 %collective-permute-done.2.refs_3_ = f32[2,5,8,128]{3,2,1,0:T(8,128)S(1)} collective-permute-done((f32[2,5,8,128]{3,2,1,0:T(8,128)S(1)}, f32[2,5,8,128]{3,2,1,0:T(8,128)S(1)}, u32[]{:S(2)}, u32[]{:S(2)}) %collective-permute-start.2) | collective-permute-done | bytes 40992 | tf_op jit(solution)/shard_map/ppermute | solution.py:479
  9.6 2.8 %collective-permute-done.1.refs_2_ = f32[2,5,8,128]{3,2,1,0:T(8,128)S(1)} collective-permute-done((f32[2,5,8,128]{3,2,1,0:T(8,128)S(1)}, f32[2,5,8,128]{3,2,1,0:T(8,128)S(1)}, u32[]{:S(2)}, u32[]{:S(2)}) %collective-permute-start.1) | collective-permute-done | bytes 40992 | tf_op jit(solution)/shard_map/ppermute | solution.py:479
  12.9 1.1 %collective-permute-done.3.other_ref = f32[2,19,8,128]{3,2,1,0:T(8,128)S(1)} collective-permute-done((f32[2,19,8,128]{3,2,1,0:T(8,128)S(1)}, f32[2,19,8,128]{3,2,1,0:T(8,128)S(1)}, u32[]{:S(2)}, u32[]{:S(2)}) %collective-permute-start.3) | collective-permute-done | bytes 155680 | tf_op jit(solution)/shard_map/ppermute | solution.py:479
  14.1 2.4 %collective-permute-start.4 = (f32[2,7,8,128]{3,2,1,0:T(8,128)S(1)}, f32[2,7,8,128]{3,2,1,0:T(8,128)S(1)}, u32[]{:S(2)}, u32[]{:S(2)}) collective-permute-start(f32[2,7,8,128]{3,2,1,0:T(8,128)S(1)} %get-tuple-element.47), channel_id=1, source_target_pairs={{0,7},{1,6},{2,5},{3,4},{4,3},{5,2},{6,1},{7,0},{8,15},{9,14},{10,... | collective-permute-start | bytes 172040 | tf_op jit(solution)/shard_map/ppermute | solution.py:479
  17.2 1.6 %collective-permute-done.4.refs_1_ = f32[2,7,8,128]{3,2,1,0:T(8,128)S(1)} collective-permute-done((f32[2,7,8,128]{3,2,1,0:T(8,128)S(1)}, f32[2,7,8,128]{3,2,1,0:T(8,128)S(1)}, u32[]{:S(2)}, u32[]{:S(2)}) %collective-permute-start.4) | collective-permute-done | bytes 57376 | tf_op jit(solution)/shard_map/ppermute | solution.py:479
  18.8 1.5 %collective-permute-done.5.refs_2_ = f32[2,7,8,128]{3,2,1,0:T(8,128)S(1)} collective-permute-done((f32[2,7,8,128]{3,2,1,0:T(8,128)S(1)}, f32[2,7,8,128]{3,2,1,0:T(8,128)S(1)}, u32[]{:S(2)}, u32[]{:S(2)}) %collective-permute-start.5) | collective-permute-done | bytes 57376 | tf_op jit(solution)/shard_map/ppermute | solution.py:479
  20.7 0.7 %shard_map.89 = (f32[1,5,8,128]{3,2,1,0:T(8,128)S(1)}, f32[2,3,4,128]{3,2,1,0:T(4,128)S(1)}, f32[7,8,128]{2,1,0:T(8,128)S(1)}, f32[7,8,128]{2,1,0:T(8,128)S(1)}) custom-call(s32[4,4]{1,0:T(4,128)S(4)} %get-tuple-element.34.spots_ref, f32[4,2,16,512]{3,2,1,0:T(8,128)S(1)} %get-tuple-element.35.jac_ref, ...), custom_call_target="tpu_custom_call" | custom-call | tf_op jit(solution)/shard_map/pallas_call | solution.py:509
  21.4 2.2 %collective-permute-start.9 = (f32[1,5,8,128]{3,2,1,0:T(8,128)S(1)}, f32[1,5,8,128]{3,2,1,0:T(8,128)S(1)}, u32[]{:S(2)}, u32[]{:S(2)}) collective-permute-start(f32[1,5,8,128]{3,2,1,0:T(8,128)S(1)} %get-tuple-element.52.refs_0_), channel_id=1, source_target_pairs={{0,25},{1,24},{2,27},{3,26},{4,29},{5,28},{6,31},{7,30},{8,17},{9,... | collective-permute-start | bytes 61448 | tf_op jit(solution)/shard_map/ppermute | solution.py:479
  23.6 0.5 %collective-permute-start.8 = (f32[1,5,8,128]{3,2,1,0:T(8,128)S(1)}, f32[1,5,8,128]{3,2,1,0:T(8,128)S(1)}, u32[]{:S(2)}, u32[]{:S(2)}) collective-permute-start(f32[1,5,8,128]{3,2,1,0:T(8,128)S(1)} %get-tuple-element.52.refs_0_), channel_id=1, source_target_pairs={{0,17},{1,16},{2,19},{3,18},{4,21},{5,20},{6,23},{7,22},{8,25},{9,... | collective-permute-start | bytes 61448 | tf_op jit(solution)/shard_map/ppermute | solution.py:479
  24.1 1.2 %collective-permute-start.7 = (f32[1,5,8,128]{3,2,1,0:T(8,128)S(1)}, f32[1,5,8,128]{3,2,1,0:T(8,128)S(1)}, u32[]{:S(2)}, u32[]{:S(2)}) collective-permute-start(f32[1,5,8,128]{3,2,1,0:T(8,128)S(1)} %get-tuple-element.52.refs_0_), channel_id=1, source_target_pairs={{0,9},{1,8},{2,11},{3,10},{4,13},{5,12},{6,15},{7,14},{8,1},{9,0},... | collective-permute-start | bytes 61448 | tf_op jit(solution)/shard_map/ppermute | solution.py:479
  25.4 1.1 %collective-permute-done.9.refs_3_ = f32[1,5,8,128]{3,2,1,0:T(8,128)S(1)} collective-permute-done((f32[1,5,8,128]{3,2,1,0:T(8,128)S(1)}, f32[1,5,8,128]{3,2,1,0:T(8,128)S(1)}, u32[]{:S(2)}, u32[]{:S(2)}) %collective-permute-start.9) | collective-permute-done | bytes 20512 | tf_op jit(solution)/shard_map/ppermute | solution.py:479
  26.5 1.5 %collective-permute-done.8.refs_2_ = f32[1,5,8,128]{3,2,1,0:T(8,128)S(1)} collective-permute-done((f32[1,5,8,128]{3,2,1,0:T(8,128)S(1)}, f32[1,5,8,128]{3,2,1,0:T(8,128)S(1)}, u32[]{:S(2)}, u32[]{:S(2)}) %collective-permute-start.8) | collective-permute-done | bytes 20512 | tf_op jit(solution)/shard_map/ppermute | solution.py:479
  28.5 0.9 %collective-permute-done.10.other_ref = f32[1,19,8,128]{3,2,1,0:T(8,128)S(1)} collective-permute-done((f32[1,19,8,128]{3,2,1,0:T(8,128)S(1)}, f32[1,19,8,128]{3,2,1,0:T(8,128)S(1)}, u32[]{:S(2)}, u32[]{:S(2)}) %collective-permute-start.10) | collective-permute-done | bytes 77856 | tf_op jit(solution)/shard_map/ppermute | solution.py:479
  29.5 2.1 %collective-permute-start.11 = (f32[1,7,8,128]{3,2,1,0:T(8,128)S(1)}, f32[1,7,8,128]{3,2,1,0:T(8,128)S(1)}, u32[]{:S(2)}, u32[]{:S(2)}) collective-permute-start(f32[1,7,8,128]{3,2,1,0:T(8,128)S(1)} %get-tuple-element.56), channel_id=1, source_target_pairs={{0,7},{1,6},{2,5},{3,4},{4,3},{5,2},{6,1},{7,0},{8,15},{9,14},{10,... | collective-permute-start | bytes 86024 | tf_op jit(solution)/shard_map/ppermute | solution.py:479
  31.6 0.4 collective-permute-start.12
  32.0 0.7 %collective-permute-start.13 = (f32[1,7,8,128]{3,2,1,0:T(8,128)S(1)}, f32[1,7,8,128]{3,2,1,0:T(8,128)S(1)}, u32[]{:S(2)}, u32[]{:S(2)}) collective-permute-start(f32[1,7,8,128]{3,2,1,0:T(8,128)S(1)} %get-tuple-element.58), channel_id=1, source_target_pairs={{0,3},{1,2},{2,1},{3,0},{4,7},{5,6},{6,5},{7,4},{8,11},{9,10},{10,... | collective-permute-start | bytes 86024 | tf_op jit(solution)/shard_map/ppermute | solution.py:479
  32.7 1.0 %collective-permute-done.11.refs_1_ = f32[1,7,8,128]{3,2,1,0:T(8,128)S(1)} collective-permute-done((f32[1,7,8,128]{3,2,1,0:T(8,128)S(1)}, f32[1,7,8,128]{3,2,1,0:T(8,128)S(1)}, u32[]{:S(2)}, u32[]{:S(2)}) %collective-permute-start.11) | collective-permute-done | bytes 28704 | tf_op jit(solution)/shard_map/ppermute | solution.py:479
  33.7 1.1 %collective-permute-done.12.refs_2_ = f32[1,7,8,128]{3,2,1,0:T(8,128)S(1)} collective-permute-done((f32[1,7,8,128]{3,2,1,0:T(8,128)S(1)}, f32[1,7,8,128]{3,2,1,0:T(8,128)S(1)}, u32[]{:S(2)}, u32[]{:S(2)}) %collective-permute-start.12) | collective-permute-done | bytes 28704 | tf_op jit(solution)/shard_map/ppermute | solution.py:479
  35.3 0.7 %shard_map.92 = (f32[32,1,128]{2,1,0:T(1,128)S(1)}, f32[8,128]{1,0:T(8,128)S(1)}, f32[2,576]{1,0:T(2,128)S(1)}, f32[3,4,128]{2,1,0:T(4,128)S(1)}) custom-call(s32[4,4]{1,0:T(4,128)S(4)} %get-tuple-element.34.spots_ref, f32[4,2,16,512]{3,2,1,0:T(8,128)S(1)} %get-tuple-element.35.jac_ref, bf16[4,512,128]{2,1,0:T(8,128)(2,1)S(1)} %get-tuple-element.36.land_hot_ref, ...), custom_call_target="tpu_custom_call" | custom-call | tf_op jit(solution)/shard_map/pallas_call | solution.py:509
  36.0 10.5 %all_to_all.5.sums_ref = f32[32,1,128]{2,1,0:T(1,128)S(1)} all-to-all(f32[32,1,128]{2,1,0:T(1,128)S(1)} %get-tuple-element.59), channel_id=1, replica_groups=mesh['row'=8,'col'=4] {'row','col'}, dimensions={0} | all-to-all | bytes 32768 | tf_op jit(solution)/shard_map/all_to_all | solution.py:588
  46.5 0.7 %shard_map.93 = (f32[576]{0:T(1024)}, f32[3,4,128]{2,1,0:T(4,128)}) custom-call(f32[32,1,128]{2,1,0:T(1,128)S(1)} %all_to_all.5.sums_ref, f32[8,128]{1,0:T(8,128)S(1)} %get-tuple-element.60.known_ref, f32[2,576]{1,0:T(2,128)S(1)} %get-tuple-element.61.cam_ref, f32[2,3,4,128]{3,2,1,0:T(4,128)S(1)} %get-tuple-element.62.back_ref, ...), custom_call_target="tpu_custom_call" | custom-call | tf_op jit(solution)/shard_map/pallas_call | solution.py:509
  (13 shorter events, 2.7 us)
Async XLA Ops:
  3.0 6.5 %collective-permute-start.2 = (f32[2,5,8,128]{3,2,1,0:T(8,128)S(1)}, f32[2,5,8,128]{3,2,1,0:T(8,128)S(1)}, u32[]{:S(2)}, u32[]{:S(2)}) collective-permute-start(f32[2,5,8,128]{3,2,1,0:T(8,128)S(1)} %get-tuple-element.43.refs_0_), channel_id=1, source_target_pairs={{0,25},{1,24},{2,27},{3,26},{4,29},{5,28},{6,31},{7,30},{8,17},{9,... | collective-permute-start | bytes 122888 | tf_op jit(solution)/shard_map/ppermute | solution.py:479
  7.6 4.7 %collective-permute-start.1 = (f32[2,5,8,128]{3,2,1,0:T(8,128)S(1)}, f32[2,5,8,128]{3,2,1,0:T(8,128)S(1)}, u32[]{:S(2)}, u32[]{:S(2)}) collective-permute-start(f32[2,5,8,128]{3,2,1,0:T(8,128)S(1)} %get-tuple-element.43.refs_0_), channel_id=1, source_target_pairs={{0,17},{1,16},{2,19},{3,18},{4,21},{5,20},{6,23},{7,22},{8,25},{9,... | collective-permute-start | bytes 122888 | tf_op jit(solution)/shard_map/ppermute | solution.py:479
  7.6 4.7 %collective-permute-start = (f32[2,5,8,128]{3,2,1,0:T(8,128)S(1)}, f32[2,5,8,128]{3,2,1,0:T(8,128)S(1)}, u32[]{:S(2)}, u32[]{:S(2)}) collective-permute-start(f32[2,5,8,128]{3,2,1,0:T(8,128)S(1)} %get-tuple-element.43.refs_0_), channel_id=1, source_target_pairs={{0,9},{1,8},{2,11},{3,10},{4,13},{5,12},{6,15},{7,14},{8,1},{9,0},... | collective-permute-start | bytes 122888 | tf_op jit(solution)/shard_map/ppermute | solution.py:479
  12.6 1.4 %collective-permute-start.3 = (f32[2,19,8,128]{3,2,1,0:T(8,128)S(1)}, f32[2,19,8,128]{3,2,1,0:T(8,128)S(1)}, u32[]{:S(2)}, u32[]{:S(2)}) collective-permute-start(f32[2,19,8,128]{3,2,1,0:T(8,128)S(1)} %get-tuple-element.45), channel_id=1, source_target_pairs={{0,1},{1,0},{2,3},{3,2},{4,5},{5,4},{6,7},{7,6},{8,9},{9,8},{10,11... | collective-permute-start | bytes 466952 | tf_op jit(solution)/shard_map/ppermute | solution.py:479
  14.1 4.8 %collective-permute-start.4 = (f32[2,7,8,128]{3,2,1,0:T(8,128)S(1)}, f32[2,7,8,128]{3,2,1,0:T(8,128)S(1)}, u32[]{:S(2)}, u32[]{:S(2)}) collective-permute-start(f32[2,7,8,128]{3,2,1,0:T(8,128)S(1)} %get-tuple-element.47), channel_id=1, source_target_pairs={{0,7},{1,6},{2,5},{3,4},{4,3},{5,2},{6,1},{7,0},{8,15},{9,14},{10,... | collective-permute-start | bytes 172040 | tf_op jit(solution)/shard_map/ppermute | solution.py:479
  16.5 3.9 %collective-permute-start.5 = (f32[2,7,8,128]{3,2,1,0:T(8,128)S(1)}, f32[2,7,8,128]{3,2,1,0:T(8,128)S(1)}, u32[]{:S(2)}, u32[]{:S(2)}) collective-permute-start(f32[2,7,8,128]{3,2,1,0:T(8,128)S(1)} %get-tuple-element.48), channel_id=1, source_target_pairs={{0,5},{1,4},{2,7},{3,6},{4,1},{5,0},{6,3},{7,2},{8,13},{9,12},{10,... | collective-permute-start | bytes 172040 | tf_op jit(solution)/shard_map/ppermute | solution.py:479
  16.8 3.8 %collective-permute-start.6 = (f32[2,7,8,128]{3,2,1,0:T(8,128)S(1)}, f32[2,7,8,128]{3,2,1,0:T(8,128)S(1)}, u32[]{:S(2)}, u32[]{:S(2)}) collective-permute-start(f32[2,7,8,128]{3,2,1,0:T(8,128)S(1)} %get-tuple-element.49), channel_id=1, source_target_pairs={{0,3},{1,2},{2,1},{3,0},{4,7},{5,6},{6,5},{7,4},{8,11},{9,10},{10,... | collective-permute-start | bytes 172040 | tf_op jit(solution)/shard_map/ppermute | solution.py:479
  21.4 5.1 %collective-permute-start.9 = (f32[1,5,8,128]{3,2,1,0:T(8,128)S(1)}, f32[1,5,8,128]{3,2,1,0:T(8,128)S(1)}, u32[]{:S(2)}, u32[]{:S(2)}) collective-permute-start(f32[1,5,8,128]{3,2,1,0:T(8,128)S(1)} %get-tuple-element.52.refs_0_), channel_id=1, source_target_pairs={{0,25},{1,24},{2,27},{3,26},{4,29},{5,28},{6,31},{7,30},{8,17},{9,... | collective-permute-start | bytes 61448 | tf_op jit(solution)/shard_map/ppermute | solution.py:479
  23.6 4.3 %collective-permute-start.8 = (f32[1,5,8,128]{3,2,1,0:T(8,128)S(1)}, f32[1,5,8,128]{3,2,1,0:T(8,128)S(1)}, u32[]{:S(2)}, u32[]{:S(2)}) collective-permute-start(f32[1,5,8,128]{3,2,1,0:T(8,128)S(1)} %get-tuple-element.52.refs_0_), channel_id=1, source_target_pairs={{0,17},{1,16},{2,19},{3,18},{4,21},{5,20},{6,23},{7,22},{8,25},{9,... | collective-permute-start | bytes 61448 | tf_op jit(solution)/shard_map/ppermute | solution.py:479
  24.1 3.8 %collective-permute-start.7 = (f32[1,5,8,128]{3,2,1,0:T(8,128)S(1)}, f32[1,5,8,128]{3,2,1,0:T(8,128)S(1)}, u32[]{:S(2)}, u32[]{:S(2)}) collective-permute-start(f32[1,5,8,128]{3,2,1,0:T(8,128)S(1)} %get-tuple-element.52.refs_0_), channel_id=1, source_target_pairs={{0,9},{1,8},{2,11},{3,10},{4,13},{5,12},{6,15},{7,14},{8,1},{9,0},... | collective-permute-start | bytes 61448 | tf_op jit(solution)/shard_map/ppermute | solution.py:479
  28.1 1.3 %collective-permute-start.10 = (f32[1,19,8,128]{3,2,1,0:T(8,128)S(1)}, f32[1,19,8,128]{3,2,1,0:T(8,128)S(1)}, u32[]{:S(2)}, u32[]{:S(2)}) collective-permute-start(f32[1,19,8,128]{3,2,1,0:T(8,128)S(1)} %get-tuple-element.54), channel_id=1, source_target_pairs={{0,1},{1,0},{2,3},{3,2},{4,5},{5,4},{6,7},{7,6},{8,9},{9,8},{10,11... | collective-permute-start | bytes 233480 | tf_op jit(solution)/shard_map/ppermute | solution.py:479
  29.5 4.3 %collective-permute-start.11 = (f32[1,7,8,128]{3,2,1,0:T(8,128)S(1)}, f32[1,7,8,128]{3,2,1,0:T(8,128)S(1)}, u32[]{:S(2)}, u32[]{:S(2)}) collective-permute-start(f32[1,7,8,128]{3,2,1,0:T(8,128)S(1)} %get-tuple-element.56), channel_id=1, source_target_pairs={{0,7},{1,6},{2,5},{3,4},{4,3},{5,2},{6,1},{7,0},{8,15},{9,14},{10,... | collective-permute-start | bytes 86024 | tf_op jit(solution)/shard_map/ppermute | solution.py:479
  31.6 3.3 %collective-permute-start.12 = (f32[1,7,8,128]{3,2,1,0:T(8,128)S(1)}, f32[1,7,8,128]{3,2,1,0:T(8,128)S(1)}, u32[]{:S(2)}, u32[]{:S(2)}) collective-permute-start(f32[1,7,8,128]{3,2,1,0:T(8,128)S(1)} %get-tuple-element.57), channel_id=1, source_target_pairs={{0,5},{1,4},{2,7},{3,6},{4,1},{5,0},{6,3},{7,2},{8,13},{9,12},{10,... | collective-permute-start | bytes 86024 | tf_op jit(solution)/shard_map/ppermute | solution.py:479
  32.0 3.3 %collective-permute-start.13 = (f32[1,7,8,128]{3,2,1,0:T(8,128)S(1)}, f32[1,7,8,128]{3,2,1,0:T(8,128)S(1)}, u32[]{:S(2)}, u32[]{:S(2)}) collective-permute-start(f32[1,7,8,128]{3,2,1,0:T(8,128)S(1)} %get-tuple-element.58), channel_id=1, source_target_pairs={{0,3},{1,2},{2,1},{3,0},{4,7},{5,6},{6,5},{7,4},{8,11},{9,10},{10,... | collective-permute-start | bytes 86024 | tf_op jit(solution)/shard_map/ppermute | solution.py:479

commit v9 on v8

--- a/solution.py
+++ b/solution.py
@@ -102,7 +102,8 @@
 
 
 def load_tile(ref, tiles, t):
-    ninth = ref[tiles + t // 8, pl.ds(t % 8, 1), :]
+    here = lax.broadcasted_iota(jnp.int32, (8, LANES), 0) == t % 8
+    ninth = jnp.sum(jnp.where(here, ref[tiles + t // 8], 0.0), axis=0, keepdims=True)
     return jnp.concatenate([ref[t], ninth, jnp.zeros((7, LANES), jnp.float32)], axis=0)
 
 
@@ -400,18 +401,20 @@
     def row(part, i):
         return part[tiles + i // 8, i % 8 : i % 8 + 1]
 
-    halves = []
-    for part in parts:
-        for i in range(pairs):
-            t = row_tiles + i
-            value = jnp.concatenate([part[t], row(part, t), jnp.zeros((7, LANES), jnp.float32)], axis=0)
-            halves.append((row(part, tiles + 1 + i), value))
-    folded = []
+    halves = [(row(part, tiles + 1 + i), part[row_tiles + i]) for part in parts for i in range(pairs)]
+    ids = jnp.concatenate([group for group, _ in halves], axis=0)
+    rows = jnp.concatenate([row(part, row_tiles + i) for part in parts for i in range(pairs)], axis=0)
+    folded, ninths = [], []
     for group in range(2 * col_tiles):
-        total = sum(jnp.where(ids == float(group), value, 0.0) for ids, value in halves)
+        total = sum(jnp.where(group_row == float(group), value, 0.0) for group_row, value in halves)
+        ninth = jnp.sum(jnp.where(ids == float(group), rows, 0.0), axis=0, keepdims=True)
         folded.append(total + pltpu.roll(total, CAM, 1))
-    lower = lane_ids(16) < CAM
-    return [jnp.where(lower, folded[2 * t], folded[2 * t + 1]) for t in range(col_tiles)]
+        ninths.append(ninth + pltpu.roll(ninth, CAM, 1))
+    lower = lane_ids(8) < CAM
+    return [
+        (jnp.where(lower, folded[2 * t], folded[2 * t + 1]), jnp.where(lower[:1], ninths[2 * t], ninths[2 * t + 1]))
+        for t in range(col_tiles)
+    ]
 
 
 def kept_tiles(n_col, row_tiles, col_tiles, middle):
@@ -437,9 +440,11 @@
             by_column.setdefault(mask % n_col, []).append(part)
             by_row.setdefault(mask // n_col, []).append(part)
         for bits, sources in by_column.items():
-            for i, total in enumerate(column_tiles(sources, row_tiles, col_tiles, pairs)):
-                whole_ref[v, (col ^ bits) * col_tiles + i] = total[:8]
-                ninth_ref[v, pl.ds((col ^ bits) * col_tiles + i, 1), :] = total[8:9]
+            totals = column_tiles(sources, row_tiles, col_tiles, pairs)
+            start = (col ^ bits) * col_tiles
+            for i, total in enumerate(totals):
+                whole_ref[v, start + i] = total[0]
+            ninth_ref[v, pl.ds(start, col_tiles), :] = jnp.concatenate([total[1] for total in totals], axis=0)
         for bits, sources in by_row.items():
             total = sum(sources)
             start = (row ^ bits) * row_tiles
@@ -448,11 +453,20 @@
                 ninth_ref[v, pl.ds(start + i, 1), :] += total[tiles + i // 8, i % 8 : i % 8 + 1]
         for core, out_ref in zip((col % 2, 1 - col % 2), out_refs):
             columns = [(col // 2 ^ y) * 2 + 1 - core for y in ys] + [col // 2 * 2 + core]
-            places = [column * col_tiles + i for column in columns for i in range(col_tiles)]
-            places += [(row ^ bits) * row_tiles + i for bits in rows for i in range(row_tiles)]
-            for i, t in enumerate(places):
-                out_ref[v, i] = whole_ref[v, t]
-            write_ninths(out_ref.at[v], sent, [ninth_ref[v, pl.ds(t, 1), :] for t in places], sums)
+            runs = [(column * col_tiles, col_tiles) for column in columns]
+            runs += [((row ^ bits) * row_tiles, row_tiles) for bits in rows]
+            for i in range(sent, packed(sent)):
+                out_ref[v, i] = jnp.zeros((8, LANES), jnp.float32)
+            place = 0
+            for start, length in runs:
+                for i in range(length):
+                    out_ref[v, place + i] = whole_ref[v, start + i]
+                step = length if place % 8 + length <= 8 else 1
+                for i in range(0, length, step):
+                    at = place + i
+                    out_ref[v, sent + at // 8, at % 8 : at % 8 + step, :] = ninth_ref[v, pl.ds(start + i, step), :]
+                place += length
+            out_ref[v, sent + sent // 8, sent % 8 : sent % 8 + 1, :] = sums
 
 
 def spread_kernel(n_row, n_col, cams, middle, mine_ref, other_ref, *out_refs):
@@ -521,7 +535,7 @@
             core_kernel,
             tuple(map(in_vmem, [part] + exchange(part, lead[1:], n_dev))),
             (shape(vectors, packed(sent), 8, LANES),) * 2,
-            (pltpu.VMEM((vectors, cams // LANES, 8, LANES), f32), pltpu.VMEM((vectors, cams // LANES, LANES), f32)),
+            (pltpu.VMEM((vectors, cams // LANES, 8, LANES), f32), pltpu.VMEM((vectors, cams // LANES + 8, LANES), f32)),
             (n_row, n_col, cams, tuple(lead), tuple(middle), pair_tiles),
         )
         (other,) = exchange(other, [1], n_dev)

time: 47.4 us -> 47.4 us (level)
  no operation moved by 1% of the time
where the time goes in v9:
time: 47.4 us; the launch traced here: 47.2 us
  starting transfers between devices  16.6 us (35%)
  waiting for transfers between devices  14.4 us (30%)
  blocking collectives  10.5 us (22%)
  Pallas kernels  4.97 us (10%)
  between operations  0.67 us (1%)
    ppermute x14, starting transfers between devices, exchange(): lax.ppermute(x, AXES, [(i, i ^ mask) for i in range(n_dev)])  16.6 us
    ppermute x14, waiting for transfers between devices, exchange(): lax.ppermute(x, AXES, [(i, i ^ mask) for i in range(n_dev)])  14.4 us
    all_to_all x1, blocking collectives, per_device(): gathered = lax.all_to_all(partial, AXES, 0, 0, tiled=True)  10.5 us
    pallas_call x8, Pallas kernels, call(): pl.pallas_call(functools.partial(kernel, *whole), out_shape=out_shape, in...  4.97 us
  transfers between devices with their start and end apart: 14, of which 12 were waited for; matrix products, arithmetic and copies ran while one was open for 0% of the time, Pallas kernels for 0%

profile of v9, /device:TPU:0, one launch (start us, length us, event | category | flops | bytes accessed | tf_op | source)
XLA Modules:
  0.0 47.2 jit_solution(10946006054670458694)
XLA Ops:
  0.6 2.4 %shard_map.86 = (f32[2,5,8,128]{3,2,1,0:T(8,128)S(1)}, f32[4,2,16,512]{3,2,1,0:T(8,128)S(1)}, bf16[4,512,128]{2,1,0:T(8,128)(2,1)S(1)}, bf16[4,512,128]{2,1,0:T(...) custom-call(s32[2,4]{1,0:T(2,128)} %bitcast.6, ...), custom_call_target="tpu_custom_call" | custom-call | tf_op jit(solution)/shard_map/pallas_call | solution.py:523
  3.0 4.6 %collective-permute-start.2 = (f32[2,5,8,128]{3,2,1,0:T(8,128)S(1)}, f32[2,5,8,128]{3,2,1,0:T(8,128)S(1)}, u32[]{:S(2)}, u32[]{:S(2)}) collective-permute-start(f32[2,5,8,128]{3,2,1,0:T(8,128)S(1)} %get-tuple-element.43.refs_0_), channel_id=1, source_target_pairs={{0,25},{1,24},{2,27},{3,26},{4,29},{5,28},{6,31},{7,30},{8,17},{9,... | collective-permute-start | bytes 122888 | tf_op jit(solution)/shard_map/ppermute | solution.py:493
  7.6 0.9 %collective-permute-start = (f32[2,5,8,128]{3,2,1,0:T(8,128)S(1)}, f32[2,5,8,128]{3,2,1,0:T(8,128)S(1)}, u32[]{:S(2)}, u32[]{:S(2)}) collective-permute-start(f32[2,5,8,128]{3,2,1,0:T(8,128)S(1)} %get-tuple-element.43.refs_0_), channel_id=1, source_target_pairs={{0,9},{1,8},{2,11},{3,10},{4,13},{5,12},{6,15},{7,14},{8,1},{9,0},... | collective-permute-start | bytes 122888 | tf_op jit(solution)/shard_map/ppermute | solution.py:493
  8.5 1.0 %collective-permute-done.2.refs_3_ = f32[2,5,8,128]{3,2,1,0:T(8,128)S(1)} collective-permute-done((f32[2,5,8,128]{3,2,1,0:T(8,128)S(1)}, f32[2,5,8,128]{3,2,1,0:T(8,128)S(1)}, u32[]{:S(2)}, u32[]{:S(2)}) %collective-permute-start.2) | collective-permute-done | bytes 40992 | tf_op jit(solution)/shard_map/ppermute | solution.py:493
  9.6 2.8 %collective-permute-done.1.refs_2_ = f32[2,5,8,128]{3,2,1,0:T(8,128)S(1)} collective-permute-done((f32[2,5,8,128]{3,2,1,0:T(8,128)S(1)}, f32[2,5,8,128]{3,2,1,0:T(8,128)S(1)}, u32[]{:S(2)}, u32[]{:S(2)}) %collective-permute-start.1) | collective-permute-done | bytes 40992 | tf_op jit(solution)/shard_map/ppermute | solution.py:493
  12.9 1.1 %collective-permute-done.3.other_ref = f32[2,19,8,128]{3,2,1,0:T(8,128)S(1)} collective-permute-done((f32[2,19,8,128]{3,2,1,0:T(8,128)S(1)}, f32[2,19,8,128]{3,2,1,0:T(8,128)S(1)}, u32[]{:S(2)}, u32[]{:S(2)}) %collective-permute-start.3) | collective-permute-done | bytes 155680 | tf_op jit(solution)/shard_map/ppermute | solution.py:493
  14.0 2.4 %collective-permute-start.4 = (f32[2,7,8,128]{3,2,1,0:T(8,128)S(1)}, f32[2,7,8,128]{3,2,1,0:T(8,128)S(1)}, u32[]{:S(2)}, u32[]{:S(2)}) collective-permute-start(f32[2,7,8,128]{3,2,1,0:T(8,128)S(1)} %get-tuple-element.47), channel_id=1, source_target_pairs={{0,7},{1,6},{2,5},{3,4},{4,3},{5,2},{6,1},{7,0},{8,15},{9,14},{10,... | collective-permute-start | bytes 172040 | tf_op jit(solution)/shard_map/ppermute | solution.py:493
  17.2 1.6 %collective-permute-done.4.refs_1_ = f32[2,7,8,128]{3,2,1,0:T(8,128)S(1)} collective-permute-done((f32[2,7,8,128]{3,2,1,0:T(8,128)S(1)}, f32[2,7,8,128]{3,2,1,0:T(8,128)S(1)}, u32[]{:S(2)}, u32[]{:S(2)}) %collective-permute-start.4) | collective-permute-done | bytes 57376 | tf_op jit(solution)/shard_map/ppermute | solution.py:493
  18.8 1.5 %collective-permute-done.5.refs_2_ = f32[2,7,8,128]{3,2,1,0:T(8,128)S(1)} collective-permute-done((f32[2,7,8,128]{3,2,1,0:T(8,128)S(1)}, f32[2,7,8,128]{3,2,1,0:T(8,128)S(1)}, u32[]{:S(2)}, u32[]{:S(2)}) %collective-permute-start.5) | collective-permute-done | bytes 57376 | tf_op jit(solution)/shard_map/ppermute | solution.py:493
  20.6 0.7 %shard_map.89 = (f32[1,5,8,128]{3,2,1,0:T(8,128)S(1)}, f32[2,3,4,128]{3,2,1,0:T(4,128)S(1)}, f32[7,8,128]{2,1,0:T(8,128)S(1)}, f32[7,8,128]{2,1,0:T(8,128)S(1)}) custom-call(s32[4,4]{1,0:T(4,128)S(4)} %get-tuple-element.34.spots_ref, f32[4,2,16,512]{3,2,1,0:T(8,128)S(1)} %get-tuple-element.35.jac_ref, ...), custom_call_target="tpu_custom_call" | custom-call | tf_op jit(solution)/shard_map/pallas_call | solution.py:523
  21.4 2.2 %collective-permute-start.9 = (f32[1,5,8,128]{3,2,1,0:T(8,128)S(1)}, f32[1,5,8,128]{3,2,1,0:T(8,128)S(1)}, u32[]{:S(2)}, u32[]{:S(2)}) collective-permute-start(f32[1,5,8,128]{3,2,1,0:T(8,128)S(1)} %get-tuple-element.52.refs_0_), channel_id=1, source_target_pairs={{0,25},{1,24},{2,27},{3,26},{4,29},{5,28},{6,31},{7,30},{8,17},{9,... | collective-permute-start | bytes 61448 | tf_op jit(solution)/shard_map/ppermute | solution.py:493
  23.6 0.5 %collective-permute-start.8 = (f32[1,5,8,128]{3,2,1,0:T(8,128)S(1)}, f32[1,5,8,128]{3,2,1,0:T(8,128)S(1)}, u32[]{:S(2)}, u32[]{:S(2)}) collective-permute-start(f32[1,5,8,128]{3,2,1,0:T(8,128)S(1)} %get-tuple-element.52.refs_0_), channel_id=1, source_target_pairs={{0,17},{1,16},{2,19},{3,18},{4,21},{5,20},{6,23},{7,22},{8,25},{9,... | collective-permute-start | bytes 61448 | tf_op jit(solution)/shard_map/ppermute | solution.py:493
  24.1 1.2 %collective-permute-start.7 = (f32[1,5,8,128]{3,2,1,0:T(8,128)S(1)}, f32[1,5,8,128]{3,2,1,0:T(8,128)S(1)}, u32[]{:S(2)}, u32[]{:S(2)}) collective-permute-start(f32[1,5,8,128]{3,2,1,0:T(8,128)S(1)} %get-tuple-element.52.refs_0_), channel_id=1, source_target_pairs={{0,9},{1,8},{2,11},{3,10},{4,13},{5,12},{6,15},{7,14},{8,1},{9,0},... | collective-permute-start | bytes 61448 | tf_op jit(solution)/shard_map/ppermute | solution.py:493
  25.3 1.1 %collective-permute-done.9.refs_3_ = f32[1,5,8,128]{3,2,1,0:T(8,128)S(1)} collective-permute-done((f32[1,5,8,128]{3,2,1,0:T(8,128)S(1)}, f32[1,5,8,128]{3,2,1,0:T(8,128)S(1)}, u32[]{:S(2)}, u32[]{:S(2)}) %collective-permute-start.9) | collective-permute-done | bytes 20512 | tf_op jit(solution)/shard_map/ppermute | solution.py:493
  26.4 1.5 %collective-permute-done.8.refs_2_ = f32[1,5,8,128]{3,2,1,0:T(8,128)S(1)} collective-permute-done((f32[1,5,8,128]{3,2,1,0:T(8,128)S(1)}, f32[1,5,8,128]{3,2,1,0:T(8,128)S(1)}, u32[]{:S(2)}, u32[]{:S(2)}) %collective-permute-start.8) | collective-permute-done | bytes 20512 | tf_op jit(solution)/shard_map/ppermute | solution.py:493
  28.1 0.4 collective-permute-start.10
  28.5 0.9 %collective-permute-done.10.other_ref = f32[1,19,8,128]{3,2,1,0:T(8,128)S(1)} collective-permute-done((f32[1,19,8,128]{3,2,1,0:T(8,128)S(1)}, f32[1,19,8,128]{3,2,1,0:T(8,128)S(1)}, u32[]{:S(2)}, u32[]{:S(2)}) %collective-permute-start.10) | collective-permute-done | bytes 77856 | tf_op jit(solution)/shard_map/ppermute | solution.py:493
  29.4 2.1 %collective-permute-start.11 = (f32[1,7,8,128]{3,2,1,0:T(8,128)S(1)}, f32[1,7,8,128]{3,2,1,0:T(8,128)S(1)}, u32[]{:S(2)}, u32[]{:S(2)}) collective-permute-start(f32[1,7,8,128]{3,2,1,0:T(8,128)S(1)} %get-tuple-element.56), channel_id=1, source_target_pairs={{0,7},{1,6},{2,5},{3,4},{4,3},{5,2},{6,1},{7,0},{8,15},{9,14},{10,... | collective-permute-start | bytes 86024 | tf_op jit(solution)/shard_map/ppermute | solution.py:493
  32.0 0.7 %collective-permute-start.13 = (f32[1,7,8,128]{3,2,1,0:T(8,128)S(1)}, f32[1,7,8,128]{3,2,1,0:T(8,128)S(1)}, u32[]{:S(2)}, u32[]{:S(2)}) collective-permute-start(f32[1,7,8,128]{3,2,1,0:T(8,128)S(1)} %get-tuple-element.58), channel_id=1, source_target_pairs={{0,3},{1,2},{2,1},{3,0},{4,7},{5,6},{6,5},{7,4},{8,11},{9,10},{10,... | collective-permute-start | bytes 86024 | tf_op jit(solution)/shard_map/ppermute | solution.py:493
  32.6 1.0 %collective-permute-done.11.refs_1_ = f32[1,7,8,128]{3,2,1,0:T(8,128)S(1)} collective-permute-done((f32[1,7,8,128]{3,2,1,0:T(8,128)S(1)}, f32[1,7,8,128]{3,2,1,0:T(8,128)S(1)}, u32[]{:S(2)}, u32[]{:S(2)}) %collective-permute-start.11) | collective-permute-done | bytes 28704 | tf_op jit(solution)/shard_map/ppermute | solution.py:493
  33.7 1.2 %collective-permute-done.12.refs_2_ = f32[1,7,8,128]{3,2,1,0:T(8,128)S(1)} collective-permute-done((f32[1,7,8,128]{3,2,1,0:T(8,128)S(1)}, f32[1,7,8,128]{3,2,1,0:T(8,128)S(1)}, u32[]{:S(2)}, u32[]{:S(2)}) %collective-permute-start.12) | collective-permute-done | bytes 28704 | tf_op jit(solution)/shard_map/ppermute | solution.py:493
  35.2 0.7 %shard_map.92 = (f32[32,1,128]{2,1,0:T(1,128)S(1)}, f32[8,128]{1,0:T(8,128)S(1)}, f32[2,576]{1,0:T(2,128)S(1)}, f32[3,4,128]{2,1,0:T(4,128)S(1)}) custom-call(s32[4,4]{1,0:T(4,128)S(4)} %get-tuple-element.34.spots_ref, f32[4,2,16,512]{3,2,1,0:T(8,128)S(1)} %get-tuple-element.35.jac_ref, bf16[4,512,128]{2,1,0:T(8,128)(2,1)S(1)} %get-tuple-element.36.land_hot_ref, ...), custom_call_target="tpu_custom_call" | custom-call | tf_op jit(solution)/shard_map/pallas_call | solution.py:523
  35.9 10.5 %all_to_all.5.sums_ref = f32[32,1,128]{2,1,0:T(1,128)S(1)} all-to-all(f32[32,1,128]{2,1,0:T(1,128)S(1)} %get-tuple-element.59), channel_id=1, replica_groups=mesh['row'=8,'col'=4] {'row','col'}, dimensions={0} | all-to-all | bytes 32768 | tf_op jit(solution)/shard_map/all_to_all | solution.py:602
  46.5 0.7 %shard_map.93 = (f32[576]{0:T(1024)}, f32[3,4,128]{2,1,0:T(4,128)}) custom-call(f32[32,1,128]{2,1,0:T(1,128)S(1)} %all_to_all.5.sums_ref, f32[8,128]{1,0:T(8,128)S(1)} %get-tuple-element.60.known_ref, f32[2,576]{1,0:T(2,128)S(1)} %get-tuple-element.61.cam_ref, f32[2,3,4,128]{3,2,1,0:T(4,128)S(1)} %get-tuple-element.62.back_ref, ...), custom_call_target="tpu_custom_call" | custom-call | tf_op jit(solution)/shard_map/pallas_call | solution.py:523
  (13 shorter events, 2.6 us)
Async XLA Ops:
  3.0 6.5 %collective-permute-start.2 = (f32[2,5,8,128]{3,2,1,0:T(8,128)S(1)}, f32[2,5,8,128]{3,2,1,0:T(8,128)S(1)}, u32[]{:S(2)}, u32[]{:S(2)}) collective-permute-start(f32[2,5,8,128]{3,2,1,0:T(8,128)S(1)} %get-tuple-element.43.refs_0_), channel_id=1, source_target_pairs={{0,25},{1,24},{2,27},{3,26},{4,29},{5,28},{6,31},{7,30},{8,17},{9,... | collective-permute-start | bytes 122888 | tf_op jit(solution)/shard_map/ppermute | solution.py:493
  7.6 4.7 %collective-permute-start.1 = (f32[2,5,8,128]{3,2,1,0:T(8,128)S(1)}, f32[2,5,8,128]{3,2,1,0:T(8,128)S(1)}, u32[]{:S(2)}, u32[]{:S(2)}) collective-permute-start(f32[2,5,8,128]{3,2,1,0:T(8,128)S(1)} %get-tuple-element.43.refs_0_), channel_id=1, source_target_pairs={{0,17},{1,16},{2,19},{3,18},{4,21},{5,20},{6,23},{7,22},{8,25},{9,... | collective-permute-start | bytes 122888 | tf_op jit(solution)/shard_map/ppermute | solution.py:493
  7.6 4.7 %collective-permute-start = (f32[2,5,8,128]{3,2,1,0:T(8,128)S(1)}, f32[2,5,8,128]{3,2,1,0:T(8,128)S(1)}, u32[]{:S(2)}, u32[]{:S(2)}) collective-permute-start(f32[2,5,8,128]{3,2,1,0:T(8,128)S(1)} %get-tuple-element.43.refs_0_), channel_id=1, source_target_pairs={{0,9},{1,8},{2,11},{3,10},{4,13},{5,12},{6,15},{7,14},{8,1},{9,0},... | collective-permute-start | bytes 122888 | tf_op jit(solution)/shard_map/ppermute | solution.py:493
  12.5 1.4 %collective-permute-start.3 = (f32[2,19,8,128]{3,2,1,0:T(8,128)S(1)}, f32[2,19,8,128]{3,2,1,0:T(8,128)S(1)}, u32[]{:S(2)}, u32[]{:S(2)}) collective-permute-start(f32[2,19,8,128]{3,2,1,0:T(8,128)S(1)} %get-tuple-element.45), channel_id=1, source_target_pairs={{0,1},{1,0},{2,3},{3,2},{4,5},{5,4},{6,7},{7,6},{8,9},{9,8},{10,11... | collective-permute-start | bytes 466952 | tf_op jit(solution)/shard_map/ppermute | solution.py:493
  14.0 4.8 %collective-permute-start.4 = (f32[2,7,8,128]{3,2,1,0:T(8,128)S(1)}, f32[2,7,8,128]{3,2,1,0:T(8,128)S(1)}, u32[]{:S(2)}, u32[]{:S(2)}) collective-permute-start(f32[2,7,8,128]{3,2,1,0:T(8,128)S(1)} %get-tuple-element.47), channel_id=1, source_target_pairs={{0,7},{1,6},{2,5},{3,4},{4,3},{5,2},{6,1},{7,0},{8,15},{9,14},{10,... | collective-permute-start | bytes 172040 | tf_op jit(solution)/shard_map/ppermute | solution.py:493
  16.4 3.9 %collective-permute-start.5 = (f32[2,7,8,128]{3,2,1,0:T(8,128)S(1)}, f32[2,7,8,128]{3,2,1,0:T(8,128)S(1)}, u32[]{:S(2)}, u32[]{:S(2)}) collective-permute-start(f32[2,7,8,128]{3,2,1,0:T(8,128)S(1)} %get-tuple-element.48), channel_id=1, source_target_pairs={{0,5},{1,4},{2,7},{3,6},{4,1},{5,0},{6,3},{7,2},{8,13},{9,12},{10,... | collective-permute-start | bytes 172040 | tf_op jit(solution)/shard_map/ppermute | solution.py:493
  16.8 3.8 %collective-permute-start.6 = (f32[2,7,8,128]{3,2,1,0:T(8,128)S(1)}, f32[2,7,8,128]{3,2,1,0:T(8,128)S(1)}, u32[]{:S(2)}, u32[]{:S(2)}) collective-permute-start(f32[2,7,8,128]{3,2,1,0:T(8,128)S(1)} %get-tuple-element.49), channel_id=1, source_target_pairs={{0,3},{1,2},{2,1},{3,0},{4,7},{5,6},{6,5},{7,4},{8,11},{9,10},{10,... | collective-permute-start | bytes 172040 | tf_op jit(solution)/shard_map/ppermute | solution.py:493
  21.4 5.1 %collective-permute-start.9 = (f32[1,5,8,128]{3,2,1,0:T(8,128)S(1)}, f32[1,5,8,128]{3,2,1,0:T(8,128)S(1)}, u32[]{:S(2)}, u32[]{:S(2)}) collective-permute-start(f32[1,5,8,128]{3,2,1,0:T(8,128)S(1)} %get-tuple-element.52.refs_0_), channel_id=1, source_target_pairs={{0,25},{1,24},{2,27},{3,26},{4,29},{5,28},{6,31},{7,30},{8,17},{9,... | collective-permute-start | bytes 61448 | tf_op jit(solution)/shard_map/ppermute | solution.py:493
  23.6 4.3 %collective-permute-start.8 = (f32[1,5,8,128]{3,2,1,0:T(8,128)S(1)}, f32[1,5,8,128]{3,2,1,0:T(8,128)S(1)}, u32[]{:S(2)}, u32[]{:S(2)}) collective-permute-start(f32[1,5,8,128]{3,2,1,0:T(8,128)S(1)} %get-tuple-element.52.refs_0_), channel_id=1, source_target_pairs={{0,17},{1,16},{2,19},{3,18},{4,21},{5,20},{6,23},{7,22},{8,25},{9,... | collective-permute-start | bytes 61448 | tf_op jit(solution)/shard_map/ppermute | solution.py:493
  24.1 3.8 %collective-permute-start.7 = (f32[1,5,8,128]{3,2,1,0:T(8,128)S(1)}, f32[1,5,8,128]{3,2,1,0:T(8,128)S(1)}, u32[]{:S(2)}, u32[]{:S(2)}) collective-permute-start(f32[1,5,8,128]{3,2,1,0:T(8,128)S(1)} %get-tuple-element.52.refs_0_), channel_id=1, source_target_pairs={{0,9},{1,8},{2,11},{3,10},{4,13},{5,12},{6,15},{7,14},{8,1},{9,0},... | collective-permute-start | bytes 61448 | tf_op jit(solution)/shard_map/ppermute | solution.py:493
  28.1 1.3 %collective-permute-start.10 = (f32[1,19,8,128]{3,2,1,0:T(8,128)S(1)}, f32[1,19,8,128]{3,2,1,0:T(8,128)S(1)}, u32[]{:S(2)}, u32[]{:S(2)}) collective-permute-start(f32[1,19,8,128]{3,2,1,0:T(8,128)S(1)} %get-tuple-element.54), channel_id=1, source_target_pairs={{0,1},{1,0},{2,3},{3,2},{4,5},{5,4},{6,7},{7,6},{8,9},{9,8},{10,11... | collective-permute-start | bytes 233480 | tf_op jit(solution)/shard_map/ppermute | solution.py:493
  29.4 4.3 %collective-permute-start.11 = (f32[1,7,8,128]{3,2,1,0:T(8,128)S(1)}, f32[1,7,8,128]{3,2,1,0:T(8,128)S(1)}, u32[]{:S(2)}, u32[]{:S(2)}) collective-permute-start(f32[1,7,8,128]{3,2,1,0:T(8,128)S(1)} %get-tuple-element.56), channel_id=1, source_target_pairs={{0,7},{1,6},{2,5},{3,4},{4,3},{5,2},{6,1},{7,0},{8,15},{9,14},{10,... | collective-permute-start | bytes 86024 | tf_op jit(solution)/shard_map/ppermute | solution.py:493
  31.6 3.3 %collective-permute-start.12 = (f32[1,7,8,128]{3,2,1,0:T(8,128)S(1)}, f32[1,7,8,128]{3,2,1,0:T(8,128)S(1)}, u32[]{:S(2)}, u32[]{:S(2)}) collective-permute-start(f32[1,7,8,128]{3,2,1,0:T(8,128)S(1)} %get-tuple-element.57), channel_id=1, source_target_pairs={{0,5},{1,4},{2,7},{3,6},{4,1},{5,0},{6,3},{7,2},{8,13},{9,12},{10,... | collective-permute-start | bytes 86024 | tf_op jit(solution)/shard_map/ppermute | solution.py:493
  32.0 3.3 %collective-permute-start.13 = (f32[1,7,8,128]{3,2,1,0:T(8,128)S(1)}, f32[1,7,8,128]{3,2,1,0:T(8,128)S(1)}, u32[]{:S(2)}, u32[]{:S(2)}) collective-permute-start(f32[1,7,8,128]{3,2,1,0:T(8,128)S(1)} %get-tuple-element.58), channel_id=1, source_target_pairs={{0,3},{1,2},{2,1},{3,0},{4,7},{5,6},{6,5},{7,4},{8,11},{9,10},{10,... | collective-permute-start | bytes 86024 | tf_op jit(solution)/shard_map/ppermute | solution.py:493

commit v10 on v9

--- a/solution.py
+++ b/solution.py
@@ -305,19 +305,47 @@
     return total_sum(sum(u[k][r] * v[k][r] for k in range(len(u)) for r in range(2)))
 
 
-def add_up(refs):
+def widen(x, n_row, n_col, row_tiles, col_tiles, mask):
+    low, ratio = n_row // 4, col_tiles // row_tiles
+    row, col = lax.axis_index("row"), lax.axis_index("col")
+    place = shared_row(low, ratio, col, (row ^ (mask // n_col)) % low)
+    held = 2 * row_tiles
+    vectors = []
+    for v in range(x.shape[0]):
+
+        def ninth(t):
+            return x[v, held + t // 8, t % 8 : t % 8 + 1]
+
+        tiles = [x[v, i] for i in range(row_tiles)]
+        rows = [ninth(i) for i in range(row_tiles)]
+        for j in range(ratio):
+            for i in range(row_tiles, held):
+                tiles.append(jnp.where(place == j, x[v, i], 0.0))
+                rows.append(jnp.where(place == j, ninth(i), 0.0))
+        rows.append(ninth(held))
+        tiles += [stack_rows(rows[start : start + 8], 8) for start in range(0, len(rows), 8)]
+        vectors.append(jnp.stack(tiles))
+    return jnp.stack(vectors)
+
+
+def add_up(refs, n_row, n_col, cams, middle):
+    row_tiles = cams // n_row // LANES
+    col_tiles = cams // n_col // LANES
     total = refs[0][...]
-    for ref in refs[1:]:
-        total = total + ref[...]
+    for mask, ref in zip(middle[1:], refs[1:]):
+        piece = ref[...]
+        if is_short(n_row, n_col, row_tiles, col_tiles, mask):
+            piece = widen(piece, n_row, n_col, row_tiles, col_tiles, mask)
+        total = total + piece
     return total
 
 
-def first_kernel(n_row, n_col, cams, pieces, spots_ref, jac_ref, cam_hot_ref, land_hot_ref, index_ref, m_ref, fac_ref, damp_tile_ref, *refs):
-    part_ref, back_ref, right_ref, precond_ref, p_ref = refs[pieces:]
+def first_kernel(n_row, n_col, cams, middle, spots_ref, jac_ref, cam_hot_ref, land_hot_ref, index_ref, m_ref, fac_ref, damp_tile_ref, *refs):
+    part_ref, back_ref, right_ref, precond_ref, p_ref = refs[len(middle) :]
     row_tiles = cams // n_row // LANES
     tiles = row_tiles + cams // n_col // LANES
     each = range(jac_ref.shape[0])
-    sums = add_up(refs[:pieces])
+    sums = add_up(refs[: len(middle)], n_row, n_col, cams, middle)
     right, precond = sums[0], 1.0 / sums[1]
     right_ref[...] = right
     precond_ref[...] = precond
@@ -341,13 +369,13 @@
     write_parts(part_ref.at[0], row_tiles, spots, images, (own_tile, damped), in_lanes([norm_now, energy]))
 
 
-def second_kernel(n_row, n_col, cams, pieces, spots_ref, jac_ref, land_hot_ref, index_ref, m_ref, fac_ref, damp_tile_ref, select_ref, right_ref, precond_ref, *refs):
-    sums_ref, known_ref, cam_ref, solved_ref, p_ref, scratch_ref = refs[pieces:]
+def second_kernel(n_row, n_col, cams, middle, spots_ref, jac_ref, land_hot_ref, index_ref, m_ref, fac_ref, damp_tile_ref, select_ref, right_ref, precond_ref, *refs):
+    sums_ref, known_ref, cam_ref, solved_ref, p_ref, scratch_ref = refs[len(middle) :]
     row_tiles = cams // n_row // LANES
     tiles = row_tiles + cams // n_col // LANES
     each = range(jac_ref.shape[0])
     shard = cam_ref.shape[1]
-    image = add_up(refs[:pieces])[0]
+    image = add_up(refs[: len(middle)], n_row, n_col, cams, middle)[0]
     sums = image[tiles + tiles // 8, tiles % 8 : tiles % 8 + 1]
     norm_now, energy_now = sums[:, 0:1], sums[:, 1:2]
     alpha = norm_now / energy_now
@@ -469,11 +497,21 @@
             out_ref[v, sent + sent // 8, sent % 8 : sent % 8 + 1, :] = sums
 
 
+def is_short(n_row, n_col, row_tiles, col_tiles, mask):
+    return mask % n_col > 1 and col_tiles % row_tiles == 0 and col_tiles // row_tiles <= n_row // 4
+
+
+def shared_row(low, ratio, column, digit):
+    return (digit + low * ratio * column - ratio * column) % low
+
+
 def spread_kernel(n_row, n_col, cams, middle, mine_ref, other_ref, *out_refs):
     row_tiles = cams // n_row // LANES
     col_tiles = cams // n_col // LANES
     tiles = row_tiles + col_tiles
     ys, rows, sent = kept_tiles(n_col, row_tiles, col_tiles, middle)
+    low, ratio = n_row // 4, col_tiles // row_tiles
+    row, col = lax.axis_index("row"), lax.axis_index("col")
     for v in range(mine_ref.shape[0]):
         total = mine_ref[v] + other_ref[v]
 
@@ -484,9 +522,24 @@
             row_start = (len(ys) + 1) * col_tiles + rows.index(mask // n_col) * row_tiles
             col_start = (ys.index(mask % n_col // 2) if mask else len(ys)) * col_tiles
             places = [row_start + i for i in range(row_tiles)] + [col_start + i for i in range(col_tiles)]
-            for i, t in enumerate(places):
-                out_ref[v, i] = total[t]
-            write_ninths(out_ref.at[v], tiles, [ninth(t) for t in places], ninth(sent))
+            if not is_short(n_row, n_col, row_tiles, col_tiles, mask):
+                for i, t in enumerate(places):
+                    out_ref[v, i] = total[t]
+                write_ninths(out_ref.at[v], tiles, [ninth(t) for t in places], ninth(sent))
+                continue
+            column = (col // 2 ^ (mask % n_col // 2)) * 2 + 1 - col % 2
+            place = shared_row(low, ratio, column, row % low)
+            ninths = []
+            for i in range(2 * row_tiles):
+                if i < row_tiles:
+                    value, last = total[row_start + i], ninth(row_start + i)
+                else:
+                    starts = [col_start + j * row_tiles + i - row_tiles for j in range(ratio)]
+                    value = sum(jnp.where(place == j, total[t], 0.0) for j, t in enumerate(starts))
+                    last = sum(jnp.where(place == j, ninth(t), 0.0) for j, t in enumerate(starts))
+                out_ref[v, i] = value
+                ninths.append(last)
+            write_ninths(out_ref.at[v], 2 * row_tiles, ninths, ninth(sent))
 
 
 def exchange(x, masks, n_dev):
@@ -517,7 +570,7 @@
     low = n_row // 4
     over_z = [0] + [z * low * n_col + 1 for z in range(1, 4)]
     over_xy = [x * n_col + y * 2 for x in range(low) for y in range(n_col // 2)]
-    over_xy = [0] + [mask + 1 for mask in over_xy[1:]]
+    over_xy = [0] + [mask + 1 for mask in over_xy[:0:-1]]
 
     def call(kernel, operands, out_shape, scratch=(), whole=(n_row, n_col, cams), specs=None, out_specs=None):
         return pl.pallas_call(
@@ -542,7 +595,10 @@
         to_send = call(
             spread_kernel,
             (in_vmem(mine), in_vmem(other)),
-            (shape(vectors, packed(tiles), 8, LANES),) * len(middle),
+            tuple(
+                shape(vectors, packed(2 * row_tiles if is_short(n_row, n_col, row_tiles, col_tiles, mask) else tiles), 8, LANES)
+                for mask in middle
+            ),
             (),
             (n_row, n_col, cams, tuple(middle)),
         )
@@ -576,7 +632,7 @@
         specs=[smem] + [vmem] * 6,
         out_specs=(vmem,) * 9 + (smem,),
     )
-    sums = all_reduce(part, over_z, over_xy[:1] + over_xy[:0:-1])
+    sums = all_reduce(part, over_z, over_xy)
     jac, cam_hot, land_hot, index, m, fac, damp_tile, select = map(
         in_vmem, (jac, cam_hot, land_hot, index, m, fac, damp_tile, select)
     )
@@ -587,16 +643,16 @@
         (spots, jac, cam_hot, land_hot, index, m, fac, damp_tile, *sums),
         (shape(1, part_tiles, 8, LANES), shape(2, 3, count, LM), vector, vector),
         (vector,),
-        (n_row, n_col, cams, len(sums)),
+        (n_row, n_col, cams, tuple(over_xy)),
         specs=[smem] + [vmem] * (7 + len(sums)),
     )
-    image = all_reduce(part, over_z, over_xy[:1] + over_xy[:0:-1])
+    image = all_reduce(part, over_z, over_xy)
     partial, known, cam_flat, solved = call(
         second_kernel,
         (spots, jac, land_hot, index, m, fac, damp_tile, select, in_vmem(right), in_vmem(precond), *image),
         (shape(n_dev, 1, LANES), shape(8, LANES), shape(2, shard), shape(3, count, LM)),
         (vector, pltpu.VMEM((3, packed(tiles), 8, LANES), f32)),
-        (n_row, n_col, cams, len(image)),
+        (n_row, n_col, cams, tuple(over_xy)),
         specs=[smem] + [vmem] * (9 + len(image)),
     )
     gathered = lax.all_to_all(partial, AXES, 0, 0, tiled=True)

time: 47.4 us -> 47.4 us (level)
  blocking collectives: 10.5 us -> 9.9 us
  waiting for transfers between devices: 14.4 us -> 15 us
    ppermute x14, waiting for transfers between devices: 14.4 us -> 15 us  [exchange(): lax.ppermute(x, AXES, [(i, i ^ mask) for i in range(n_dev)])]
    all_to_all x1, blocking collectives: 10.5 us -> 9.9 us  [per_device(): gathered = lax.all_to_all(partial, AXES, 0, 0, tiled=True)]
  transfers between devices with their start and end apart: 14 -> 14, of which waited for: 12 -> 10; matrix products, arithmetic and copies ran while one was open for 0% -> 0% of each run, Pallas kernels for 0% -> 0%
where the time goes in v10:
time: 47.4 us; the launch traced here: 47.3 us
  starting transfers between devices  16.6 us (35%)
  waiting for transfers between devices  15 us (32%)
  blocking collectives  9.9 us (21%)
  Pallas kernels  5.02 us (11%)
  between operations  0.68 us (1%)
    ppermute x14, starting transfers between devices, exchange(): lax.ppermute(x, AXES, [(i, i ^ mask) for i in range(n_dev)])  16.6 us
    ppermute x14, waiting for transfers between devices, exchange(): lax.ppermute(x, AXES, [(i, i ^ mask) for i in range(n_dev)])  15 us
    all_to_all x1, blocking collectives, per_device(): gathered = lax.all_to_all(partial, AXES, 0, 0, tiled=True)  9.9 us
    pallas_call x8, Pallas kernels, call(): pl.pallas_call(functools.partial(kernel, *whole), out_shape=out_shape, in...  5.02 us
  transfers between devices with their start and end apart: 14, of which 10 were waited for; matrix products, arithmetic and copies ran while one was open for 0% of the time, Pallas kernels for 0%

profile of v10, /device:TPU:0, one launch (start us, length us, event | category | flops | bytes accessed | tf_op | source)
XLA Modules:
  0.0 47.3 jit_solution(17868218630435995205)
XLA Ops:
  0.6 2.4 %shard_map.86 = (f32[2,5,8,128]{3,2,1,0:T(8,128)S(1)}, f32[4,2,16,512]{3,2,1,0:T(8,128)S(1)}, bf16[4,512,128]{2,1,0:T(8,128)(2,1)S(1)}, bf16[4,512,128]{2,1,0:T(...) custom-call(s32[2,4]{1,0:T(2,128)} %bitcast.6, ...), custom_call_target="tpu_custom_call" | custom-call | tf_op jit(solution)/shard_map/pallas_call | solution.py:576
  3.0 4.6 %collective-permute-start.2 = (f32[2,5,8,128]{3,2,1,0:T(8,128)S(1)}, f32[2,5,8,128]{3,2,1,0:T(8,128)S(1)}, u32[]{:S(2)}, u32[]{:S(2)}) collective-permute-start(f32[2,5,8,128]{3,2,1,0:T(8,128)S(1)} %get-tuple-element.43.refs_0_), channel_id=1, source_target_pairs={{0,25},{1,24},{2,27},{3,26},{4,29},{5,28},{6,31},{7,30},{8,17},{9,... | collective-permute-start | bytes 122888 | tf_op jit(solution)/shard_map/ppermute | solution.py:546
  7.6 0.9 %collective-permute-start = (f32[2,5,8,128]{3,2,1,0:T(8,128)S(1)}, f32[2,5,8,128]{3,2,1,0:T(8,128)S(1)}, u32[]{:S(2)}, u32[]{:S(2)}) collective-permute-start(f32[2,5,8,128]{3,2,1,0:T(8,128)S(1)} %get-tuple-element.43.refs_0_), channel_id=1, source_target_pairs={{0,9},{1,8},{2,11},{3,10},{4,13},{5,12},{6,15},{7,14},{8,1},{9,0},... | collective-permute-start | bytes 122888 | tf_op jit(solution)/shard_map/ppermute | solution.py:546
  8.5 1.0 %collective-permute-done.2.refs_3_ = f32[2,5,8,128]{3,2,1,0:T(8,128)S(1)} collective-permute-done((f32[2,5,8,128]{3,2,1,0:T(8,128)S(1)}, f32[2,5,8,128]{3,2,1,0:T(8,128)S(1)}, u32[]{:S(2)}, u32[]{:S(2)}) %collective-permute-start.2) | collective-permute-done | bytes 40992 | tf_op jit(solution)/shard_map/ppermute | solution.py:546
  9.6 2.8 %collective-permute-done.1.refs_2_ = f32[2,5,8,128]{3,2,1,0:T(8,128)S(1)} collective-permute-done((f32[2,5,8,128]{3,2,1,0:T(8,128)S(1)}, f32[2,5,8,128]{3,2,1,0:T(8,128)S(1)}, u32[]{:S(2)}, u32[]{:S(2)}) %collective-permute-start.1) | collective-permute-done | bytes 40992 | tf_op jit(solution)/shard_map/ppermute | solution.py:546
  12.9 1.1 %collective-permute-done.3.other_ref = f32[2,19,8,128]{3,2,1,0:T(8,128)S(1)} collective-permute-done((f32[2,19,8,128]{3,2,1,0:T(8,128)S(1)}, f32[2,19,8,128]{3,2,1,0:T(8,128)S(1)}, u32[]{:S(2)}, u32[]{:S(2)}) %collective-permute-start.3) | collective-permute-done | bytes 155680 | tf_op jit(solution)/shard_map/ppermute | solution.py:546
  14.0 1.4 %collective-permute-start.5 = (f32[2,7,8,128]{3,2,1,0:T(8,128)S(1)}, f32[2,7,8,128]{3,2,1,0:T(8,128)S(1)}, u32[]{:S(2)}, u32[]{:S(2)}) collective-permute-start(f32[2,7,8,128]{3,2,1,0:T(8,128)S(1)} %get-tuple-element.48), channel_id=1, source_target_pairs={{0,5},{1,4},{2,7},{3,6},{4,1},{5,0},{6,3},{7,2},{8,13},{9,12},{10,... | collective-permute-start | bytes 172040 | tf_op jit(solution)/shard_map/ppermute | solution.py:546
  15.5 1.3 %collective-permute-start.4 = (f32[2,5,8,128]{3,2,1,0:T(8,128)S(1)}, f32[2,5,8,128]{3,2,1,0:T(8,128)S(1)}, u32[]{:S(2)}, u32[]{:S(2)}) collective-permute-start(f32[2,5,8,128]{3,2,1,0:T(8,128)S(1)} %get-tuple-element.47), channel_id=1, source_target_pairs={{0,7},{1,6},{2,5},{3,4},{4,3},{5,2},{6,1},{7,0},{8,15},{9,14},{10,... | collective-permute-start | bytes 122888 | tf_op jit(solution)/shard_map/ppermute | solution.py:546
  17.2 2.7 %collective-permute-done.4.refs_1_ = f32[2,5,8,128]{3,2,1,0:T(8,128)S(1)} collective-permute-done((f32[2,5,8,128]{3,2,1,0:T(8,128)S(1)}, f32[2,5,8,128]{3,2,1,0:T(8,128)S(1)}, u32[]{:S(2)}, u32[]{:S(2)}) %collective-permute-start.4) | collective-permute-done | bytes 40992 | tf_op jit(solution)/shard_map/ppermute | solution.py:546
  19.9 1.1 %collective-permute-done.6.refs_3_ = f32[2,5,8,128]{3,2,1,0:T(8,128)S(1)} collective-permute-done((f32[2,5,8,128]{3,2,1,0:T(8,128)S(1)}, f32[2,5,8,128]{3,2,1,0:T(8,128)S(1)}, u32[]{:S(2)}, u32[]{:S(2)}) %collective-permute-start.6) | collective-permute-done | bytes 40992 | tf_op jit(solution)/shard_map/ppermute | solution.py:546
  21.1 0.8 %shard_map.89 = (f32[1,5,8,128]{3,2,1,0:T(8,128)S(1)}, f32[2,3,4,128]{3,2,1,0:T(4,128)S(1)}, f32[7,8,128]{2,1,0:T(8,128)S(1)}, f32[7,8,128]{2,1,0:T(8,128)S(1)}) custom-call(s32[4,4]{1,0:T(4,128)S(4)} %get-tuple-element.34.spots_ref, f32[4,2,16,512]{3,2,1,0:T(8,128)S(1)} %get-tuple-element.35.jac_ref, ...), custom_call_target="tpu_custom_call" | custom-call | tf_op jit(solution)/shard_map/pallas_call | solution.py:576
  21.8 2.1 %collective-permute-start.9 = (f32[1,5,8,128]{3,2,1,0:T(8,128)S(1)}, f32[1,5,8,128]{3,2,1,0:T(8,128)S(1)}, u32[]{:S(2)}, u32[]{:S(2)}) collective-permute-start(f32[1,5,8,128]{3,2,1,0:T(8,128)S(1)} %get-tuple-element.52.refs_0_), channel_id=1, source_target_pairs={{0,25},{1,24},{2,27},{3,26},{4,29},{5,28},{6,31},{7,30},{8,17},{9,... | collective-permute-start | bytes 61448 | tf_op jit(solution)/shard_map/ppermute | solution.py:546
  24.0 0.6 %collective-permute-start.8 = (f32[1,5,8,128]{3,2,1,0:T(8,128)S(1)}, f32[1,5,8,128]{3,2,1,0:T(8,128)S(1)}, u32[]{:S(2)}, u32[]{:S(2)}) collective-permute-start(f32[1,5,8,128]{3,2,1,0:T(8,128)S(1)} %get-tuple-element.52.refs_0_), channel_id=1, source_target_pairs={{0,17},{1,16},{2,19},{3,18},{4,21},{5,20},{6,23},{7,22},{8,25},{9,... | collective-permute-start | bytes 61448 | tf_op jit(solution)/shard_map/ppermute | solution.py:546
  24.6 1.2 %collective-permute-start.7 = (f32[1,5,8,128]{3,2,1,0:T(8,128)S(1)}, f32[1,5,8,128]{3,2,1,0:T(8,128)S(1)}, u32[]{:S(2)}, u32[]{:S(2)}) collective-permute-start(f32[1,5,8,128]{3,2,1,0:T(8,128)S(1)} %get-tuple-element.52.refs_0_), channel_id=1, source_target_pairs={{0,9},{1,8},{2,11},{3,10},{4,13},{5,12},{6,15},{7,14},{8,1},{9,0},... | collective-permute-start | bytes 61448 | tf_op jit(solution)/shard_map/ppermute | solution.py:546
  25.7 1.2 %collective-permute-done.9.refs_3_ = f32[1,5,8,128]{3,2,1,0:T(8,128)S(1)} collective-permute-done((f32[1,5,8,128]{3,2,1,0:T(8,128)S(1)}, f32[1,5,8,128]{3,2,1,0:T(8,128)S(1)}, u32[]{:S(2)}, u32[]{:S(2)}) %collective-permute-start.9) | collective-permute-done | bytes 20512 | tf_op jit(solution)/shard_map/ppermute | solution.py:546
  26.9 1.3 %collective-permute-done.8.refs_2_ = f32[1,5,8,128]{3,2,1,0:T(8,128)S(1)} collective-permute-done((f32[1,5,8,128]{3,2,1,0:T(8,128)S(1)}, f32[1,5,8,128]{3,2,1,0:T(8,128)S(1)}, u32[]{:S(2)}, u32[]{:S(2)}) %collective-permute-start.8) | collective-permute-done | bytes 20512 | tf_op jit(solution)/shard_map/ppermute | solution.py:546
  28.9 0.9 %collective-permute-done.10.other_ref = f32[1,19,8,128]{3,2,1,0:T(8,128)S(1)} collective-permute-done((f32[1,19,8,128]{3,2,1,0:T(8,128)S(1)}, f32[1,19,8,128]{3,2,1,0:T(8,128)S(1)}, u32[]{:S(2)}, u32[]{:S(2)}) %collective-permute-start.10) | collective-permute-done | bytes 77856 | tf_op jit(solution)/shard_map/ppermute | solution.py:546
  29.9 1.4 %collective-permute-start.12 = (f32[1,7,8,128]{3,2,1,0:T(8,128)S(1)}, f32[1,7,8,128]{3,2,1,0:T(8,128)S(1)}, u32[]{:S(2)}, u32[]{:S(2)}) collective-permute-start(f32[1,7,8,128]{3,2,1,0:T(8,128)S(1)} %get-tuple-element.57), channel_id=1, source_target_pairs={{0,5},{1,4},{2,7},{3,6},{4,1},{5,0},{6,3},{7,2},{8,13},{9,12},{10,... | collective-permute-start | bytes 86024 | tf_op jit(solution)/shard_map/ppermute | solution.py:546
  31.3 0.9 %collective-permute-start.11 = (f32[1,5,8,128]{3,2,1,0:T(8,128)S(1)}, f32[1,5,8,128]{3,2,1,0:T(8,128)S(1)}, u32[]{:S(2)}, u32[]{:S(2)}) collective-permute-start(f32[1,5,8,128]{3,2,1,0:T(8,128)S(1)} %get-tuple-element.56), channel_id=1, source_target_pairs={{0,7},{1,6},{2,5},{3,4},{4,3},{5,2},{6,1},{7,0},{8,15},{9,14},{10,... | collective-permute-start | bytes 61448 | tf_op jit(solution)/shard_map/ppermute | solution.py:546
  32.2 0.9 %collective-permute-start.13 = (f32[1,5,8,128]{3,2,1,0:T(8,128)S(1)}, f32[1,5,8,128]{3,2,1,0:T(8,128)S(1)}, u32[]{:S(2)}, u32[]{:S(2)}) collective-permute-start(f32[1,5,8,128]{3,2,1,0:T(8,128)S(1)} %get-tuple-element.58), channel_id=1, source_target_pairs={{0,3},{1,2},{2,1},{3,0},{4,7},{5,6},{6,5},{7,4},{8,11},{9,10},{10,... | collective-permute-start | bytes 61448 | tf_op jit(solution)/shard_map/ppermute | solution.py:546
  33.1 2.4 %collective-permute-done.11.refs_1_ = f32[1,5,8,128]{3,2,1,0:T(8,128)S(1)} collective-permute-done((f32[1,5,8,128]{3,2,1,0:T(8,128)S(1)}, f32[1,5,8,128]{3,2,1,0:T(8,128)S(1)}, u32[]{:S(2)}, u32[]{:S(2)}) %collective-permute-start.11) | collective-permute-done | bytes 20512 | tf_op jit(solution)/shard_map/ppermute | solution.py:546
  35.9 0.7 %shard_map.92 = (f32[32,1,128]{2,1,0:T(1,128)S(1)}, f32[8,128]{1,0:T(8,128)S(1)}, f32[2,576]{1,0:T(2,128)S(1)}, f32[3,4,128]{2,1,0:T(4,128)S(1)}) custom-call(s32[4,4]{1,0:T(4,128)S(4)} %get-tuple-element.34.spots_ref, f32[4,2,16,512]{3,2,1,0:T(8,128)S(1)} %get-tuple-element.35.jac_ref, bf16[4,512,128]{2,1,0:T(8,128)(2,1)S(1)} %get-tuple-element.36.land_hot_ref, ...), custom_call_target="tpu_custom_call" | custom-call | tf_op jit(solution)/shard_map/pallas_call | solution.py:576
  36.6 9.9 %all_to_all.5.sums_ref = f32[32,1,128]{2,1,0:T(1,128)S(1)} all-to-all(f32[32,1,128]{2,1,0:T(1,128)S(1)} %get-tuple-element.59), channel_id=1, replica_groups=mesh['row'=8,'col'=4] {'row','col'}, dimensions={0} | all-to-all | bytes 32768 | tf_op jit(solution)/shard_map/all_to_all | solution.py:658
  46.5 0.7 %shard_map.93 = (f32[576]{0:T(1024)}, f32[3,4,128]{2,1,0:T(4,128)}) custom-call(f32[32,1,128]{2,1,0:T(1,128)S(1)} %all_to_all.5.sums_ref, f32[8,128]{1,0:T(8,128)S(1)} %get-tuple-element.60.known_ref, f32[2,576]{1,0:T(2,128)S(1)} %get-tuple-element.61.cam_ref, f32[2,3,4,128]{3,2,1,0:T(4,128)S(1)} %get-tuple-element.62.back_ref, ...), custom_call_target="tpu_custom_call" | custom-call | tf_op jit(solution)/shard_map/pallas_call | solution.py:576
  (13 shorter events, 2.1 us)
Async XLA Ops:
  3.0 6.5 %collective-permute-start.2 = (f32[2,5,8,128]{3,2,1,0:T(8,128)S(1)}, f32[2,5,8,128]{3,2,1,0:T(8,128)S(1)}, u32[]{:S(2)}, u32[]{:S(2)}) collective-permute-start(f32[2,5,8,128]{3,2,1,0:T(8,128)S(1)} %get-tuple-element.43.refs_0_), channel_id=1, source_target_pairs={{0,25},{1,24},{2,27},{3,26},{4,29},{5,28},{6,31},{7,30},{8,17},{9,... | collective-permute-start | bytes 122888 | tf_op jit(solution)/shard_map/ppermute | solution.py:546
  7.6 4.7 %collective-permute-start.1 = (f32[2,5,8,128]{3,2,1,0:T(8,128)S(1)}, f32[2,5,8,128]{3,2,1,0:T(8,128)S(1)}, u32[]{:S(2)}, u32[]{:S(2)}) collective-permute-start(f32[2,5,8,128]{3,2,1,0:T(8,128)S(1)} %get-tuple-element.43.refs_0_), channel_id=1, source_target_pairs={{0,17},{1,16},{2,19},{3,18},{4,21},{5,20},{6,23},{7,22},{8,25},{9,... | collective-permute-start | bytes 122888 | tf_op jit(solution)/shard_map/ppermute | solution.py:546
  7.6 4.7 %collective-permute-start = (f32[2,5,8,128]{3,2,1,0:T(8,128)S(1)}, f32[2,5,8,128]{3,2,1,0:T(8,128)S(1)}, u32[]{:S(2)}, u32[]{:S(2)}) collective-permute-start(f32[2,5,8,128]{3,2,1,0:T(8,128)S(1)} %get-tuple-element.43.refs_0_), channel_id=1, source_target_pairs={{0,9},{1,8},{2,11},{3,10},{4,13},{5,12},{6,15},{7,14},{8,1},{9,0},... | collective-permute-start | bytes 122888 | tf_op jit(solution)/shard_map/ppermute | solution.py:546
  12.5 1.4 %collective-permute-start.3 = (f32[2,19,8,128]{3,2,1,0:T(8,128)S(1)}, f32[2,19,8,128]{3,2,1,0:T(8,128)S(1)}, u32[]{:S(2)}, u32[]{:S(2)}) collective-permute-start(f32[2,19,8,128]{3,2,1,0:T(8,128)S(1)} %get-tuple-element.45), channel_id=1, source_target_pairs={{0,1},{1,0},{2,3},{3,2},{4,5},{5,4},{6,7},{7,6},{8,9},{9,8},{10,11... | collective-permute-start | bytes 466952 | tf_op jit(solution)/shard_map/ppermute | solution.py:546
  14.0 7.1 %collective-permute-start.5 = (f32[2,7,8,128]{3,2,1,0:T(8,128)S(1)}, f32[2,7,8,128]{3,2,1,0:T(8,128)S(1)}, u32[]{:S(2)}, u32[]{:S(2)}) collective-permute-start(f32[2,7,8,128]{3,2,1,0:T(8,128)S(1)} %get-tuple-element.48), channel_id=1, source_target_pairs={{0,5},{1,4},{2,7},{3,6},{4,1},{5,0},{6,3},{7,2},{8,13},{9,12},{10,... | collective-permute-start | bytes 172040 | tf_op jit(solution)/shard_map/ppermute | solution.py:546
  15.5 4.5 %collective-permute-start.4 = (f32[2,5,8,128]{3,2,1,0:T(8,128)S(1)}, f32[2,5,8,128]{3,2,1,0:T(8,128)S(1)}, u32[]{:S(2)}, u32[]{:S(2)}) collective-permute-start(f32[2,5,8,128]{3,2,1,0:T(8,128)S(1)} %get-tuple-element.47), channel_id=1, source_target_pairs={{0,7},{1,6},{2,5},{3,4},{4,3},{5,2},{6,1},{7,0},{8,15},{9,14},{10,... | collective-permute-start | bytes 122888 | tf_op jit(solution)/shard_map/ppermute | solution.py:546
  16.8 4.3 %collective-permute-start.6 = (f32[2,5,8,128]{3,2,1,0:T(8,128)S(1)}, f32[2,5,8,128]{3,2,1,0:T(8,128)S(1)}, u32[]{:S(2)}, u32[]{:S(2)}) collective-permute-start(f32[2,5,8,128]{3,2,1,0:T(8,128)S(1)} %get-tuple-element.49), channel_id=1, source_target_pairs={{0,3},{1,2},{2,1},{3,0},{4,7},{5,6},{6,5},{7,4},{8,11},{9,10},{10,... | collective-permute-start | bytes 122888 | tf_op jit(solution)/shard_map/ppermute | solution.py:546
  21.8 5.1 %collective-permute-start.9 = (f32[1,5,8,128]{3,2,1,0:T(8,128)S(1)}, f32[1,5,8,128]{3,2,1,0:T(8,128)S(1)}, u32[]{:S(2)}, u32[]{:S(2)}) collective-permute-start(f32[1,5,8,128]{3,2,1,0:T(8,128)S(1)} %get-tuple-element.52.refs_0_), channel_id=1, source_target_pairs={{0,25},{1,24},{2,27},{3,26},{4,29},{5,28},{6,31},{7,30},{8,17},{9,... | collective-permute-start | bytes 61448 | tf_op jit(solution)/shard_map/ppermute | solution.py:546
  24.0 4.3 %collective-permute-start.8 = (f32[1,5,8,128]{3,2,1,0:T(8,128)S(1)}, f32[1,5,8,128]{3,2,1,0:T(8,128)S(1)}, u32[]{:S(2)}, u32[]{:S(2)}) collective-permute-start(f32[1,5,8,128]{3,2,1,0:T(8,128)S(1)} %get-tuple-element.52.refs_0_), channel_id=1, source_target_pairs={{0,17},{1,16},{2,19},{3,18},{4,21},{5,20},{6,23},{7,22},{8,25},{9,... | collective-permute-start | bytes 61448 | tf_op jit(solution)/shard_map/ppermute | solution.py:546
  24.6 3.7 %collective-permute-start.7 = (f32[1,5,8,128]{3,2,1,0:T(8,128)S(1)}, f32[1,5,8,128]{3,2,1,0:T(8,128)S(1)}, u32[]{:S(2)}, u32[]{:S(2)}) collective-permute-start(f32[1,5,8,128]{3,2,1,0:T(8,128)S(1)} %get-tuple-element.52.refs_0_), channel_id=1, source_target_pairs={{0,9},{1,8},{2,11},{3,10},{4,13},{5,12},{6,15},{7,14},{8,1},{9,0},... | collective-permute-start | bytes 61448 | tf_op jit(solution)/shard_map/ppermute | solution.py:546
  28.4 1.4 %collective-permute-start.10 = (f32[1,19,8,128]{3,2,1,0:T(8,128)S(1)}, f32[1,19,8,128]{3,2,1,0:T(8,128)S(1)}, u32[]{:S(2)}, u32[]{:S(2)}) collective-permute-start(f32[1,19,8,128]{3,2,1,0:T(8,128)S(1)} %get-tuple-element.54), channel_id=1, source_target_pairs={{0,1},{1,0},{2,3},{3,2},{4,5},{5,4},{6,7},{7,6},{8,9},{9,8},{10,11... | collective-permute-start | bytes 233480 | tf_op jit(solution)/shard_map/ppermute | solution.py:546
  29.9 6.1 %collective-permute-start.12 = (f32[1,7,8,128]{3,2,1,0:T(8,128)S(1)}, f32[1,7,8,128]{3,2,1,0:T(8,128)S(1)}, u32[]{:S(2)}, u32[]{:S(2)}) collective-permute-start(f32[1,7,8,128]{3,2,1,0:T(8,128)S(1)} %get-tuple-element.57), channel_id=1, source_target_pairs={{0,5},{1,4},{2,7},{3,6},{4,1},{5,0},{6,3},{7,2},{8,13},{9,12},{10,... | collective-permute-start | bytes 86024 | tf_op jit(solution)/shard_map/ppermute | solution.py:546
  31.3 4.2 %collective-permute-start.11 = (f32[1,5,8,128]{3,2,1,0:T(8,128)S(1)}, f32[1,5,8,128]{3,2,1,0:T(8,128)S(1)}, u32[]{:S(2)}, u32[]{:S(2)}) collective-permute-start(f32[1,5,8,128]{3,2,1,0:T(8,128)S(1)} %get-tuple-element.56), channel_id=1, source_target_pairs={{0,7},{1,6},{2,5},{3,4},{4,3},{5,2},{6,1},{7,0},{8,15},{9,14},{10,... | collective-permute-start | bytes 61448 | tf_op jit(solution)/shard_map/ppermute | solution.py:546
  32.2 3.7 %collective-permute-start.13 = (f32[1,5,8,128]{3,2,1,0:T(8,128)S(1)}, f32[1,5,8,128]{3,2,1,0:T(8,128)S(1)}, u32[]{:S(2)}, u32[]{:S(2)}) collective-permute-start(f32[1,5,8,128]{3,2,1,0:T(8,128)S(1)} %get-tuple-element.58), channel_id=1, source_target_pairs={{0,3},{1,2},{2,1},{3,0},{4,7},{5,6},{6,5},{7,4},{8,11},{9,10},{10,... | collective-permute-start | bytes 61448 | tf_op jit(solution)/shard_map/ppermute | solution.py:546
